TPU v7x, 32 devices: a whole 2x2x4 slice. The times are simulated.
32 devices in a mesh: pipe: 4 (over z), seq: 8 (over y, x, core).
Axes of the slice: x: 2, y: 2, z: 4, core: 2. Of those that a mesh axis runs over, the one named last changes fastest.
Arguments:
- section_input: bfloat16 [4, 2048, 1024], P('pipe', 'seq'), may hold values from -6 to 6
- saved_input: bfloat16 [4, 2048, 1024], P('pipe', 'seq'), may hold values from -6 to 6
- grad_output: bfloat16 [4, 2048, 1024], P('pipe', 'seq'), may hold values from -6 to 6
- w_qkv: bfloat16 [4, 3072, 1024], P('pipe'), may hold values from -0.1875 to 0.1875
- w_out: bfloat16 [4, 1024, 1024], P('pipe'), may hold values from -0.75 to 0.75
- tile_cluster: int32 [16], replicated, may hold values from 0 to 7, as said below
Outputs:
- next_input: bfloat16 [4, 2048, 1024], P('pipe', 'seq')
- grad_input: bfloat16 [4, 2048, 1024], P('pipe', 'seq')
Inputs may be any that keep to these rules, and one draw needn't show every extreme that they name: `tile_cluster`: each of the 8 ids names between 1 and 3 tiles, and some id names exactly 3. The id of tile i leaves the remainder i % 1 when divided by 1.
All inputs are finite; a program needn't handle non-finite values.
Results may differ from a plain program's by a relative error of at most 0.007.
Values may be sent and summed in bfloat16 or wider, within the bound.
No kernel may reach another device: no remote copies, remote signals or barrier semaphores. Data moves between devices by JAX's collectives and lax.ppermute only.
A program may use at most 128 MiB of HBM per device.

v0:
```python
import functools

import jax
import jax.numpy as jnp
from jax import lax
from jax.experimental import pallas as pl
from jax.experimental.pallas import tpu as pltpu
from jax.sharding import PartitionSpec as P

HEADS = 8
HD = 128
TILE = 128
EPSILON = 1e-05
VMEM_LIMIT = 48 * 1024 * 1024
NT = (((1,), (1,)), ((), ()))
NN = (((1,), (0,)), ((), ()))
TN = (((0,), (0,)), ((), ()))


def dot(left, right, dims):
    return lax.dot_general(left, right, dims, preferred_element_type=jnp.float32)


def vmem():
    return pl.BlockSpec(memory_space=pltpu.VMEM)


def params():
    return pltpu.CompilerParams(vmem_limit_bytes=VMEM_LIMIT)


def rows_rsqrt(values):
    return lax.rsqrt(jnp.mean(values * values, axis=-1, keepdims=True) + EPSILON)


def project_kernel(parts, group, *refs):
    if parts == 4:
        x_ref, up_ref, w_ref, wo_ref, out_ref, scale_ref, normed = refs
    else:
        x_ref, w_ref, out_ref, normed = refs
    part, block = pl.program_id(0), pl.program_id(1)

    @pl.when((part == 0) & (block == 0))
    def _():
        x = x_ref[...].astype(jnp.float32)
        normed[...] = (x * rows_rsqrt(x)).astype(jnp.bfloat16)

    @pl.when(part < 3)
    def _():
        mixed = dot(normed[...], w_ref[...], NT)
        for j in range(group):
            u = mixed[:, j * HD : (j + 1) * HD]
            scale = jnp.where(part < 2, rows_rsqrt(u), 1.0)
            out_ref[j, 0] = (u * scale).astype(jnp.bfloat16)
            if parts == 4:
                lane = lax.broadcasted_iota(jnp.int32, (u.shape[0], HD), 1)
                column = part * HEADS + block * group + j

                @pl.when(part < 2)
                def _():
                    scale_ref[...] = jnp.where(lane == column, scale, scale_ref[...])

    if parts == 4:

        @pl.when(part == 3)
        def _():
            g = dot(up_ref[...], wo_ref[...], NT)
            for j in range(group):
                out_ref[j, 0] = g[:, j * HD : (j + 1) * HD].astype(jnp.bfloat16)


def project(x, w_rows, up=None, w_fin=None):
    tokens, width = x.shape
    group = 4
    blocks = HEADS // group
    parts = 3 if up is None else 4
    whole = pl.BlockSpec((tokens, width), lambda p, b: (0, 0))
    w_spec = pl.BlockSpec(
        (group * HD, width),
        lambda p, b: (jnp.where(p < 3, p * blocks + b, 3 * blocks - 1), 0),
    )
    wo_spec = pl.BlockSpec((group * HD, width), lambda p, b: (jnp.where(p < 3, 0, b), 0))
    out_spec = pl.BlockSpec((group, 1, tokens, HD), lambda p, b: (b, p, 0, 0))
    out = jax.ShapeDtypeStruct((HEADS, parts, tokens, HD), jnp.bfloat16)
    if up is None:
        operands, in_specs = (x, w_rows), [whole, w_spec]
        outs, out_specs = out, out_spec
    else:
        operands, in_specs = (x, up, w_rows, w_fin), [whole, whole, w_spec, wo_spec]
        outs = (out, jax.ShapeDtypeStruct((tokens, HD), jnp.float32))
        out_specs = (out_spec, pl.BlockSpec((tokens, HD), lambda p, b: (0, 0)))
    return pl.pallas_call(
        functools.partial(project_kernel, parts, group),
        grid=(parts, blocks),
        in_specs=in_specs,
        out_specs=out_specs,
        out_shape=outs,
        scratch_shapes=[pltpu.VMEM((tokens, width), jnp.bfloat16)],
        compiler_params=params(),
        cost_estimate=pl.CostEstimate(
            flops=2 * parts * tokens * width * HEADS * HD,
            bytes_accessed=2 * parts * width * HEADS * HD,
            transcendentals=0,
        ),
    )(*operands)


def forward_body(n, tiles, in_ref, out_ref):
    def load(c):
        return jnp.concatenate([in_ref[t // 2, c, t % 2] for t in tiles], axis=0)

    q, k, v = load(0), load(1), load(2)
    weights = jnp.exp(dot(q, k, NT) * (HD ** -0.5)).astype(jnp.bfloat16)
    wide = jnp.concatenate([v, jnp.ones_like(v)], axis=1)
    sums = dot(weights, wide, NN)
    result = (sums[:, :HD] / sums[:, HD:]).astype(jnp.bfloat16)
    for i, t in enumerate(tiles):
        out_ref[t // 2, 0, t % 2] = result[i * TILE : (i + 1) * TILE]


def backward_body(n, tiles, in_ref, out_ref):
    def load(c):
        return jnp.concatenate([in_ref[t // 2, c, t % 2] for t in tiles], axis=0)

    q, k, v, g = load(0), load(1), load(2), load(3)
    factor = HD ** -0.5
    weights = jnp.exp(dot(k, q, NT) * factor)
    softmax = weights * (1.0 / jnp.sum(weights, axis=0, keepdims=True))
    soft_low = softmax.astype(jnp.bfloat16)
    grad_soft = dot(v, g, NT)
    delta = jnp.sum(soft_low.astype(jnp.float32) * grad_soft, axis=0, keepdims=True)
    grad_scores = (softmax * (grad_soft - delta)).astype(jnp.bfloat16)
    results = (
        dot(grad_scores, k, TN) * factor,
        dot(grad_scores, q, NN) * factor,
        dot(soft_low, g, NN),
    )
    for c, result in enumerate(results):
        low = result.astype(jnp.bfloat16)
        for i, t in enumerate(tiles):
            out_ref[t // 2, c, t % 2] = low[i * TILE : (i + 1) * TILE]


def attend_kernel(body, clusters, capacity, spacing, cluster_ref, res_ref, in_ref, out_ref, count, member):
    tiles = in_ref.shape[0] * in_ref.shape[2]
    for c in range(clusters):
        count[c] = 0

    def enter(t, carry):
        c = cluster_ref[t * spacing + res_ref[0]] // spacing
        place = count[c]
        member[c * capacity + place] = t
        count[c] = place + 1
        return carry

    lax.fori_loop(0, tiles, enter, 0)

    def visit(c, carry):
        for n in range(1, capacity + 1):

            @pl.when(count[c] == n)
            def _():
                body(n, [member[c * capacity + i] for i in range(n)], in_ref, out_ref)

        return carry

    lax.fori_loop(0, clusters, visit, 0)


def attend(body, tile_cluster, residue, arrived, spacing, parts_out, flops):
    sources, parts, tokens, _ = arrived.shape
    tiled = arrived.reshape(sources * tokens // (2 * TILE), parts, 2, TILE, HD)
    tiles = 2 * tiled.shape[0]
    clusters = tiles // 2
    capacity = 3
    smem = pl.BlockSpec(memory_space=pltpu.SMEM)
    out = pl.pallas_call(
        functools.partial(attend_kernel, body, clusters, capacity, spacing),
        in_specs=[smem, smem, vmem()],
        out_specs=vmem(),
        out_shape=jax.ShapeDtypeStruct((tiled.shape[0], parts_out, 2, TILE, HD), jnp.bfloat16),
        scratch_shapes=[
            pltpu.SMEM((clusters,), jnp.int32),
            pltpu.SMEM((clusters * capacity,), jnp.int32),
        ],
        compiler_params=params(),
        cost_estimate=pl.CostEstimate(flops=flops, bytes_accessed=1 << 21, transcendentals=0),
    )(tile_cluster, residue, tiled)
    return out.reshape(tiled.shape[0], parts_out, 2 * TILE, HD)


def finish_kernel(att_ref, x_ref, w_ref, out_ref):
    att = jnp.concatenate([att_ref[h, 0] for h in range(HEADS)], axis=1)
    update = dot(att, w_ref[...], NN)
    out_ref[...] = (x_ref[...].astype(jnp.float32) + update).astype(jnp.bfloat16)


def finish(attention, current, w_fin):
    tokens, width = current.shape
    block = 256
    return pl.pallas_call(
        finish_kernel,
        grid=(width // block,),
        in_specs=[
            pl.BlockSpec((HEADS, 1, tokens, HD), lambda b: (0, 0, 0, 0)),
            pl.BlockSpec((tokens, block), lambda b: (0, b)),
            pl.BlockSpec((HEADS * HD, block), lambda b: (0, b)),
        ],
        out_specs=pl.BlockSpec((tokens, block), lambda b: (0, b)),
        out_shape=jax.ShapeDtypeStruct((tokens, width), jnp.bfloat16),
        compiler_params=params(),
        cost_estimate=pl.CostEstimate(flops=1 << 29, bytes_accessed=1 << 22, transcendentals=0),
    )(attention, current, w_fin)


def finish_back_kernel(group, grad_ref, kept_ref, scale_ref, x_ref, up_ref, w_ref, out_ref, total):
    part, block = pl.program_id(0), pl.program_id(1)
    blocks = pl.num_programs(1)
    pieces = []
    lane = lax.broadcasted_iota(jnp.int32, scale_ref.shape, 1)
    for j in range(group):
        g = grad_ref[j, 0].astype(jnp.float32)
        unit = kept_ref[j, 0].astype(jnp.float32)
        column = part * HEADS + block * group + j
        scale = jnp.sum(jnp.where(lane == column, scale_ref[...], 0.0), axis=1, keepdims=True)
        pulled = scale * (g - unit * jnp.mean(unit * g, axis=1, keepdims=True))
        pieces.append(jnp.where(part < 2, pulled, g).astype(jnp.bfloat16))
    product = dot(jnp.concatenate(pieces, axis=1), w_ref[...], NN)
    first = (part == 0) & (block == 0)

    @pl.when(first)
    def _():
        total[...] = product

    @pl.when(jnp.logical_not(first))
    def _():
        total[...] += product

    @pl.when((part == 2) & (block == blocks - 1))
    def _():
        x = x_ref[...].astype(jnp.float32)
        scale = rows_rsqrt(x)
        unit = x * scale
        g = total[...]
        pulled = scale * (g - unit * jnp.mean(unit * g, axis=1, keepdims=True))
        out_ref[...] = (up_ref[...].astype(jnp.float32) + pulled).astype(jnp.bfloat16)


def finish_back(grads, kept, scales, stored, upstream, w_rows):
    tokens, width = stored.shape
    group = 4
    blocks = HEADS // group
    whole = pl.BlockSpec((tokens, width), lambda p, b: (0, 0))
    heads = pl.BlockSpec((group, 1, tokens, HD), lambda p, b: (b, p, 0, 0))
    return pl.pallas_call(
        functools.partial(finish_back_kernel, group),
        grid=(3, blocks),
        in_specs=[
            heads,
            heads,
            pl.BlockSpec((tokens, HD), lambda p, b: (0, 0)),
            whole,
            whole,
            pl.BlockSpec((group * HD, width), lambda p, b: (p * blocks + b, 0)),
        ],
        out_specs=whole,
        out_shape=jax.ShapeDtypeStruct((tokens, width), jnp.bfloat16),
        scratch_shapes=[pltpu.VMEM((tokens, width), jnp.float32)],
        compiler_params=params(),
        cost_estimate=pl.CostEstimate(flops=3 << 29, bytes_accessed=1 << 23, transcendentals=0),
    )(grads, kept, scales, stored, upstream, w_rows)


def all_swap(blocks):
    return lax.all_to_all(blocks, "seq", split_axis=0, concat_axis=0, tiled=True)


def to_heads(headed, own, spacing):
    if spacing == 1:
        return all_swap(headed)
    heads, parts, tokens, _ = headed.shape
    held = tokens // TILE
    places = spacing // held
    tiled = headed.reshape(heads, parts, held, TILE, HD).transpose(0, 2, 1, 3, 4)
    padded = jnp.zeros((heads, places, held, parts, TILE, HD), headed.dtype)
    padded = lax.dynamic_update_slice_in_dim(padded, tiled[:, None], own % places, 1)
    arrived = all_swap(padded.reshape(heads * spacing, parts, TILE, HD))
    arrived = arrived.reshape(-1, places, parts, TILE, HD)
    mine = lax.dynamic_index_in_dim(arrived, own % spacing // held, 1, keepdims=False)
    paired = mine.reshape(-1, 2, parts, TILE, HD).transpose(0, 2, 1, 3, 4)
    return paired.reshape(-1, parts, 2 * TILE, HD)


def to_tokens(results, own, spacing, tokens):
    if spacing == 1:
        return all_swap(results)
    sources, parts, _, _ = results.shape
    held = tokens // TILE
    places = spacing // held
    tiled = results.reshape(sources, parts, 2, TILE, HD).transpose(0, 2, 1, 3, 4)
    tiled = tiled.reshape(-1, 1, parts, TILE, HD)
    padded = jnp.zeros((tiled.shape[0], places, parts, TILE, HD), results.dtype)
    padded = lax.dynamic_update_slice_in_dim(padded, tiled, own % spacing // held, 1)
    returned = all_swap(padded.reshape(-1, parts, TILE, HD))
    returned = returned.reshape(HEADS, places, held, parts, TILE, HD)
    mine = lax.dynamic_index_in_dim(returned, own % places, 1, keepdims=False)
    return mine.transpose(0, 2, 1, 3, 4).reshape(HEADS, parts, tokens, HD)


def passed_along(block, axis, distance):
    devices = range(lax.axis_size(axis))
    route = [(i - distance, i) for i in devices if i - distance in devices]
    return lax.ppermute(block, axis, route)


def per_device(section_input, saved_input, grad_output, w_qkv, w_out, tile_cluster):
    current, stored, upstream = section_input[0], saved_input[0], grad_output[0]
    w_rows, w_fin = w_qkv[0], w_out[0]
    tokens = current.shape[0]
    spacing = lax.axis_size("seq") // HEADS
    own = lax.axis_index("seq")
    residue = (own % spacing).astype(jnp.int32)[None]
    visit = functools.partial(attend, spacing=spacing)

    sent = project(current, w_rows)
    arrived = to_heads(sent, own, spacing)
    sent_back, scales = project(stored, w_rows, upstream, w_fin)
    arrived_back = to_heads(sent_back, own, spacing)
    outputs = visit(forward_body, tile_cluster, residue, arrived, parts_out=1, flops=1 << 30)
    returned = to_tokens(outputs, own, spacing, tokens)
    grads = visit(backward_body, tile_cluster, residue, arrived_back, parts_out=3, flops=3 << 30)
    returned_back = to_tokens(grads, own, spacing, tokens)
    result = finish(returned, current, w_fin)
    next_input = passed_along(result, "pipe", 1)
    grad_self = finish_back(returned_back, sent_back, scales, stored, upstream, w_rows)
    grad_input = passed_along(grad_self, "pipe", -1)
    return (next_input[None], grad_input[None])


def solution(mesh):
    return jax.shard_map(
        per_device,
        mesh=mesh,
        in_specs=(
            P("pipe", "seq", None),
            P("pipe", "seq", None),
            P("pipe", "seq", None),
            P("pipe", None, None),
            P("pipe", None, None),
            P(),
        ),
        out_specs=(P("pipe", "seq", None), P("pipe", "seq", None)),
        check_vma=False,
    )
```

profile of v0, /device:TPU:18, one launch (start us, length us, event | category | flops | bytes accessed | tf_op | source)
XLA Modules:
  0.0 132.1 jit_solution(546879378738594179)
XLA Ops:
  0.6 0.0 copy-start.4
  0.6 1.0 copy-done.4
  1.7 6.7 %shard_map.77 = bf16[8,3,256,128]{3,2,1,0:T(8,128)(2,1)S(1)} custom-call(bf16[256,1024]{1,0:T(8,128)(2,1)S(1)} %bitcast.13, bf16[3072,1024]{1,0:T(8,128)(2,1)} %bitcast.20), custom_call_target="tpu_custom_call" | custom-call | flops 1610612736 | bytes 6291456 | tf_op jit(solution)/shard_map/pallas_call | solution.py:92
  8.4 0.0 copy-start.3
  8.4 1.1 copy-done.3
  9.5 0.0 copy-start
  9.5 0.0 copy-start.6
  9.5 0.0 copy-start.7
  9.5 5.0 %all-to-all-start = ((bf16[8,3,256,128]{3,2,1,0:T(8,128)(2,1)}), bf16[8,3,256,128]{3,2,1,0:T(8,128)(2,1)}, u32[]{:S(2)}, u32[]{:S(2)}) async-start(bf16[8,3,256,128]{3,2,1,0:T(8,128)(2,1)} %copy-done.3), calls=%async_computation | async-start | bytes 3145728 | tf_op jit(solution)/shard_map/all_to_all | solution.py:275
  14.5 0.0 copy-done
  14.5 0.0 copy-done.6
  14.5 0.0 copy-done.7
  14.5 8.9 %shard_map.80 = (bf16[8,4,256,128]{3,2,1,0:T(8,128)(2,1)S(1)}, f32[256,128]{1,0:T(8,128)S(1)}) custom-call(bf16[256,1024]{1,0:T(8,128)(2,1)S(1)} %bitcast.15, bf16[256,1024]{1,0:T(8,128)(2,1)S(1)} %bitcast.17, bf16[3072,1024]{1,0:T(8,128)(2,1)} %bitcast.21, bf16[1024,1024]{1,0:T(8,128)(2,1)S(1)} %bitcast.11), custom_call_target="tpu_custom_call" | custom-call | flops 2147483648 | bytes 8388608 | tf_op jit(solution)/shard_map/pallas_call | solution.py:92
  23.5 0.0 copy-start.1
  23.5 1.3 %copy-done.1 = bf16[8,4,256,128]{3,2,1,0:T(8,128)(2,1)} copy-done((bf16[8,4,256,128]{3,2,1,0:T(8,128)(2,1)}, bf16[8,4,256,128]{3,2,1,0:T(8,128)(2,1)S(1)}, u32[]{:S(2)}) %copy-start.1) | copy-done | bytes 2097176
  24.8 9.3 %all-to-all-done = bf16[8,3,256,128]{3,2,1,0:T(8,128)(2,1)} async-done(((bf16[8,3,256,128]{3,2,1,0:T(8,128)(2,1)}), bf16[8,3,256,128]{3,2,1,0:T(8,128)(2,1)}, u32[]{:S(2)}, u32[]{:S(2)}) %all-to-all-start) | async-done | bytes 1572896 | tf_op jit(solution)/shard_map/all_to_all | solution.py:275
  34.1 0.0 copy-start.10
  34.1 5.9 %all-to-all-start.2 = ((bf16[8,4,256,128]{3,2,1,0:T(8,128)(2,1)}), bf16[8,4,256,128]{3,2,1,0:T(8,128)(2,1)}, u32[]{:S(2)}, u32[]{:S(2)}) async-start(bf16[8,4,256,128]{3,2,1,0:T(8,128)(2,1)} %copy-done.1), calls=%async_computation.2 | async-start | bytes 4194304 | tf_op jit(solution)/shard_map/all_to_all | solution.py:275
  40.0 0.0 copy-done.10
  40.0 5.9 %shard_map.78 = bf16[8,1,2,128,128]{4,3,2,1,0:T(8,128)(2,1)} custom-call(s32[16]{0:T(128)S(1)} %copy-done.10, s32[1]{0:T(128)} %constant.15.clone.1.res_ref, bf16[8,3,2,128,128]{4,3,2,1,0:T(8,128)(2,1)} %bitcast.2.in_ref), custom_call_target="tpu_custom_call" | custom-call | flops 1073741824 | bytes 2097152 | tf_op jit(solution)/shard_map/pallas_call | solution.py:177
  45.9 19.3 %all-to-all-done.2 = bf16[8,4,256,128]{3,2,1,0:T(8,128)(2,1)} async-done(((bf16[8,4,256,128]{3,2,1,0:T(8,128)(2,1)}), bf16[8,4,256,128]{3,2,1,0:T(8,128)(2,1)}, u32[]{:S(2)}, u32[]{:S(2)}) %all-to-all-start.2) | async-done | bytes 2097184 | tf_op jit(solution)/shard_map/all_to_all | solution.py:275
  65.3 5.6 %all-to-all-start.1 = ((bf16[8,1,256,128]{3,2,1,0:T(8,128)(2,1)}), bf16[8,1,256,128]{3,2,1,0:T(8,128)(2,1)}, u32[]{:S(2)}, u32[]{:S(2)}) async-start(bf16[8,1,256,128]{3,2,1,0:T(8,128)(2,1)} %bitcast.3), calls=%async_computation.1 | async-start | bytes 1048576 | tf_op jit(solution)/shard_map/all_to_all | solution.py:275
  70.8 7.2 %shard_map.81 = bf16[8,3,2,128,128]{4,3,2,1,0:T(8,128)(2,1)S(1)} custom-call(s32[16]{0:T(128)S(1)} %copy-done.10, s32[1]{0:T(128)} %constant.15.clone.1.res_ref, bf16[8,4,2,128,128]{4,3,2,1,0:T(8,128)(2,1)} %bitcast.8.in_ref), custom_call_target="tpu_custom_call" | custom-call | flops 3221225472 | bytes 2097152 | tf_op jit(solution)/shard_map/pallas_call | solution.py:177
  78.0 0.0 copy-start.9
  78.0 1.2 copy-done.9
  79.2 0.0 copy-start.5
  79.2 0.1 all-to-all-done.1.att_ref
  79.2 5.7 %all-to-all-start.3 = ((bf16[8,3,256,128]{3,2,1,0:T(8,128)(2,1)}), bf16[8,3,256,128]{3,2,1,0:T(8,128)(2,1)}, u32[]{:S(2)}, u32[]{:S(2)}) async-start(bf16[8,3,256,128]{3,2,1,0:T(8,128)(2,1)} %bitcast.19), calls=%async_computation.3 | async-start | bytes 3145728 | tf_op jit(solution)/shard_map/all_to_all | solution.py:275
  84.9 0.0 copy-done.5
  84.9 3.5 %shard_map.79 = bf16[256,1024]{1,0:T(8,128)(2,1)} custom-call(bf16[8,1,256,128]{3,2,1,0:T(8,128)(2,1)} %all-to-all-done.1.att_ref, bf16[256,1024]{1,0:T(8,128)(2,1)S(1)} %bitcast.14, bf16[1024,1024]{1,0:T(8,128)(2,1)S(1)} %bitcast.12), custom_call_target="tpu_custom_call" | custom-call | flops 536870912 | bytes 4194304 | tf_op jit(solution)/shard_map/pallas_call | solution.py:201
  88.4 3.5 %collective-permute-start = (bf16[256,1024]{1,0:T(8,128)(2,1)}, bf16[256,1024]{1,0:T(8,128)(2,1)S(1)}, u32[]{:S(2)}, u32[]{:S(2)}) collective-permute-start(bf16[256,1024]{1,0:T(8,128)(2,1)} %shard_map.79), channel_id=1, source_target_pairs={{0,8},{8,16},{16,24},{1,9},{9,17},{17,25},{2,10},{10,18},{18,26},{... | collective-permute-start | bytes 1572872 | tf_op jit(solution)/shard_map/ppermute | solution.py:313
  91.9 12.7 %all-to-all-done.3.grad_ref = bf16[8,3,256,128]{3,2,1,0:T(8,128)(2,1)} async-done(((bf16[8,3,256,128]{3,2,1,0:T(8,128)(2,1)}), bf16[8,3,256,128]{3,2,1,0:T(8,128)(2,1)}, u32[]{:S(2)}, u32[]{:S(2)}) %all-to-all-start.3) | async-done | bytes 1572896 | tf_op jit(solution)/shard_map/all_to_all | solution.py:275
  104.5 0.0 copy-start.2
  104.5 1.6 %copy-done.2 = bf16[8,4,256,128]{3,2,1,0:T(8,128)(2,1)S(1)} copy-done((bf16[8,4,256,128]{3,2,1,0:T(8,128)(2,1)S(1)}, bf16[8,4,256,128]{3,2,1,0:T(8,128)(2,1)}, u32[]{:S(2)}) %copy-start.2) | copy-done | bytes 2097176
  106.1 0.0 copy-start.8
  106.1 1.0 copy-done.8
  107.2 7.5 %shard_map.82 = bf16[256,1024]{1,0:T(8,128)(2,1)S(1)} custom-call(bf16[8,3,256,128]{3,2,1,0:T(8,128)(2,1)} %all-to-all-done.3.grad_ref, bf16[8,4,256,128]{3,2,1,0:T(8,128)(2,1)S(1)} %copy-done.2, f32[256,128]{1,0:T(8,128)S(1)} %get-tuple-element.5.scale_ref, bf16[256,1024]{1,0:T(8,128)(2,1)S(1)} %bitcast.16, bf16[256,1024]{1,0:T(8,128)(2,1)S(1)} %bitcast.18, ...), custom_call_target="tpu_custom_call" | custom-call | flops 1610612736 | bytes 8388608 | tf_op jit(solution)/shard_map/pallas_call | solution.py:255
  114.7 2.4 %collective-permute-start.1 = (bf16[256,1024]{1,0:T(8,128)(2,1)S(1)}, bf16[256,1024]{1,0:T(8,128)(2,1)S(1)}, u32[]{:S(2)}, u32[]{:S(2)}) collective-permute-start(bf16[256,1024]{1,0:T(8,128)(2,1)S(1)} %shard_map.82), channel_id=1, source_target_pairs={{8,0},{16,8},{24,16},{9,1},{17,9},{25,17},{10,2},{18,10},{26,18},{... | collective-permute-start | bytes 1572872 | tf_op jit(solution)/shard_map/ppermute | solution.py:313
  117.1 0.0 collective-permute-done
  117.1 13.4 %collective-permute-done.1 = bf16[256,1024]{1,0:T(8,128)(2,1)S(1)} collective-permute-done((bf16[256,1024]{1,0:T(8,128)(2,1)S(1)}, bf16[256,1024]{1,0:T(8,128)(2,1)S(1)}, u32[]{:S(2)}, u32[]{:S(2)}) %collective-permute-start.1) | collective-permute-done | bytes 524320 | tf_op jit(solution)/shard_map/ppermute | solution.py:313
  130.5 0.8 copy.10
  131.3 0.8 copy.11
Async XLA Ops:
  0.6 1.0 copy-start.4
  8.4 1.1 copy-start.3
  9.5 5.0 %copy-start = (bf16[1,1024,1024]{2,1,0:T(8,128)(2,1)S(1)}, bf16[1,1024,1024]{2,1,0:T(8,128)(2,1)}, u32[]{:S(2)}) copy-start(bf16[1,1024,1024]{2,1,0:T(8,128)(2,1)} %param.10) | copy-start | bytes 6291460
  9.5 5.0 %copy-start.6 = (bf16[1,256,1024]{2,1,0:T(8,128)(2,1)S(1)}, bf16[1,256,1024]{2,1,0:T(8,128)(2,1)}, u32[]{:S(2)}) copy-start(bf16[1,256,1024]{2,1,0:T(8,128)(2,1)} %param.7) | copy-start | bytes 1572868
  9.5 5.0 %copy-start.7 = (bf16[1,256,1024]{2,1,0:T(8,128)(2,1)S(1)}, bf16[1,256,1024]{2,1,0:T(8,128)(2,1)}, u32[]{:S(2)}) copy-start(bf16[1,256,1024]{2,1,0:T(8,128)(2,1)} %param.8) | copy-start | bytes 1572868
  9.5 24.6 %all-to-all-start = ((bf16[8,3,256,128]{3,2,1,0:T(8,128)(2,1)}), bf16[8,3,256,128]{3,2,1,0:T(8,128)(2,1)}, u32[]{:S(2)}, u32[]{:S(2)}) async-start(bf16[8,3,256,128]{3,2,1,0:T(8,128)(2,1)} %copy-done.3), calls=%async_computation | async-start | bytes 3145728 | tf_op jit(solution)/shard_map/all_to_all | solution.py:275
  23.5 1.3 %copy-start.1 = (bf16[8,4,256,128]{3,2,1,0:T(8,128)(2,1)}, bf16[8,4,256,128]{3,2,1,0:T(8,128)(2,1)S(1)}, u32[]{:S(2)}) copy-start(bf16[8,4,256,128]{3,2,1,0:T(8,128)(2,1)S(1)} %get-tuple-element.4.kept_ref) | copy-start | bytes 6291460
  34.1 5.9 %copy-start.10 = (s32[16]{0:T(128)S(1)}, s32[16]{0:T(128)}, u32[]{:S(2)}) copy-start(s32[16]{0:T(128)} %cluster_ref.3) | copy-start | bytes 196
  34.1 31.1 %all-to-all-start.2 = ((bf16[8,4,256,128]{3,2,1,0:T(8,128)(2,1)}), bf16[8,4,256,128]{3,2,1,0:T(8,128)(2,1)}, u32[]{:S(2)}, u32[]{:S(2)}) async-start(bf16[8,4,256,128]{3,2,1,0:T(8,128)(2,1)} %copy-done.1), calls=%async_computation.2 | async-start | bytes 4194304 | tf_op jit(solution)/shard_map/all_to_all | solution.py:275
  65.3 14.0 %all-to-all-start.1 = ((bf16[8,1,256,128]{3,2,1,0:T(8,128)(2,1)}), bf16[8,1,256,128]{3,2,1,0:T(8,128)(2,1)}, u32[]{:S(2)}, u32[]{:S(2)}) async-start(bf16[8,1,256,128]{3,2,1,0:T(8,128)(2,1)} %bitcast.3), calls=%async_computation.1 | async-start | bytes 1048576 | tf_op jit(solution)/shard_map/all_to_all | solution.py:275
  78.0 1.2 copy-start.9
  79.2 5.7 %copy-start.5 = (bf16[1,256,1024]{2,1,0:T(8,128)(2,1)S(1)}, bf16[1,256,1024]{2,1,0:T(8,128)(2,1)}, u32[]{:S(2)}) copy-start(bf16[1,256,1024]{2,1,0:T(8,128)(2,1)} %param.6) | copy-start | bytes 1572868
  79.2 25.3 %all-to-all-start.3 = ((bf16[8,3,256,128]{3,2,1,0:T(8,128)(2,1)}), bf16[8,3,256,128]{3,2,1,0:T(8,128)(2,1)}, u32[]{:S(2)}, u32[]{:S(2)}) async-start(bf16[8,3,256,128]{3,2,1,0:T(8,128)(2,1)} %bitcast.19), calls=%async_computation.3 | async-start | bytes 3145728 | tf_op jit(solution)/shard_map/all_to_all | solution.py:275
  88.4 28.7 %collective-permute-start = (bf16[256,1024]{1,0:T(8,128)(2,1)}, bf16[256,1024]{1,0:T(8,128)(2,1)S(1)}, u32[]{:S(2)}, u32[]{:S(2)}) collective-permute-start(bf16[256,1024]{1,0:T(8,128)(2,1)} %shard_map.79), channel_id=1, source_target_pairs={{0,8},{8,16},{16,24},{1,9},{9,17},{17,25},{2,10},{10,18},{18,26},{... | collective-permute-start | bytes 1572872 | tf_op jit(solution)/shard_map/ppermute | solution.py:313
  104.5 1.6 %copy-start.2 = (bf16[8,4,256,128]{3,2,1,0:T(8,128)(2,1)S(1)}, bf16[8,4,256,128]{3,2,1,0:T(8,128)(2,1)}, u32[]{:S(2)}) copy-start(bf16[8,4,256,128]{3,2,1,0:T(8,128)(2,1)} %copy-done.1) | copy-start | bytes 6291460
  106.1 1.0 copy-start.8
  114.7 15.8 %collective-permute-start.1 = (bf16[256,1024]{1,0:T(8,128)(2,1)S(1)}, bf16[256,1024]{1,0:T(8,128)(2,1)S(1)}, u32[]{:S(2)}, u32[]{:S(2)}) collective-permute-start(bf16[256,1024]{1,0:T(8,128)(2,1)S(1)} %shard_map.82), channel_id=1, source_target_pairs={{8,0},{16,8},{24,16},{9,1},{17,9},{25,17},{10,2},{18,10},{26,18},{... | collective-permute-start | bytes 1572872 | tf_op jit(solution)/shard_map/ppermute | solution.py:313
where the time goes:
time: 133 us; the launch traced here: 132 us
  waiting for transfers between devices  54.8 us (41%)
  Pallas kernels  39.7 us (30%)
  starting transfers between devices  27.9 us (21%)
  local copies, waits for them, and re-layouts  8.88 us (7%)
    all_to_all x4, waiting for transfers between devices, all_swap(): lax.all_to_all(blocks, 'seq', split_axis=0, concat_axis=0, tiled=True)  41.4 us
    all_to_all x4, starting transfers between devices, all_swap(): lax.all_to_all(blocks, 'seq', split_axis=0, concat_axis=0, tiled=True)  22.1 us
    pallas_call x2, Pallas kernels, project(): pl.pallas_call(functools.partial(project_kernel, parts, group), grid=(par...  15.6 us
    ppermute x2, waiting for transfers between devices, passed_along(): return lax.ppermute(block, axis, route)  13.4 us
    pallas_call x2, Pallas kernels, attend(): pl.pallas_call(functools.partial(attend_kernel, body, clusters, capacity,...  13.1 us
    unnamed x24, local copies, waits for them, and re-layouts  8.88 us
    pallas_call x1, Pallas kernels, finish_back(): pl.pallas_call(functools.partial(finish_back_kernel, group), grid=(3, blo...  7.53 us
    ppermute x2, starting transfers between devices, passed_along(): return lax.ppermute(block, axis, route)  5.83 us
  transfers between devices with their start and end apart: 6, of which 5 were waited for; matrix products, arithmetic and copies ran while one was open for 0% of the time, Pallas kernels for 25%

commit v1 on v0

v1 whole, which is shorter than its diff:
```python
import functools

import jax
import jax.numpy as jnp
from jax import lax
from jax.experimental import pallas as pl
from jax.experimental.pallas import tpu as pltpu
from jax.sharding import PartitionSpec as P

HEADS = 8
HD = 128
TILE = 128
CAPACITY = 3
EPSILON = 1e-05
VMEM_LIMIT = 40 * 1024 * 1024
NT = (((1,), (1,)), ((), ()))
NN = (((1,), (0,)), ((), ()))
TN = (((0,), (0,)), ((), ()))
ANY = pl.BlockSpec(memory_space=pl.ANY)
SMEM = pl.BlockSpec(memory_space=pltpu.SMEM)
VMEM = pl.BlockSpec(memory_space=pltpu.VMEM)


def dot(left, right, dims):
    return lax.dot_general(left, right, dims, preferred_element_type=jnp.float32)


def low(values):
    return values.astype(jnp.bfloat16)


def high(values):
    return values.astype(jnp.float32)


def rows_rsqrt(values):
    return lax.rsqrt(jnp.mean(values * values, axis=-1, keepdims=True) + EPSILON)


def call(kernel, operands, in_specs, out_shape, scratch, flops, moved):
    many = isinstance(out_shape, tuple)
    return pl.pallas_call(
        kernel,
        in_specs=in_specs,
        out_specs=tuple(VMEM for _ in out_shape) if many else VMEM,
        out_shape=out_shape,
        scratch_shapes=scratch,
        compiler_params=pltpu.CompilerParams(vmem_limit_bytes=VMEM_LIMIT),
        cost_estimate=pl.CostEstimate(flops=flops, bytes_accessed=moved, transcendentals=0),
    )(*operands)


def fetch(source, target, sem):
    copy = pltpu.make_async_copy(source, target, sem)
    copy.start()
    return copy


def forward_cluster(tiles, kept, out):
    def load(c):
        return jnp.concatenate([kept[t, :, c * HD : (c + 1) * HD] for t in tiles], axis=0)

    q, k, v = load(0), load(1), load(2)
    weights = low(jnp.exp(dot(q, k, NT) * (HD ** -0.5)))
    wide = jnp.concatenate([v, jnp.ones_like(v)], axis=1)
    sums = dot(weights, wide, NN)
    result = low(sums[:, :HD] / sums[:, HD:])
    for i, t in enumerate(tiles):
        out[t] = result[i * TILE : (i + 1) * TILE]


def backward_cluster(tiles, kept, out, scales, grads):
    def load(c):
        return jnp.concatenate([kept[t, :, c * HD : (c + 1) * HD] for t in tiles], axis=0)

    def scale(c):
        return jnp.concatenate([scales[t, :, c * HD : (c + 1) * HD] for t in tiles], axis=0)

    q, k, v = load(0), load(1), load(2)
    g = jnp.concatenate([grads[t] for t in tiles], axis=0)
    factor = HD ** -0.5
    weights = jnp.exp(dot(k, q, NT) * factor)
    softmax = weights * (1.0 / jnp.sum(weights, axis=0, keepdims=True))
    soft_low = low(softmax)
    grad_soft = dot(v, g, NT)
    delta = jnp.sum(high(soft_low) * grad_soft, axis=0, keepdims=True)
    grad_scores = low(softmax * (grad_soft - delta))
    grad_values = low(dot(soft_low, g, NN))
    results = [grad_values]
    for c, unit, grad in (
        (1, k, dot(grad_scores, q, NN)),
        (0, q, dot(grad_scores, k, TN)),
    ):
        rounded = high(low(grad * factor))
        unit = high(unit)
        mean = jnp.mean(unit * rounded, axis=1, keepdims=True)
        results.append(low(scale(c) * (rounded - unit * mean)))
    for c, result in zip((2, 1, 0), results):
        for i, t in enumerate(tiles):
            out[t, :, c * HD : (c + 1) * HD] = result[i * TILE : (i + 1) * TILE]


def head_kernel(back, pieces, spacing, *refs):
    refs = list(refs)
    cluster_ref, info_ref = refs[:2]
    x_refs = refs[2 : 2 + len(pieces)]
    refs = refs[2 + len(pieces) :]
    g_refs = [refs.pop(0) for _ in range(HEADS if back else 0)]
    w_ref = refs.pop(0)
    out_refs = [refs.pop(0) for _ in range(HEADS)]
    xbuf, wbuf, turned, kept, out, count, member, xsem, wsem = refs[:9]
    flip, head, residue = info_ref[0], info_ref[1], info_ref[2]
    tiles = kept.shape[0]
    clusters = count.shape[0]

    weights = fetch(w_ref.at[:, head], wbuf, wsem)
    copies = []
    for i, (k, start, rows) in enumerate(pieces):
        copies.append(fetch(x_refs[i], xbuf.at[k, pl.ds(start, rows)], xsem.at[i]))
    if back:
        scales, grads, gsem = refs[9:]
        g_copies = []
        for k in range(HEADS):
            g_copies.append(fetch(g_refs[k], grads.at[pl.ds(2 * (flip ^ k), 2)], gsem.at[k]))

    for c in range(clusters):
        count[c] = 0

    def enter(t, carry):
        c = cluster_ref[t * spacing + residue] // spacing
        place = count[c]
        member[c * CAPACITY + place] = t
        count[c] = place + 1
        return carry

    lax.fori_loop(0, tiles, enter, 0)

    weights.wait()
    turned[...] = wbuf[...].reshape(3 * HD, -1).T

    def project(k, carry):
        for (slot, _, _), copy in zip(pieces, copies):
            pl.when(k == slot)(copy.wait)
        x = high(xbuf[k])
        mixed = dot(low(x * rows_rsqrt(x)), turned[...], NN)
        place = 2 * (flip ^ k)
        for c in range(3):
            u = mixed[:, c * HD : (c + 1) * HD]
            if c < 2:
                scale = rows_rsqrt(u)
                u = u * scale
            for j in range(2):
                kept[place + j, :, c * HD : (c + 1) * HD] = low(u[j * TILE : (j + 1) * TILE])
                if back and c < 2:
                    scales[place + j, :, c * HD : (c + 1) * HD] = jnp.broadcast_to(
                        scale[j * TILE : (j + 1) * TILE], (TILE, HD)
                    )
        return carry

    lax.fori_loop(0, HEADS, project, 0)
    if back:
        for copy in g_copies:
            copy.wait()

    def visit(c, carry):
        for n in range(1, CAPACITY + 1):

            @pl.when(count[c] == n)
            def _():
                held = [member[c * CAPACITY + i] for i in range(n)]
                if back:
                    backward_cluster(held, kept, out, scales, grads)
                else:
                    forward_cluster(held, kept, out)

        return carry

    lax.fori_loop(0, clusters, visit, 0)
    for k in range(HEADS):
        out_refs[k][...] = out[pl.ds(2 * (flip ^ k), 2)].reshape(out_refs[k].shape)


def head_work(info, tile_cluster, pieces, w_qkv, spacing, grads=None):
    back = grads is not None
    width = w_qkv.shape[1]
    tiles = 2 * HEADS
    wide = 3 * HD if back else HD
    tokens = tiles * TILE
    operands = [tile_cluster, info] + [array for _, _, array in pieces]
    if back:
        operands += [g.reshape(2, TILE, HD) for g in grads]
    operands.append(w_qkv.reshape(3, HEADS, HD, width))
    shapes = tuple((k, start, array.shape[0]) for k, start, array in pieces)
    scratch = [
        pltpu.VMEM((HEADS, 2 * TILE, width), jnp.bfloat16),
        pltpu.VMEM((3, HD, width), jnp.bfloat16),
        pltpu.VMEM((width, 3 * HD), jnp.bfloat16),
        pltpu.VMEM((tiles, TILE, 3 * HD), jnp.bfloat16),
        pltpu.VMEM((tiles, TILE, wide), jnp.bfloat16),
        pltpu.SMEM((tiles // 2,), jnp.int32),
        pltpu.SMEM((tiles // 2 * CAPACITY,), jnp.int32),
        pltpu.SemaphoreType.DMA((len(pieces),)),
        pltpu.SemaphoreType.DMA,
    ]
    if back:
        scratch += [
            pltpu.VMEM((tiles, TILE, 2 * HD), jnp.float32),
            pltpu.VMEM((tiles, TILE, HD), jnp.bfloat16),
            pltpu.SemaphoreType.DMA((HEADS,)),
        ]
    return call(
        functools.partial(head_kernel, back, shapes, spacing),
        operands,
        [SMEM, SMEM] + [ANY] * (len(operands) - 2),
        tuple(jax.ShapeDtypeStruct((2 * TILE, wide), jnp.bfloat16) for _ in range(HEADS)),
        scratch,
        2 * tokens * width * 3 * HD + tokens * 512 * HD * (14 if back else 4),
        2 * tokens * (width + 2 * wide),
    )


def spread_kernel(info_ref, up_ref, w_ref, *refs):
    out_refs, (up, rows, up_sem, sems) = refs[:HEADS], refs[HEADS:]
    flip = info_ref[0]
    up_copy = fetch(up_ref, up, up_sem)
    copies = [fetch(w_ref.at[flip ^ k], rows.at[k], sems.at[k]) for k in range(HEADS)]
    up_copy.wait()
    for k in range(0, HEADS, 2):
        copies[k].wait()
        copies[k + 1].wait()
        pair = rows[k : k + 2].reshape(2 * HD, -1)
        g = low(dot(up[...], pair, NT))
        out_refs[k][...] = g[:, :HD]
        out_refs[k + 1][...] = g[:, HD:]


def spread_grads(info, upstream, w_fin):
    tokens, width = upstream.shape
    return call(
        spread_kernel,
        [info, upstream, w_fin.reshape(HEADS, HD, width)],
        [SMEM, ANY, ANY],
        tuple(jax.ShapeDtypeStruct((tokens, HD), jnp.bfloat16) for _ in range(HEADS)),
        [
            pltpu.VMEM((tokens, width), jnp.bfloat16),
            pltpu.VMEM((HEADS, HD, width), jnp.bfloat16),
            pltpu.SemaphoreType.DMA,
            pltpu.SemaphoreType.DMA((HEADS,)),
        ],
        2 * tokens * width * HEADS * HD,
        2 * width * HEADS * HD,
    )


def finish_kernel(info_ref, *refs):
    att_refs, (x_ref, w_ref, out_ref, rows, sems) = refs[:HEADS], refs[HEADS:]
    flip = info_ref[0]
    copies = [fetch(w_ref.at[flip ^ k], rows.at[k], sems.at[k]) for k in range(HEADS)]
    att = jnp.concatenate([ref[...] for ref in att_refs], axis=1)
    for copy in copies:
        copy.wait()
    width = x_ref.shape[1]
    block = 256
    for start in range(0, width, block):
        columns = slice(start, start + block)
        w = rows[:, :, columns].reshape(HEADS * HD, block)
        out_ref[:, columns] = low(high(x_ref[:, columns]) + dot(att, w, NN))


def finish(info, attention, current, w_fin):
    tokens, width = current.shape
    return call(
        finish_kernel,
        [info, *attention, current, w_fin.reshape(HEADS, HD, width)],
        [SMEM] + [VMEM] * (HEADS + 1) + [ANY],
        jax.ShapeDtypeStruct((tokens, width), jnp.bfloat16),
        [
            pltpu.VMEM((HEADS, HD, width), jnp.bfloat16),
            pltpu.SemaphoreType.DMA((HEADS,)),
        ],
        2 * tokens * width * HEADS * HD,
        2 * width * HEADS * HD,
    )


def finish_back_kernel(info_ref, *refs):
    grad_refs, (x_ref, up_ref, w_ref, out_ref, rows, total, sems) = refs[:HEADS], refs[HEADS:]
    flip = info_ref[0]
    copies = [fetch(w_ref.at[:, flip ^ k], rows.at[k], sems.at[k]) for k in range(HEADS)]
    width = x_ref.shape[1]
    for k in range(0, HEADS, 2):
        copies[k].wait()
        copies[k + 1].wait()
        grads = jnp.concatenate([grad_refs[k][...], grad_refs[k + 1][...]], axis=1)
        product = dot(grads, rows[k : k + 2].reshape(6 * HD, width), NN)
        if k == 0:
            total[...] = product
        else:
            total[...] += product
    x = high(x_ref[...])
    scale = rows_rsqrt(x)
    unit = x * scale
    g = total[...]
    pulled = scale * (g - unit * jnp.mean(unit * g, axis=1, keepdims=True))
    out_ref[...] = low(high(up_ref[...]) + pulled)


def finish_back(info, grads, stored, upstream, w_qkv):
    tokens, width = stored.shape
    return call(
        finish_back_kernel,
        [info, *grads, stored, upstream, w_qkv.reshape(3, HEADS, HD, width)],
        [SMEM] + [VMEM] * (HEADS + 2) + [ANY],
        jax.ShapeDtypeStruct((tokens, width), jnp.bfloat16),
        [
            pltpu.VMEM((HEADS, 3, HD, width), jnp.bfloat16),
            pltpu.VMEM((tokens, width), jnp.float32),
            pltpu.SemaphoreType.DMA((HEADS,)),
        ],
        2 * tokens * width * 3 * HEADS * HD,
        6 * width * HEADS * HD,
    )


def partner(block, distance):
    route = [(i, i ^ distance) for i in range(lax.axis_size("seq"))]
    return lax.ppermute(block, "seq", route)


def gather_rows(x):
    half = x.shape[0] // 2
    over_x, over_y = partner(x, 2), partner(x, 4)
    top, bottom = partner(over_x[:half], 4), partner(over_y[half:], 2)
    pieces = [(0, 0, x), (2, 0, over_x), (4, 0, over_y), (6, 0, top), (6, half, bottom)]
    return pieces + [(k + 1, start, partner(block, 1)) for k, start, block in pieces]


def swap(blocks):
    moved = {k: partner(blocks[k], k) for k in (2, 4, 6, 3, 5, 7, 1)}
    return [blocks[0]] + [moved[k] for k in range(1, HEADS)]


def all_swap(blocks):
    return lax.all_to_all(blocks, "seq", split_axis=0, concat_axis=0, tiled=True)


def to_heads(blocks, own, spacing):
    heads, tokens, width = blocks.shape
    held = tokens // TILE
    places = spacing // held
    tiled = blocks.reshape(heads, 1, held, TILE, width)
    padded = jnp.zeros((heads, places, held, TILE, width), blocks.dtype)
    padded = lax.dynamic_update_slice_in_dim(padded, tiled, own % places, 1)
    arrived = all_swap(padded.reshape(heads * spacing, TILE, width))
    arrived = arrived.reshape(-1, places, TILE, width)
    mine = lax.dynamic_index_in_dim(arrived, own % spacing // held, 1, keepdims=False)
    return list(mine.reshape(HEADS, 2 * TILE, width))


def to_tokens(blocks, own, spacing, tokens):
    held = tokens // TILE
    places = spacing // held
    tiled = jnp.stack(blocks).reshape(2 * HEADS, 1, TILE, -1)
    padded = jnp.zeros((2 * HEADS, places, TILE, tiled.shape[3]), tiled.dtype)
    padded = lax.dynamic_update_slice_in_dim(padded, tiled, own % spacing // held, 1)
    returned = all_swap(padded.reshape(-1, TILE, tiled.shape[3]))
    returned = returned.reshape(HEADS, places, held * TILE, tiled.shape[3])
    return list(lax.dynamic_index_in_dim(returned, own % places, 1, keepdims=False))


def passed_along(block, axis, distance):
    devices = range(lax.axis_size(axis))
    route = [(i - distance, i) for i in devices if i - distance in devices]
    return lax.ppermute(block, axis, route)


def per_device(section_input, saved_input, grad_output, w_qkv, w_out, tile_cluster):
    current, stored, upstream = section_input[0], saved_input[0], grad_output[0]
    w_rows, w_fin = w_qkv[0], w_out[0]
    tokens = current.shape[0]
    spacing = lax.axis_size("seq") // HEADS
    own = lax.axis_index("seq").astype(jnp.int32)
    if spacing == 1:
        info = jnp.stack([own, own, jnp.zeros_like(own)])
        gather, spread, collect = gather_rows, swap, swap
    else:
        info = jnp.stack([jnp.zeros_like(own), own // spacing, own % spacing])

        def gather(x):
            copies = jnp.broadcast_to(x, (HEADS, *x.shape))
            return [(k, 0, b) for k, b in enumerate(to_heads(copies, own, spacing))]

        def spread(blocks):
            return to_heads(jnp.stack(blocks), own, spacing)

        def collect(blocks):
            return to_tokens(blocks, own, spacing, tokens)

    stored_pieces = gather(stored)
    grad_attention = spread(spread_grads(info, upstream, w_fin))
    current_pieces = gather(current)
    grads = head_work(info, tile_cluster, stored_pieces, w_rows, spacing, grad_attention)
    returned_grads = collect(grads)
    outputs = head_work(info, tile_cluster, current_pieces, w_rows, spacing)
    returned = collect(outputs)
    grad_self = finish_back(info, returned_grads, stored, upstream, w_rows)
    grad_input = passed_along(grad_self, "pipe", -1)
    result = finish(info, returned, current, w_fin)
    next_input = passed_along(result, "pipe", 1)
    return (next_input[None], grad_input[None])


def solution(mesh):
    return jax.shard_map(
        per_device,
        mesh=mesh,
        in_specs=(
            P("pipe", "seq", None),
            P("pipe", "seq", None),
            P("pipe", "seq", None),
            P("pipe", None, None),
            P("pipe", None, None),
            P(),
        ),
        out_specs=(P("pipe", "seq", None), P("pipe", "seq", None)),
        check_vma=False,
    )
```

time: 133 us -> 154 us (1.16)
  waiting for transfers between devices: 54.8 us -> 75.8 us
  Pallas kernels: 39.7 us -> 30.3 us
  starting transfers between devices: 27.9 us -> 35 us
    ppermute x0 -> x39, waiting for transfers between devices: none -> 62 us  [partner(): return lax.ppermute(block, 'seq', route)]
    all_to_all x4 -> x0, waiting for transfers between devices: 41.4 us -> none  [all_swap(): lax.all_to_all(blocks, 'seq', split_axis=0, concat_axis=0, tiled=True)]
    ppermute x0 -> x39, starting transfers between devices: none -> 29.1 us  [partner(): return lax.ppermute(block, 'seq', route)]
    all_to_all x4 -> x0, starting transfers between devices: 22.1 us -> none  [all_swap(): lax.all_to_all(blocks, 'seq', split_axis=0, concat_axis=0, tiled=True)]
    pallas_call x6 -> x5, Pallas kernels: 39.7 us -> 30.3 us  [call(): pl.pallas_call(kernel, in_specs=in_specs, out_specs=tuple((VMEM for _ in...]
  transfers between devices with their start and end apart: 6 -> 41, of which waited for: 5 -> 13; matrix products, arithmetic and copies ran while one was open for 0% -> 1% of each run, Pallas kernels for 25% -> 20%
where the time goes in v1:
time: 154 us; the launch traced here: 152 us
  waiting for transfers between devices  75.8 us (49%)
  starting transfers between devices  35 us (23%)
  Pallas kernels  30.3 us (20%)
  local copies, waits for them, and re-layouts  9.89 us (6%)
    ppermute x39, waiting for transfers between devices, partner(): return lax.ppermute(block, 'seq', route)  62 us
    pallas_call x5, Pallas kernels, call(): pl.pallas_call(kernel, in_specs=in_specs, out_specs=tuple((VMEM for _ in...  30.3 us
    ppermute x39, starting transfers between devices, partner(): return lax.ppermute(block, 'seq', route)  29.1 us
    ppermute x2, waiting for transfers between devices, passed_along(): return lax.ppermute(block, axis, route)  13.8 us
    unnamed x24, local copies, waits for them, and re-layouts  8.86 us
    ppermute x2, starting transfers between devices, passed_along(): return lax.ppermute(block, axis, route)  5.88 us
  transfers between devices with their start and end apart: 41, of which 13 were waited for; matrix products, arithmetic and copies ran while one was open for 1% of the time, Pallas kernels for 20%

profile of v1, /device:TPU:18, one launch (start us, length us, event | category | flops | bytes accessed | tf_op | source)
XLA Modules:
  0.0 151.9 jit_solution(687796390538290341)
XLA Ops:
  0.6 0.6 collective-permute-start.17
  1.2 1.5 collective-permute-start
  2.7 1.5 %collective-permute-start.1 = (bf16[256,1024]{1,0:T(8,128)(2,1)}, bf16[256,1024]{1,0:T(8,128)(2,1)S(1)}, u32[]{:S(2)}, u32[]{:S(2)}) collective-permute-start(bf16[256,1024]{1,0:T(8,128)(2,1)} %bitcast.26), channel_id=1, source_target_pairs={{0,4},{1,5},{2,6},{3,7},{4,0},{5,1},{6,2},{7,3},{8,12},{9,13},{10,... | collective-permute-start | bytes 1572872 | tf_op jit(solution)/shard_map/ppermute | solution.py:327
  4.3 1.7 %copy-done.1 = bf16[1,1024,1024]{2,1,0:T(8,128)(2,1)S(1)} copy-done((bf16[1,1024,1024]{2,1,0:T(8,128)(2,1)S(1)}, bf16[1,1024,1024]{2,1,0:T(8,128)(2,1)}, u32[]{:S(2)}) %copy-start.1) | copy-done | bytes 2097176
  6.0 1.0 copy-done.3
  7.1 2.6 %shard_map.79 = (bf16[256,128]{1,0:T(8,128)(2,1)S(1)}, bf16[256,128]{1,0:T(8,128)(2,1)S(1)}, bf16[256,128]{1,0:T(8,128)(2,1)S(1)}, bf16[256,128]{1,0:T(8,128)(2,...) custom-call(s32[3]{0:T(128)S(1)} %pad_add_fusion.refs_1_.info_ref, ...), custom_call_target="tpu_custom_call" | custom-call | flops 536870912 | bytes 2097152 | tf_op jit(solution)/shard_map/pallas_call | solution.py:42
  9.8 0.6 collective-permute-start.29
  10.4 15.7 %collective-permute-done.28 = bf16[256,128]{1,0:T(8,128)(2,1)S(1)} collective-permute-done((bf16[256,128]{1,0:T(8,128)(2,1)S(1)}, bf16[256,128]{1,0:T(8,128)(2,1)S(1)}, u32[]{:S(2)}, u32[]{:S(2)}) %collective-permute-start.28) | collective-permute-done | bytes 65568 | tf_op jit(solution)/shard_map/ppermute | solution.py:327
  26.1 1.5 %collective-permute-start.18 = (bf16[256,1024]{1,0:T(8,128)(2,1)}, bf16[256,1024]{1,0:T(8,128)(2,1)S(1)}, u32[]{:S(2)}, u32[]{:S(2)}) collective-permute-start(bf16[256,1024]{1,0:T(8,128)(2,1)} %bitcast.31), channel_id=1, source_target_pairs={{0,4},{1,5},{2,6},{3,7},{4,0},{5,1},{6,2},{7,3},{8,12},{9,13},{10,... | collective-permute-start | bytes 1572872 | tf_op jit(solution)/shard_map/ppermute | solution.py:327
  27.6 0.8 collective-permute-start.30
  28.4 14.1 %collective-permute-done.30 = bf16[256,128]{1,0:T(8,128)(2,1)S(1)} collective-permute-done((bf16[256,128]{1,0:T(8,128)(2,1)S(1)}, bf16[256,128]{1,0:T(8,128)(2,1)S(1)}, u32[]{:S(2)}, u32[]{:S(2)}) %collective-permute-start.30) | collective-permute-done | bytes 65568 | tf_op jit(solution)/shard_map/ppermute | solution.py:327
  42.6 1.4 collective-permute-start.31
  44.0 1.3 collective-permute-start.32
  45.6 1.0 slice.18
  46.7 1.4 collective-permute-done.31
  48.0 1.9 %collective-permute-start.19 = (bf16[128,1024]{1,0:T(8,128)(2,1)S(1)}, bf16[128,1024]{1,0:T(8,128)(2,1)S(1)}, u32[]{:S(2)}, u32[]{:S(2)}) collective-permute-start(bf16[128,1024]{1,0:T(8,128)(2,1)S(1)} %slice.18), channel_id=1, source_target_pairs={{0,4},{1,5},{2,6},{3,7},{4,0},{5,1},{6,2},{7,3},{8,12},{9,13},{10,... | collective-permute-start | bytes 786440 | tf_op jit(solution)/shard_map/ppermute | solution.py:327
  50.4 0.7 collective-permute-start.3
  51.0 1.3 collective-permute-start.27
  52.4 7.6 %collective-permute-done.27 = bf16[256,128]{1,0:T(8,128)(2,1)S(1)} collective-permute-done((bf16[256,128]{1,0:T(8,128)(2,1)S(1)}, bf16[256,128]{1,0:T(8,128)(2,1)S(1)}, u32[]{:S(2)}, u32[]{:S(2)}) %collective-permute-start.27) | collective-permute-done | bytes 65568 | tf_op jit(solution)/shard_map/ppermute | solution.py:327
  60.0 0.5 collective-permute-start.20
  60.5 0.5 collective-permute-start.6
  61.4 0.5 collective-permute-start.8
  61.9 5.5 %collective-permute-done.20.refs_6_ = bf16[128,1024]{1,0:T(8,128)(2,1)S(1)} collective-permute-done((bf16[128,1024]{1,0:T(8,128)(2,1)S(1)}, bf16[128,1024]{1,0:T(8,128)(2,1)S(1)}, u32[]{:S(2)}, u32[]{:S(2)}) %collective-permute-start.20) | collective-permute-done | bytes 262176 | tf_op jit(solution)/shard_map/ppermute | solution.py:327
  67.4 0.5 collective-permute-start.22
  68.5 2.8 %copy-done = bf16[1,3072,1024]{2,1,0:T(8,128)(2,1)S(1)} copy-done((bf16[1,3072,1024]{2,1,0:T(8,128)(2,1)S(1)}, bf16[1,3072,1024]{2,1,0:T(8,128)(2,1)}, u32[]{:S(2)}) %copy-start) | copy-done | bytes 6291480
  71.3 1.0 copy-done.5
  72.3 0.7 copy-done.8
  73.0 9.7 %shard_map.77 = (bf16[256,128]{1,0:T(8,128)(2,1)S(1)}, bf16[256,128]{1,0:T(8,128)(2,1)S(1)}, bf16[256,128]{1,0:T(8,128)(2,1)S(1)}, bf16[256,128]{1,0:T(8,128)(2,...) custom-call(s32[16]{0:T(128)S(1)} %copy-done.8, ...), custom_call_target="tpu_custom_call" | custom-call | flops 2147483648 | bytes 5242880 | tf_op jit(solution)/shard_map/pallas_call | solution.py:42
  83.2 12.6 %shard_map.80 = (bf16[256,384]{1,0:T(8,128)(2,1)S(1)}, bf16[256,384]{1,0:T(8,128)(2,1)S(1)}, bf16[256,384]{1,0:T(8,128)(2,1)S(1)}, bf16[256,384]{1,0:T(8,128)(2,...) custom-call(s32[16]{0:T(128)S(1)} %copy-done.8, ...), custom_call_target="tpu_custom_call" | custom-call | flops 3489660928 | bytes 7340032 | tf_op jit(solution)/shard_map/pallas_call | solution.py:42
  96.0 1.7 %collective-permute-start.34 = (bf16[256,384]{1,0:T(8,128)(2,1)S(1)}, bf16[256,384]{1,0:T(8,128)(2,1)S(1)}, u32[]{:S(2)}, u32[]{:S(2)}) collective-permute-start(bf16[256,384]{1,0:T(8,128)(2,1)S(1)} %get-tuple-element.44), channel_id=1, source_target_pairs={{0,2},{1,3},{2,0},{3,1},{4,6},{5,7},{6,4},{7,5},{8,10},{9,11},{10,... | collective-permute-start | bytes 589832 | tf_op jit(solution)/shard_map/ppermute | solution.py:327
  97.7 1.6 %collective-permute-start.12 = (bf16[256,128]{1,0:T(8,128)(2,1)S(1)}, bf16[256,128]{1,0:T(8,128)(2,1)S(1)}, u32[]{:S(2)}, u32[]{:S(2)}) collective-permute-start(bf16[256,128]{1,0:T(8,128)(2,1)S(1)} %get-tuple-element.30), channel_id=1, source_target_pairs={{0,4},{1,5},{2,6},{3,7},{4,0},{5,1},{6,2},{7,3},{8,12},{9,13},{10,... | collective-permute-start | bytes 196616 | tf_op jit(solution)/shard_map/ppermute | solution.py:327
  99.5 4.5 %collective-permute-done.11.refs_3_ = bf16[256,128]{1,0:T(8,128)(2,1)S(1)} collective-permute-done((bf16[256,128]{1,0:T(8,128)(2,1)S(1)}, bf16[256,128]{1,0:T(8,128)(2,1)S(1)}, u32[]{:S(2)}, u32[]{:S(2)}) %collective-permute-start.11) | collective-permute-done | bytes 65568 | tf_op jit(solution)/shard_map/ppermute | solution.py:327
  104.0 1.3 collective-permute-start.14
  105.3 1.3 collective-permute-start.15
  107.1 2.3 %collective-permute-done.14.refs_6_ = bf16[256,128]{1,0:T(8,128)(2,1)S(1)} collective-permute-done((bf16[256,128]{1,0:T(8,128)(2,1)S(1)}, bf16[256,128]{1,0:T(8,128)(2,1)S(1)}, u32[]{:S(2)}, u32[]{:S(2)}) %collective-permute-start.14) | collective-permute-done | bytes 65568 | tf_op jit(solution)/shard_map/ppermute | solution.py:327
  109.4 0.7 collective-permute-start.35
  110.5 1.7 %collective-permute-start.36 = (bf16[256,384]{1,0:T(8,128)(2,1)S(1)}, bf16[256,384]{1,0:T(8,128)(2,1)S(1)}, u32[]{:S(2)}, u32[]{:S(2)}) collective-permute-start(bf16[256,384]{1,0:T(8,128)(2,1)S(1)} %get-tuple-element.46), channel_id=1, source_target_pairs={{0,4},{1,5},{2,6},{3,7},{4,0},{5,1},{6,2},{7,3},{8,12},{9,13},{10,... | collective-permute-start | bytes 589832 | tf_op jit(solution)/shard_map/ppermute | solution.py:327
  112.5 1.4 collective-permute-start.38
  113.9 1.0 collective-permute-start.39
  114.9 1.5 %shard_map.78 = bf16[256,1024]{1,0:T(8,128)(2,1)S(1)} custom-call(s32[3]{0:T(128)S(1)} %pad_add_fusion.refs_1_.info_ref, bf16[256,128]{1,0:T(8,128)(2,1)S(1)} %get-tuple-element.26.refs_0_, bf16[256,128]{1,0:T(8,128)(2,1)S(1)} %collective-permute-done.9.refs_1_, bf16[256,128]{1,0:T(8,128)(2,1)S(1)} %collective-permute-done.10.refs_2_, ...), custom_call_target="tpu_custom_call" | custom-call | flops 536870912 | bytes 2097152 | tf_op jit(solution)/shard_map/pallas_call | solution.py:42
  116.5 3.5 %collective-permute-start.16 = (bf16[256,1024]{1,0:T(8,128)(2,1)S(1)}, bf16[256,1024]{1,0:T(8,128)(2,1)S(1)}, u32[]{:S(2)}, u32[]{:S(2)}) collective-permute-start(bf16[256,1024]{1,0:T(8,128)(2,1)S(1)} %shard_map.78), channel_id=1, source_target_pairs={{0,8},{8,16},{16,24},{1,9},{9,17},{17,25},{2,10},{10,18},{18,26},{... | collective-permute-start | bytes 1572872 | tf_op jit(solution)/shard_map/ppermute | solution.py:374
  120.0 6.6 %collective-permute-done.36.refs_4_ = bf16[256,384]{1,0:T(8,128)(2,1)S(1)} collective-permute-done((bf16[256,384]{1,0:T(8,128)(2,1)S(1)}, bf16[256,384]{1,0:T(8,128)(2,1)S(1)}, u32[]{:S(2)}, u32[]{:S(2)}) %collective-permute-start.36) | collective-permute-done | bytes 196640 | tf_op jit(solution)/shard_map/ppermute | solution.py:327
  126.7 3.6 %collective-permute-done.37.refs_5_ = bf16[256,384]{1,0:T(8,128)(2,1)S(1)} collective-permute-done((bf16[256,384]{1,0:T(8,128)(2,1)S(1)}, bf16[256,384]{1,0:T(8,128)(2,1)S(1)}, u32[]{:S(2)}, u32[]{:S(2)}) %collective-permute-start.37) | collective-permute-done | bytes 196640 | tf_op jit(solution)/shard_map/ppermute | solution.py:327
  130.3 3.9 %shard_map.81 = bf16[256,1024]{1,0:T(8,128)(2,1)S(1)} custom-call(s32[3]{0:T(128)S(1)} %pad_add_fusion.refs_1_.info_ref, bf16[256,384]{1,0:T(8,128)(2,1)S(1)} %get-tuple-element.42.refs_0_, bf16[256,384]{1,0:T(8,128)(2,1)S(1)} %collective-permute-done.33.refs_1_, bf16[256,384]{1,0:T(8,128)(2,1)S(1)} %collective-permute-done.34.refs_2_, ...), custom_call_target="tpu_custom_call" | custom-call | flops 1610612736 | bytes 6291456 | tf_op jit(solution)/shard_map/pallas_call | solution.py:42
  134.2 2.4 %collective-permute-start.40 = (bf16[256,1024]{1,0:T(8,128)(2,1)S(1)}, bf16[256,1024]{1,0:T(8,128)(2,1)S(1)}, u32[]{:S(2)}, u32[]{:S(2)}) collective-permute-start(bf16[256,1024]{1,0:T(8,128)(2,1)S(1)} %shard_map.81), channel_id=1, source_target_pairs={{8,0},{16,8},{24,16},{9,1},{17,9},{25,17},{10,2},{18,10},{26,18},{... | collective-permute-start | bytes 1572872 | tf_op jit(solution)/shard_map/ppermute | solution.py:374
  136.6 13.8 %collective-permute-done.40 = bf16[256,1024]{1,0:T(8,128)(2,1)S(1)} collective-permute-done((bf16[256,1024]{1,0:T(8,128)(2,1)S(1)}, bf16[256,1024]{1,0:T(8,128)(2,1)S(1)}, u32[]{:S(2)}, u32[]{:S(2)}) %collective-permute-start.40) | collective-permute-done | bytes 524320 | tf_op jit(solution)/shard_map/ppermute | solution.py:374
  150.3 0.8 copy.10
  151.1 0.8 copy.11
  (69 shorter events, 4.1 us)
Async XLA Ops:
  0.6 42.0 %collective-permute-start.17 = (bf16[256,1024]{1,0:T(8,128)(2,1)}, bf16[256,1024]{1,0:T(8,128)(2,1)}, u32[]{:S(2)}, u32[]{:S(2)}) collective-permute-start(bf16[256,1024]{1,0:T(8,128)(2,1)} %bitcast.30), channel_id=1, source_target_pairs={{0,2},{1,3},{2,0},{3,1},{4,6},{5,7},{6,4},{7,5},{8,10},{9,11},{10,... | collective-permute-start | bytes 1572872 | tf_op jit(solution)/shard_map/ppermute | solution.py:327
  1.2 42.7 %collective-permute-start = (bf16[256,1024]{1,0:T(8,128)(2,1)}, bf16[256,1024]{1,0:T(8,128)(2,1)S(1)}, u32[]{:S(2)}, u32[]{:S(2)}) collective-permute-start(bf16[256,1024]{1,0:T(8,128)(2,1)} %bitcast.25), channel_id=1, source_target_pairs={{0,2},{1,3},{2,0},{3,1},{4,6},{5,7},{6,4},{7,5},{8,10},{9,11},{10,... | collective-permute-start | bytes 1572872 | tf_op jit(solution)/shard_map/ppermute | solution.py:327
  2.7 42.5 %collective-permute-start.1 = (bf16[256,1024]{1,0:T(8,128)(2,1)}, bf16[256,1024]{1,0:T(8,128)(2,1)S(1)}, u32[]{:S(2)}, u32[]{:S(2)}) collective-permute-start(bf16[256,1024]{1,0:T(8,128)(2,1)} %bitcast.26), channel_id=1, source_target_pairs={{0,4},{1,5},{2,6},{3,7},{4,0},{5,1},{6,2},{7,3},{8,12},{9,13},{10,... | collective-permute-start | bytes 1572872 | tf_op jit(solution)/shard_map/ppermute | solution.py:327
  4.2 78.9 %slice-start = ((s8[6291456]{0:T(1024)(128)(4,1)}), s8[2097152]{0:T(1024)(128)(4,1)S(1)}, s32[]{:S(2)}) async-start(s8[6291456]{0:T(1024)(128)(4,1)} %bitcast.17), calls=%async_computation | async-start | bytes 4194304
  9.7 16.3 %collective-permute-start.28 = (bf16[256,128]{1,0:T(8,128)(2,1)S(1)}, bf16[256,128]{1,0:T(8,128)(2,1)S(1)}, u32[]{:S(2)}, u32[]{:S(2)}) collective-permute-start(bf16[256,128]{1,0:T(8,128)(2,1)S(1)} %get-tuple-element.37), channel_id=1, source_target_pairs={{0,3},{1,2},{2,1},{3,0},{4,7},{5,6},{6,5},{7,4},{8,11},{9,10},{10,... | collective-permute-start | bytes 196616 | tf_op jit(solution)/shard_map/ppermute | solution.py:327
  9.8 17.8 %collective-permute-start.29 = (bf16[256,128]{1,0:T(8,128)(2,1)S(1)}, bf16[256,128]{1,0:T(8,128)(2,1)S(1)}, u32[]{:S(2)}, u32[]{:S(2)}) collective-permute-start(bf16[256,128]{1,0:T(8,128)(2,1)S(1)} %get-tuple-element.38), channel_id=1, source_target_pairs={{0,4},{1,5},{2,6},{3,7},{4,0},{5,1},{6,2},{7,3},{8,12},{9,13},{10,... | collective-permute-start | bytes 196616 | tf_op jit(solution)/shard_map/ppermute | solution.py:327
  26.1 25.0 %collective-permute-start.18 = (bf16[256,1024]{1,0:T(8,128)(2,1)}, bf16[256,1024]{1,0:T(8,128)(2,1)S(1)}, u32[]{:S(2)}, u32[]{:S(2)}) collective-permute-start(bf16[256,1024]{1,0:T(8,128)(2,1)} %bitcast.31), channel_id=1, source_target_pairs={{0,4},{1,5},{2,6},{3,7},{4,0},{5,1},{6,2},{7,3},{8,12},{9,13},{10,... | collective-permute-start | bytes 1572872 | tf_op jit(solution)/shard_map/ppermute | solution.py:327
  27.6 14.9 %collective-permute-start.30 = (bf16[256,128]{1,0:T(8,128)(2,1)S(1)}, bf16[256,128]{1,0:T(8,128)(2,1)S(1)}, u32[]{:S(2)}, u32[]{:S(2)}) collective-permute-start(bf16[256,128]{1,0:T(8,128)(2,1)S(1)} %get-tuple-element.39), channel_id=1, source_target_pairs={{0,5},{1,4},{2,7},{3,6},{4,1},{5,0},{6,3},{7,2},{8,13},{9,12},{10,... | collective-permute-start | bytes 196616 | tf_op jit(solution)/shard_map/ppermute | solution.py:327
  42.5 18.1 %collective-permute-start.4 = (bf16[256,1024]{1,0:T(8,128)(2,1)}, bf16[256,1024]{1,0:T(8,128)(2,1)S(1)}, u32[]{:S(2)}, u32[]{:S(2)}) collective-permute-start(bf16[256,1024]{1,0:T(8,128)(2,1)} %bitcast.27), channel_id=1, source_target_pairs={{0,1},{1,0},{2,3},{3,2},{4,5},{5,4},{6,7},{7,6},{8,9},{9,8},{10,11... | collective-permute-start | bytes 1572872 | tf_op jit(solution)/shard_map/ppermute | solution.py:327
  42.6 5.4 %collective-permute-start.31 = (bf16[256,128]{1,0:T(8,128)(2,1)S(1)}, bf16[256,128]{1,0:T(8,128)(2,1)S(1)}, u32[]{:S(2)}, u32[]{:S(2)}) collective-permute-start(bf16[256,128]{1,0:T(8,128)(2,1)S(1)} %get-tuple-element.40), channel_id=1, source_target_pairs={{0,6},{1,7},{2,4},{3,5},{4,2},{5,3},{6,0},{7,1},{8,14},{9,15},{10,... | collective-permute-start | bytes 196616 | tf_op jit(solution)/shard_map/ppermute | solution.py:327
  44.0 5.9 %collective-permute-start.32 = (bf16[256,128]{1,0:T(8,128)(2,1)S(1)}, bf16[256,128]{1,0:T(8,128)(2,1)S(1)}, u32[]{:S(2)}, u32[]{:S(2)}) collective-permute-start(bf16[256,128]{1,0:T(8,128)(2,1)S(1)} %get-tuple-element.41), channel_id=1, source_target_pairs={{0,7},{1,6},{2,5},{3,4},{4,3},{5,2},{6,1},{7,0},{8,15},{9,14},{10,... | collective-permute-start | bytes 196616 | tf_op jit(solution)/shard_map/ppermute | solution.py:327
  45.3 37.9 %copy-start.7 = (bf16[1,256,1024]{2,1,0:T(8,128)(2,1)S(1)}, bf16[1,256,1024]{2,1,0:T(8,128)(2,1)}, u32[]{:S(2)}) copy-start(bf16[1,256,1024]{2,1,0:T(8,128)(2,1)} %param.7) | copy-start | bytes 1572868
  45.3 5.1 %collective-permute-start.26 = (bf16[256,128]{1,0:T(8,128)(2,1)S(1)}, bf16[256,128]{1,0:T(8,128)(2,1)S(1)}, u32[]{:S(2)}, u32[]{:S(2)}) collective-permute-start(bf16[256,128]{1,0:T(8,128)(2,1)S(1)} %get-tuple-element.35), channel_id=1, source_target_pairs={{0,1},{1,0},{2,3},{3,2},{4,5},{5,4},{6,7},{7,6},{8,9},{9,8},{10,11... | collective-permute-start | bytes 196616 | tf_op jit(solution)/shard_map/ppermute | solution.py:327
  48.0 12.5 %collective-permute-start.19 = (bf16[128,1024]{1,0:T(8,128)(2,1)S(1)}, bf16[128,1024]{1,0:T(8,128)(2,1)S(1)}, u32[]{:S(2)}, u32[]{:S(2)}) collective-permute-start(bf16[128,1024]{1,0:T(8,128)(2,1)S(1)} %slice.18), channel_id=1, source_target_pairs={{0,4},{1,5},{2,6},{3,7},{4,0},{5,1},{6,2},{7,3},{8,12},{9,13},{10,... | collective-permute-start | bytes 786440 | tf_op jit(solution)/shard_map/ppermute | solution.py:327
  49.9 11.5 %collective-permute-start.2 = (bf16[128,1024]{1,0:T(8,128)(2,1)S(1)}, bf16[128,1024]{1,0:T(8,128)(2,1)S(1)}, u32[]{:S(2)}, u32[]{:S(2)}) collective-permute-start(bf16[128,1024]{1,0:T(8,128)(2,1)S(1)} %slice.16), channel_id=1, source_target_pairs={{0,4},{1,5},{2,6},{3,7},{4,0},{5,1},{6,2},{7,3},{8,12},{9,13},{10,... | collective-permute-start | bytes 786440 | tf_op jit(solution)/shard_map/ppermute | solution.py:327
  50.4 11.0 %collective-permute-start.3 = (bf16[128,1024]{1,0:T(8,128)(2,1)S(1)}, bf16[128,1024]{1,0:T(8,128)(2,1)S(1)}, u32[]{:S(2)}, u32[]{:S(2)}) collective-permute-start(bf16[128,1024]{1,0:T(8,128)(2,1)S(1)} %slice.17), channel_id=1, source_target_pairs={{0,2},{1,3},{2,0},{3,1},{4,6},{5,7},{6,4},{7,5},{8,10},{9,11},{10,... | collective-permute-start | bytes 786440 | tf_op jit(solution)/shard_map/ppermute | solution.py:327
  51.0 8.9 %collective-permute-start.27 = (bf16[256,128]{1,0:T(8,128)(2,1)S(1)}, bf16[256,128]{1,0:T(8,128)(2,1)S(1)}, u32[]{:S(2)}, u32[]{:S(2)}) collective-permute-start(bf16[256,128]{1,0:T(8,128)(2,1)S(1)} %get-tuple-element.36), channel_id=1, source_target_pairs={{0,2},{1,3},{2,0},{3,1},{4,6},{5,7},{6,4},{7,5},{8,10},{9,11},{10,... | collective-permute-start | bytes 196616 | tf_op jit(solution)/shard_map/ppermute | solution.py:327
  60.0 7.4 %collective-permute-start.20 = (bf16[128,1024]{1,0:T(8,128)(2,1)S(1)}, bf16[128,1024]{1,0:T(8,128)(2,1)S(1)}, u32[]{:S(2)}, u32[]{:S(2)}) collective-permute-start(bf16[128,1024]{1,0:T(8,128)(2,1)S(1)} %slice.19), channel_id=1, source_target_pairs={{0,2},{1,3},{2,0},{3,1},{4,6},{5,7},{6,4},{7,5},{8,10},{9,11},{10,... | collective-permute-start | bytes 786440 | tf_op jit(solution)/shard_map/ppermute | solution.py:327
  60.5 7.4 %collective-permute-start.5 = (bf16[256,1024]{1,0:T(8,128)(2,1)S(1)}, bf16[256,1024]{1,0:T(8,128)(2,1)S(1)}, u32[]{:S(2)}, u32[]{:S(2)}) collective-permute-start(bf16[256,1024]{1,0:T(8,128)(2,1)S(1)} %collective-permute-done.refs_3_), channel_id=1, source_target_pairs={{0,1},{1,0},{2,3},{3,2},{4,5},{5,4},{6,7},{7,6},{8,9},{9,8},{10,11... | collective-permute-start | bytes 1572872 | tf_op jit(solution)/shard_map/ppermute | solution.py:327
  60.5 7.9 %collective-permute-start.6 = (bf16[256,1024]{1,0:T(8,128)(2,1)S(1)}, bf16[256,1024]{1,0:T(8,128)(2,1)S(1)}, u32[]{:S(2)}, u32[]{:S(2)}) collective-permute-start(bf16[256,1024]{1,0:T(8,128)(2,1)S(1)} %collective-permute-done.1.refs_4_), channel_id=1, source_target_pairs={{0,1},{1,0},{2,3},{3,2},{4,5},{5,4},{6,7},{7,6},{8,9},{9,8},{10,11... | collective-permute-start | bytes 1572872 | tf_op jit(solution)/shard_map/ppermute | solution.py:327
  61.4 6.0 %collective-permute-start.7 = (bf16[128,1024]{1,0:T(8,128)(2,1)S(1)}, bf16[128,1024]{1,0:T(8,128)(2,1)S(1)}, u32[]{:S(2)}, u32[]{:S(2)}) collective-permute-start(bf16[128,1024]{1,0:T(8,128)(2,1)S(1)} %collective-permute-done.2.refs_5_), channel_id=1, source_target_pairs={{0,1},{1,0},{2,3},{3,2},{4,5},{5,4},{6,7},{7,6},{8,9},{9,8},{10,11... | collective-permute-start | bytes 786440 | tf_op jit(solution)/shard_map/ppermute | solution.py:327
  61.4 6.5 %collective-permute-start.8 = (bf16[128,1024]{1,0:T(8,128)(2,1)S(1)}, bf16[128,1024]{1,0:T(8,128)(2,1)S(1)}, u32[]{:S(2)}, u32[]{:S(2)}) collective-permute-start(bf16[128,1024]{1,0:T(8,128)(2,1)S(1)} %collective-permute-done.3.refs_6_), channel_id=1, source_target_pairs={{0,1},{1,0},{2,3},{3,2},{4,5},{5,4},{6,7},{7,6},{8,9},{9,8},{10,11... | collective-permute-start | bytes 786440 | tf_op jit(solution)/shard_map/ppermute | solution.py:327
  67.4 15.3 %collective-permute-start.21 = (bf16[256,1024]{1,0:T(8,128)(2,1)}, bf16[256,1024]{1,0:T(8,128)(2,1)S(1)}, u32[]{:S(2)}, u32[]{:S(2)}) collective-permute-start(bf16[256,1024]{1,0:T(8,128)(2,1)} %bitcast.32), channel_id=1, source_target_pairs={{0,1},{1,0},{2,3},{3,2},{4,5},{5,4},{6,7},{7,6},{8,9},{9,8},{10,11... | collective-permute-start | bytes 1572872 | tf_op jit(solution)/shard_map/ppermute | solution.py:327
  67.4 15.7 %collective-permute-start.22 = (bf16[256,1024]{1,0:T(8,128)(2,1)}, bf16[256,1024]{1,0:T(8,128)(2,1)S(1)}, u32[]{:S(2)}, u32[]{:S(2)}) collective-permute-start(bf16[256,1024]{1,0:T(8,128)(2,1)} %collective-permute-done.17.refs_3_), channel_id=1, source_target_pairs={{0,1},{1,0},{2,3},{3,2},{4,5},{5,4},{6,7},{7,6},{8,9},{9,8},{10,11... | collective-permute-start | bytes 1572872 | tf_op jit(solution)/shard_map/ppermute | solution.py:327
  67.9 15.2 %collective-permute-start.23 = (bf16[256,1024]{1,0:T(8,128)(2,1)S(1)}, bf16[256,1024]{1,0:T(8,128)(2,1)S(1)}, u32[]{:S(2)}, u32[]{:S(2)}) collective-permute-start(bf16[256,1024]{1,0:T(8,128)(2,1)S(1)} %collective-permute-done.18.refs_4_), channel_id=1, source_target_pairs={{0,1},{1,0},{2,3},{3,2},{4,5},{5,4},{6,7},{7,6},{8,9},{9,8},{10,11... | collective-permute-start | bytes 1572872 | tf_op jit(solution)/shard_map/ppermute | solution.py:327
  68.0 15.1 %collective-permute-start.24 = (bf16[128,1024]{1,0:T(8,128)(2,1)S(1)}, bf16[128,1024]{1,0:T(8,128)(2,1)S(1)}, u32[]{:S(2)}, u32[]{:S(2)}) collective-permute-start(bf16[128,1024]{1,0:T(8,128)(2,1)S(1)} %collective-permute-done.19.refs_5_), channel_id=1, source_target_pairs={{0,1},{1,0},{2,3},{3,2},{4,5},{5,4},{6,7},{7,6},{8,9},{9,8},{10,11... | collective-permute-start | bytes 786440 | tf_op jit(solution)/shard_map/ppermute | solution.py:327
  68.4 14.7 %collective-permute-start.25 = (bf16[128,1024]{1,0:T(8,128)(2,1)S(1)}, bf16[128,1024]{1,0:T(8,128)(2,1)S(1)}, u32[]{:S(2)}, u32[]{:S(2)}) collective-permute-start(bf16[128,1024]{1,0:T(8,128)(2,1)S(1)} %collective-permute-done.20.refs_6_), channel_id=1, source_target_pairs={{0,1},{1,0},{2,3},{3,2},{4,5},{5,4},{6,7},{7,6},{8,9},{9,8},{10,11... | collective-permute-start | bytes 786440 | tf_op jit(solution)/shard_map/ppermute | solution.py:327
  68.5 2.8 %copy-start = (bf16[1,3072,1024]{2,1,0:T(8,128)(2,1)S(1)}, bf16[1,3072,1024]{2,1,0:T(8,128)(2,1)}, u32[]{:S(2)}) copy-start(bf16[1,3072,1024]{2,1,0:T(8,128)(2,1)} %param.9) | copy-start | bytes 18874372
  73.0 10.2 %slice-start.1 = ((s8[6291456]{0:T(1024)(128)(4,1)}), s8[4194304]{0:T(1024)(128)(4,1)S(1)}, s32[]{:S(2)}) async-start(s8[6291456]{0:T(1024)(128)(4,1)} %bitcast.17), calls=%async_computation.1 | async-start | bytes 8388608
  82.7 16.7 %collective-permute-start.10 = (bf16[256,128]{1,0:T(8,128)(2,1)S(1)}, bf16[256,128]{1,0:T(8,128)(2,1)S(1)}, u32[]{:S(2)}, u32[]{:S(2)}) collective-permute-start(bf16[256,128]{1,0:T(8,128)(2,1)S(1)} %get-tuple-element.28), channel_id=1, source_target_pairs={{0,2},{1,3},{2,0},{3,1},{4,6},{5,7},{6,4},{7,5},{8,10},{9,11},{10,... | collective-permute-start | bytes 196616 | tf_op jit(solution)/shard_map/ppermute | solution.py:327
  83.2 31.8 %copy-start.2 = (bf16[1,1024,1024]{2,1,0:T(8,128)(2,1)S(1)}, bf16[1,1024,1024]{2,1,0:T(8,128)(2,1)}, u32[]{:S(2)}) copy-start(bf16[1,1024,1024]{2,1,0:T(8,128)(2,1)} %param.10) | copy-start | bytes 6291460
  83.2 31.8 %copy-start.6 = (bf16[1,256,1024]{2,1,0:T(8,128)(2,1)S(1)}, bf16[1,256,1024]{2,1,0:T(8,128)(2,1)}, u32[]{:S(2)}) copy-start(bf16[1,256,1024]{2,1,0:T(8,128)(2,1)} %param.6) | copy-start | bytes 1572868
  83.2 47.1 %copy-start.4 = (bf16[1,256,1024]{2,1,0:T(8,128)(2,1)S(1)}, bf16[1,256,1024]{2,1,0:T(8,128)(2,1)}, u32[]{:S(2)}) copy-start(bf16[1,256,1024]{2,1,0:T(8,128)(2,1)} %param.8) | copy-start | bytes 1572868
  95.8 16.7 %collective-permute-start.33 = (bf16[256,384]{1,0:T(8,128)(2,1)S(1)}, bf16[256,384]{1,0:T(8,128)(2,1)S(1)}, u32[]{:S(2)}, u32[]{:S(2)}) collective-permute-start(bf16[256,384]{1,0:T(8,128)(2,1)S(1)} %get-tuple-element.43), channel_id=1, source_target_pairs={{0,1},{1,0},{2,3},{3,2},{4,5},{5,4},{6,7},{7,6},{8,9},{9,8},{10,11... | collective-permute-start | bytes 589832 | tf_op jit(solution)/shard_map/ppermute | solution.py:327
  96.0 17.9 %collective-permute-start.34 = (bf16[256,384]{1,0:T(8,128)(2,1)S(1)}, bf16[256,384]{1,0:T(8,128)(2,1)S(1)}, u32[]{:S(2)}, u32[]{:S(2)}) collective-permute-start(bf16[256,384]{1,0:T(8,128)(2,1)S(1)} %get-tuple-element.44), channel_id=1, source_target_pairs={{0,2},{1,3},{2,0},{3,1},{4,6},{5,7},{6,4},{7,5},{8,10},{9,11},{10,... | collective-permute-start | bytes 589832 | tf_op jit(solution)/shard_map/ppermute | solution.py:327
  97.7 6.3 %collective-permute-start.11 = (bf16[256,128]{1,0:T(8,128)(2,1)S(1)}, bf16[256,128]{1,0:T(8,128)(2,1)S(1)}, u32[]{:S(2)}, u32[]{:S(2)}) collective-permute-start(bf16[256,128]{1,0:T(8,128)(2,1)S(1)} %get-tuple-element.29), channel_id=1, source_target_pairs={{0,3},{1,2},{2,1},{3,0},{4,7},{5,6},{6,5},{7,4},{8,11},{9,10},{10,... | collective-permute-start | bytes 196616 | tf_op jit(solution)/shard_map/ppermute | solution.py:327
  97.7 7.6 %collective-permute-start.12 = (bf16[256,128]{1,0:T(8,128)(2,1)S(1)}, bf16[256,128]{1,0:T(8,128)(2,1)S(1)}, u32[]{:S(2)}, u32[]{:S(2)}) collective-permute-start(bf16[256,128]{1,0:T(8,128)(2,1)S(1)} %get-tuple-element.30), channel_id=1, source_target_pairs={{0,4},{1,5},{2,6},{3,7},{4,0},{5,1},{6,2},{7,3},{8,12},{9,13},{10,... | collective-permute-start | bytes 196616 | tf_op jit(solution)/shard_map/ppermute | solution.py:327
  99.4 7.3 %collective-permute-start.13 = (bf16[256,128]{1,0:T(8,128)(2,1)S(1)}, bf16[256,128]{1,0:T(8,128)(2,1)S(1)}, u32[]{:S(2)}, u32[]{:S(2)}) collective-permute-start(bf16[256,128]{1,0:T(8,128)(2,1)S(1)} %get-tuple-element.31), channel_id=1, source_target_pairs={{0,5},{1,4},{2,7},{3,6},{4,1},{5,0},{6,3},{7,2},{8,13},{9,12},{10,... | collective-permute-start | bytes 196616 | tf_op jit(solution)/shard_map/ppermute | solution.py:327
  104.0 5.4 %collective-permute-start.14 = (bf16[256,128]{1,0:T(8,128)(2,1)S(1)}, bf16[256,128]{1,0:T(8,128)(2,1)S(1)}, u32[]{:S(2)}, u32[]{:S(2)}) collective-permute-start(bf16[256,128]{1,0:T(8,128)(2,1)S(1)} %get-tuple-element.32), channel_id=1, source_target_pairs={{0,6},{1,7},{2,4},{3,5},{4,2},{5,3},{6,0},{7,1},{8,14},{9,15},{10,... | collective-permute-start | bytes 196616 | tf_op jit(solution)/shard_map/ppermute | solution.py:327
  105.3 5.1 %collective-permute-start.15 = (bf16[256,128]{1,0:T(8,128)(2,1)S(1)}, bf16[256,128]{1,0:T(8,128)(2,1)S(1)}, u32[]{:S(2)}, u32[]{:S(2)}) collective-permute-start(bf16[256,128]{1,0:T(8,128)(2,1)S(1)} %get-tuple-element.33), channel_id=1, source_target_pairs={{0,7},{1,6},{2,5},{3,4},{4,3},{5,2},{6,1},{7,0},{8,15},{9,14},{10,... | collective-permute-start | bytes 196616 | tf_op jit(solution)/shard_map/ppermute | solution.py:327
  106.7 5.5 %collective-permute-start.9 = (bf16[256,128]{1,0:T(8,128)(2,1)S(1)}, bf16[256,128]{1,0:T(8,128)(2,1)S(1)}, u32[]{:S(2)}, u32[]{:S(2)}) collective-permute-start(bf16[256,128]{1,0:T(8,128)(2,1)S(1)} %get-tuple-element.27), channel_id=1, source_target_pairs={{0,1},{1,0},{2,3},{3,2},{4,5},{5,4},{6,7},{7,6},{8,9},{9,8},{10,11... | collective-permute-start | bytes 196616 | tf_op jit(solution)/shard_map/ppermute | solution.py:327
  109.4 7.1 %collective-permute-start.35 = (bf16[256,384]{1,0:T(8,128)(2,1)S(1)}, bf16[256,384]{1,0:T(8,128)(2,1)S(1)}, u32[]{:S(2)}, u32[]{:S(2)}) collective-permute-start(bf16[256,384]{1,0:T(8,128)(2,1)S(1)} %get-tuple-element.45), channel_id=1, source_target_pairs={{0,3},{1,2},{2,1},{3,0},{4,7},{5,6},{6,5},{7,4},{8,11},{9,10},{10,... | collective-permute-start | bytes 589832 | tf_op jit(solution)/shard_map/ppermute | solution.py:327
  110.5 16.2 %collective-permute-start.36 = (bf16[256,384]{1,0:T(8,128)(2,1)S(1)}, bf16[256,384]{1,0:T(8,128)(2,1)S(1)}, u32[]{:S(2)}, u32[]{:S(2)}) collective-permute-start(bf16[256,384]{1,0:T(8,128)(2,1)S(1)} %get-tuple-element.46), channel_id=1, source_target_pairs={{0,4},{1,5},{2,6},{3,7},{4,0},{5,1},{6,2},{7,3},{8,12},{9,13},{10,... | collective-permute-start | bytes 589832 | tf_op jit(solution)/shard_map/ppermute | solution.py:327
  112.2 18.1 %collective-permute-start.37 = (bf16[256,384]{1,0:T(8,128)(2,1)S(1)}, bf16[256,384]{1,0:T(8,128)(2,1)S(1)}, u32[]{:S(2)}, u32[]{:S(2)}) collective-permute-start(bf16[256,384]{1,0:T(8,128)(2,1)S(1)} %get-tuple-element.47), channel_id=1, source_target_pairs={{0,5},{1,4},{2,7},{3,6},{4,1},{5,0},{6,3},{7,2},{8,13},{9,12},{10,... | collective-permute-start | bytes 589832 | tf_op jit(solution)/shard_map/ppermute | solution.py:327
  112.5 17.8 %collective-permute-start.38 = (bf16[256,384]{1,0:T(8,128)(2,1)S(1)}, bf16[256,384]{1,0:T(8,128)(2,1)S(1)}, u32[]{:S(2)}, u32[]{:S(2)}) collective-permute-start(bf16[256,384]{1,0:T(8,128)(2,1)S(1)} %get-tuple-element.48), channel_id=1, source_target_pairs={{0,6},{1,7},{2,4},{3,5},{4,2},{5,3},{6,0},{7,1},{8,14},{9,15},{10,... | collective-permute-start | bytes 589832 | tf_op jit(solution)/shard_map/ppermute | solution.py:327
  113.9 16.4 %collective-permute-start.39 = (bf16[256,384]{1,0:T(8,128)(2,1)S(1)}, bf16[256,384]{1,0:T(8,128)(2,1)S(1)}, u32[]{:S(2)}, u32[]{:S(2)}) collective-permute-start(bf16[256,384]{1,0:T(8,128)(2,1)S(1)} %get-tuple-element.49), channel_id=1, source_target_pairs={{0,7},{1,6},{2,5},{3,4},{4,3},{5,2},{6,1},{7,0},{8,15},{9,14},{10,... | collective-permute-start | bytes 589832 | tf_op jit(solution)/shard_map/ppermute | solution.py:327
  116.5 20.0 %collective-permute-start.16 = (bf16[256,1024]{1,0:T(8,128)(2,1)S(1)}, bf16[256,1024]{1,0:T(8,128)(2,1)S(1)}, u32[]{:S(2)}, u32[]{:S(2)}) collective-permute-start(bf16[256,1024]{1,0:T(8,128)(2,1)S(1)} %shard_map.78), channel_id=1, source_target_pairs={{0,8},{8,16},{16,24},{1,9},{9,17},{17,25},{2,10},{10,18},{18,26},{... | collective-permute-start | bytes 1572872 | tf_op jit(solution)/shard_map/ppermute | solution.py:374
  134.2 16.2 %collective-permute-start.40 = (bf16[256,1024]{1,0:T(8,128)(2,1)S(1)}, bf16[256,1024]{1,0:T(8,128)(2,1)S(1)}, u32[]{:S(2)}, u32[]{:S(2)}) collective-permute-start(bf16[256,1024]{1,0:T(8,128)(2,1)S(1)} %shard_map.81), channel_id=1, source_target_pairs={{8,0},{16,8},{24,16},{9,1},{17,9},{25,17},{10,2},{18,10},{26,18},{... | collective-permute-start | bytes 1572872 | tf_op jit(solution)/shard_map/ppermute | solution.py:374
  (4 other events, 4.5 us)

commit v2 on v1

--- a/solution.py
+++ b/solution.py
@@ -12,11 +12,11 @@
 TILE = 128
 CAPACITY = 3
 EPSILON = 1e-05
-VMEM_LIMIT = 40 * 1024 * 1024
+VMEM_LIMIT = 24 * 1024 * 1024
 NT = (((1,), (1,)), ((), ()))
 NN = (((1,), (0,)), ((), ()))
 TN = (((0,), (0,)), ((), ()))
-ANY = pl.BlockSpec(memory_space=pl.ANY)
+HBM = pl.BlockSpec(memory_space=pltpu.HBM)
 SMEM = pl.BlockSpec(memory_space=pltpu.SMEM)
 VMEM = pl.BlockSpec(memory_space=pltpu.VMEM)
 
@@ -101,14 +101,12 @@
 
 
 def head_kernel(back, pieces, spacing, *refs):
-    refs = list(refs)
     cluster_ref, info_ref = refs[:2]
     x_refs = refs[2 : 2 + len(pieces)]
     refs = refs[2 + len(pieces) :]
-    g_refs = [refs.pop(0) for _ in range(HEADS if back else 0)]
-    w_ref = refs.pop(0)
-    out_refs = [refs.pop(0) for _ in range(HEADS)]
-    xbuf, wbuf, turned, kept, out, count, member, xsem, wsem = refs[:9]
+    if back:
+        g_ref, refs = refs[0], refs[1:]
+    w_ref, out, xbuf, wbuf, turned, kept, count, member, xsem, wsem = refs[:10]
     flip, head, residue = info_ref[0], info_ref[1], info_ref[2]
     tiles = kept.shape[0]
     clusters = count.shape[0]
@@ -118,10 +116,8 @@
     for i, (k, start, rows) in enumerate(pieces):
         copies.append(fetch(x_refs[i], xbuf.at[k, pl.ds(start, rows)], xsem.at[i]))
     if back:
-        scales, grads, gsem = refs[9:]
-        g_copies = []
-        for k in range(HEADS):
-            g_copies.append(fetch(g_refs[k], grads.at[pl.ds(2 * (flip ^ k), 2)], gsem.at[k]))
+        scales, grads, gsem = refs[10:]
+        g_copy = fetch(g_ref, grads, gsem)
 
     for c in range(clusters):
         count[c] = 0
@@ -141,8 +137,11 @@
     def project(k, carry):
         for (slot, _, _), copy in zip(pieces, copies):
             pl.when(k == slot)(copy.wait)
-        x = high(xbuf[k])
-        mixed = dot(low(x * rows_rsqrt(x)), turned[...], NN)
+        normed = xbuf[k]
+        if back:
+            x = high(normed)
+            normed = low(x * rows_rsqrt(x))
+        mixed = dot(normed, turned[...], NN)
         place = 2 * (flip ^ k)
         for c in range(3):
             u = mixed[:, c * HD : (c + 1) * HD]
@@ -159,8 +158,7 @@
 
     lax.fori_loop(0, HEADS, project, 0)
     if back:
-        for copy in g_copies:
-            copy.wait()
+        g_copy.wait()
 
     def visit(c, carry):
         for n in range(1, CAPACITY + 1):
@@ -176,8 +174,6 @@
         return carry
 
     lax.fori_loop(0, clusters, visit, 0)
-    for k in range(HEADS):
-        out_refs[k][...] = out[pl.ds(2 * (flip ^ k), 2)].reshape(out_refs[k].shape)
 
 
 def head_work(info, tile_cluster, pieces, w_qkv, spacing, grads=None):
@@ -188,7 +184,7 @@
     tokens = tiles * TILE
     operands = [tile_cluster, info] + [array for _, _, array in pieces]
     if back:
-        operands += [g.reshape(2, TILE, HD) for g in grads]
+        operands.append(grads.reshape(tiles, TILE, HD))
     operands.append(w_qkv.reshape(3, HEADS, HD, width))
     shapes = tuple((k, start, array.shape[0]) for k, start, array in pieces)
     scratch = [
@@ -196,7 +192,6 @@
         pltpu.VMEM((3, HD, width), jnp.bfloat16),
         pltpu.VMEM((width, 3 * HD), jnp.bfloat16),
         pltpu.VMEM((tiles, TILE, 3 * HD), jnp.bfloat16),
-        pltpu.VMEM((tiles, TILE, wide), jnp.bfloat16),
         pltpu.SMEM((tiles // 2,), jnp.int32),
         pltpu.SMEM((tiles // 2 * CAPACITY,), jnp.int32),
         pltpu.SemaphoreType.DMA((len(pieces),)),
@@ -206,74 +201,56 @@
         scratch += [
             pltpu.VMEM((tiles, TILE, 2 * HD), jnp.float32),
             pltpu.VMEM((tiles, TILE, HD), jnp.bfloat16),
-            pltpu.SemaphoreType.DMA((HEADS,)),
+            pltpu.SemaphoreType.DMA,
         ]
-    return call(
+    out = call(
         functools.partial(head_kernel, back, shapes, spacing),
         operands,
-        [SMEM, SMEM] + [ANY] * (len(operands) - 2),
-        tuple(jax.ShapeDtypeStruct((2 * TILE, wide), jnp.bfloat16) for _ in range(HEADS)),
+        [SMEM, SMEM] + [HBM] * (len(operands) - 2),
+        jax.ShapeDtypeStruct((tiles, TILE, wide), jnp.bfloat16),
         scratch,
         2 * tokens * width * 3 * HD + tokens * 512 * HD * (14 if back else 4),
         2 * tokens * (width + 2 * wide),
     )
-
-
-def spread_kernel(info_ref, up_ref, w_ref, *refs):
-    out_refs, (up, rows, up_sem, sems) = refs[:HEADS], refs[HEADS:]
-    flip = info_ref[0]
-    up_copy = fetch(up_ref, up, up_sem)
-    copies = [fetch(w_ref.at[flip ^ k], rows.at[k], sems.at[k]) for k in range(HEADS)]
-    up_copy.wait()
+    return out.reshape(HEADS, 2 * TILE, wide)
+
+
+def norm_kernel(x_ref, *refs):
+    out_ref = refs[-1]
+    x = high(x_ref[...])
+    out_ref[...] = low(x * rows_rsqrt(x))
+
+
+def norm_after(x, earlier):
+    return call(
+        norm_kernel,
+        [x, *earlier],
+        [VMEM] + [HBM] * len(earlier),
+        jax.ShapeDtypeStruct(x.shape, jnp.bfloat16),
+        [],
+        4 * x.size,
+        4 * x.size,
+    )
+
+
+def spread_kernel(up_ref, w_ref, out_ref, rows, sems):
+    copies = [fetch(w_ref.at[k], rows.at[k], sems.at[k]) for k in range(HEADS)]
     for k in range(0, HEADS, 2):
         copies[k].wait()
         copies[k + 1].wait()
         pair = rows[k : k + 2].reshape(2 * HD, -1)
-        g = low(dot(up[...], pair, NT))
-        out_refs[k][...] = g[:, :HD]
-        out_refs[k + 1][...] = g[:, HD:]
-
-
-def spread_grads(info, upstream, w_fin):
+        g = low(dot(up_ref[...], pair, NT))
+        out_ref[k] = g[:, :HD]
+        out_ref[k + 1] = g[:, HD:]
+
+
+def spread_grads(upstream, w_fin):
     tokens, width = upstream.shape
     return call(
         spread_kernel,
-        [info, upstream, w_fin.reshape(HEADS, HD, width)],
-        [SMEM, ANY, ANY],
-        tuple(jax.ShapeDtypeStruct((tokens, HD), jnp.bfloat16) for _ in range(HEADS)),
-        [
-            pltpu.VMEM((tokens, width), jnp.bfloat16),
-            pltpu.VMEM((HEADS, HD, width), jnp.bfloat16),
-            pltpu.SemaphoreType.DMA,
-            pltpu.SemaphoreType.DMA((HEADS,)),
-        ],
-        2 * tokens * width * HEADS * HD,
-        2 * width * HEADS * HD,
-    )
-
-
-def finish_kernel(info_ref, *refs):
-    att_refs, (x_ref, w_ref, out_ref, rows, sems) = refs[:HEADS], refs[HEADS:]
-    flip = info_ref[0]
-    copies = [fetch(w_ref.at[flip ^ k], rows.at[k], sems.at[k]) for k in range(HEADS)]
-    att = jnp.concatenate([ref[...] for ref in att_refs], axis=1)
-    for copy in copies:
-        copy.wait()
-    width = x_ref.shape[1]
-    block = 256
-    for start in range(0, width, block):
-        columns = slice(start, start + block)
-        w = rows[:, :, columns].reshape(HEADS * HD, block)
-        out_ref[:, columns] = low(high(x_ref[:, columns]) + dot(att, w, NN))
-
-
-def finish(info, attention, current, w_fin):
-    tokens, width = current.shape
-    return call(
-        finish_kernel,
-        [info, *attention, current, w_fin.reshape(HEADS, HD, width)],
-        [SMEM] + [VMEM] * (HEADS + 1) + [ANY],
-        jax.ShapeDtypeStruct((tokens, width), jnp.bfloat16),
+        [upstream, w_fin.reshape(HEADS, HD, width)],
+        [VMEM, HBM],
+        jax.ShapeDtypeStruct((HEADS, tokens, HD), jnp.bfloat16),
         [
             pltpu.VMEM((HEADS, HD, width), jnp.bfloat16),
             pltpu.SemaphoreType.DMA((HEADS,)),
@@ -283,17 +260,34 @@
     )
 
 
-def finish_back_kernel(info_ref, *refs):
-    grad_refs, (x_ref, up_ref, w_ref, out_ref, rows, total, sems) = refs[:HEADS], refs[HEADS:]
-    flip = info_ref[0]
-    copies = [fetch(w_ref.at[:, flip ^ k], rows.at[k], sems.at[k]) for k in range(HEADS)]
-    width = x_ref.shape[1]
-    for k in range(0, HEADS, 2):
-        copies[k].wait()
-        copies[k + 1].wait()
-        grads = jnp.concatenate([grad_refs[k][...], grad_refs[k + 1][...]], axis=1)
-        product = dot(grads, rows[k : k + 2].reshape(6 * HD, width), NN)
-        if k == 0:
+def finish_kernel(att_ref, x_ref, w_ref, out_ref):
+    att = jnp.concatenate([att_ref[k] for k in range(HEADS)], axis=1)
+    block = 256
+    for start in range(0, x_ref.shape[1], block):
+        columns = slice(start, start + block)
+        out_ref[:, columns] = low(high(x_ref[:, columns]) + dot(att, w_ref[:, columns], NN))
+
+
+def finish(attention, current, w_fin):
+    tokens, width = current.shape
+    return call(
+        finish_kernel,
+        [attention, current, w_fin],
+        [VMEM] * 3,
+        jax.ShapeDtypeStruct((tokens, width), jnp.bfloat16),
+        [],
+        2 * tokens * width * HEADS * HD,
+        2 * width * HEADS * HD,
+    )
+
+
+def finish_back_kernel(grad_ref, x_ref, up_ref, w_ref, out_ref, total):
+    for c in range(3):
+        grads = jnp.concatenate(
+            [grad_ref[k, :, c * HD : (c + 1) * HD] for k in range(HEADS)], axis=1
+        )
+        product = dot(grads, w_ref[c * HEADS * HD : (c + 1) * HEADS * HD], NN)
+        if c == 0:
             total[...] = product
         else:
             total[...] += product
@@ -305,18 +299,14 @@
     out_ref[...] = low(high(up_ref[...]) + pulled)
 
 
-def finish_back(info, grads, stored, upstream, w_qkv):
+def finish_back(grads, stored, upstream, w_qkv):
     tokens, width = stored.shape
     return call(
         finish_back_kernel,
-        [info, *grads, stored, upstream, w_qkv.reshape(3, HEADS, HD, width)],
-        [SMEM] + [VMEM] * (HEADS + 2) + [ANY],
+        [grads, stored, upstream, w_qkv],
+        [VMEM] * 4,
         jax.ShapeDtypeStruct((tokens, width), jnp.bfloat16),
-        [
-            pltpu.VMEM((HEADS, 3, HD, width), jnp.bfloat16),
-            pltpu.VMEM((tokens, width), jnp.float32),
-            pltpu.SemaphoreType.DMA((HEADS,)),
-        ],
+        [pltpu.VMEM((tokens, width), jnp.float32)],
         2 * tokens * width * 3 * HEADS * HD,
         6 * width * HEADS * HD,
     )
@@ -333,11 +323,6 @@
     top, bottom = partner(over_x[:half], 4), partner(over_y[half:], 2)
     pieces = [(0, 0, x), (2, 0, over_x), (4, 0, over_y), (6, 0, top), (6, half, bottom)]
     return pieces + [(k + 1, start, partner(block, 1)) for k, start, block in pieces]
-
-
-def swap(blocks):
-    moved = {k: partner(blocks[k], k) for k in (2, 4, 6, 3, 5, 7, 1)}
-    return [blocks[0]] + [moved[k] for k in range(1, HEADS)]
 
 
 def all_swap(blocks):
@@ -354,18 +339,18 @@
     arrived = all_swap(padded.reshape(heads * spacing, TILE, width))
     arrived = arrived.reshape(-1, places, TILE, width)
     mine = lax.dynamic_index_in_dim(arrived, own % spacing // held, 1, keepdims=False)
-    return list(mine.reshape(HEADS, 2 * TILE, width))
+    return mine.reshape(HEADS, 2 * TILE, width)
 
 
 def to_tokens(blocks, own, spacing, tokens):
     held = tokens // TILE
     places = spacing // held
-    tiled = jnp.stack(blocks).reshape(2 * HEADS, 1, TILE, -1)
+    tiled = blocks.reshape(2 * HEADS, 1, TILE, -1)
     padded = jnp.zeros((2 * HEADS, places, TILE, tiled.shape[3]), tiled.dtype)
     padded = lax.dynamic_update_slice_in_dim(padded, tiled, own % spacing // held, 1)
     returned = all_swap(padded.reshape(-1, TILE, tiled.shape[3]))
     returned = returned.reshape(HEADS, places, held * TILE, tiled.shape[3])
-    return list(lax.dynamic_index_in_dim(returned, own % places, 1, keepdims=False))
+    return lax.dynamic_index_in_dim(returned, own % places, 1, keepdims=False)
 
 
 def passed_along(block, axis, distance):
@@ -382,30 +367,31 @@
     own = lax.axis_index("seq").astype(jnp.int32)
     if spacing == 1:
         info = jnp.stack([own, own, jnp.zeros_like(own)])
-        gather, spread, collect = gather_rows, swap, swap
+        gather, spread, collect = gather_rows, all_swap, all_swap
     else:
         info = jnp.stack([jnp.zeros_like(own), own // spacing, own % spacing])
 
         def gather(x):
             copies = jnp.broadcast_to(x, (HEADS, *x.shape))
-            return [(k, 0, b) for k, b in enumerate(to_heads(copies, own, spacing))]
+            return [(k, 0, block) for k, block in enumerate(to_heads(copies, own, spacing))]
 
         def spread(blocks):
-            return to_heads(jnp.stack(blocks), own, spacing)
+            return to_heads(blocks, own, spacing)
 
         def collect(blocks):
             return to_tokens(blocks, own, spacing, tokens)
 
     stored_pieces = gather(stored)
-    grad_attention = spread(spread_grads(info, upstream, w_fin))
-    current_pieces = gather(current)
+    grad_attention = spread(spread_grads(upstream, w_fin))
+    earlier = [block for k, _, block in stored_pieces if k == HEADS - 2]
+    current_pieces = gather(norm_after(current, earlier))
     grads = head_work(info, tile_cluster, stored_pieces, w_rows, spacing, grad_attention)
     returned_grads = collect(grads)
     outputs = head_work(info, tile_cluster, current_pieces, w_rows, spacing)
     returned = collect(outputs)
-    grad_self = finish_back(info, returned_grads, stored, upstream, w_rows)
+    grad_self = finish_back(returned_grads, stored, upstream, w_rows)
     grad_input = passed_along(grad_self, "pipe", -1)
-    result = finish(info, returned, current, w_fin)
+    result = finish(returned, current, w_fin)
     next_input = passed_along(result, "pipe", 1)
     return (next_input[None], grad_input[None])
 

time: 154 us -> 144 us (0.935)
  waiting for transfers between devices: 75.8 us -> 60.4 us
  local copies, waits for them, and re-layouts: 9.89 us -> 20.4 us
  starting transfers between devices: 35 us -> 31.4 us
    ppermute x39 -> x18, waiting for transfers between devices: 62 us -> 32.4 us  [partner(): return lax.ppermute(block, 'seq', route)]
    ppermute x39 -> x18, starting transfers between devices: 29.1 us -> 10.8 us  [partner(): return lax.ppermute(block, 'seq', route)]
    all_to_all x0 -> x3, starting transfers between devices: none -> 14.7 us  [all_swap(): lax.all_to_all(blocks, 'seq', split_axis=0, concat_axis=0, tiled=True)]
    all_to_all x0 -> x3, waiting for transfers between devices: none -> 14.6 us  [all_swap(): lax.all_to_all(blocks, 'seq', split_axis=0, concat_axis=0, tiled=True)]
    unnamed x24 -> x42, local copies, waits for them, and re-layouts: 8.86 us -> 19.4 us
    pallas_call x5 -> x6, Pallas kernels: 30.3 us -> 29.9 us  [call(): pl.pallas_call(kernel, in_specs=in_specs, out_specs=tuple((VMEM for _ in...]
  transfers between devices with their start and end apart: 41 -> 23, of which waited for: 13 -> 9; matrix products, arithmetic and copies ran while one was open for 1% -> 1% of each run, Pallas kernels for 20% -> 21%
where the time goes in v2:
time: 144 us; the launch traced here: 143 us
  waiting for transfers between devices  60.4 us (42%)
  starting transfers between devices  31.4 us (22%)
  Pallas kernels  29.9 us (21%)
  local copies, waits for them, and re-layouts  20.4 us (14%)
    ppermute x18, waiting for transfers between devices, partner(): return lax.ppermute(block, 'seq', route)  32.4 us
    pallas_call x6, Pallas kernels, call(): pl.pallas_call(kernel, in_specs=in_specs, out_specs=tuple((VMEM for _ in...  29.9 us
    unnamed x42, local copies, waits for them, and re-layouts  19.4 us
    all_to_all x3, starting transfers between devices, all_swap(): lax.all_to_all(blocks, 'seq', split_axis=0, concat_axis=0, tiled=True)  14.7 us
    all_to_all x3, waiting for transfers between devices, all_swap(): lax.all_to_all(blocks, 'seq', split_axis=0, concat_axis=0, tiled=True)  14.6 us
    ppermute x2, waiting for transfers between devices, passed_along(): return lax.ppermute(block, axis, route)  13.4 us
    ppermute x18, starting transfers between devices, partner(): return lax.ppermute(block, 'seq', route)  10.8 us
    ppermute x2, starting transfers between devices, passed_along(): return lax.ppermute(block, axis, route)  5.83 us
  transfers between devices with their start and end apart: 23, of which 9 were waited for; matrix products, arithmetic and copies ran while one was open for 1% of the time, Pallas kernels for 21%

profile of v2, /device:TPU:18, one launch (start us, length us, event | category | flops | bytes accessed | tf_op | source)
XLA Modules:
  0.0 142.9 jit_solution(9324529674512674543)
XLA Ops:
  0.6 0.6 collective-permute-start
  1.2 1.5 %collective-permute-start.2 = (bf16[256,1024]{1,0:T(8,128)(2,1)}, bf16[256,1024]{1,0:T(8,128)(2,1)S(1)}, u32[]{:S(2)}, u32[]{:S(2)}) collective-permute-start(bf16[256,1024]{1,0:T(8,128)(2,1)} %bitcast.24), channel_id=1, source_target_pairs={{0,4},{1,5},{2,6},{3,7},{4,0},{5,1},{6,2},{7,3},{8,12},{9,13},{10,... | collective-permute-start | bytes 1572872 | tf_op jit(solution)/shard_map/ppermute | solution.py:317
  2.8 11.8 %collective-permute-done.refs_3_ = bf16[256,1024]{1,0:T(8,128)(2,1)S(1)} collective-permute-done((bf16[256,1024]{1,0:T(8,128)(2,1)}, bf16[256,1024]{1,0:T(8,128)(2,1)S(1)}, u32[]{:S(2)}, u32[]{:S(2)}) %collective-permute-start) | collective-permute-done | bytes 524320 | tf_op jit(solution)/shard_map/ppermute | solution.py:317
  14.6 1.6 %collective-permute-start.1 = (bf16[128,1024]{1,0:T(8,128)(2,1)S(1)}, bf16[128,1024]{1,0:T(8,128)(2,1)S(1)}, u32[]{:S(2)}, u32[]{:S(2)}) collective-permute-start(bf16[128,1024]{1,0:T(8,128)(2,1)S(1)} %slice.16), channel_id=1, source_target_pairs={{0,4},{1,5},{2,6},{3,7},{4,0},{5,1},{6,2},{7,3},{8,12},{9,13},{10,... | collective-permute-start | bytes 786440 | tf_op jit(solution)/shard_map/ppermute | solution.py:317
  16.2 0.6 collective-permute-start.3
  16.8 5.0 %collective-permute-done.1.refs_0_.refs_5_ = bf16[128,1024]{1,0:T(8,128)(2,1)S(1)} collective-permute-done((bf16[128,1024]{1,0:T(8,128)(2,1)S(1)}, bf16[128,1024]{1,0:T(8,128)(2,1)S(1)}, u32[]{:S(2)}, u32[]{:S(2)}) %collective-permute-start.1) | collective-permute-done | bytes 262176 | tf_op jit(solution)/shard_map/ppermute | solution.py:317
  21.8 1.3 collective-permute-done.3.refs_1_.refs_6_
  23.2 1.1 copy-done.4
  24.3 0.2 shard_map.77.refs_2_
  24.5 0.6 collective-permute-start.4
  25.1 1.1 collective-permute-start.5
  26.2 10.0 %collective-permute-done.4.refs_3_ = bf16[256,1024]{1,0:T(8,128)(2,1)S(1)} collective-permute-done((bf16[256,1024]{1,0:T(8,128)(2,1)S(1)}, bf16[256,1024]{1,0:T(8,128)(2,1)S(1)}, u32[]{:S(2)}, u32[]{:S(2)}) %collective-permute-start.4) | collective-permute-done | bytes 524320 | tf_op jit(solution)/shard_map/ppermute | solution.py:317
  36.2 0.6 collective-permute-start.6
  36.8 0.3 collective-permute-done.5.refs_4_
  37.1 1.0 slice.19
  38.1 2.5 %collective-permute-start.7 = (bf16[128,1024]{1,0:T(8,128)(2,1)S(1)}, bf16[128,1024]{1,0:T(8,128)(2,1)}, u32[]{:S(2)}, u32[]{:S(2)}) collective-permute-start(bf16[128,1024]{1,0:T(8,128)(2,1)S(1)} %slice.19), channel_id=1, source_target_pairs={{0,2},{1,3},{2,0},{3,1},{4,6},{5,7},{6,4},{7,5},{8,10},{9,11},{10,... | collective-permute-start | bytes 786440 | tf_op jit(solution)/shard_map/ppermute | solution.py:317
  40.6 0.5 collective-permute-start.9
  41.1 1.5 %collective-permute-done.6.refs_5_ = bf16[128,1024]{1,0:T(8,128)(2,1)S(1)} collective-permute-done((bf16[128,1024]{1,0:T(8,128)(2,1)S(1)}, bf16[128,1024]{1,0:T(8,128)(2,1)S(1)}, u32[]{:S(2)}, u32[]{:S(2)}) %collective-permute-start.6) | collective-permute-done | bytes 262176 | tf_op jit(solution)/shard_map/ppermute | solution.py:317
  42.6 2.4 %collective-permute-done.7.refs_6_ = bf16[128,1024]{1,0:T(8,128)(2,1)} collective-permute-done((bf16[128,1024]{1,0:T(8,128)(2,1)S(1)}, bf16[128,1024]{1,0:T(8,128)(2,1)}, u32[]{:S(2)}, u32[]{:S(2)}) %collective-permute-start.7) | collective-permute-done | bytes 262176 | tf_op jit(solution)/shard_map/ppermute | solution.py:317
  45.1 2.9 %shard_map.80 = bf16[8,256,128]{2,1,0:T(8,128)(2,1)} custom-call(bf16[256,1024]{1,0:T(8,128)(2,1)S(1)} %bitcast.20, bf16[8,128,1024]{2,1,0:T(8,128)(2,1)S(1)} %bitcast.16), custom_call_target="tpu_custom_call" | custom-call | flops 536870912 | bytes 2097152 | tf_op jit(solution)/shard_map/pallas_call | solution.py:42
  47.9 6.1 %all-to-all-start.1 = ((bf16[8,256,128]{2,1,0:T(8,128)(2,1)}), bf16[8,256,128]{2,1,0:T(8,128)(2,1)}, u32[]{:S(2)}, u32[]{:S(2)}) async-start(bf16[8,256,128]{2,1,0:T(8,128)(2,1)} %shard_map.80), calls=%async_computation.1 | async-start | bytes 1048576 | tf_op jit(solution)/shard_map/all_to_all | solution.py:329
  54.0 0.1 collective-permute-start.14
  54.2 0.4 collective-permute-start.15
  54.5 0.1 collective-permute-start.16
  54.8 0.4 collective-permute-start.17
  55.3 2.8 %copy-done = bf16[1,3072,1024]{2,1,0:T(8,128)(2,1)S(1)} copy-done((bf16[1,3072,1024]{2,1,0:T(8,128)(2,1)S(1)}, bf16[1,3072,1024]{2,1,0:T(8,128)(2,1)}, u32[]{:S(2)}) %copy-start) | copy-done | bytes 6291480
  58.1 10.1 %shard_map.78 = bf16[16,128,128]{2,1,0:T(8,128)(2,1)} custom-call(s32[16]{0:T(128)S(1)} %copy-done.19, s32[3]{0:T(128)S(1)} %pad_add_fusion.refs_1_, bf16[256,1024]{1,0:T(8,128)(2,1)S(1)} %shard_map.77.refs_2_, bf16[256,1024]{1,0:T(8,128)(2,1)S(1)} %collective-permute-done.4.refs_3_, bf16[256,1024]{1,0:T(8,128)(2,1)} %collective-permute-done.5.refs_4_, ...), custom_call_target="tpu_custom_call" | custom-call | flops 2147483648 | bytes 5242880 | tf_op jit(solution)/shard_map/pallas_call | solution.py:42
  68.2 4.3 %all-to-all-start = ((bf16[8,256,128]{2,1,0:T(8,128)(2,1)}), bf16[8,256,128]{2,1,0:T(8,128)(2,1)S(1)}, u32[]{:S(2)}, u32[]{:S(2)}) async-start(bf16[8,256,128]{2,1,0:T(8,128)(2,1)} %bitcast.4), calls=%async_computation | async-start | bytes 1048576 | tf_op jit(solution)/shard_map/all_to_all | solution.py:329
  72.5 2.8 %copy-done.1 = bf16[1,3072,1024]{2,1,0:T(8,128)(2,1)S(1)} copy-done((bf16[1,3072,1024]{2,1,0:T(8,128)(2,1)S(1)}, bf16[1,3072,1024]{2,1,0:T(8,128)(2,1)}, u32[]{:S(2)}) %copy-start.1) | copy-done | bytes 6291480
  75.3 1.0 copy-done.9
  76.3 0.9 copy-done.12
  77.3 0.9 copy-done.14
  78.2 1.0 copy-done.16
  79.2 1.0 copy-done.18
  80.3 11.8 %shard_map.81 = bf16[16,128,384]{2,1,0:T(8,128)(2,1)S(1)} custom-call(s32[16]{0:T(128)S(1)} %copy-done.19, s32[3]{0:T(128)S(1)} %pad_add_fusion.refs_1_, bf16[256,1024]{1,0:T(8,128)(2,1)S(1)} %bitcast.26, bf16[256,1024]{1,0:T(8,128)(2,1)S(1)} %copy-done.16, bf16[256,1024]{1,0:T(8,128)(2,1)S(1)} %copy-done.18, bf16[128,1024]{1,0:T(8,128)(2,1)S(1)} %copy-done.12, ...), custom_call_target="tpu_custom_call" | custom-call | flops 3489660928 | bytes 7340032 | tf_op jit(solution)/shard_map/pallas_call | solution.py:42
  92.1 1.2 copy-done.8
  93.3 4.4 %all-to-all-start.2 = ((bf16[8,256,384]{2,1,0:T(8,128)(2,1)}), bf16[8,256,384]{2,1,0:T(8,128)(2,1)}, u32[]{:S(2)}, u32[]{:S(2)}) async-start(bf16[8,256,384]{2,1,0:T(8,128)(2,1)} %bitcast.22), calls=%async_computation.2 | async-start | bytes 3145728 | tf_op jit(solution)/shard_map/all_to_all | solution.py:329
  97.7 1.5 %shard_map.79 = bf16[256,1024]{1,0:T(8,128)(2,1)} custom-call(bf16[8,256,128]{2,1,0:T(8,128)(2,1)S(1)} %all-to-all-done.att_ref, bf16[256,1024]{1,0:T(8,128)(2,1)S(1)} %bitcast.19, bf16[1024,1024]{1,0:T(8,128)(2,1)S(1)} %bitcast.17), custom_call_target="tpu_custom_call" | custom-call | flops 536870912 | bytes 2097152 | tf_op jit(solution)/shard_map/pallas_call | solution.py:42
  99.2 3.5 %collective-permute-start.13 = (bf16[256,1024]{1,0:T(8,128)(2,1)}, bf16[256,1024]{1,0:T(8,128)(2,1)S(1)}, u32[]{:S(2)}, u32[]{:S(2)}) collective-permute-start(bf16[256,1024]{1,0:T(8,128)(2,1)} %shard_map.79), channel_id=1, source_target_pairs={{0,8},{8,16},{16,24},{1,9},{9,17},{17,25},{2,10},{10,18},{18,26},{... | collective-permute-start | bytes 1572872 | tf_op jit(solution)/shard_map/ppermute | solution.py:359
  102.7 14.6 %all-to-all-done.2.grad_ref = bf16[8,256,384]{2,1,0:T(8,128)(2,1)} async-done(((bf16[8,256,384]{2,1,0:T(8,128)(2,1)}), bf16[8,256,384]{2,1,0:T(8,128)(2,1)}, u32[]{:S(2)}, u32[]{:S(2)}) %all-to-all-start.2) | async-done | bytes 1572896 | tf_op jit(solution)/shard_map/all_to_all | solution.py:329
  117.3 2.8 %copy-done.2 = bf16[1,3072,1024]{2,1,0:T(8,128)(2,1)S(1)} copy-done((bf16[1,3072,1024]{2,1,0:T(8,128)(2,1)S(1)}, bf16[1,3072,1024]{2,1,0:T(8,128)(2,1)}, u32[]{:S(2)}) %copy-start.2) | copy-done | bytes 6291480
  120.0 1.0 copy-done.7
  121.1 1.0 copy-done.10
  122.1 3.4 %shard_map.82 = bf16[256,1024]{1,0:T(8,128)(2,1)S(1)} custom-call(bf16[8,256,384]{2,1,0:T(8,128)(2,1)} %all-to-all-done.2.grad_ref, bf16[256,1024]{1,0:T(8,128)(2,1)S(1)} %bitcast.27, bf16[256,1024]{1,0:T(8,128)(2,1)S(1)} %bitcast.21, bf16[3072,1024]{1,0:T(8,128)(2,1)S(1)} %bitcast.15), custom_call_target="tpu_custom_call" | custom-call | flops 1610612736 | bytes 6291456 | tf_op jit(solution)/shard_map/pallas_call | solution.py:42
  125.6 2.4 %collective-permute-start.19 = (bf16[256,1024]{1,0:T(8,128)(2,1)S(1)}, bf16[256,1024]{1,0:T(8,128)(2,1)S(1)}, u32[]{:S(2)}, u32[]{:S(2)}) collective-permute-start(bf16[256,1024]{1,0:T(8,128)(2,1)S(1)} %shard_map.82), channel_id=1, source_target_pairs={{8,0},{16,8},{24,16},{9,1},{17,9},{25,17},{10,2},{18,10},{26,18},{... | collective-permute-start | bytes 1572872 | tf_op jit(solution)/shard_map/ppermute | solution.py:359
  127.9 13.4 %collective-permute-done.19 = bf16[256,1024]{1,0:T(8,128)(2,1)S(1)} collective-permute-done((bf16[256,1024]{1,0:T(8,128)(2,1)S(1)}, bf16[256,1024]{1,0:T(8,128)(2,1)S(1)}, u32[]{:S(2)}, u32[]{:S(2)}) %collective-permute-start.19) | collective-permute-done | bytes 524320 | tf_op jit(solution)/shard_map/ppermute | solution.py:359
  141.3 0.8 copy.10
  142.1 0.8 copy.11
  (51 shorter events, 0.4 us)
Async XLA Ops:
  0.6 44.4 %copy-start.3 = (bf16[1,1024,1024]{2,1,0:T(8,128)(2,1)S(1)}, bf16[1,1024,1024]{2,1,0:T(8,128)(2,1)}, u32[]{:S(2)}) copy-start(bf16[1,1024,1024]{2,1,0:T(8,128)(2,1)} %param.10) | copy-start | bytes 6291460
  0.6 13.9 %collective-permute-start = (bf16[256,1024]{1,0:T(8,128)(2,1)}, bf16[256,1024]{1,0:T(8,128)(2,1)S(1)}, u32[]{:S(2)}, u32[]{:S(2)}) collective-permute-start(bf16[256,1024]{1,0:T(8,128)(2,1)} %bitcast.23), channel_id=1, source_target_pairs={{0,2},{1,3},{2,0},{3,1},{4,6},{5,7},{6,4},{7,5},{8,10},{9,11},{10,... | collective-permute-start | bytes 1572872 | tf_op jit(solution)/shard_map/ppermute | solution.py:317
  1.2 15.0 %collective-permute-start.2 = (bf16[256,1024]{1,0:T(8,128)(2,1)}, bf16[256,1024]{1,0:T(8,128)(2,1)S(1)}, u32[]{:S(2)}, u32[]{:S(2)}) collective-permute-start(bf16[256,1024]{1,0:T(8,128)(2,1)} %bitcast.24), channel_id=1, source_target_pairs={{0,4},{1,5},{2,6},{3,7},{4,0},{5,1},{6,2},{7,3},{8,12},{9,13},{10,... | collective-permute-start | bytes 1572872 | tf_op jit(solution)/shard_map/ppermute | solution.py:317
  14.6 8.6 %copy-start.15 = (bf16[256,1024]{1,0:T(8,128)(2,1)}, bf16[256,1024]{1,0:T(8,128)(2,1)S(1)}, u32[]{:S(2)}) copy-start(bf16[256,1024]{1,0:T(8,128)(2,1)S(1)} %collective-permute-done.refs_3_) | copy-start | bytes 1572868
  14.6 7.2 %collective-permute-start.1 = (bf16[128,1024]{1,0:T(8,128)(2,1)S(1)}, bf16[128,1024]{1,0:T(8,128)(2,1)S(1)}, u32[]{:S(2)}, u32[]{:S(2)}) collective-permute-start(bf16[128,1024]{1,0:T(8,128)(2,1)S(1)} %slice.16), channel_id=1, source_target_pairs={{0,4},{1,5},{2,6},{3,7},{4,0},{5,1},{6,2},{7,3},{8,12},{9,13},{10,... | collective-permute-start | bytes 786440 | tf_op jit(solution)/shard_map/ppermute | solution.py:317
  16.2 7.0 %copy-start.17 = (bf16[256,1024]{1,0:T(8,128)(2,1)}, bf16[256,1024]{1,0:T(8,128)(2,1)S(1)}, u32[]{:S(2)}) copy-start(bf16[256,1024]{1,0:T(8,128)(2,1)S(1)} %collective-permute-done.2.refs_4_) | copy-start | bytes 1572868
  16.2 7.0 %collective-permute-start.3 = (bf16[128,1024]{1,0:T(8,128)(2,1)S(1)}, bf16[128,1024]{1,0:T(8,128)(2,1)S(1)}, u32[]{:S(2)}, u32[]{:S(2)}) collective-permute-start(bf16[128,1024]{1,0:T(8,128)(2,1)S(1)} %slice.17), channel_id=1, source_target_pairs={{0,2},{1,3},{2,0},{3,1},{4,6},{5,7},{6,4},{7,5},{8,10},{9,11},{10,... | collective-permute-start | bytes 786440 | tf_op jit(solution)/shard_map/ppermute | solution.py:317
  21.8 20.8 %copy-start.11 = (bf16[128,1024]{1,0:T(8,128)(2,1)}, bf16[128,1024]{1,0:T(8,128)(2,1)S(1)}, u32[]{:S(2)}) copy-start(bf16[128,1024]{1,0:T(8,128)(2,1)S(1)} %collective-permute-done.1.refs_0_.refs_5_) | copy-start | bytes 786436
  23.2 19.5 %copy-start.13 = (bf16[128,1024]{1,0:T(8,128)(2,1)}, bf16[128,1024]{1,0:T(8,128)(2,1)S(1)}, u32[]{:S(2)}) copy-start(bf16[128,1024]{1,0:T(8,128)(2,1)S(1)} %collective-permute-done.3.refs_1_.refs_6_) | copy-start | bytes 786436
  23.2 1.1 copy-start.4
  24.3 20.7 %copy-start.6 = (bf16[1,256,1024]{2,1,0:T(8,128)(2,1)S(1)}, bf16[1,256,1024]{2,1,0:T(8,128)(2,1)}, u32[]{:S(2)}) copy-start(bf16[1,256,1024]{2,1,0:T(8,128)(2,1)} %param.8) | copy-start | bytes 1572868
  24.5 11.7 %collective-permute-start.4 = (bf16[256,1024]{1,0:T(8,128)(2,1)S(1)}, bf16[256,1024]{1,0:T(8,128)(2,1)S(1)}, u32[]{:S(2)}, u32[]{:S(2)}) collective-permute-start(bf16[256,1024]{1,0:T(8,128)(2,1)S(1)} %shard_map.77.refs_2_), channel_id=1, source_target_pairs={{0,2},{1,3},{2,0},{3,1},{4,6},{5,7},{6,4},{7,5},{8,10},{9,11},{10,... | collective-permute-start | bytes 1572872 | tf_op jit(solution)/shard_map/ppermute | solution.py:317
  25.1 12.0 %collective-permute-start.5 = (bf16[256,1024]{1,0:T(8,128)(2,1)S(1)}, bf16[256,1024]{1,0:T(8,128)(2,1)}, u32[]{:S(2)}, u32[]{:S(2)}) collective-permute-start(bf16[256,1024]{1,0:T(8,128)(2,1)S(1)} %shard_map.77.refs_2_), channel_id=1, source_target_pairs={{0,4},{1,5},{2,6},{3,7},{4,0},{5,1},{6,2},{7,3},{8,12},{9,13},{10,... | collective-permute-start | bytes 1572872 | tf_op jit(solution)/shard_map/ppermute | solution.py:317
  26.2 27.8 %collective-permute-start.8 = (bf16[256,1024]{1,0:T(8,128)(2,1)S(1)}, bf16[256,1024]{1,0:T(8,128)(2,1)}, u32[]{:S(2)}, u32[]{:S(2)}) collective-permute-start(bf16[256,1024]{1,0:T(8,128)(2,1)S(1)} %shard_map.77.refs_2_), channel_id=1, source_target_pairs={{0,1},{1,0},{2,3},{3,2},{4,5},{5,4},{6,7},{7,6},{8,9},{9,8},{10,11... | collective-permute-start | bytes 1572872 | tf_op jit(solution)/shard_map/ppermute | solution.py:317
  36.2 6.4 %collective-permute-start.6 = (bf16[128,1024]{1,0:T(8,128)(2,1)S(1)}, bf16[128,1024]{1,0:T(8,128)(2,1)S(1)}, u32[]{:S(2)}, u32[]{:S(2)}) collective-permute-start(bf16[128,1024]{1,0:T(8,128)(2,1)S(1)} %slice.18), channel_id=1, source_target_pairs={{0,4},{1,5},{2,6},{3,7},{4,0},{5,1},{6,2},{7,3},{8,12},{9,13},{10,... | collective-permute-start | bytes 786440 | tf_op jit(solution)/shard_map/ppermute | solution.py:317
  38.1 7.0 %collective-permute-start.7 = (bf16[128,1024]{1,0:T(8,128)(2,1)S(1)}, bf16[128,1024]{1,0:T(8,128)(2,1)}, u32[]{:S(2)}, u32[]{:S(2)}) collective-permute-start(bf16[128,1024]{1,0:T(8,128)(2,1)S(1)} %slice.19), channel_id=1, source_target_pairs={{0,2},{1,3},{2,0},{3,1},{4,6},{5,7},{6,4},{7,5},{8,10},{9,11},{10,... | collective-permute-start | bytes 786440 | tf_op jit(solution)/shard_map/ppermute | solution.py:317
  40.6 14.2 %collective-permute-start.10 = (bf16[256,1024]{1,0:T(8,128)(2,1)}, bf16[256,1024]{1,0:T(8,128)(2,1)}, u32[]{:S(2)}, u32[]{:S(2)}) collective-permute-start(bf16[256,1024]{1,0:T(8,128)(2,1)} %collective-permute-done.5.refs_4_), channel_id=1, source_target_pairs={{0,1},{1,0},{2,3},{3,2},{4,5},{5,4},{6,7},{7,6},{8,9},{9,8},{10,11... | collective-permute-start | bytes 1572872 | tf_op jit(solution)/shard_map/ppermute | solution.py:317
  40.6 14.6 %collective-permute-start.9 = (bf16[256,1024]{1,0:T(8,128)(2,1)S(1)}, bf16[256,1024]{1,0:T(8,128)(2,1)}, u32[]{:S(2)}, u32[]{:S(2)}) collective-permute-start(bf16[256,1024]{1,0:T(8,128)(2,1)S(1)} %collective-permute-done.4.refs_3_), channel_id=1, source_target_pairs={{0,1},{1,0},{2,3},{3,2},{4,5},{5,4},{6,7},{7,6},{8,9},{9,8},{10,11... | collective-permute-start | bytes 1572872 | tf_op jit(solution)/shard_map/ppermute | solution.py:317
  42.6 11.5 %collective-permute-start.11 = (bf16[128,1024]{1,0:T(8,128)(2,1)S(1)}, bf16[128,1024]{1,0:T(8,128)(2,1)}, u32[]{:S(2)}, u32[]{:S(2)}) collective-permute-start(bf16[128,1024]{1,0:T(8,128)(2,1)S(1)} %collective-permute-done.6.refs_5_), channel_id=1, source_target_pairs={{0,1},{1,0},{2,3},{3,2},{4,5},{5,4},{6,7},{7,6},{8,9},{9,8},{10,11... | collective-permute-start | bytes 786440 | tf_op jit(solution)/shard_map/ppermute | solution.py:317
  45.0 9.5 %collective-permute-start.12 = (bf16[128,1024]{1,0:T(8,128)(2,1)}, bf16[128,1024]{1,0:T(8,128)(2,1)}, u32[]{:S(2)}, u32[]{:S(2)}) collective-permute-start(bf16[128,1024]{1,0:T(8,128)(2,1)} %collective-permute-done.7.refs_6_), channel_id=1, source_target_pairs={{0,1},{1,0},{2,3},{3,2},{4,5},{5,4},{6,7},{7,6},{8,9},{9,8},{10,11... | collective-permute-start | bytes 786440 | tf_op jit(solution)/shard_map/ppermute | solution.py:317
  45.0 10.2 %copy-start.19 = (s32[16]{0:T(128)S(1)}, s32[16]{0:T(128)}, u32[]{:S(2)}) copy-start(s32[16]{0:T(128)} %refs_0_.3) | copy-start | bytes 196
  47.9 20.2 %all-to-all-start.1 = ((bf16[8,256,128]{2,1,0:T(8,128)(2,1)}), bf16[8,256,128]{2,1,0:T(8,128)(2,1)}, u32[]{:S(2)}, u32[]{:S(2)}) async-start(bf16[8,256,128]{2,1,0:T(8,128)(2,1)} %shard_map.80), calls=%async_computation.1 | async-start | bytes 1048576 | tf_op jit(solution)/shard_map/all_to_all | solution.py:329
  54.0 18.4 %collective-permute-start.14 = (bf16[256,1024]{1,0:T(8,128)(2,1)}, bf16[256,1024]{1,0:T(8,128)(2,1)}, u32[]{:S(2)}, u32[]{:S(2)}) collective-permute-start(bf16[256,1024]{1,0:T(8,128)(2,1)} %bitcast.25), channel_id=1, source_target_pairs={{0,1},{1,0},{2,3},{3,2},{4,5},{5,4},{6,7},{7,6},{8,9},{9,8},{10,11... | collective-permute-start | bytes 1572872 | tf_op jit(solution)/shard_map/ppermute | solution.py:317
  54.2 18.3 %collective-permute-start.15 = (bf16[256,1024]{1,0:T(8,128)(2,1)}, bf16[256,1024]{1,0:T(8,128)(2,1)}, u32[]{:S(2)}, u32[]{:S(2)}) collective-permute-start(bf16[256,1024]{1,0:T(8,128)(2,1)} %copy-done.15), channel_id=1, source_target_pairs={{0,1},{1,0},{2,3},{3,2},{4,5},{5,4},{6,7},{7,6},{8,9},{9,8},{10,11... | collective-permute-start | bytes 1572872 | tf_op jit(solution)/shard_map/ppermute | solution.py:317
  54.5 17.9 %collective-permute-start.16 = (bf16[256,1024]{1,0:T(8,128)(2,1)}, bf16[256,1024]{1,0:T(8,128)(2,1)}, u32[]{:S(2)}, u32[]{:S(2)}) collective-permute-start(bf16[256,1024]{1,0:T(8,128)(2,1)} %copy-done.17), channel_id=1, source_target_pairs={{0,1},{1,0},{2,3},{3,2},{4,5},{5,4},{6,7},{7,6},{8,9},{9,8},{10,11... | collective-permute-start | bytes 1572872 | tf_op jit(solution)/shard_map/ppermute | solution.py:317
  54.8 17.7 %collective-permute-start.17 = (bf16[128,1024]{1,0:T(8,128)(2,1)}, bf16[128,1024]{1,0:T(8,128)(2,1)}, u32[]{:S(2)}, u32[]{:S(2)}) collective-permute-start(bf16[128,1024]{1,0:T(8,128)(2,1)} %copy-done.11), channel_id=1, source_target_pairs={{0,1},{1,0},{2,3},{3,2},{4,5},{5,4},{6,7},{7,6},{8,9},{9,8},{10,11... | collective-permute-start | bytes 786440 | tf_op jit(solution)/shard_map/ppermute | solution.py:317
  55.1 17.3 %collective-permute-start.18 = (bf16[128,1024]{1,0:T(8,128)(2,1)}, bf16[128,1024]{1,0:T(8,128)(2,1)}, u32[]{:S(2)}, u32[]{:S(2)}) collective-permute-start(bf16[128,1024]{1,0:T(8,128)(2,1)} %copy-done.13), channel_id=1, source_target_pairs={{0,1},{1,0},{2,3},{3,2},{4,5},{5,4},{6,7},{7,6},{8,9},{9,8},{10,11... | collective-permute-start | bytes 786440 | tf_op jit(solution)/shard_map/ppermute | solution.py:317
  55.3 2.8 %copy-start = (bf16[1,3072,1024]{2,1,0:T(8,128)(2,1)S(1)}, bf16[1,3072,1024]{2,1,0:T(8,128)(2,1)}, u32[]{:S(2)}) copy-start(bf16[1,3072,1024]{2,1,0:T(8,128)(2,1)} %param.9) | copy-start | bytes 18874372
  68.2 25.1 %all-to-all-start = ((bf16[8,256,128]{2,1,0:T(8,128)(2,1)}), bf16[8,256,128]{2,1,0:T(8,128)(2,1)S(1)}, u32[]{:S(2)}, u32[]{:S(2)}) async-start(bf16[8,256,128]{2,1,0:T(8,128)(2,1)} %bitcast.4), calls=%async_computation | async-start | bytes 1048576 | tf_op jit(solution)/shard_map/all_to_all | solution.py:329
  72.5 2.8 %copy-start.1 = (bf16[1,3072,1024]{2,1,0:T(8,128)(2,1)S(1)}, bf16[1,3072,1024]{2,1,0:T(8,128)(2,1)}, u32[]{:S(2)}) copy-start(bf16[1,3072,1024]{2,1,0:T(8,128)(2,1)} %param.9) | copy-start | bytes 18874372
  75.3 1.0 copy-start.9
  76.3 0.9 copy-start.12
  77.3 0.9 copy-start.14
  78.2 1.0 copy-start.16
  79.2 1.0 copy-start.18
  92.1 1.2 copy-start.8
  93.3 4.4 %copy-start.5 = (bf16[1,256,1024]{2,1,0:T(8,128)(2,1)S(1)}, bf16[1,256,1024]{2,1,0:T(8,128)(2,1)}, u32[]{:S(2)}) copy-start(bf16[1,256,1024]{2,1,0:T(8,128)(2,1)} %param.6) | copy-start | bytes 1572868
  93.3 24.0 %all-to-all-start.2 = ((bf16[8,256,384]{2,1,0:T(8,128)(2,1)}), bf16[8,256,384]{2,1,0:T(8,128)(2,1)}, u32[]{:S(2)}, u32[]{:S(2)}) async-start(bf16[8,256,384]{2,1,0:T(8,128)(2,1)} %bitcast.22), calls=%async_computation.2 | async-start | bytes 3145728 | tf_op jit(solution)/shard_map/all_to_all | solution.py:329
  99.2 28.7 %collective-permute-start.13 = (bf16[256,1024]{1,0:T(8,128)(2,1)}, bf16[256,1024]{1,0:T(8,128)(2,1)S(1)}, u32[]{:S(2)}, u32[]{:S(2)}) collective-permute-start(bf16[256,1024]{1,0:T(8,128)(2,1)} %shard_map.79), channel_id=1, source_target_pairs={{0,8},{8,16},{16,24},{1,9},{9,17},{17,25},{2,10},{10,18},{18,26},{... | collective-permute-start | bytes 1572872 | tf_op jit(solution)/shard_map/ppermute | solution.py:359
  117.3 2.8 %copy-start.2 = (bf16[1,3072,1024]{2,1,0:T(8,128)(2,1)S(1)}, bf16[1,3072,1024]{2,1,0:T(8,128)(2,1)}, u32[]{:S(2)}) copy-start(bf16[1,3072,1024]{2,1,0:T(8,128)(2,1)} %param.9) | copy-start | bytes 18874372
  120.0 1.0 copy-start.7
  121.1 1.0 copy-start.10
  125.6 15.8 %collective-permute-start.19 = (bf16[256,1024]{1,0:T(8,128)(2,1)S(1)}, bf16[256,1024]{1,0:T(8,128)(2,1)S(1)}, u32[]{:S(2)}, u32[]{:S(2)}) collective-permute-start(bf16[256,1024]{1,0:T(8,128)(2,1)S(1)} %shard_map.82), channel_id=1, source_target_pairs={{8,0},{16,8},{24,16},{9,1},{17,9},{25,17},{10,2},{18,10},{26,18},{... | collective-permute-start | bytes 1572872 | tf_op jit(solution)/shard_map/ppermute | solution.py:359

commit v3 on v2

--- a/solution.py
+++ b/solution.py
@@ -12,7 +12,7 @@
 TILE = 128
 CAPACITY = 3
 EPSILON = 1e-05
-VMEM_LIMIT = 24 * 1024 * 1024
+MIB = 1024 * 1024
 NT = (((1,), (1,)), ((), ()))
 NN = (((1,), (0,)), ((), ()))
 TN = (((0,), (0,)), ((), ()))
@@ -37,15 +37,14 @@
     return lax.rsqrt(jnp.mean(values * values, axis=-1, keepdims=True) + EPSILON)
 
 
-def call(kernel, operands, in_specs, out_shape, scratch, flops, moved):
-    many = isinstance(out_shape, tuple)
+def call(kernel, operands, in_specs, out_shape, scratch, flops, moved, grant=24 * MIB):
     return pl.pallas_call(
         kernel,
         in_specs=in_specs,
-        out_specs=tuple(VMEM for _ in out_shape) if many else VMEM,
+        out_specs=VMEM,
         out_shape=out_shape,
         scratch_shapes=scratch,
-        compiler_params=pltpu.CompilerParams(vmem_limit_bytes=VMEM_LIMIT),
+        compiler_params=pltpu.CompilerParams(vmem_limit_bytes=grant),
         cost_estimate=pl.CostEstimate(flops=flops, bytes_accessed=moved, transcendentals=0),
     )(*operands)
 
@@ -100,13 +99,14 @@
             out[t, :, c * HD : (c + 1) * HD] = result[i * TILE : (i + 1) * TILE]
 
 
-def head_kernel(back, pieces, spacing, *refs):
+def head_kernel(back, unread, pieces, spacing, *refs):
     cluster_ref, info_ref = refs[:2]
     x_refs = refs[2 : 2 + len(pieces)]
     refs = refs[2 + len(pieces) :]
     if back:
         g_ref, refs = refs[0], refs[1:]
-    w_ref, out, xbuf, wbuf, turned, kept, count, member, xsem, wsem = refs[:10]
+    w_ref, refs = refs[0], refs[1 + unread :]
+    out, xbuf, wbuf, turned, kept, count, member, xsem, wsem = refs[:9]
     flip, head, residue = info_ref[0], info_ref[1], info_ref[2]
     tiles = kept.shape[0]
     clusters = count.shape[0]
@@ -116,7 +116,7 @@
     for i, (k, start, rows) in enumerate(pieces):
         copies.append(fetch(x_refs[i], xbuf.at[k, pl.ds(start, rows)], xsem.at[i]))
     if back:
-        scales, grads, gsem = refs[10:]
+        scales, grads, gsem = refs[9:]
         g_copy = fetch(g_ref, grads, gsem)
 
     for c in range(clusters):
@@ -176,7 +176,7 @@
     lax.fori_loop(0, clusters, visit, 0)
 
 
-def head_work(info, tile_cluster, pieces, w_qkv, spacing, grads=None):
+def head_work(info, tile_cluster, pieces, w_qkv, spacing, grads=None, earlier=()):
     back = grads is not None
     width = w_qkv.shape[1]
     tiles = 2 * HEADS
@@ -185,7 +185,7 @@
     operands = [tile_cluster, info] + [array for _, _, array in pieces]
     if back:
         operands.append(grads.reshape(tiles, TILE, HD))
-    operands.append(w_qkv.reshape(3, HEADS, HD, width))
+    operands += [w_qkv.reshape(3, HEADS, HD, width), *earlier]
     shapes = tuple((k, start, array.shape[0]) for k, start, array in pieces)
     scratch = [
         pltpu.VMEM((HEADS, 2 * TILE, width), jnp.bfloat16),
@@ -204,13 +204,14 @@
             pltpu.SemaphoreType.DMA,
         ]
     out = call(
-        functools.partial(head_kernel, back, shapes, spacing),
+        functools.partial(head_kernel, back, len(earlier), shapes, spacing),
         operands,
         [SMEM, SMEM] + [HBM] * (len(operands) - 2),
         jax.ShapeDtypeStruct((tiles, TILE, wide), jnp.bfloat16),
         scratch,
         2 * tokens * width * 3 * HD + tokens * 512 * HD * (14 if back else 4),
         2 * tokens * (width + 2 * wide),
+        grant=58 * MIB,
     )
     return out.reshape(HEADS, 2 * TILE, wide)
 
@@ -384,10 +385,12 @@
     stored_pieces = gather(stored)
     grad_attention = spread(spread_grads(upstream, w_fin))
     earlier = [block for k, _, block in stored_pieces if k == HEADS - 2]
-    current_pieces = gather(norm_after(current, earlier))
+    current_pieces = gather(norm_after(current, [*earlier, grad_attention]))
     grads = head_work(info, tile_cluster, stored_pieces, w_rows, spacing, grad_attention)
     returned_grads = collect(grads)
-    outputs = head_work(info, tile_cluster, current_pieces, w_rows, spacing)
+    outputs = head_work(
+        info, tile_cluster, current_pieces, w_rows, spacing, earlier=(grads,)
+    )
     returned = collect(outputs)
     grad_self = finish_back(returned_grads, stored, upstream, w_rows)
     grad_input = passed_along(grad_self, "pipe", -1)

time: 144 us -> 146 us (1.014)
  blocking collectives: 0 us -> 12.9 us
  local copies, waits for them, and re-layouts: 20.4 us -> 13.9 us
  starting transfers between devices: 31.4 us -> 26.2 us
  Pallas kernels: 29.9 us -> 34.6 us
  waiting for transfers between devices: 60.4 us -> 56.4 us
    all_to_all x0 -> x1, blocking collectives: none -> 12.9 us  [all_swap(): lax.all_to_all(blocks, 'seq', split_axis=0, concat_axis=0, tiled=True)]
    ppermute x18, waiting for transfers between devices: 32.4 us -> 24.4 us  [partner(): return lax.ppermute(block, 'seq', route)]
    unnamed x42 -> x54, local copies, waits for them, and re-layouts: 19.4 us -> 11.5 us
    pallas_call x6, Pallas kernels: 29.9 us -> 34.6 us  [call(): pl.pallas_call(kernel, in_specs=in_specs, out_specs=VMEM, out_shape=out_s...]
    all_to_all x3 -> x2, waiting for transfers between devices: 14.6 us -> 18.7 us  [all_swap(): lax.all_to_all(blocks, 'seq', split_axis=0, concat_axis=0, tiled=True)]
    all_to_all x3 -> x2, starting transfers between devices: 14.7 us -> 10.7 us  [all_swap(): lax.all_to_all(blocks, 'seq', split_axis=0, concat_axis=0, tiled=True)]
  transfers between devices with their start and end apart: 23 -> 22, of which waited for: 9 -> 9; matrix products, arithmetic and copies ran while one was open for 1% -> 2% of each run, Pallas kernels for 21% -> 16%
where the time goes in v3:
time: 146 us
  waiting for transfers between devices  56.4 us (39%)
  Pallas kernels  34.6 us (24%)
  starting transfers between devices  26.2 us (18%)
  local copies, waits for them, and re-layouts  13.9 us (10%)
  blocking collectives  12.9 us (9%)
    pallas_call x6, Pallas kernels, call(): pl.pallas_call(kernel, in_specs=in_specs, out_specs=VMEM, out_shape=out_s...  34.6 us
    ppermute x18, waiting for transfers between devices, partner(): return lax.ppermute(block, 'seq', route)  24.4 us
    all_to_all x2, waiting for transfers between devices, all_swap(): lax.all_to_all(blocks, 'seq', split_axis=0, concat_axis=0, tiled=True)  18.7 us
    ppermute x2, waiting for transfers between devices, passed_along(): return lax.ppermute(block, axis, route)  13.4 us
    all_to_all x1, blocking collectives, all_swap(): lax.all_to_all(blocks, 'seq', split_axis=0, concat_axis=0, tiled=True)  12.9 us
    unnamed x54, local copies, waits for them, and re-layouts  11.5 us
    all_to_all x2, starting transfers between devices, all_swap(): lax.all_to_all(blocks, 'seq', split_axis=0, concat_axis=0, tiled=True)  10.7 us
    ppermute x18, starting transfers between devices, partner(): return lax.ppermute(block, 'seq', route)  9.66 us
  transfers between devices with their start and end apart: 22, of which 9 were waited for; matrix products, arithmetic and copies ran while one was open for 2% of the time, Pallas kernels for 16%

profile of v3, /device:TPU:18, one launch (start us, length us, event | category | flops | bytes accessed | tf_op | source)
XLA Modules:
  0.0 145.6 jit_solution(1648872618678648368)
XLA Ops:
  0.6 0.6 collective-permute-start
  1.2 1.5 %collective-permute-start.2 = (bf16[256,1024]{1,0:T(8,128)(2,1)}, bf16[256,1024]{1,0:T(8,128)(2,1)S(1)}, u32[]{:S(2)}, u32[]{:S(2)}) collective-permute-start(bf16[256,1024]{1,0:T(8,128)(2,1)} %bitcast.24), channel_id=1, source_target_pairs={{0,4},{1,5},{2,6},{3,7},{4,0},{5,1},{6,2},{7,3},{8,12},{9,13},{10,... | collective-permute-start | bytes 1572872 | tf_op jit(solution)/shard_map/ppermute | solution.py:318
  2.8 1.6 %copy-done.1 = bf16[1,1024,1024]{2,1,0:T(8,128)(2,1)S(1)} copy-done((bf16[1,1024,1024]{2,1,0:T(8,128)(2,1)S(1)}, bf16[1,1024,1024]{2,1,0:T(8,128)(2,1)}, u32[]{:S(2)}) %copy-start.1) | copy-done | bytes 2097176
  4.3 1.0 copy-done.4
  5.4 2.8 %shard_map.77 = bf16[8,256,128]{2,1,0:T(8,128)(2,1)} custom-call(bf16[256,1024]{1,0:T(8,128)(2,1)S(1)} %bitcast.20, bf16[8,128,1024]{2,1,0:T(8,128)(2,1)S(1)} %bitcast.16), custom_call_target="tpu_custom_call" | custom-call | flops 536870912 | bytes 2097152 | tf_op jit(solution)/shard_map/pallas_call | solution.py:41
  8.2 5.0 %all-to-all-start = ((bf16[8,256,128]{2,1,0:T(8,128)(2,1)}), bf16[8,256,128]{2,1,0:T(8,128)(2,1)S(1)}, u32[]{:S(2)}, u32[]{:S(2)}) async-start(bf16[8,256,128]{2,1,0:T(8,128)(2,1)} %shard_map.77), calls=%async_computation | async-start | bytes 1048576 | tf_op jit(solution)/shard_map/all_to_all | solution.py:330
  13.3 1.3 collective-permute-done.refs_3_
  14.6 0.8 copy-done.17
  15.4 1.6 %collective-permute-start.1 = (bf16[128,1024]{1,0:T(8,128)(2,1)S(1)}, bf16[128,1024]{1,0:T(8,128)(2,1)S(1)}, u32[]{:S(2)}, u32[]{:S(2)}) collective-permute-start(bf16[128,1024]{1,0:T(8,128)(2,1)S(1)} %slice.16), channel_id=1, source_target_pairs={{0,4},{1,5},{2,6},{3,7},{4,0},{5,1},{6,2},{7,3},{8,12},{9,13},{10,... | collective-permute-start | bytes 786440 | tf_op jit(solution)/shard_map/ppermute | solution.py:318
  17.0 0.6 collective-permute-start.3
  17.6 4.0 %all-to-all-done.refs_2_ = bf16[8,256,128]{2,1,0:T(8,128)(2,1)S(1)} async-done(((bf16[8,256,128]{2,1,0:T(8,128)(2,1)}), bf16[8,256,128]{2,1,0:T(8,128)(2,1)S(1)}, u32[]{:S(2)}, u32[]{:S(2)}) %all-to-all-start) | async-done | bytes 524320 | tf_op jit(solution)/shard_map/all_to_all | solution.py:330
  21.6 5.6 %collective-permute-done.1.refs_0_.refs_5_ = bf16[128,1024]{1,0:T(8,128)(2,1)S(1)} collective-permute-done((bf16[128,1024]{1,0:T(8,128)(2,1)S(1)}, bf16[128,1024]{1,0:T(8,128)(2,1)S(1)}, u32[]{:S(2)}, u32[]{:S(2)}) %collective-permute-start.1) | collective-permute-done | bytes 262176 | tf_op jit(solution)/shard_map/ppermute | solution.py:318
  27.2 0.2 shard_map.78.refs_2_
  27.4 0.6 collective-permute-start.4
  28.1 1.4 collective-permute-start.5
  29.5 0.5 collective-permute-start.14
  30.0 0.1 collective-permute-start.15
  30.1 11.3 %collective-permute-done.4.refs_3_ = bf16[256,1024]{1,0:T(8,128)(2,1)S(1)} collective-permute-done((bf16[256,1024]{1,0:T(8,128)(2,1)S(1)}, bf16[256,1024]{1,0:T(8,128)(2,1)S(1)}, u32[]{:S(2)}, u32[]{:S(2)}) %collective-permute-start.4) | collective-permute-done | bytes 524320 | tf_op jit(solution)/shard_map/ppermute | solution.py:318
  41.4 0.2 collective-permute-done.5.refs_4_
  41.6 0.3 collective-permute-start.17
  41.9 0.7 slice.18
  42.6 1.7 %slice.19 = bf16[128,1024]{1,0:T(8,128)(2,1)} slice(bf16[256,1024]{1,0:T(8,128)(2,1)} %collective-permute-done.5.refs_4_), slice={[128:256], [0:1024]} | slice | bytes 524288 | tf_op jit(solution)/shard_map/slice | solution.py:324
  44.3 0.9 collective-permute-start.6
  45.2 0.8 collective-permute-start.7
  46.1 0.5 collective-permute-start.10
  46.6 0.1 collective-permute-start.9
  46.8 0.2 copy-done.22
  46.9 0.4 copy-done.23
  47.4 0.6 pad_add_fusion.refs_1_
  48.0 4.9 %collective-permute-done.6.refs_5_ = bf16[128,1024]{1,0:T(8,128)(2,1)S(1)} collective-permute-done((bf16[128,1024]{1,0:T(8,128)(2,1)}, bf16[128,1024]{1,0:T(8,128)(2,1)S(1)}, u32[]{:S(2)}, u32[]{:S(2)}) %collective-permute-start.6) | collective-permute-done | bytes 262176 | tf_op jit(solution)/shard_map/ppermute | solution.py:318
  52.9 1.1 collective-permute-done.7.refs_6_
  54.0 14.9 %shard_map.79 = bf16[16,128,384]{2,1,0:T(8,128)(2,1)} custom-call(s32[16]{0:T(128)} %refs_0_.3, s32[3]{0:T(128)} %pad_add_fusion.refs_1_, bf16[256,1024]{1,0:T(8,128)(2,1)} %bitcast.25, bf16[256,1024]{1,0:T(8,128)(2,1)} %copy-done.17, bf16[256,1024]{1,0:T(8,128)(2,1)} %copy-done.19, bf16[128,1024]{1,0:T(8,128)(2,1)} %copy-done.10, ...), custom_call_target="tpu_custom_call" | custom-call | flops 3489660928 | bytes 7340032 | tf_op jit(solution)/shard_map/pallas_call | solution.py:41
  69.0 0.7 copy-done.13
  69.8 0.1 copy-done.15
  69.9 11.7 %shard_map.80 = bf16[16,128,128]{2,1,0:T(8,128)(2,1)} custom-call(s32[16]{0:T(128)} %refs_0_.3, s32[3]{0:T(128)} %pad_add_fusion.refs_1_, bf16[256,1024]{1,0:T(8,128)(2,1)} %copy-done.6, bf16[256,1024]{1,0:T(8,128)(2,1)} %copy-done.12, bf16[256,1024]{1,0:T(8,128)(2,1)} %collective-permute-done.5.refs_4_, bf16[128,1024]{1,0:T(8,128)(2,1)} %copy-done.14, ...), custom_call_target="tpu_custom_call" | custom-call | flops 2147483648 | bytes 5242880 | tf_op jit(solution)/shard_map/pallas_call | solution.py:41
  81.7 12.9 %all_to_all.15.att_ref = bf16[8,256,128]{2,1,0:T(8,128)(2,1)S(1)} all-to-all(bf16[8,256,128]{2,1,0:T(8,128)(2,1)} %bitcast.30), channel_id=1, replica_groups=mesh['pipe'=4,'seq'=8] {'seq'}, dimensions={0} | all-to-all | bytes 1048576 | tf_op jit(solution)/shard_map/all_to_all | solution.py:330
  94.6 5.6 %all-to-all-start.2 = ((bf16[8,256,384]{2,1,0:T(8,128)(2,1)}), bf16[8,256,384]{2,1,0:T(8,128)(2,1)}, u32[]{:S(2)}, u32[]{:S(2)}) async-start(bf16[8,256,384]{2,1,0:T(8,128)(2,1)} %bitcast.29), calls=%async_computation.2 | async-start | bytes 3145728 | tf_op jit(solution)/shard_map/all_to_all | solution.py:330
  100.3 1.5 %shard_map.81 = bf16[256,1024]{1,0:T(8,128)(2,1)} custom-call(bf16[8,256,128]{2,1,0:T(8,128)(2,1)S(1)} %all_to_all.15.att_ref, bf16[256,1024]{1,0:T(8,128)(2,1)S(1)} %bitcast.19, bf16[1024,1024]{1,0:T(8,128)(2,1)S(1)} %bitcast.17), custom_call_target="tpu_custom_call" | custom-call | flops 536870912 | bytes 2097152 | tf_op jit(solution)/shard_map/pallas_call | solution.py:41
  101.8 3.5 %collective-permute-start.18 = (bf16[256,1024]{1,0:T(8,128)(2,1)}, bf16[256,1024]{1,0:T(8,128)(2,1)S(1)}, u32[]{:S(2)}, u32[]{:S(2)}) collective-permute-start(bf16[256,1024]{1,0:T(8,128)(2,1)} %shard_map.81), channel_id=1, source_target_pairs={{0,8},{8,16},{16,24},{1,9},{9,17},{17,25},{2,10},{10,18},{18,26},{... | collective-permute-start | bytes 1572872 | tf_op jit(solution)/shard_map/ppermute | solution.py:360
  105.2 14.6 %all-to-all-done.2.grad_ref = bf16[8,256,384]{2,1,0:T(8,128)(2,1)} async-done(((bf16[8,256,384]{2,1,0:T(8,128)(2,1)}), bf16[8,256,384]{2,1,0:T(8,128)(2,1)}, u32[]{:S(2)}, u32[]{:S(2)}) %all-to-all-start.2) | async-done | bytes 1572896 | tf_op jit(solution)/shard_map/all_to_all | solution.py:330
  119.9 2.8 %copy-done = bf16[1,3072,1024]{2,1,0:T(8,128)(2,1)S(1)} copy-done((bf16[1,3072,1024]{2,1,0:T(8,128)(2,1)S(1)}, bf16[1,3072,1024]{2,1,0:T(8,128)(2,1)}, u32[]{:S(2)}) %copy-start) | copy-done | bytes 6291480
  122.7 1.0 copy-done.5
  123.7 1.0 copy-done.9
  124.8 3.4 %shard_map.82 = bf16[256,1024]{1,0:T(8,128)(2,1)S(1)} custom-call(bf16[8,256,384]{2,1,0:T(8,128)(2,1)} %all-to-all-done.2.grad_ref, bf16[256,1024]{1,0:T(8,128)(2,1)S(1)} %bitcast.27, bf16[256,1024]{1,0:T(8,128)(2,1)S(1)} %bitcast.21, bf16[3072,1024]{1,0:T(8,128)(2,1)S(1)} %bitcast.15), custom_call_target="tpu_custom_call" | custom-call | flops 1610612736 | bytes 6291456 | tf_op jit(solution)/shard_map/pallas_call | solution.py:41
  128.2 2.4 %collective-permute-start.19 = (bf16[256,1024]{1,0:T(8,128)(2,1)S(1)}, bf16[256,1024]{1,0:T(8,128)(2,1)S(1)}, u32[]{:S(2)}, u32[]{:S(2)}) collective-permute-start(bf16[256,1024]{1,0:T(8,128)(2,1)S(1)} %shard_map.82), channel_id=1, source_target_pairs={{8,0},{16,8},{24,16},{9,1},{17,9},{25,17},{10,2},{18,10},{26,18},{... | collective-permute-start | bytes 1572872 | tf_op jit(solution)/shard_map/ppermute | solution.py:360
  130.6 13.4 %collective-permute-done.19 = bf16[256,1024]{1,0:T(8,128)(2,1)S(1)} collective-permute-done((bf16[256,1024]{1,0:T(8,128)(2,1)S(1)}, bf16[256,1024]{1,0:T(8,128)(2,1)S(1)}, u32[]{:S(2)}, u32[]{:S(2)}) %collective-permute-start.19) | collective-permute-done | bytes 524320 | tf_op jit(solution)/shard_map/ppermute | solution.py:360
  144.0 0.8 copy.10
  144.8 0.8 copy.11
  (62 shorter events, 0.3 us)
Async XLA Ops:
  0.6 13.9 %collective-permute-start = (bf16[256,1024]{1,0:T(8,128)(2,1)}, bf16[256,1024]{1,0:T(8,128)(2,1)S(1)}, u32[]{:S(2)}, u32[]{:S(2)}) collective-permute-start(bf16[256,1024]{1,0:T(8,128)(2,1)} %bitcast.23), channel_id=1, source_target_pairs={{0,2},{1,3},{2,0},{3,1},{4,6},{5,7},{6,4},{7,5},{8,10},{9,11},{10,... | collective-permute-start | bytes 1572872 | tf_op jit(solution)/shard_map/ppermute | solution.py:318
  1.2 15.8 %collective-permute-start.2 = (bf16[256,1024]{1,0:T(8,128)(2,1)}, bf16[256,1024]{1,0:T(8,128)(2,1)S(1)}, u32[]{:S(2)}, u32[]{:S(2)}) collective-permute-start(bf16[256,1024]{1,0:T(8,128)(2,1)} %bitcast.24), channel_id=1, source_target_pairs={{0,4},{1,5},{2,6},{3,7},{4,0},{5,1},{6,2},{7,3},{8,12},{9,13},{10,... | collective-permute-start | bytes 1572872 | tf_op jit(solution)/shard_map/ppermute | solution.py:318
  2.7 1.6 %copy-start.1 = (bf16[1,1024,1024]{2,1,0:T(8,128)(2,1)S(1)}, bf16[1,1024,1024]{2,1,0:T(8,128)(2,1)}, u32[]{:S(2)}) copy-start(bf16[1,1024,1024]{2,1,0:T(8,128)(2,1)} %param.10) | copy-start | bytes 6291460
  4.3 1.0 copy-start.4
  5.4 21.8 %copy-start.3 = (bf16[1,256,1024]{2,1,0:T(8,128)(2,1)S(1)}, bf16[1,256,1024]{2,1,0:T(8,128)(2,1)}, u32[]{:S(2)}) copy-start(bf16[1,256,1024]{2,1,0:T(8,128)(2,1)} %param.6) | copy-start | bytes 1572868
  8.2 21.3 %copy-start.8 = (bf16[1,256,1024]{2,1,0:T(8,128)(2,1)S(1)}, bf16[1,256,1024]{2,1,0:T(8,128)(2,1)}, u32[]{:S(2)}) copy-start(bf16[1,256,1024]{2,1,0:T(8,128)(2,1)} %param.7) | copy-start | bytes 1572868
  8.2 13.4 %all-to-all-start = ((bf16[8,256,128]{2,1,0:T(8,128)(2,1)}), bf16[8,256,128]{2,1,0:T(8,128)(2,1)S(1)}, u32[]{:S(2)}, u32[]{:S(2)}) async-start(bf16[8,256,128]{2,1,0:T(8,128)(2,1)} %shard_map.77), calls=%async_computation | async-start | bytes 1048576 | tf_op jit(solution)/shard_map/all_to_all | solution.py:330
  14.6 0.8 copy-start.17
  15.4 11.8 %collective-permute-start.1 = (bf16[128,1024]{1,0:T(8,128)(2,1)S(1)}, bf16[128,1024]{1,0:T(8,128)(2,1)S(1)}, u32[]{:S(2)}, u32[]{:S(2)}) collective-permute-start(bf16[128,1024]{1,0:T(8,128)(2,1)S(1)} %slice.16), channel_id=1, source_target_pairs={{0,4},{1,5},{2,6},{3,7},{4,0},{5,1},{6,2},{7,3},{8,12},{9,13},{10,... | collective-permute-start | bytes 786440 | tf_op jit(solution)/shard_map/ppermute | solution.py:318
  17.0 10.2 %copy-start.19 = (bf16[256,1024]{1,0:T(8,128)(2,1)}, bf16[256,1024]{1,0:T(8,128)(2,1)S(1)}, u32[]{:S(2)}) copy-start(bf16[256,1024]{1,0:T(8,128)(2,1)S(1)} %collective-permute-done.2.refs_4_) | copy-start | bytes 1572868
  17.0 10.2 %collective-permute-start.3 = (bf16[128,1024]{1,0:T(8,128)(2,1)S(1)}, bf16[128,1024]{1,0:T(8,128)(2,1)S(1)}, u32[]{:S(2)}, u32[]{:S(2)}) collective-permute-start(bf16[128,1024]{1,0:T(8,128)(2,1)S(1)} %slice.17), channel_id=1, source_target_pairs={{0,2},{1,3},{2,0},{3,1},{4,6},{5,7},{6,4},{7,5},{8,10},{9,11},{10,... | collective-permute-start | bytes 786440 | tf_op jit(solution)/shard_map/ppermute | solution.py:318
  21.6 32.4 %copy-start.7 = (bf16[8,256,128]{2,1,0:T(8,128)(2,1)}, bf16[8,256,128]{2,1,0:T(8,128)(2,1)S(1)}, u32[]{:S(2)}) copy-start(bf16[8,256,128]{2,1,0:T(8,128)(2,1)S(1)} %all-to-all-done.refs_2_) | copy-start | bytes 1572868
  21.6 7.9 %copy-start.18 = (bf16[256,1024]{1,0:T(8,128)(2,1)S(1)}, bf16[256,1024]{1,0:T(8,128)(2,1)}, u32[]{:S(2)}) copy-start(bf16[256,1024]{1,0:T(8,128)(2,1)} %copy-done.17) | copy-start | bytes 1572868
  27.2 26.8 %copy-start.10 = (bf16[128,1024]{1,0:T(8,128)(2,1)}, bf16[128,1024]{1,0:T(8,128)(2,1)S(1)}, u32[]{:S(2)}) copy-start(bf16[128,1024]{1,0:T(8,128)(2,1)S(1)} %collective-permute-done.1.refs_0_.refs_5_) | copy-start | bytes 786436
  27.2 26.8 %copy-start.11 = (bf16[128,1024]{1,0:T(8,128)(2,1)}, bf16[128,1024]{1,0:T(8,128)(2,1)S(1)}, u32[]{:S(2)}) copy-start(bf16[128,1024]{1,0:T(8,128)(2,1)S(1)} %collective-permute-done.3.refs_1_.refs_6_) | copy-start | bytes 786436
  27.2 2.8 %copy-start.20 = (bf16[256,1024]{1,0:T(8,128)(2,1)S(1)}, bf16[256,1024]{1,0:T(8,128)(2,1)}, u32[]{:S(2)}) copy-start(bf16[256,1024]{1,0:T(8,128)(2,1)} %copy-done.19) | copy-start | bytes 1572868
  27.4 41.5 %copy-start.6 = (bf16[256,1024]{1,0:T(8,128)(2,1)}, bf16[256,1024]{1,0:T(8,128)(2,1)S(1)}, u32[]{:S(2)}) copy-start(bf16[256,1024]{1,0:T(8,128)(2,1)S(1)} %shard_map.78.refs_2_) | copy-start | bytes 1572868
  27.4 14.0 %collective-permute-start.4 = (bf16[256,1024]{1,0:T(8,128)(2,1)S(1)}, bf16[256,1024]{1,0:T(8,128)(2,1)S(1)}, u32[]{:S(2)}, u32[]{:S(2)}) collective-permute-start(bf16[256,1024]{1,0:T(8,128)(2,1)S(1)} %shard_map.78.refs_2_), channel_id=1, source_target_pairs={{0,2},{1,3},{2,0},{3,1},{4,6},{5,7},{6,4},{7,5},{8,10},{9,11},{10,... | collective-permute-start | bytes 1572872 | tf_op jit(solution)/shard_map/ppermute | solution.py:318
  28.1 13.5 %collective-permute-start.5 = (bf16[256,1024]{1,0:T(8,128)(2,1)S(1)}, bf16[256,1024]{1,0:T(8,128)(2,1)}, u32[]{:S(2)}, u32[]{:S(2)}) collective-permute-start(bf16[256,1024]{1,0:T(8,128)(2,1)S(1)} %shard_map.78.refs_2_), channel_id=1, source_target_pairs={{0,4},{1,5},{2,6},{3,7},{4,0},{5,1},{6,2},{7,3},{8,12},{9,13},{10,... | collective-permute-start | bytes 1572872 | tf_op jit(solution)/shard_map/ppermute | solution.py:318
  29.5 14.8 %collective-permute-start.13 = (bf16[256,1024]{1,0:T(8,128)(2,1)S(1)}, bf16[256,1024]{1,0:T(8,128)(2,1)S(1)}, u32[]{:S(2)}, u32[]{:S(2)}) collective-permute-start(bf16[256,1024]{1,0:T(8,128)(2,1)S(1)} %bitcast.26), channel_id=1, source_target_pairs={{0,1},{1,0},{2,3},{3,2},{4,5},{5,4},{6,7},{7,6},{8,9},{9,8},{10,11... | collective-permute-start | bytes 1572872 | tf_op jit(solution)/shard_map/ppermute | solution.py:318
  29.5 16.5 %collective-permute-start.14 = (bf16[256,1024]{1,0:T(8,128)(2,1)S(1)}, bf16[256,1024]{1,0:T(8,128)(2,1)S(1)}, u32[]{:S(2)}, u32[]{:S(2)}) collective-permute-start(bf16[256,1024]{1,0:T(8,128)(2,1)S(1)} %copy-done.18), channel_id=1, source_target_pairs={{0,1},{1,0},{2,3},{3,2},{4,5},{5,4},{6,7},{7,6},{8,9},{9,8},{10,11... | collective-permute-start | bytes 1572872 | tf_op jit(solution)/shard_map/ppermute | solution.py:318
  30.0 16.5 %collective-permute-start.15 = (bf16[256,1024]{1,0:T(8,128)(2,1)S(1)}, bf16[256,1024]{1,0:T(8,128)(2,1)S(1)}, u32[]{:S(2)}, u32[]{:S(2)}) collective-permute-start(bf16[256,1024]{1,0:T(8,128)(2,1)S(1)} %copy-done.20), channel_id=1, source_target_pairs={{0,1},{1,0},{2,3},{3,2},{4,5},{5,4},{6,7},{7,6},{8,9},{9,8},{10,11... | collective-permute-start | bytes 1572872 | tf_op jit(solution)/shard_map/ppermute | solution.py:318
  41.4 27.5 %copy-start.12 = (bf16[256,1024]{1,0:T(8,128)(2,1)}, bf16[256,1024]{1,0:T(8,128)(2,1)S(1)}, u32[]{:S(2)}) copy-start(bf16[256,1024]{1,0:T(8,128)(2,1)S(1)} %collective-permute-done.4.refs_3_) | copy-start | bytes 1572868
  41.4 3.8 %collective-permute-start.16 = (bf16[128,1024]{1,0:T(8,128)(2,1)S(1)}, bf16[128,1024]{1,0:T(8,128)(2,1)S(1)}, u32[]{:S(2)}, u32[]{:S(2)}) collective-permute-start(bf16[128,1024]{1,0:T(8,128)(2,1)S(1)} %collective-permute-done.1.refs_0_.refs_5_), channel_id=1, source_target_pairs={{0,1},{1,0},{2,3},{3,2},{4,5},{5,4},{6,7},{7,6},{8,9},{9,8},{10,11... | collective-permute-start | bytes 786440 | tf_op jit(solution)/shard_map/ppermute | solution.py:318
  41.6 4.5 %collective-permute-start.17 = (bf16[128,1024]{1,0:T(8,128)(2,1)S(1)}, bf16[128,1024]{1,0:T(8,128)(2,1)S(1)}, u32[]{:S(2)}, u32[]{:S(2)}) collective-permute-start(bf16[128,1024]{1,0:T(8,128)(2,1)S(1)} %collective-permute-done.3.refs_1_.refs_6_), channel_id=1, source_target_pairs={{0,1},{1,0},{2,3},{3,2},{4,5},{5,4},{6,7},{7,6},{8,9},{9,8},{10,11... | collective-permute-start | bytes 786440 | tf_op jit(solution)/shard_map/ppermute | solution.py:318
  44.3 2.3 %copy-start.21 = (bf16[256,1024]{1,0:T(8,128)(2,1)}, bf16[256,1024]{1,0:T(8,128)(2,1)S(1)}, u32[]{:S(2)}) copy-start(bf16[256,1024]{1,0:T(8,128)(2,1)S(1)} %collective-permute-done.13.refs_7_) | copy-start | bytes 1572868
  44.3 8.6 %collective-permute-start.6 = (bf16[128,1024]{1,0:T(8,128)(2,1)}, bf16[128,1024]{1,0:T(8,128)(2,1)S(1)}, u32[]{:S(2)}, u32[]{:S(2)}) collective-permute-start(bf16[128,1024]{1,0:T(8,128)(2,1)} %slice.18), channel_id=1, source_target_pairs={{0,4},{1,5},{2,6},{3,7},{4,0},{5,1},{6,2},{7,3},{8,12},{9,13},{10,... | collective-permute-start | bytes 786440 | tf_op jit(solution)/shard_map/ppermute | solution.py:318
  45.2 1.5 %copy-start.24 = (bf16[128,1024]{1,0:T(8,128)(2,1)}, bf16[128,1024]{1,0:T(8,128)(2,1)S(1)}, u32[]{:S(2)}) copy-start(bf16[128,1024]{1,0:T(8,128)(2,1)S(1)} %collective-permute-done.16.refs_10_) | copy-start | bytes 786436
  45.2 8.8 %collective-permute-start.7 = (bf16[128,1024]{1,0:T(8,128)(2,1)}, bf16[128,1024]{1,0:T(8,128)(2,1)}, u32[]{:S(2)}, u32[]{:S(2)}) collective-permute-start(bf16[128,1024]{1,0:T(8,128)(2,1)} %slice.19), channel_id=1, source_target_pairs={{0,2},{1,3},{2,0},{3,1},{4,6},{5,7},{6,4},{7,5},{8,10},{9,11},{10,... | collective-permute-start | bytes 786440 | tf_op jit(solution)/shard_map/ppermute | solution.py:318
  46.0 0.7 copy-start.25
  46.0 22.9 %collective-permute-start.8 = (bf16[256,1024]{1,0:T(8,128)(2,1)S(1)}, bf16[256,1024]{1,0:T(8,128)(2,1)S(1)}, u32[]{:S(2)}, u32[]{:S(2)}) collective-permute-start(bf16[256,1024]{1,0:T(8,128)(2,1)S(1)} %shard_map.78.refs_2_), channel_id=1, source_target_pairs={{0,1},{1,0},{2,3},{3,2},{4,5},{5,4},{6,7},{7,6},{8,9},{9,8},{10,11... | collective-permute-start | bytes 1572872 | tf_op jit(solution)/shard_map/ppermute | solution.py:318
  46.1 0.9 copy-start.22
  46.1 22.9 %collective-permute-start.10 = (bf16[256,1024]{1,0:T(8,128)(2,1)}, bf16[256,1024]{1,0:T(8,128)(2,1)}, u32[]{:S(2)}, u32[]{:S(2)}) collective-permute-start(bf16[256,1024]{1,0:T(8,128)(2,1)} %collective-permute-done.5.refs_4_), channel_id=1, source_target_pairs={{0,1},{1,0},{2,3},{3,2},{4,5},{5,4},{6,7},{7,6},{8,9},{9,8},{10,11... | collective-permute-start | bytes 1572872 | tf_op jit(solution)/shard_map/ppermute | solution.py:318
  46.6 0.8 copy-start.23
  46.6 22.4 %collective-permute-start.9 = (bf16[256,1024]{1,0:T(8,128)(2,1)S(1)}, bf16[256,1024]{1,0:T(8,128)(2,1)}, u32[]{:S(2)}, u32[]{:S(2)}) collective-permute-start(bf16[256,1024]{1,0:T(8,128)(2,1)S(1)} %collective-permute-done.4.refs_3_), channel_id=1, source_target_pairs={{0,1},{1,0},{2,3},{3,2},{4,5},{5,4},{6,7},{7,6},{8,9},{9,8},{10,11... | collective-permute-start | bytes 1572872 | tf_op jit(solution)/shard_map/ppermute | solution.py:318
  52.9 16.0 %copy-start.14 = (bf16[128,1024]{1,0:T(8,128)(2,1)}, bf16[128,1024]{1,0:T(8,128)(2,1)S(1)}, u32[]{:S(2)}) copy-start(bf16[128,1024]{1,0:T(8,128)(2,1)S(1)} %collective-permute-done.6.refs_5_) | copy-start | bytes 786436
  52.9 16.1 %collective-permute-start.11 = (bf16[128,1024]{1,0:T(8,128)(2,1)S(1)}, bf16[128,1024]{1,0:T(8,128)(2,1)S(1)}, u32[]{:S(2)}, u32[]{:S(2)}) collective-permute-start(bf16[128,1024]{1,0:T(8,128)(2,1)S(1)} %collective-permute-done.6.refs_5_), channel_id=1, source_target_pairs={{0,1},{1,0},{2,3},{3,2},{4,5},{5,4},{6,7},{7,6},{8,9},{9,8},{10,11... | collective-permute-start | bytes 786440 | tf_op jit(solution)/shard_map/ppermute | solution.py:318
  54.0 15.0 %collective-permute-start.12 = (bf16[128,1024]{1,0:T(8,128)(2,1)}, bf16[128,1024]{1,0:T(8,128)(2,1)S(1)}, u32[]{:S(2)}, u32[]{:S(2)}) collective-permute-start(bf16[128,1024]{1,0:T(8,128)(2,1)} %collective-permute-done.7.refs_6_), channel_id=1, source_target_pairs={{0,1},{1,0},{2,3},{3,2},{4,5},{5,4},{6,7},{7,6},{8,9},{9,8},{10,11... | collective-permute-start | bytes 786440 | tf_op jit(solution)/shard_map/ppermute | solution.py:318
  69.0 0.8 copy-start.13
  69.0 0.9 copy-start.15
  69.0 0.9 copy-start.16
  81.7 18.6 %copy-start.2 = (bf16[1,1024,1024]{2,1,0:T(8,128)(2,1)S(1)}, bf16[1,1024,1024]{2,1,0:T(8,128)(2,1)}, u32[]{:S(2)}) copy-start(bf16[1,1024,1024]{2,1,0:T(8,128)(2,1)} %param.10) | copy-start | bytes 6291460
  94.6 25.3 %all-to-all-start.2 = ((bf16[8,256,384]{2,1,0:T(8,128)(2,1)}), bf16[8,256,384]{2,1,0:T(8,128)(2,1)}, u32[]{:S(2)}, u32[]{:S(2)}) async-start(bf16[8,256,384]{2,1,0:T(8,128)(2,1)} %bitcast.29), calls=%async_computation.2 | async-start | bytes 3145728 | tf_op jit(solution)/shard_map/all_to_all | solution.py:330
  101.8 28.8 %collective-permute-start.18 = (bf16[256,1024]{1,0:T(8,128)(2,1)}, bf16[256,1024]{1,0:T(8,128)(2,1)S(1)}, u32[]{:S(2)}, u32[]{:S(2)}) collective-permute-start(bf16[256,1024]{1,0:T(8,128)(2,1)} %shard_map.81), channel_id=1, source_target_pairs={{0,8},{8,16},{16,24},{1,9},{9,17},{17,25},{2,10},{10,18},{18,26},{... | collective-permute-start | bytes 1572872 | tf_op jit(solution)/shard_map/ppermute | solution.py:360
  119.9 2.8 %copy-start = (bf16[1,3072,1024]{2,1,0:T(8,128)(2,1)S(1)}, bf16[1,3072,1024]{2,1,0:T(8,128)(2,1)}, u32[]{:S(2)}) copy-start(bf16[1,3072,1024]{2,1,0:T(8,128)(2,1)} %param.9) | copy-start | bytes 18874372
  122.7 1.0 copy-start.5
  123.7 1.0 copy-start.9
  128.2 15.8 %collective-permute-start.19 = (bf16[256,1024]{1,0:T(8,128)(2,1)S(1)}, bf16[256,1024]{1,0:T(8,128)(2,1)S(1)}, u32[]{:S(2)}, u32[]{:S(2)}) collective-permute-start(bf16[256,1024]{1,0:T(8,128)(2,1)S(1)} %shard_map.82), channel_id=1, source_target_pairs={{8,0},{16,8},{24,16},{9,1},{17,9},{25,17},{10,2},{18,10},{26,18},{... | collective-permute-start | bytes 1572872 | tf_op jit(solution)/shard_map/ppermute | solution.py:360

commit v4 on v3

--- a/solution.py
+++ b/solution.py
@@ -16,7 +16,7 @@
 NT = (((1,), (1,)), ((), ()))
 NN = (((1,), (0,)), ((), ()))
 TN = (((0,), (0,)), ((), ()))
-HBM = pl.BlockSpec(memory_space=pltpu.HBM)
+HBM = pl.BlockSpec(memory_space=pl.ANY)
 SMEM = pl.BlockSpec(memory_space=pltpu.SMEM)
 VMEM = pl.BlockSpec(memory_space=pltpu.VMEM)
 
@@ -100,25 +100,17 @@
 
 
 def head_kernel(back, unread, pieces, spacing, *refs):
-    cluster_ref, info_ref = refs[:2]
-    x_refs = refs[2 : 2 + len(pieces)]
-    refs = refs[2 + len(pieces) :]
+    cluster_ref, info_ref, w_ref = refs[:3]
+    x_refs = refs[3 : 3 + len(pieces)]
+    refs = refs[3 + len(pieces) :]
     if back:
-        g_ref, refs = refs[0], refs[1:]
-    w_ref, refs = refs[0], refs[1 + unread :]
-    out, xbuf, wbuf, turned, kept, count, member, xsem, wsem = refs[:9]
-    flip, head, residue = info_ref[0], info_ref[1], info_ref[2]
+        grads, refs = refs[0], refs[1:]
+    out, kept, count, member = refs[unread : unread + 4]
+    if back:
+        scales = refs[unread + 4]
+    flip, residue = info_ref[0], info_ref[2]
     tiles = kept.shape[0]
     clusters = count.shape[0]
-
-    weights = fetch(w_ref.at[:, head], wbuf, wsem)
-    copies = []
-    for i, (k, start, rows) in enumerate(pieces):
-        copies.append(fetch(x_refs[i], xbuf.at[k, pl.ds(start, rows)], xsem.at[i]))
-    if back:
-        scales, grads, gsem = refs[9:]
-        g_copy = fetch(g_ref, grads, gsem)
-
     for c in range(clusters):
         count[c] = 0
 
@@ -131,34 +123,25 @@
 
     lax.fori_loop(0, tiles, enter, 0)
 
-    weights.wait()
-    turned[...] = wbuf[...].reshape(3 * HD, -1).T
-
-    def project(k, carry):
-        for (slot, _, _), copy in zip(pieces, copies):
-            pl.when(k == slot)(copy.wait)
-        normed = xbuf[k]
+    weights = w_ref[...]
+    for (slot, start, rows), x_ref in zip(pieces, x_refs):
+        normed = x_ref[...]
         if back:
             x = high(normed)
             normed = low(x * rows_rsqrt(x))
-        mixed = dot(normed, turned[...], NN)
-        place = 2 * (flip ^ k)
+        mixed = dot(normed, weights, NT)
+        place = 2 * (flip ^ slot) + start // TILE
         for c in range(3):
             u = mixed[:, c * HD : (c + 1) * HD]
             if c < 2:
                 scale = rows_rsqrt(u)
                 u = u * scale
-            for j in range(2):
+            for j in range(rows // TILE):
                 kept[place + j, :, c * HD : (c + 1) * HD] = low(u[j * TILE : (j + 1) * TILE])
                 if back and c < 2:
                     scales[place + j, :, c * HD : (c + 1) * HD] = jnp.broadcast_to(
                         scale[j * TILE : (j + 1) * TILE], (TILE, HD)
                     )
-        return carry
-
-    lax.fori_loop(0, HEADS, project, 0)
-    if back:
-        g_copy.wait()
 
     def visit(c, carry):
         for n in range(1, CAPACITY + 1):
@@ -176,44 +159,47 @@
     lax.fori_loop(0, clusters, visit, 0)
 
 
-def head_work(info, tile_cluster, pieces, w_qkv, spacing, grads=None, earlier=()):
+def head_work(info, tile_cluster, pieces, weights, spacing, grads=None, earlier=()):
     back = grads is not None
-    width = w_qkv.shape[1]
+    width = weights.shape[1]
     tiles = 2 * HEADS
     wide = 3 * HD if back else HD
     tokens = tiles * TILE
-    operands = [tile_cluster, info] + [array for _, _, array in pieces]
+    operands = [tile_cluster, info, weights] + [array for _, _, array in pieces]
     if back:
         operands.append(grads.reshape(tiles, TILE, HD))
-    operands += [w_qkv.reshape(3, HEADS, HD, width), *earlier]
-    shapes = tuple((k, start, array.shape[0]) for k, start, array in pieces)
     scratch = [
-        pltpu.VMEM((HEADS, 2 * TILE, width), jnp.bfloat16),
-        pltpu.VMEM((3, HD, width), jnp.bfloat16),
-        pltpu.VMEM((width, 3 * HD), jnp.bfloat16),
         pltpu.VMEM((tiles, TILE, 3 * HD), jnp.bfloat16),
         pltpu.SMEM((tiles // 2,), jnp.int32),
         pltpu.SMEM((tiles // 2 * CAPACITY,), jnp.int32),
-        pltpu.SemaphoreType.DMA((len(pieces),)),
-        pltpu.SemaphoreType.DMA,
     ]
     if back:
-        scratch += [
-            pltpu.VMEM((tiles, TILE, 2 * HD), jnp.float32),
-            pltpu.VMEM((tiles, TILE, HD), jnp.bfloat16),
-            pltpu.SemaphoreType.DMA,
-        ]
+        scratch.append(pltpu.VMEM((tiles, TILE, 2 * HD), jnp.float32))
+    shapes = tuple((k, start, array.shape[0]) for k, start, array in pieces)
     out = call(
         functools.partial(head_kernel, back, len(earlier), shapes, spacing),
-        operands,
-        [SMEM, SMEM] + [HBM] * (len(operands) - 2),
+        operands + list(earlier),
+        [SMEM, SMEM] + [VMEM] * (len(operands) - 2) + [HBM] * len(earlier),
         jax.ShapeDtypeStruct((tiles, TILE, wide), jnp.bfloat16),
         scratch,
         2 * tokens * width * 3 * HD + tokens * 512 * HD * (14 if back else 4),
         2 * tokens * (width + 2 * wide),
-        grant=58 * MIB,
     )
     return out.reshape(HEADS, 2 * TILE, wide)
+
+
+def nothing(*refs):
+    pass
+
+
+def gate(arrays, earlier):
+    return pl.pallas_call(
+        nothing,
+        in_specs=[HBM] * (len(arrays) + len(earlier)),
+        out_specs=[HBM] * len(arrays),
+        out_shape=[jax.ShapeDtypeStruct(a.shape, a.dtype) for a in arrays],
+        input_output_aliases={i: i for i in range(len(arrays))},
+    )(*arrays, *earlier)
 
 
 def norm_kernel(x_ref, *refs):
@@ -318,9 +304,11 @@
     return lax.ppermute(block, "seq", route)
 
 
-def gather_rows(x):
+def gather_rows(x, earlier=()):
     half = x.shape[0] // 2
     over_x, over_y = partner(x, 2), partner(x, 4)
+    if earlier:
+        over_x, over_y = gate([over_x, over_y], earlier)
     top, bottom = partner(over_x[:half], 4), partner(over_y[half:], 2)
     pieces = [(0, 0, x), (2, 0, over_x), (4, 0, over_y), (6, 0, top), (6, half, bottom)]
     return pieces + [(k + 1, start, partner(block, 1)) for k, start, block in pieces]
@@ -372,7 +360,7 @@
     else:
         info = jnp.stack([jnp.zeros_like(own), own // spacing, own % spacing])
 
-        def gather(x):
+        def gather(x, earlier=()):
             copies = jnp.broadcast_to(x, (HEADS, *x.shape))
             return [(k, 0, block) for k, block in enumerate(to_heads(copies, own, spacing))]
 
@@ -382,16 +370,20 @@
         def collect(blocks):
             return to_tokens(blocks, own, spacing, tokens)
 
+    own_head = w_rows.reshape(3, HEADS, HD, -1)
+    own_head = lax.dynamic_index_in_dim(own_head, info[1], 1, keepdims=False)
+    own_head = own_head.reshape(3 * HD, -1)
     stored_pieces = gather(stored)
     grad_attention = spread(spread_grads(upstream, w_fin))
     earlier = [block for k, _, block in stored_pieces if k == HEADS - 2]
-    current_pieces = gather(norm_after(current, [*earlier, grad_attention]))
-    grads = head_work(info, tile_cluster, stored_pieces, w_rows, spacing, grad_attention)
+    normed = norm_after(current, [*earlier, grad_attention])
+    grads = head_work(info, tile_cluster, stored_pieces, own_head, spacing, grad_attention)
+    current_pieces = gather(normed, [grads])
     returned_grads = collect(grads)
     outputs = head_work(
-        info, tile_cluster, current_pieces, w_rows, spacing, earlier=(grads,)
-    )
-    returned = collect(outputs)
+        info, tile_cluster, current_pieces, own_head, spacing, earlier=(grads,)
+    )
+    returned = collect(gate([outputs], [returned_grads])[0])
     grad_self = finish_back(returned_grads, stored, upstream, w_rows)
     grad_input = passed_along(grad_self, "pipe", -1)
     result = finish(returned, current, w_fin)

time: 146 us -> 145 us (level)
  blocking collectives: 12.9 us -> 0 us
  Pallas kernels: 34.6 us -> 26.7 us
  waiting for transfers between devices: 56.4 us -> 63.9 us
  local copies, waits for them, and re-layouts: 13.9 us -> 20.4 us
  starting transfers between devices: 26.2 us -> 31.3 us
    ppermute x18, waiting for transfers between devices: 24.4 us -> 45.4 us  [partner(): return lax.ppermute(block, 'seq', route)]
    all_to_all x1 -> x0, blocking collectives: 12.9 us -> none  [all_swap(): lax.all_to_all(blocks, 'seq', split_axis=0, concat_axis=0, tiled=True)]
    all_to_all x2 -> x3, waiting for transfers between devices: 18.7 us -> 6.45 us  [all_swap(): lax.all_to_all(blocks, 'seq', split_axis=0, concat_axis=0, tiled=True)]
    pallas_call x6, Pallas kernels: 34.6 us -> 26.7 us  [call(): pl.pallas_call(kernel, in_specs=in_specs, out_specs=VMEM, out_shape=out_s...]
    unnamed x54 -> x44, local copies, waits for them, and re-layouts: 11.5 us -> 17.3 us
    all_to_all x2 -> x3, starting transfers between devices: 10.7 us -> 15 us  [all_swap(): lax.all_to_all(blocks, 'seq', split_axis=0, concat_axis=0, tiled=True)]
  transfers between devices with their start and end apart: 22 -> 23, of which waited for: 9 -> 10; matrix products, arithmetic and copies ran while one was open for 2% -> 2% of each run, Pallas kernels for 16% -> 10%
where the time goes in v4:
time: 145 us; the launch traced here: 143 us
  waiting for transfers between devices  63.9 us (44%)
  starting transfers between devices  31.3 us (22%)
  Pallas kernels  26.7 us (18%)
  local copies, waits for them, and re-layouts  20.4 us (14%)
    ppermute x18, waiting for transfers between devices, partner(): return lax.ppermute(block, 'seq', route)  45.4 us
    pallas_call x6, Pallas kernels, call(): pl.pallas_call(kernel, in_specs=in_specs, out_specs=VMEM, out_shape=out_s...  26.7 us
    unnamed x44, local copies, waits for them, and re-layouts  17.3 us
    all_to_all x3, starting transfers between devices, all_swap(): lax.all_to_all(blocks, 'seq', split_axis=0, concat_axis=0, tiled=True)  15 us
    ppermute x2, waiting for transfers between devices, passed_along(): return lax.ppermute(block, axis, route)  12.1 us
    ppermute x18, starting transfers between devices, partner(): return lax.ppermute(block, 'seq', route)  10.4 us
    all_to_all x3, waiting for transfers between devices, all_swap(): lax.all_to_all(blocks, 'seq', split_axis=0, concat_axis=0, tiled=True)  6.45 us
    ppermute x2, starting transfers between devices, passed_along(): return lax.ppermute(block, axis, route)  5.86 us
  transfers between devices with their start and end apart: 23, of which 10 were waited for; matrix products, arithmetic and copies ran while one was open for 2% of the time, Pallas kernels for 10%

profile of v4, /device:TPU:18, one launch (start us, length us, event | category | flops | bytes accessed | tf_op | source)
XLA Modules:
  0.0 143.2 jit_solution(5962838994910404640)
XLA Ops:
  0.6 1.6 %collective-permute-start.2 = (bf16[256,1024]{1,0:T(8,128)(2,1)}, bf16[256,1024]{1,0:T(8,128)(2,1)S(1)}, u32[]{:S(2)}, u32[]{:S(2)}) collective-permute-start(bf16[256,1024]{1,0:T(8,128)(2,1)} %bitcast.28), channel_id=1, source_target_pairs={{0,4},{1,5},{2,6},{3,7},{4,0},{5,1},{6,2},{7,3},{8,12},{9,13},{10,... | collective-permute-start | bytes 1572872 | tf_op jit(solution)/shard_map/ppermute | solution.py:304
  2.2 0.5 collective-permute-start
  2.8 11.8 %collective-permute-done.2.refs_5_ = bf16[256,1024]{1,0:T(8,128)(2,1)S(1)} collective-permute-done((bf16[256,1024]{1,0:T(8,128)(2,1)}, bf16[256,1024]{1,0:T(8,128)(2,1)S(1)}, u32[]{:S(2)}, u32[]{:S(2)}) %collective-permute-start.2) | collective-permute-done | bytes 524320 | tf_op jit(solution)/shard_map/ppermute | solution.py:304
  14.6 0.6 collective-permute-start.3
  15.2 0.6 collective-permute-done.refs_4_
  15.8 1.0 collective-permute-start.1
  16.8 0.5 collective-permute-start.8
  17.3 1.6 %copy-done.2 = bf16[1,1024,1024]{2,1,0:T(8,128)(2,1)S(1)} copy-done((bf16[1,1024,1024]{2,1,0:T(8,128)(2,1)S(1)}, bf16[1,1024,1024]{2,1,0:T(8,128)(2,1)}, u32[]{:S(2)}) %copy-start.2) | copy-done | bytes 2097176
  18.9 1.0 copy-done.6
  19.9 2.8 %shard_map.77 = bf16[8,256,128]{2,1,0:T(8,128)(2,1)} custom-call(bf16[256,1024]{1,0:T(8,128)(2,1)S(1)} %bitcast.21, bf16[8,128,1024]{2,1,0:T(8,128)(2,1)S(1)} %bitcast.16), custom_call_target="tpu_custom_call" | custom-call | flops 536870912 | bytes 2097152 | tf_op jit(solution)/shard_map/pallas_call | solution.py:41
  22.8 5.0 %all-to-all-start = ((bf16[8,256,128]{2,1,0:T(8,128)(2,1)}), bf16[8,256,128]{2,1,0:T(8,128)(2,1)S(1)}, u32[]{:S(2)}, u32[]{:S(2)}) async-start(bf16[8,256,128]{2,1,0:T(8,128)(2,1)} %shard_map.77), calls=%async_computation | async-start | bytes 1048576 | tf_op jit(solution)/shard_map/all_to_all | solution.py:318
  28.5 1.2 constant_dynamic-slice_fusion
  29.7 6.4 %all-to-all-done.refs_2_ = bf16[8,256,128]{2,1,0:T(8,128)(2,1)S(1)} async-done(((bf16[8,256,128]{2,1,0:T(8,128)(2,1)}), bf16[8,256,128]{2,1,0:T(8,128)(2,1)S(1)}, u32[]{:S(2)}, u32[]{:S(2)}) %all-to-all-start) | async-done | bytes 524320 | tf_op jit(solution)/shard_map/all_to_all | solution.py:318
  36.2 11.7 %shard_map.79 = bf16[16,128,384]{2,1,0:T(8,128)(2,1)} custom-call(s32[16]{0:T(128)S(1)} %copy-done.20, s32[3]{0:T(128)S(1)} %pad_add_fusion.refs_1_, bf16[384,1024]{1,0:T(8,128)(2,1)S(1)} %bitcast.26, bf16[256,1024]{1,0:T(8,128)(2,1)S(1)} %bitcast.31, bf16[256,1024]{1,0:T(8,128)(2,1)S(1)} %collective-permute-done.refs_4_, ...), custom_call_target="tpu_custom_call" | custom-call | flops 3489660928 | bytes 7340032 | tf_op jit(solution)/shard_map/pallas_call | solution.py:41
  48.0 5.1 %all-to-all-start.1 = ((bf16[8,256,384]{2,1,0:T(8,128)(2,1)}), bf16[8,256,384]{2,1,0:T(8,128)(2,1)S(1)}, u32[]{:S(2)}, u32[]{:S(2)}) async-start(bf16[8,256,384]{2,1,0:T(8,128)(2,1)} %bitcast.8.refs_2_.refs_13_), calls=%async_computation.1 | async-start | bytes 3145728 | tf_op jit(solution)/shard_map/all_to_all | solution.py:318
  53.1 0.9 copy-done.17
  54.0 0.9 copy-done.19
  55.0 1.0 shard_map.78.refs_3_
  56.0 1.9 %collective-permute-start.5 = (bf16[256,1024]{1,0:T(8,128)(2,1)}, bf16[256,1024]{1,0:T(8,128)(2,1)S(1)}, u32[]{:S(2)}, u32[]{:S(2)}) collective-permute-start(bf16[256,1024]{1,0:T(8,128)(2,1)} %shard_map.78.refs_3_), channel_id=1, source_target_pairs={{0,4},{1,5},{2,6},{3,7},{4,0},{5,1},{6,2},{7,3},{8,12},{9,13},{10,... | collective-permute-start | bytes 1572872 | tf_op jit(solution)/shard_map/ppermute | solution.py:304
  58.0 24.8 %collective-permute-done.4.refs_0_ = bf16[256,1024]{1,0:T(8,128)(2,1)S(1)} collective-permute-done((bf16[256,1024]{1,0:T(8,128)(2,1)}, bf16[256,1024]{1,0:T(8,128)(2,1)S(1)}, u32[]{:S(2)}, u32[]{:S(2)}) %collective-permute-start.4) | collective-permute-done | bytes 524320 | tf_op jit(solution)/shard_map/ppermute | solution.py:304
  82.8 1.0 collective-permute-done.5.refs_1_
  83.8 0.8 copy-done.12
  84.6 1.0 slice.14
  85.6 1.5 %collective-permute-start.11 = (bf16[128,1024]{1,0:T(8,128)(2,1)S(1)}, bf16[128,1024]{1,0:T(8,128)(2,1)S(1)}, u32[]{:S(2)}, u32[]{:S(2)}) collective-permute-start(bf16[128,1024]{1,0:T(8,128)(2,1)S(1)} %slice.14), channel_id=1, source_target_pairs={{0,4},{1,5},{2,6},{3,7},{4,0},{5,1},{6,2},{7,3},{8,12},{9,13},{10,... | collective-permute-start | bytes 786440 | tf_op jit(solution)/shard_map/ppermute | solution.py:304
  87.1 1.0 slice.15
  88.1 1.5 %collective-permute-start.12 = (bf16[128,1024]{1,0:T(8,128)(2,1)S(1)}, bf16[128,1024]{1,0:T(8,128)(2,1)S(1)}, u32[]{:S(2)}, u32[]{:S(2)}) collective-permute-start(bf16[128,1024]{1,0:T(8,128)(2,1)S(1)} %slice.15), channel_id=1, source_target_pairs={{0,2},{1,3},{2,0},{3,1},{4,6},{5,7},{6,4},{7,5},{8,10},{9,11},{10,... | collective-permute-start | bytes 786440 | tf_op jit(solution)/shard_map/ppermute | solution.py:304
  89.6 0.5 collective-permute-start.15
  90.1 3.8 %collective-permute-done.11.refs_6_ = bf16[128,1024]{1,0:T(8,128)(2,1)S(1)} collective-permute-done((bf16[128,1024]{1,0:T(8,128)(2,1)S(1)}, bf16[128,1024]{1,0:T(8,128)(2,1)S(1)}, u32[]{:S(2)}, u32[]{:S(2)}) %collective-permute-start.11) | collective-permute-done | bytes 262176 | tf_op jit(solution)/shard_map/ppermute | solution.py:304
  94.0 1.8 %collective-permute-done.12.refs_7_ = bf16[128,1024]{1,0:T(8,128)(2,1)S(1)} collective-permute-done((bf16[128,1024]{1,0:T(8,128)(2,1)S(1)}, bf16[128,1024]{1,0:T(8,128)(2,1)S(1)}, u32[]{:S(2)}, u32[]{:S(2)}) %collective-permute-start.12) | collective-permute-done | bytes 262176 | tf_op jit(solution)/shard_map/ppermute | solution.py:304
  95.7 1.5 %collective-permute-done.17.refs_12_ = bf16[128,1024]{1,0:T(8,128)(2,1)S(1)} collective-permute-done((bf16[128,1024]{1,0:T(8,128)(2,1)S(1)}, bf16[128,1024]{1,0:T(8,128)(2,1)S(1)}, u32[]{:S(2)}, u32[]{:S(2)}) %collective-permute-start.17) | collective-permute-done | bytes 262176 | tf_op jit(solution)/shard_map/ppermute | solution.py:304
  97.3 1.0 copy-done.11
  98.3 1.0 copy-done.13
  99.3 7.6 %shard_map.81 = bf16[16,128,128]{2,1,0:T(8,128)(2,1)S(1)} custom-call(s32[16]{0:T(128)S(1)} %copy-done.20, s32[3]{0:T(128)S(1)} %pad_add_fusion.refs_1_, bf16[384,1024]{1,0:T(8,128)(2,1)S(1)} %bitcast.27, bf16[256,1024]{1,0:T(8,128)(2,1)} %shard_map.78.refs_3_, bf16[256,1024]{1,0:T(8,128)(2,1)S(1)} %copy-done.11, bf16[256,1024]{1,0:T(8,128)(2,1)S(1)} %copy-done.13, ...), custom_call_target="tpu_custom_call" | custom-call | flops 2147483648 | bytes 5242880 | tf_op jit(solution)/shard_map/pallas_call | solution.py:41
  107.0 0.8 copy-done.5
  107.8 1.2 copy-done
  109.0 4.9 %all-to-all-start.2 = ((bf16[8,256,128]{2,1,0:T(8,128)(2,1)}), bf16[8,256,128]{2,1,0:T(8,128)(2,1)S(1)}, u32[]{:S(2)}, u32[]{:S(2)}) async-start(bf16[8,256,128]{2,1,0:T(8,128)(2,1)} %shard_map.82), calls=%async_computation.2 | async-start | bytes 1048576 | tf_op jit(solution)/shard_map/all_to_all | solution.py:318
  113.9 1.4 copy-done.1
  115.3 2.8 %copy-done.4 = bf16[1,3072,1024]{2,1,0:T(8,128)(2,1)S(1)} copy-done((bf16[1,3072,1024]{2,1,0:T(8,128)(2,1)S(1)}, bf16[1,3072,1024]{2,1,0:T(8,128)(2,1)}, u32[]{:S(2)}) %copy-start.4) | copy-done | bytes 6291480
  118.1 1.0 copy-done.15
  119.1 2.8 %shard_map.84 = bf16[256,1024]{1,0:T(8,128)(2,1)} custom-call(bf16[8,256,384]{2,1,0:T(8,128)(2,1)S(1)} %copy-done.1, bf16[256,1024]{1,0:T(8,128)(2,1)S(1)} %bitcast.32, bf16[256,1024]{1,0:T(8,128)(2,1)S(1)} %bitcast.22, bf16[3072,1024]{1,0:T(8,128)(2,1)S(1)} %bitcast.19), custom_call_target="tpu_custom_call" | custom-call | flops 1610612736 | bytes 6291456 | tf_op jit(solution)/shard_map/pallas_call | solution.py:41
  121.9 2.3 %collective-permute-start.19 = (bf16[256,1024]{1,0:T(8,128)(2,1)}, bf16[256,1024]{1,0:T(8,128)(2,1)S(1)}, u32[]{:S(2)}, u32[]{:S(2)}) collective-permute-start(bf16[256,1024]{1,0:T(8,128)(2,1)} %shard_map.84), channel_id=1, source_target_pairs={{8,0},{16,8},{24,16},{9,1},{17,9},{25,17},{10,2},{18,10},{26,18},{... | collective-permute-start | bytes 1572872 | tf_op jit(solution)/shard_map/ppermute | solution.py:348
  124.3 1.0 copy-done.9
  125.3 0.7 shard_map.83
  126.0 3.5 %collective-permute-start.18 = (bf16[256,1024]{1,0:T(8,128)(2,1)S(1)}, bf16[256,1024]{1,0:T(8,128)(2,1)S(1)}, u32[]{:S(2)}, u32[]{:S(2)}) collective-permute-start(bf16[256,1024]{1,0:T(8,128)(2,1)S(1)} %shard_map.83), channel_id=1, source_target_pairs={{0,8},{8,16},{16,24},{1,9},{9,17},{17,25},{2,10},{10,18},{18,26},{... | collective-permute-start | bytes 1572872 | tf_op jit(solution)/shard_map/ppermute | solution.py:348
  129.6 8.4 %collective-permute-done.19 = bf16[256,1024]{1,0:T(8,128)(2,1)S(1)} collective-permute-done((bf16[256,1024]{1,0:T(8,128)(2,1)}, bf16[256,1024]{1,0:T(8,128)(2,1)S(1)}, u32[]{:S(2)}, u32[]{:S(2)}) %collective-permute-start.19) | collective-permute-done | bytes 524320 | tf_op jit(solution)/shard_map/ppermute | solution.py:348
  138.0 3.6 %collective-permute-done.18 = bf16[256,1024]{1,0:T(8,128)(2,1)S(1)} collective-permute-done((bf16[256,1024]{1,0:T(8,128)(2,1)S(1)}, bf16[256,1024]{1,0:T(8,128)(2,1)S(1)}, u32[]{:S(2)}, u32[]{:S(2)}) %collective-permute-start.18) | collective-permute-done | bytes 524320 | tf_op jit(solution)/shard_map/ppermute | solution.py:348
  141.6 0.8 copy.18
  142.4 0.8 copy.19
  (56 shorter events, 0.9 us)
Async XLA Ops:
  0.6 13.9 %collective-permute-start.2 = (bf16[256,1024]{1,0:T(8,128)(2,1)}, bf16[256,1024]{1,0:T(8,128)(2,1)S(1)}, u32[]{:S(2)}, u32[]{:S(2)}) collective-permute-start(bf16[256,1024]{1,0:T(8,128)(2,1)} %bitcast.28), channel_id=1, source_target_pairs={{0,4},{1,5},{2,6},{3,7},{4,0},{5,1},{6,2},{7,3},{8,12},{9,13},{10,... | collective-permute-start | bytes 1572872 | tf_op jit(solution)/shard_map/ppermute | solution.py:304
  2.2 13.6 %collective-permute-start = (bf16[256,1024]{1,0:T(8,128)(2,1)}, bf16[256,1024]{1,0:T(8,128)(2,1)S(1)}, u32[]{:S(2)}, u32[]{:S(2)}) collective-permute-start(bf16[256,1024]{1,0:T(8,128)(2,1)} %bitcast.29), channel_id=1, source_target_pairs={{0,2},{1,3},{2,0},{3,1},{4,6},{5,7},{6,4},{7,5},{8,10},{9,11},{10,... | collective-permute-start | bytes 1572872 | tf_op jit(solution)/shard_map/ppermute | solution.py:304
  2.7 33.4 %collective-permute-start.6 = (bf16[256,1024]{1,0:T(8,128)(2,1)}, bf16[256,1024]{1,0:T(8,128)(2,1)}, u32[]{:S(2)}, u32[]{:S(2)}) collective-permute-start(bf16[256,1024]{1,0:T(8,128)(2,1)} %bitcast.30), channel_id=1, source_target_pairs={{0,1},{1,0},{2,3},{3,2},{4,5},{5,4},{6,7},{7,6},{8,9},{9,8},{10,11... | collective-permute-start | bytes 1572872 | tf_op jit(solution)/shard_map/ppermute | solution.py:304
  14.6 13.3 %collective-permute-start.3 = (bf16[128,1024]{1,0:T(8,128)(2,1)S(1)}, bf16[128,1024]{1,0:T(8,128)(2,1)S(1)}, u32[]{:S(2)}, u32[]{:S(2)}) collective-permute-start(bf16[128,1024]{1,0:T(8,128)(2,1)S(1)} %slice.17), channel_id=1, source_target_pairs={{0,2},{1,3},{2,0},{3,1},{4,6},{5,7},{6,4},{7,5},{8,10},{9,11},{10,... | collective-permute-start | bytes 786440 | tf_op jit(solution)/shard_map/ppermute | solution.py:304
  15.8 12.2 %collective-permute-start.1 = (bf16[128,1024]{1,0:T(8,128)(2,1)S(1)}, bf16[128,1024]{1,0:T(8,128)(2,1)S(1)}, u32[]{:S(2)}, u32[]{:S(2)}) collective-permute-start(bf16[128,1024]{1,0:T(8,128)(2,1)S(1)} %slice.16), channel_id=1, source_target_pairs={{0,4},{1,5},{2,6},{3,7},{4,0},{5,1},{6,2},{7,3},{8,12},{9,13},{10,... | collective-permute-start | bytes 786440 | tf_op jit(solution)/shard_map/ppermute | solution.py:304
  16.8 19.4 %collective-permute-start.7 = (bf16[256,1024]{1,0:T(8,128)(2,1)S(1)}, bf16[256,1024]{1,0:T(8,128)(2,1)}, u32[]{:S(2)}, u32[]{:S(2)}) collective-permute-start(bf16[256,1024]{1,0:T(8,128)(2,1)S(1)} %collective-permute-done.refs_4_), channel_id=1, source_target_pairs={{0,1},{1,0},{2,3},{3,2},{4,5},{5,4},{6,7},{7,6},{8,9},{9,8},{10,11... | collective-permute-start | bytes 1572872 | tf_op jit(solution)/shard_map/ppermute | solution.py:304
  16.8 19.4 %collective-permute-start.8 = (bf16[256,1024]{1,0:T(8,128)(2,1)S(1)}, bf16[256,1024]{1,0:T(8,128)(2,1)}, u32[]{:S(2)}, u32[]{:S(2)}) collective-permute-start(bf16[256,1024]{1,0:T(8,128)(2,1)S(1)} %collective-permute-done.2.refs_5_), channel_id=1, source_target_pairs={{0,1},{1,0},{2,3},{3,2},{4,5},{5,4},{6,7},{7,6},{8,9},{9,8},{10,11... | collective-permute-start | bytes 1572872 | tf_op jit(solution)/shard_map/ppermute | solution.py:304
  17.3 1.6 %copy-start.2 = (bf16[1,1024,1024]{2,1,0:T(8,128)(2,1)S(1)}, bf16[1,1024,1024]{2,1,0:T(8,128)(2,1)}, u32[]{:S(2)}) copy-start(bf16[1,1024,1024]{2,1,0:T(8,128)(2,1)} %param.10) | copy-start | bytes 6291460
  18.9 1.0 copy-start.6
  22.8 13.4 %copy-start.14 = (bf16[1,256,1024]{2,1,0:T(8,128)(2,1)S(1)}, bf16[1,256,1024]{2,1,0:T(8,128)(2,1)}, u32[]{:S(2)}) copy-start(bf16[1,256,1024]{2,1,0:T(8,128)(2,1)} %param.7) | copy-start | bytes 1572868
  22.8 13.4 %copy-start.20 = (s32[16]{0:T(128)S(1)}, s32[16]{0:T(128)}, u32[]{:S(2)}) copy-start(s32[16]{0:T(128)} %refs_0_.3) | copy-start | bytes 196
  22.8 13.3 %all-to-all-start = ((bf16[8,256,128]{2,1,0:T(8,128)(2,1)}), bf16[8,256,128]{2,1,0:T(8,128)(2,1)S(1)}, u32[]{:S(2)}, u32[]{:S(2)}) async-start(bf16[8,256,128]{2,1,0:T(8,128)(2,1)} %shard_map.77), calls=%async_computation | async-start | bytes 1048576 | tf_op jit(solution)/shard_map/all_to_all | solution.py:318
  27.9 20.1 %copy-start.16 = (bf16[128,1024]{1,0:T(8,128)(2,1)}, bf16[128,1024]{1,0:T(8,128)(2,1)S(1)}, u32[]{:S(2)}) copy-start(bf16[128,1024]{1,0:T(8,128)(2,1)S(1)} %collective-permute-done.3.refs_1_.refs_7_) | copy-start | bytes 786436
  27.9 8.3 %collective-permute-start.10 = (bf16[128,1024]{1,0:T(8,128)(2,1)S(1)}, bf16[128,1024]{1,0:T(8,128)(2,1)}, u32[]{:S(2)}, u32[]{:S(2)}) collective-permute-start(bf16[128,1024]{1,0:T(8,128)(2,1)S(1)} %collective-permute-done.3.refs_1_.refs_7_), channel_id=1, source_target_pairs={{0,1},{1,0},{2,3},{3,2},{4,5},{5,4},{6,7},{7,6},{8,9},{9,8},{10,11... | collective-permute-start | bytes 786440 | tf_op jit(solution)/shard_map/ppermute | solution.py:304
  28.1 19.9 %copy-start.18 = (bf16[128,1024]{1,0:T(8,128)(2,1)}, bf16[128,1024]{1,0:T(8,128)(2,1)S(1)}, u32[]{:S(2)}) copy-start(bf16[128,1024]{1,0:T(8,128)(2,1)S(1)} %collective-permute-done.1.refs_0_.refs_6_) | copy-start | bytes 786436
  28.1 8.1 %collective-permute-start.9 = (bf16[128,1024]{1,0:T(8,128)(2,1)S(1)}, bf16[128,1024]{1,0:T(8,128)(2,1)}, u32[]{:S(2)}, u32[]{:S(2)}) collective-permute-start(bf16[128,1024]{1,0:T(8,128)(2,1)S(1)} %collective-permute-done.1.refs_0_.refs_6_), channel_id=1, source_target_pairs={{0,1},{1,0},{2,3},{3,2},{4,5},{5,4},{6,7},{7,6},{8,9},{9,8},{10,11... | collective-permute-start | bytes 786440 | tf_op jit(solution)/shard_map/ppermute | solution.py:304
  47.9 5.1 %copy-start.8 = (bf16[1,256,1024]{2,1,0:T(8,128)(2,1)S(1)}, bf16[1,256,1024]{2,1,0:T(8,128)(2,1)}, u32[]{:S(2)}) copy-start(bf16[1,256,1024]{2,1,0:T(8,128)(2,1)} %param.6) | copy-start | bytes 1572868
  48.0 59.8 %all-to-all-start.1 = ((bf16[8,256,384]{2,1,0:T(8,128)(2,1)}), bf16[8,256,384]{2,1,0:T(8,128)(2,1)S(1)}, u32[]{:S(2)}, u32[]{:S(2)}) async-start(bf16[8,256,384]{2,1,0:T(8,128)(2,1)} %bitcast.8.refs_2_.refs_13_), calls=%async_computation.1 | async-start | bytes 3145728 | tf_op jit(solution)/shard_map/all_to_all | solution.py:318
  53.1 1.0 copy-start.17
  54.0 0.9 copy-start.19
  55.9 26.8 %collective-permute-start.4 = (bf16[256,1024]{1,0:T(8,128)(2,1)}, bf16[256,1024]{1,0:T(8,128)(2,1)S(1)}, u32[]{:S(2)}, u32[]{:S(2)}) collective-permute-start(bf16[256,1024]{1,0:T(8,128)(2,1)} %shard_map.78.refs_3_), channel_id=1, source_target_pairs={{0,2},{1,3},{2,0},{3,1},{4,6},{5,7},{6,4},{7,5},{8,10},{9,11},{10,... | collective-permute-start | bytes 1572872 | tf_op jit(solution)/shard_map/ppermute | solution.py:304
  56.0 27.8 %collective-permute-start.5 = (bf16[256,1024]{1,0:T(8,128)(2,1)}, bf16[256,1024]{1,0:T(8,128)(2,1)S(1)}, u32[]{:S(2)}, u32[]{:S(2)}) collective-permute-start(bf16[256,1024]{1,0:T(8,128)(2,1)} %shard_map.78.refs_3_), channel_id=1, source_target_pairs={{0,4},{1,5},{2,6},{3,7},{4,0},{5,1},{6,2},{7,3},{8,12},{9,13},{10,... | collective-permute-start | bytes 1572872 | tf_op jit(solution)/shard_map/ppermute | solution.py:304
  58.0 37.7 %collective-permute-start.13 = (bf16[256,1024]{1,0:T(8,128)(2,1)}, bf16[256,1024]{1,0:T(8,128)(2,1)}, u32[]{:S(2)}, u32[]{:S(2)}) collective-permute-start(bf16[256,1024]{1,0:T(8,128)(2,1)} %shard_map.78.refs_3_), channel_id=1, source_target_pairs={{0,1},{1,0},{2,3},{3,2},{4,5},{5,4},{6,7},{7,6},{8,9},{9,8},{10,11... | collective-permute-start | bytes 1572872 | tf_op jit(solution)/shard_map/ppermute | solution.py:304
  82.8 1.0 copy-start.10
  83.8 0.8 copy-start.12
  85.6 8.3 %collective-permute-start.11 = (bf16[128,1024]{1,0:T(8,128)(2,1)S(1)}, bf16[128,1024]{1,0:T(8,128)(2,1)S(1)}, u32[]{:S(2)}, u32[]{:S(2)}) collective-permute-start(bf16[128,1024]{1,0:T(8,128)(2,1)S(1)} %slice.14), channel_id=1, source_target_pairs={{0,4},{1,5},{2,6},{3,7},{4,0},{5,1},{6,2},{7,3},{8,12},{9,13},{10,... | collective-permute-start | bytes 786440 | tf_op jit(solution)/shard_map/ppermute | solution.py:304
  88.1 7.6 %collective-permute-start.12 = (bf16[128,1024]{1,0:T(8,128)(2,1)S(1)}, bf16[128,1024]{1,0:T(8,128)(2,1)S(1)}, u32[]{:S(2)}, u32[]{:S(2)}) collective-permute-start(bf16[128,1024]{1,0:T(8,128)(2,1)S(1)} %slice.15), channel_id=1, source_target_pairs={{0,2},{1,3},{2,0},{3,1},{4,6},{5,7},{6,4},{7,5},{8,10},{9,11},{10,... | collective-permute-start | bytes 786440 | tf_op jit(solution)/shard_map/ppermute | solution.py:304
  89.6 7.6 %collective-permute-start.14 = (bf16[256,1024]{1,0:T(8,128)(2,1)}, bf16[256,1024]{1,0:T(8,128)(2,1)S(1)}, u32[]{:S(2)}, u32[]{:S(2)}) collective-permute-start(bf16[256,1024]{1,0:T(8,128)(2,1)} %get-tuple-element.4.refs_4_), channel_id=1, source_target_pairs={{0,1},{1,0},{2,3},{3,2},{4,5},{5,4},{6,7},{7,6},{8,9},{9,8},{10,11... | collective-permute-start | bytes 1572872 | tf_op jit(solution)/shard_map/ppermute | solution.py:304
  89.6 7.6 %collective-permute-start.15 = (bf16[256,1024]{1,0:T(8,128)(2,1)}, bf16[256,1024]{1,0:T(8,128)(2,1)S(1)}, u32[]{:S(2)}, u32[]{:S(2)}) collective-permute-start(bf16[256,1024]{1,0:T(8,128)(2,1)} %get-tuple-element.5.refs_5_), channel_id=1, source_target_pairs={{0,1},{1,0},{2,3},{3,2},{4,5},{5,4},{6,7},{7,6},{8,9},{9,8},{10,11... | collective-permute-start | bytes 1572872 | tf_op jit(solution)/shard_map/ppermute | solution.py:304
  94.0 1.8 %collective-permute-start.16 = (bf16[128,1024]{1,0:T(8,128)(2,1)S(1)}, bf16[128,1024]{1,0:T(8,128)(2,1)S(1)}, u32[]{:S(2)}, u32[]{:S(2)}) collective-permute-start(bf16[128,1024]{1,0:T(8,128)(2,1)S(1)} %collective-permute-done.11.refs_6_), channel_id=1, source_target_pairs={{0,1},{1,0},{2,3},{3,2},{4,5},{5,4},{6,7},{7,6},{8,9},{9,8},{10,11... | collective-permute-start | bytes 786440 | tf_op jit(solution)/shard_map/ppermute | solution.py:304
  95.7 1.5 %collective-permute-start.17 = (bf16[128,1024]{1,0:T(8,128)(2,1)S(1)}, bf16[128,1024]{1,0:T(8,128)(2,1)S(1)}, u32[]{:S(2)}, u32[]{:S(2)}) collective-permute-start(bf16[128,1024]{1,0:T(8,128)(2,1)S(1)} %collective-permute-done.12.refs_7_), channel_id=1, source_target_pairs={{0,1},{1,0},{2,3},{3,2},{4,5},{5,4},{6,7},{7,6},{8,9},{9,8},{10,11... | collective-permute-start | bytes 786440 | tf_op jit(solution)/shard_map/ppermute | solution.py:304
  97.3 1.0 copy-start.11
  98.3 1.0 copy-start.13
  107.0 0.8 copy-start.5
  107.8 6.1 %copy-start.7 = (bf16[1,256,1024]{2,1,0:T(8,128)(2,1)S(1)}, bf16[1,256,1024]{2,1,0:T(8,128)(2,1)}, u32[]{:S(2)}) copy-start(bf16[1,256,1024]{2,1,0:T(8,128)(2,1)} %param.8) | copy-start | bytes 1572868
  107.8 1.2 copy-start
  109.0 15.3 %all-to-all-start.2 = ((bf16[8,256,128]{2,1,0:T(8,128)(2,1)}), bf16[8,256,128]{2,1,0:T(8,128)(2,1)S(1)}, u32[]{:S(2)}, u32[]{:S(2)}) async-start(bf16[8,256,128]{2,1,0:T(8,128)(2,1)} %shard_map.82), calls=%async_computation.2 | async-start | bytes 1048576 | tf_op jit(solution)/shard_map/all_to_all | solution.py:318
  113.9 1.4 copy-start.1
  115.3 2.8 %copy-start.4 = (bf16[1,3072,1024]{2,1,0:T(8,128)(2,1)S(1)}, bf16[1,3072,1024]{2,1,0:T(8,128)(2,1)}, u32[]{:S(2)}) copy-start(bf16[1,3072,1024]{2,1,0:T(8,128)(2,1)} %param.9) | copy-start | bytes 18874372
  118.1 1.0 copy-start.15
  119.1 5.2 %copy-start.3 = (bf16[1,1024,1024]{2,1,0:T(8,128)(2,1)S(1)}, bf16[1,1024,1024]{2,1,0:T(8,128)(2,1)}, u32[]{:S(2)}) copy-start(bf16[1,1024,1024]{2,1,0:T(8,128)(2,1)} %param.10) | copy-start | bytes 6291460
  121.9 16.1 %collective-permute-start.19 = (bf16[256,1024]{1,0:T(8,128)(2,1)}, bf16[256,1024]{1,0:T(8,128)(2,1)S(1)}, u32[]{:S(2)}, u32[]{:S(2)}) collective-permute-start(bf16[256,1024]{1,0:T(8,128)(2,1)} %shard_map.84), channel_id=1, source_target_pairs={{8,0},{16,8},{24,16},{9,1},{17,9},{25,17},{10,2},{18,10},{26,18},{... | collective-permute-start | bytes 1572872 | tf_op jit(solution)/shard_map/ppermute | solution.py:348
  124.3 1.0 copy-start.9
  126.0 15.6 %collective-permute-start.18 = (bf16[256,1024]{1,0:T(8,128)(2,1)S(1)}, bf16[256,1024]{1,0:T(8,128)(2,1)S(1)}, u32[]{:S(2)}, u32[]{:S(2)}) collective-permute-start(bf16[256,1024]{1,0:T(8,128)(2,1)S(1)} %shard_map.83), channel_id=1, source_target_pairs={{0,8},{8,16},{16,24},{1,9},{9,17},{17,25},{2,10},{10,18},{18,26},{... | collective-permute-start | bytes 1572872 | tf_op jit(solution)/shard_map/ppermute | solution.py:348

commit v5 on v4

--- a/solution.py
+++ b/solution.py
@@ -13,6 +13,7 @@
 CAPACITY = 3
 EPSILON = 1e-05
 MIB = 1024 * 1024
+MICROSECOND = 1150000000
 NT = (((1,), (1,)), ((), ()))
 NN = (((1,), (0,)), ((), ()))
 TN = (((0,), (0,)), ((), ()))
@@ -182,23 +183,30 @@
         [SMEM, SMEM] + [VMEM] * (len(operands) - 2) + [HBM] * len(earlier),
         jax.ShapeDtypeStruct((tiles, TILE, wide), jnp.bfloat16),
         scratch,
-        2 * tokens * width * 3 * HD + tokens * 512 * HD * (14 if back else 4),
+        MICROSECOND * (12 if back else 8),
         2 * tokens * (width + 2 * wide),
     )
     return out.reshape(HEADS, 2 * TILE, wide)
 
 
-def nothing(*refs):
-    pass
-
-
-def gate(arrays, earlier):
+def copy_kernel(starts, *refs):
+    count = len(starts)
+    outs, sems = refs[-count - 1 : -1], refs[-1]
+    copies = [
+        fetch(refs[i].at[pl.ds(start, outs[i].shape[0])], outs[i], sems.at[i])
+        for i, start in enumerate(starts)
+    ]
+    for copy in copies:
+        copy.wait()
+
+
+def rows_after(arrays, starts, rows, earlier):
     return pl.pallas_call(
-        nothing,
+        functools.partial(copy_kernel, starts),
         in_specs=[HBM] * (len(arrays) + len(earlier)),
         out_specs=[HBM] * len(arrays),
-        out_shape=[jax.ShapeDtypeStruct(a.shape, a.dtype) for a in arrays],
-        input_output_aliases={i: i for i in range(len(arrays))},
+        out_shape=[jax.ShapeDtypeStruct((rows, *a.shape[1:]), a.dtype) for a in arrays],
+        scratch_shapes=[pltpu.SemaphoreType.DMA((len(arrays),))],
     )(*arrays, *earlier)
 
 
@@ -242,7 +250,7 @@
             pltpu.VMEM((HEADS, HD, width), jnp.bfloat16),
             pltpu.SemaphoreType.DMA((HEADS,)),
         ],
-        2 * tokens * width * HEADS * HD,
+        MICROSECOND * 3,
         2 * width * HEADS * HD,
     )
 
@@ -304,12 +312,11 @@
     return lax.ppermute(block, "seq", route)
 
 
-def gather_rows(x, earlier=()):
+def gather_rows(x, earlier):
     half = x.shape[0] // 2
     over_x, over_y = partner(x, 2), partner(x, 4)
-    if earlier:
-        over_x, over_y = gate([over_x, over_y], earlier)
-    top, bottom = partner(over_x[:half], 4), partner(over_y[half:], 2)
+    top, bottom = rows_after([over_x, over_y], [0, half], half, earlier)
+    top, bottom = partner(top, 4), partner(bottom, 2)
     pieces = [(0, 0, x), (2, 0, over_x), (4, 0, over_y), (6, 0, top), (6, half, bottom)]
     return pieces + [(k + 1, start, partner(block, 1)) for k, start, block in pieces]
 
@@ -360,7 +367,7 @@
     else:
         info = jnp.stack([jnp.zeros_like(own), own // spacing, own % spacing])
 
-        def gather(x, earlier=()):
+        def gather(x, earlier):
             copies = jnp.broadcast_to(x, (HEADS, *x.shape))
             return [(k, 0, block) for k, block in enumerate(to_heads(copies, own, spacing))]
 
@@ -373,17 +380,21 @@
     own_head = w_rows.reshape(3, HEADS, HD, -1)
     own_head = lax.dynamic_index_in_dim(own_head, info[1], 1, keepdims=False)
     own_head = own_head.reshape(3 * HD, -1)
-    stored_pieces = gather(stored)
-    grad_attention = spread(spread_grads(upstream, w_fin))
+    spreading = spread_grads(upstream, w_fin)
+    stored_pieces = gather(stored, [spreading])
+    grad_attention = spread(spreading)
     earlier = [block for k, _, block in stored_pieces if k == HEADS - 2]
     normed = norm_after(current, [*earlier, grad_attention])
-    grads = head_work(info, tile_cluster, stored_pieces, own_head, spacing, grad_attention)
+    grads = head_work(
+        info, tile_cluster, stored_pieces, own_head, spacing, grad_attention, [normed]
+    )
     current_pieces = gather(normed, [grads])
     returned_grads = collect(grads)
     outputs = head_work(
-        info, tile_cluster, current_pieces, own_head, spacing, earlier=(grads,)
-    )
-    returned = collect(gate([outputs], [returned_grads])[0])
+        info, tile_cluster, current_pieces, own_head, spacing, earlier=[grads]
+    )
+    outputs = rows_after([outputs], [0], HEADS, [returned_grads])[0]
+    returned = collect(outputs)
     grad_self = finish_back(returned_grads, stored, upstream, w_rows)
     grad_input = passed_along(grad_self, "pipe", -1)
     result = finish(returned, current, w_fin)

time: 145 us -> 164 us (1.13)
  Pallas kernels: 26.7 us -> 77.5 us
  waiting for transfers between devices: 63.9 us -> 35 us
  local copies, waits for them, and re-layouts: 20.4 us -> 17.9 us
    pallas_call x2 -> x3, Pallas kernels: 0.01 us -> 51 us  [rows_after(): pl.pallas_call(functools.partial(copy_kernel, starts), in_specs=[HBM] * (...]
    ppermute x18, waiting for transfers between devices: 45.4 us -> 11.5 us  [partner(): return lax.ppermute(block, 'seq', route)]
    all_to_all x3, waiting for transfers between devices: 6.45 us -> 12.2 us  [all_swap(): lax.all_to_all(blocks, 'seq', split_axis=0, concat_axis=0, tiled=True)]
    slice x4 -> x0, local copies, waits for them, and re-layouts: 1.97 us -> none  [gather_rows(): top, bottom = (partner(over_x[:half], 4), partner(over_y[half:], 2))]
    unnamed x44 -> x36, local copies, waits for them, and re-layouts: 17.3 us -> 16.7 us
  transfers between devices with their start and end apart: 23 -> 23, of which waited for: 10 -> 9; matrix products, arithmetic and copies ran while one was open for 2% -> 1% of each run, Pallas kernels for 10% -> 37%
where the time goes in v5:
time: 164 us; the launch traced here: 163 us
  Pallas kernels  77.5 us (47%)
  waiting for transfers between devices  35 us (21%)
  starting transfers between devices  31.3 us (19%)
  local copies, waits for them, and re-layouts  17.9 us (11%)
    pallas_call x3, Pallas kernels, rows_after(): pl.pallas_call(functools.partial(copy_kernel, starts), in_specs=[HBM] * (...  51 us
    pallas_call x6, Pallas kernels, call(): pl.pallas_call(kernel, in_specs=in_specs, out_specs=VMEM, out_shape=out_s...  26.5 us
    unnamed x36, local copies, waits for them, and re-layouts  16.7 us
    all_to_all x3, starting transfers between devices, all_swap(): lax.all_to_all(blocks, 'seq', split_axis=0, concat_axis=0, tiled=True)  14.3 us
    all_to_all x3, waiting for transfers between devices, all_swap(): lax.all_to_all(blocks, 'seq', split_axis=0, concat_axis=0, tiled=True)  12.2 us
    ppermute x18, waiting for transfers between devices, partner(): return lax.ppermute(block, 'seq', route)  11.5 us
    ppermute x2, waiting for transfers between devices, passed_along(): return lax.ppermute(block, axis, route)  11.3 us
    ppermute x18, starting transfers between devices, partner(): return lax.ppermute(block, 'seq', route)  10.3 us
  transfers between devices with their start and end apart: 23, of which 9 were waited for; matrix products, arithmetic and copies ran while one was open for 1% of the time, Pallas kernels for 37%

profile of v5, /device:TPU:18, one launch (start us, length us, event | category | flops | bytes accessed | tf_op | source)
XLA Modules:
  0.0 162.5 jit_solution(1680732561145644700)
XLA Ops:
  0.6 0.6 collective-permute-start
  1.2 1.5 collective-permute-start.1
  2.8 1.6 copy-done.3
  4.3 1.0 copy-done.9
  5.4 2.1 %shard_map.77.refs_2_ = bf16[8,256,128]{2,1,0:T(8,128)(2,1)S(1)} custom-call(bf16[256,1024]{1,0:T(8,128)(2,1)S(1)} %bitcast.30, bf16[8,128,1024]{2,1,0:T(8,128)(2,1)S(1)} %bitcast.18), custom_call_target="tpu_custom_call" | custom-call | flops 3449999872 | bytes 2097152 | tf_op jit(solution)/shard_map/pallas_call | solution.py:42
  7.5 0.8 copy-done.5
  8.3 6.3 %collective-permute-done.refs_0_.refs_4_ = bf16[256,1024]{1,0:T(8,128)(2,1)S(1)} collective-permute-done((bf16[256,1024]{1,0:T(8,128)(2,1)}, bf16[256,1024]{1,0:T(8,128)(2,1)S(1)}, u32[]{:S(2)}, u32[]{:S(2)}) %collective-permute-start) | collective-permute-done | bytes 524320 | tf_op jit(solution)/shard_map/ppermute | solution.py:312
  14.8 0.5 copy-done.11
  15.4 0.8 copy-done.13
  16.2 17.0 %shard_map.78 = (bf16[128,1024]{1,0:T(8,128)(2,1)}, bf16[128,1024]{1,0:T(8,128)(2,1)}) custom-call(bf16[256,1024]{1,0:T(8,128)(2,1)} %copy-done.11, bf16[256,1024]{1,0:T(8,128)(2,1)} %copy-done.13, bf16[8,256,128]{2,1,0:T(8,128)(2,1)} %copy-done.5), custom_call_target="tpu_custom_call" | custom-call | tf_op jit(solution)/shard_map/pallas_call | solution.py:204
  33.2 1.0 collective-permute-start.3
  34.2 1.5 collective-permute-start.2
  35.7 0.5 collective-permute-start.8
  36.2 4.5 %all-to-all-start = ((bf16[8,256,128]{2,1,0:T(8,128)(2,1)}), bf16[8,256,128]{2,1,0:T(8,128)(2,1)S(1)}, u32[]{:S(2)}, u32[]{:S(2)}) async-start(bf16[8,256,128]{2,1,0:T(8,128)(2,1)} %copy-done.5), calls=%async_computation | async-start | bytes 1048576 | tf_op jit(solution)/shard_map/all_to_all | solution.py:325
  41.0 0.3 collective-permute-start.9
  41.4 1.2 constant_dynamic-slice_fusion
  42.6 6.4 %all-to-all-done.refs_2_ = bf16[8,256,128]{2,1,0:T(8,128)(2,1)S(1)} async-done(((bf16[8,256,128]{2,1,0:T(8,128)(2,1)}), bf16[8,256,128]{2,1,0:T(8,128)(2,1)S(1)}, u32[]{:S(2)}, u32[]{:S(2)}) %all-to-all-start) | async-done | bytes 524320 | tf_op jit(solution)/shard_map/all_to_all | solution.py:325
  49.0 1.0 shard_map.79.refs_14_.refs_3_
  50.0 1.5 collective-permute-start.4
  51.5 0.5 collective-permute-start.5
  52.1 1.0 copy-done.14
  53.1 11.7 %shard_map.80 = bf16[16,128,384]{2,1,0:T(8,128)(2,1)} custom-call(s32[16]{0:T(128)S(1)} %copy-done.16, s32[3]{0:T(128)S(1)} %pad_add_fusion.refs_1_, bf16[384,1024]{1,0:T(8,128)(2,1)S(1)} %bitcast.23, bf16[256,1024]{1,0:T(8,128)(2,1)S(1)} %bitcast.28, bf16[256,1024]{1,0:T(8,128)(2,1)S(1)} %copy-done.12, bf16[256,1024]{1,0:T(8,128)(2,1)S(1)} %copy-done.14, ...), custom_call_target="tpu_custom_call" | custom-call | flops 13799999488 | bytes 7340032 | tf_op jit(solution)/shard_map/pallas_call | solution.py:42
  64.8 17.0 %shard_map.81 = (bf16[128,1024]{1,0:T(8,128)(2,1)}, bf16[128,1024]{1,0:T(8,128)(2,1)}) custom-call(bf16[256,1024]{1,0:T(8,128)(2,1)} %collective-permute-done.4.refs_0_.refs_4_, bf16[256,1024]{1,0:T(8,128)(2,1)} %collective-permute-done.5.refs_1_.refs_5_, bf16[8,256,384]{2,1,0:T(8,128)(2,1)} %bitcast.8.refs_2_.refs_13_), custom_call_target="tpu_custom_call" | custom-call | tf_op jit(solution)/shard_map/pallas_call | solution.py:204
  81.8 1.5 collective-permute-start.11
  83.4 0.6 collective-permute-start.12
  83.9 0.5 collective-permute-start.15
  84.4 5.0 %all-to-all-start.1 = ((bf16[8,256,384]{2,1,0:T(8,128)(2,1)}), bf16[8,256,384]{2,1,0:T(8,128)(2,1)S(1)}, u32[]{:S(2)}, u32[]{:S(2)}) async-start(bf16[8,256,384]{2,1,0:T(8,128)(2,1)} %bitcast.8.refs_2_.refs_13_), calls=%async_computation.1 | async-start | bytes 3145728 | tf_op jit(solution)/shard_map/all_to_all | solution.py:325
  89.4 1.4 collective-permute-done.11.refs_6_
  90.8 1.9 %collective-permute-done.12.refs_7_ = bf16[128,1024]{1,0:T(8,128)(2,1)S(1)} collective-permute-done((bf16[128,1024]{1,0:T(8,128)(2,1)}, bf16[128,1024]{1,0:T(8,128)(2,1)S(1)}, u32[]{:S(2)}, u32[]{:S(2)}) %collective-permute-start.12) | collective-permute-done | bytes 262176 | tf_op jit(solution)/shard_map/ppermute | solution.py:312
  92.7 1.5 collective-permute-done.17.refs_12_
  94.3 8.2 %shard_map.82 = bf16[16,128,128]{2,1,0:T(8,128)(2,1)S(1)} custom-call(s32[16]{0:T(128)S(1)} %copy-done.16, s32[3]{0:T(128)S(1)} %pad_add_fusion.refs_1_, bf16[384,1024]{1,0:T(8,128)(2,1)S(1)} %bitcast.24, bf16[256,1024]{1,0:T(8,128)(2,1)} %shard_map.79.refs_14_.refs_3_, bf16[256,1024]{1,0:T(8,128)(2,1)} %collective-permute-done.4.refs_0_.refs_4_, ...), custom_call_target="tpu_custom_call" | custom-call | flops 9200000000 | bytes 5242880 | tf_op jit(solution)/shard_map/pallas_call | solution.py:42
  102.4 0.8 copy-done.15
  103.2 5.7 %all-to-all-done.1.refs_1_.grad_ref = bf16[8,256,384]{2,1,0:T(8,128)(2,1)S(1)} async-done(((bf16[8,256,384]{2,1,0:T(8,128)(2,1)}), bf16[8,256,384]{2,1,0:T(8,128)(2,1)S(1)}, u32[]{:S(2)}, u32[]{:S(2)}) %all-to-all-start.1) | async-done | bytes 1572896 | tf_op jit(solution)/shard_map/all_to_all | solution.py:325
  109.0 1.2 copy-done
  110.1 17.0 %shard_map.83 = bf16[8,256,128]{2,1,0:T(8,128)(2,1)} custom-call(bf16[8,256,128]{2,1,0:T(8,128)(2,1)} %bitcast.32, bf16[8,256,384]{2,1,0:T(8,128)(2,1)} %copy-done), custom_call_target="tpu_custom_call" | custom-call | tf_op jit(solution)/shard_map/pallas_call | solution.py:204
  127.1 4.9 %all-to-all-start.2 = ((bf16[8,256,128]{2,1,0:T(8,128)(2,1)}), bf16[8,256,128]{2,1,0:T(8,128)(2,1)S(1)}, u32[]{:S(2)}, u32[]{:S(2)}) async-start(bf16[8,256,128]{2,1,0:T(8,128)(2,1)} %shard_map.83), calls=%async_computation.2 | async-start | bytes 1048576 | tf_op jit(solution)/shard_map/all_to_all | solution.py:325
  132.0 1.4 copy-done.1
  133.5 2.8 %copy-done.2 = bf16[1,3072,1024]{2,1,0:T(8,128)(2,1)S(1)} copy-done((bf16[1,3072,1024]{2,1,0:T(8,128)(2,1)S(1)}, bf16[1,3072,1024]{2,1,0:T(8,128)(2,1)}, u32[]{:S(2)}) %copy-start.2) | copy-done | bytes 6291480
  136.2 1.0 copy-done.8
  137.3 1.0 copy-done.10
  138.3 2.8 %shard_map.85 = bf16[256,1024]{1,0:T(8,128)(2,1)} custom-call(bf16[8,256,384]{2,1,0:T(8,128)(2,1)S(1)} %copy-done.1, bf16[256,1024]{1,0:T(8,128)(2,1)S(1)} %bitcast.29, bf16[256,1024]{1,0:T(8,128)(2,1)S(1)} %bitcast.31, bf16[3072,1024]{1,0:T(8,128)(2,1)S(1)} %bitcast.17), custom_call_target="tpu_custom_call" | custom-call | flops 1610612736 | bytes 6291456 | tf_op jit(solution)/shard_map/pallas_call | solution.py:42
  141.2 2.4 %collective-permute-start.19 = (bf16[256,1024]{1,0:T(8,128)(2,1)}, bf16[256,1024]{1,0:T(8,128)(2,1)}, u32[]{:S(2)}, u32[]{:S(2)}) collective-permute-start(bf16[256,1024]{1,0:T(8,128)(2,1)} %shard_map.85), channel_id=1, source_target_pairs={{8,0},{16,8},{24,16},{9,1},{17,9},{25,17},{10,2},{18,10},{26,18},{... | collective-permute-start | bytes 1572872 | tf_op jit(solution)/shard_map/ppermute | solution.py:355
  143.5 0.7 shard_map.84
  144.3 4.3 %collective-permute-start.18 = (bf16[256,1024]{1,0:T(8,128)(2,1)S(1)}, bf16[256,1024]{1,0:T(8,128)(2,1)S(1)}, u32[]{:S(2)}, u32[]{:S(2)}) collective-permute-start(bf16[256,1024]{1,0:T(8,128)(2,1)S(1)} %shard_map.84), channel_id=1, source_target_pairs={{0,8},{8,16},{16,24},{1,9},{9,17},{17,25},{2,10},{10,18},{18,26},{... | collective-permute-start | bytes 1572872 | tf_op jit(solution)/shard_map/ppermute | solution.py:355
  148.5 8.8 %collective-permute-done.19 = bf16[256,1024]{1,0:T(8,128)(2,1)} collective-permute-done((bf16[256,1024]{1,0:T(8,128)(2,1)}, bf16[256,1024]{1,0:T(8,128)(2,1)}, u32[]{:S(2)}, u32[]{:S(2)}) %collective-permute-start.19) | collective-permute-done | bytes 524320 | tf_op jit(solution)/shard_map/ppermute | solution.py:355
  157.3 2.5 %collective-permute-done.18 = bf16[256,1024]{1,0:T(8,128)(2,1)S(1)} collective-permute-done((bf16[256,1024]{1,0:T(8,128)(2,1)S(1)}, bf16[256,1024]{1,0:T(8,128)(2,1)S(1)}, u32[]{:S(2)}, u32[]{:S(2)}) %collective-permute-start.18) | collective-permute-done | bytes 524320 | tf_op jit(solution)/shard_map/ppermute | solution.py:355
  159.9 0.8 copy.12
  160.6 1.9 %copy.13 = bf16[1,256,1024]{2,1,0:T(8,128)(2,1)} copy(bf16[1,256,1024]{2,1,0:T(8,128)(2,1)} %bitcast.13) | data formatting | bytes 1048576
  (45 shorter events, 0.7 us)
Async XLA Ops:
  0.6 13.9 %collective-permute-start = (bf16[256,1024]{1,0:T(8,128)(2,1)}, bf16[256,1024]{1,0:T(8,128)(2,1)S(1)}, u32[]{:S(2)}, u32[]{:S(2)}) collective-permute-start(bf16[256,1024]{1,0:T(8,128)(2,1)} %bitcast.25), channel_id=1, source_target_pairs={{0,2},{1,3},{2,0},{3,1},{4,6},{5,7},{6,4},{7,5},{8,10},{9,11},{10,... | collective-permute-start | bytes 1572872 | tf_op jit(solution)/shard_map/ppermute | solution.py:312
  1.2 13.6 %collective-permute-start.1 = (bf16[256,1024]{1,0:T(8,128)(2,1)}, bf16[256,1024]{1,0:T(8,128)(2,1)S(1)}, u32[]{:S(2)}, u32[]{:S(2)}) collective-permute-start(bf16[256,1024]{1,0:T(8,128)(2,1)} %bitcast.26), channel_id=1, source_target_pairs={{0,4},{1,5},{2,6},{3,7},{4,0},{5,1},{6,2},{7,3},{8,12},{9,13},{10,... | collective-permute-start | bytes 1572872 | tf_op jit(solution)/shard_map/ppermute | solution.py:312
  2.7 47.2 %collective-permute-start.6 = (bf16[256,1024]{1,0:T(8,128)(2,1)}, bf16[256,1024]{1,0:T(8,128)(2,1)}, u32[]{:S(2)}, u32[]{:S(2)}) collective-permute-start(bf16[256,1024]{1,0:T(8,128)(2,1)} %bitcast.27), channel_id=1, source_target_pairs={{0,1},{1,0},{2,3},{3,2},{4,5},{5,4},{6,7},{7,6},{8,9},{9,8},{10,11... | collective-permute-start | bytes 1572872 | tf_op jit(solution)/shard_map/ppermute | solution.py:312
  2.8 1.6 copy-start.3
  4.3 1.0 copy-start.9
  7.5 0.8 copy-start.5
  8.3 40.7 %copy-start.6 = (bf16[1,256,1024]{2,1,0:T(8,128)(2,1)S(1)}, bf16[1,256,1024]{2,1,0:T(8,128)(2,1)}, u32[]{:S(2)}) copy-start(bf16[1,256,1024]{2,1,0:T(8,128)(2,1)} %param.6) | copy-start | bytes 1572868
  14.6 0.8 copy-start.11
  15.4 0.8 copy-start.13
  33.2 7.5 %collective-permute-start.3 = (bf16[128,1024]{1,0:T(8,128)(2,1)}, bf16[128,1024]{1,0:T(8,128)(2,1)S(1)}, u32[]{:S(2)}, u32[]{:S(2)}) collective-permute-start(bf16[128,1024]{1,0:T(8,128)(2,1)} %get-tuple-element.7), channel_id=1, source_target_pairs={{0,2},{1,3},{2,0},{3,1},{4,6},{5,7},{6,4},{7,5},{8,10},{9,11},{10,... | collective-permute-start | bytes 786440 | tf_op jit(solution)/shard_map/ppermute | solution.py:312
  34.2 6.8 %collective-permute-start.2 = (bf16[128,1024]{1,0:T(8,128)(2,1)}, bf16[128,1024]{1,0:T(8,128)(2,1)S(1)}, u32[]{:S(2)}, u32[]{:S(2)}) collective-permute-start(bf16[128,1024]{1,0:T(8,128)(2,1)} %get-tuple-element.6), channel_id=1, source_target_pairs={{0,4},{1,5},{2,6},{3,7},{4,0},{5,1},{6,2},{7,3},{8,12},{9,13},{10,... | collective-permute-start | bytes 786440 | tf_op jit(solution)/shard_map/ppermute | solution.py:312
  35.7 16.3 %collective-permute-start.7 = (bf16[256,1024]{1,0:T(8,128)(2,1)}, bf16[256,1024]{1,0:T(8,128)(2,1)}, u32[]{:S(2)}, u32[]{:S(2)}) collective-permute-start(bf16[256,1024]{1,0:T(8,128)(2,1)} %copy-done.11), channel_id=1, source_target_pairs={{0,1},{1,0},{2,3},{3,2},{4,5},{5,4},{6,7},{7,6},{8,9},{9,8},{10,11... | collective-permute-start | bytes 1572872 | tf_op jit(solution)/shard_map/ppermute | solution.py:312
  35.7 16.3 %collective-permute-start.8 = (bf16[256,1024]{1,0:T(8,128)(2,1)}, bf16[256,1024]{1,0:T(8,128)(2,1)}, u32[]{:S(2)}, u32[]{:S(2)}) collective-permute-start(bf16[256,1024]{1,0:T(8,128)(2,1)} %copy-done.13), channel_id=1, source_target_pairs={{0,1},{1,0},{2,3},{3,2},{4,5},{5,4},{6,7},{7,6},{8,9},{9,8},{10,11... | collective-permute-start | bytes 1572872 | tf_op jit(solution)/shard_map/ppermute | solution.py:312
  36.2 12.8 %all-to-all-start = ((bf16[8,256,128]{2,1,0:T(8,128)(2,1)}), bf16[8,256,128]{2,1,0:T(8,128)(2,1)S(1)}, u32[]{:S(2)}, u32[]{:S(2)}) async-start(bf16[8,256,128]{2,1,0:T(8,128)(2,1)} %copy-done.5), calls=%async_computation | async-start | bytes 1048576 | tf_op jit(solution)/shard_map/all_to_all | solution.py:325
  40.7 11.3 %copy-start.7 = (bf16[1,256,1024]{2,1,0:T(8,128)(2,1)S(1)}, bf16[1,256,1024]{2,1,0:T(8,128)(2,1)}, u32[]{:S(2)}) copy-start(bf16[1,256,1024]{2,1,0:T(8,128)(2,1)} %param.7) | copy-start | bytes 1572868
  40.7 11.3 %copy-start.12 = (bf16[256,1024]{1,0:T(8,128)(2,1)S(1)}, bf16[256,1024]{1,0:T(8,128)(2,1)}, u32[]{:S(2)}) copy-start(bf16[256,1024]{1,0:T(8,128)(2,1)} %copy-done.11) | copy-start | bytes 1572868
  40.7 11.3 %copy-start.16 = (s32[16]{0:T(128)S(1)}, s32[16]{0:T(128)}, u32[]{:S(2)}) copy-start(s32[16]{0:T(128)} %refs_0_.3) | copy-start | bytes 196
  40.7 10.7 %collective-permute-start.10 = (bf16[128,1024]{1,0:T(8,128)(2,1)S(1)}, bf16[128,1024]{1,0:T(8,128)(2,1)}, u32[]{:S(2)}, u32[]{:S(2)}) collective-permute-start(bf16[128,1024]{1,0:T(8,128)(2,1)S(1)} %collective-permute-done.3.refs_1_.refs_7_), channel_id=1, source_target_pairs={{0,1},{1,0},{2,3},{3,2},{4,5},{5,4},{6,7},{7,6},{8,9},{9,8},{10,11... | collective-permute-start | bytes 786440 | tf_op jit(solution)/shard_map/ppermute | solution.py:312
  41.0 11.0 %collective-permute-start.9 = (bf16[128,1024]{1,0:T(8,128)(2,1)S(1)}, bf16[128,1024]{1,0:T(8,128)(2,1)}, u32[]{:S(2)}, u32[]{:S(2)}) collective-permute-start(bf16[128,1024]{1,0:T(8,128)(2,1)S(1)} %collective-permute-done.2.refs_0_.refs_6_), channel_id=1, source_target_pairs={{0,1},{1,0},{2,3},{3,2},{4,5},{5,4},{6,7},{7,6},{8,9},{9,8},{10,11... | collective-permute-start | bytes 786440 | tf_op jit(solution)/shard_map/ppermute | solution.py:312
  50.0 14.8 %collective-permute-start.4 = (bf16[256,1024]{1,0:T(8,128)(2,1)}, bf16[256,1024]{1,0:T(8,128)(2,1)}, u32[]{:S(2)}, u32[]{:S(2)}) collective-permute-start(bf16[256,1024]{1,0:T(8,128)(2,1)} %shard_map.79.refs_14_.refs_3_), channel_id=1, source_target_pairs={{0,2},{1,3},{2,0},{3,1},{4,6},{5,7},{6,4},{7,5},{8,10},{9,11},{10,... | collective-permute-start | bytes 1572872 | tf_op jit(solution)/shard_map/ppermute | solution.py:312
  51.5 13.4 %collective-permute-start.5 = (bf16[256,1024]{1,0:T(8,128)(2,1)}, bf16[256,1024]{1,0:T(8,128)(2,1)}, u32[]{:S(2)}, u32[]{:S(2)}) collective-permute-start(bf16[256,1024]{1,0:T(8,128)(2,1)} %shard_map.79.refs_14_.refs_3_), channel_id=1, source_target_pairs={{0,4},{1,5},{2,6},{3,7},{4,0},{5,1},{6,2},{7,3},{8,12},{9,13},{10,... | collective-permute-start | bytes 1572872 | tf_op jit(solution)/shard_map/ppermute | solution.py:312
  52.0 40.7 %collective-permute-start.13 = (bf16[256,1024]{1,0:T(8,128)(2,1)}, bf16[256,1024]{1,0:T(8,128)(2,1)}, u32[]{:S(2)}, u32[]{:S(2)}) collective-permute-start(bf16[256,1024]{1,0:T(8,128)(2,1)} %shard_map.79.refs_14_.refs_3_), channel_id=1, source_target_pairs={{0,1},{1,0},{2,3},{3,2},{4,5},{5,4},{6,7},{7,6},{8,9},{9,8},{10,11... | collective-permute-start | bytes 1572872 | tf_op jit(solution)/shard_map/ppermute | solution.py:312
  52.0 1.0 copy-start.14
  81.8 9.0 %collective-permute-start.11 = (bf16[128,1024]{1,0:T(8,128)(2,1)}, bf16[128,1024]{1,0:T(8,128)(2,1)S(1)}, u32[]{:S(2)}, u32[]{:S(2)}) collective-permute-start(bf16[128,1024]{1,0:T(8,128)(2,1)} %get-tuple-element.8), channel_id=1, source_target_pairs={{0,4},{1,5},{2,6},{3,7},{4,0},{5,1},{6,2},{7,3},{8,12},{9,13},{10,... | collective-permute-start | bytes 786440 | tf_op jit(solution)/shard_map/ppermute | solution.py:312
  83.4 9.3 %collective-permute-start.12 = (bf16[128,1024]{1,0:T(8,128)(2,1)}, bf16[128,1024]{1,0:T(8,128)(2,1)S(1)}, u32[]{:S(2)}, u32[]{:S(2)}) collective-permute-start(bf16[128,1024]{1,0:T(8,128)(2,1)} %get-tuple-element.9), channel_id=1, source_target_pairs={{0,2},{1,3},{2,0},{3,1},{4,6},{5,7},{6,4},{7,5},{8,10},{9,11},{10,... | collective-permute-start | bytes 786440 | tf_op jit(solution)/shard_map/ppermute | solution.py:312
  83.9 10.3 %collective-permute-start.14 = (bf16[256,1024]{1,0:T(8,128)(2,1)}, bf16[256,1024]{1,0:T(8,128)(2,1)}, u32[]{:S(2)}, u32[]{:S(2)}) collective-permute-start(bf16[256,1024]{1,0:T(8,128)(2,1)} %collective-permute-done.4.refs_0_.refs_4_), channel_id=1, source_target_pairs={{0,1},{1,0},{2,3},{3,2},{4,5},{5,4},{6,7},{7,6},{8,9},{9,8},{10,11... | collective-permute-start | bytes 1572872 | tf_op jit(solution)/shard_map/ppermute | solution.py:312
  83.9 10.3 %collective-permute-start.15 = (bf16[256,1024]{1,0:T(8,128)(2,1)}, bf16[256,1024]{1,0:T(8,128)(2,1)}, u32[]{:S(2)}, u32[]{:S(2)}) collective-permute-start(bf16[256,1024]{1,0:T(8,128)(2,1)} %collective-permute-done.5.refs_1_.refs_5_), channel_id=1, source_target_pairs={{0,1},{1,0},{2,3},{3,2},{4,5},{5,4},{6,7},{7,6},{8,9},{9,8},{10,11... | collective-permute-start | bytes 1572872 | tf_op jit(solution)/shard_map/ppermute | solution.py:312
  84.4 24.5 %all-to-all-start.1 = ((bf16[8,256,384]{2,1,0:T(8,128)(2,1)}), bf16[8,256,384]{2,1,0:T(8,128)(2,1)S(1)}, u32[]{:S(2)}, u32[]{:S(2)}) async-start(bf16[8,256,384]{2,1,0:T(8,128)(2,1)} %bitcast.8.refs_2_.refs_13_), calls=%async_computation.1 | async-start | bytes 3145728 | tf_op jit(solution)/shard_map/all_to_all | solution.py:325
  90.8 1.9 %collective-permute-start.16 = (bf16[128,1024]{1,0:T(8,128)(2,1)S(1)}, bf16[128,1024]{1,0:T(8,128)(2,1)S(1)}, u32[]{:S(2)}, u32[]{:S(2)}) collective-permute-start(bf16[128,1024]{1,0:T(8,128)(2,1)S(1)} %collective-permute-done.11.refs_6_), channel_id=1, source_target_pairs={{0,1},{1,0},{2,3},{3,2},{4,5},{5,4},{6,7},{7,6},{8,9},{9,8},{10,11... | collective-permute-start | bytes 786440 | tf_op jit(solution)/shard_map/ppermute | solution.py:312
  92.7 1.5 collective-permute-start.17
  102.4 0.8 copy-start.15
  109.0 1.2 copy-start
  127.1 16.4 %all-to-all-start.2 = ((bf16[8,256,128]{2,1,0:T(8,128)(2,1)}), bf16[8,256,128]{2,1,0:T(8,128)(2,1)S(1)}, u32[]{:S(2)}, u32[]{:S(2)}) async-start(bf16[8,256,128]{2,1,0:T(8,128)(2,1)} %shard_map.83), calls=%async_computation.2 | async-start | bytes 1048576 | tf_op jit(solution)/shard_map/all_to_all | solution.py:325
  132.0 1.4 copy-start.1
  133.5 2.8 %copy-start.2 = (bf16[1,3072,1024]{2,1,0:T(8,128)(2,1)S(1)}, bf16[1,3072,1024]{2,1,0:T(8,128)(2,1)}, u32[]{:S(2)}) copy-start(bf16[1,3072,1024]{2,1,0:T(8,128)(2,1)} %param.9) | copy-start | bytes 18874372
  136.2 1.0 copy-start.8
  137.3 1.0 copy-start.10
  138.3 5.2 %copy-start.4 = (bf16[1,1024,1024]{2,1,0:T(8,128)(2,1)S(1)}, bf16[1,1024,1024]{2,1,0:T(8,128)(2,1)}, u32[]{:S(2)}) copy-start(bf16[1,1024,1024]{2,1,0:T(8,128)(2,1)} %param.10) | copy-start | bytes 6291460
  141.2 16.2 %collective-permute-start.19 = (bf16[256,1024]{1,0:T(8,128)(2,1)}, bf16[256,1024]{1,0:T(8,128)(2,1)}, u32[]{:S(2)}, u32[]{:S(2)}) collective-permute-start(bf16[256,1024]{1,0:T(8,128)(2,1)} %shard_map.85), channel_id=1, source_target_pairs={{8,0},{16,8},{24,16},{9,1},{17,9},{25,17},{10,2},{18,10},{26,18},{... | collective-permute-start | bytes 1572872 | tf_op jit(solution)/shard_map/ppermute | solution.py:355
  144.3 15.6 %collective-permute-start.18 = (bf16[256,1024]{1,0:T(8,128)(2,1)S(1)}, bf16[256,1024]{1,0:T(8,128)(2,1)S(1)}, u32[]{:S(2)}, u32[]{:S(2)}) collective-permute-start(bf16[256,1024]{1,0:T(8,128)(2,1)S(1)} %shard_map.84), channel_id=1, source_target_pairs={{0,8},{8,16},{16,24},{1,9},{9,17},{17,25},{2,10},{10,18},{18,26},{... | collective-permute-start | bytes 1572872 | tf_op jit(solution)/shard_map/ppermute | solution.py:355

commit v6 on v5

--- a/solution.py
+++ b/solution.py
@@ -204,7 +204,7 @@
     return pl.pallas_call(
         functools.partial(copy_kernel, starts),
         in_specs=[HBM] * (len(arrays) + len(earlier)),
-        out_specs=[HBM] * len(arrays),
+        out_specs=[VMEM] * len(arrays),
         out_shape=[jax.ShapeDtypeStruct((rows, *a.shape[1:]), a.dtype) for a in arrays],
         scratch_shapes=[pltpu.SemaphoreType.DMA((len(arrays),))],
     )(*arrays, *earlier)

time: 164 us -> 119 us (0.73)
  Pallas kernels: 77.5 us -> 32.2 us
    pallas_call x3, Pallas kernels: 51 us -> 5.54 us  [rows_after(): pl.pallas_call(functools.partial(copy_kernel, starts), in_specs=[HBM] * (...]
  transfers between devices with their start and end apart: 23 -> 23, of which waited for: 9 -> 9; matrix products, arithmetic and copies ran while one was open for 1% -> 1% of each run, Pallas kernels for 37% -> 26%
where the time goes in v6:
time: 119 us; the launch traced here: 117 us
  waiting for transfers between devices  34.9 us (29%)
  Pallas kernels  32.2 us (27%)
  starting transfers between devices  31.3 us (26%)
  local copies, waits for them, and re-layouts  17.9 us (15%)
    pallas_call x6, Pallas kernels, call(): pl.pallas_call(kernel, in_specs=in_specs, out_specs=VMEM, out_shape=out_s...  26.7 us
    unnamed x36, local copies, waits for them, and re-layouts  16.7 us
    all_to_all x3, starting transfers between devices, all_swap(): lax.all_to_all(blocks, 'seq', split_axis=0, concat_axis=0, tiled=True)  14.3 us
    all_to_all x3, waiting for transfers between devices, all_swap(): lax.all_to_all(blocks, 'seq', split_axis=0, concat_axis=0, tiled=True)  12 us
    ppermute x18, waiting for transfers between devices, partner(): return lax.ppermute(block, 'seq', route)  11.5 us
    ppermute x2, waiting for transfers between devices, passed_along(): return lax.ppermute(block, axis, route)  11.3 us
    ppermute x18, starting transfers between devices, partner(): return lax.ppermute(block, 'seq', route)  10.3 us
    ppermute x2, starting transfers between devices, passed_along(): return lax.ppermute(block, axis, route)  6.61 us
  transfers between devices with their start and end apart: 23, of which 9 were waited for; matrix products, arithmetic and copies ran while one was open for 1% of the time, Pallas kernels for 26%

profile of v6, /device:TPU:18, one launch (start us, length us, event | category | flops | bytes accessed | tf_op | source)
XLA Modules:
  0.0 117.1 jit_solution(3336543978451134494)
XLA Ops:
  0.6 0.6 collective-permute-start
  1.2 1.5 %collective-permute-start.1 = (bf16[256,1024]{1,0:T(8,128)(2,1)}, bf16[256,1024]{1,0:T(8,128)(2,1)S(1)}, u32[]{:S(2)}, u32[]{:S(2)}) collective-permute-start(bf16[256,1024]{1,0:T(8,128)(2,1)} %bitcast.26), channel_id=1, source_target_pairs={{0,4},{1,5},{2,6},{3,7},{4,0},{5,1},{6,2},{7,3},{8,12},{9,13},{10,... | collective-permute-start | bytes 1572872 | tf_op jit(solution)/shard_map/ppermute | solution.py:312
  2.8 1.6 %copy-done.3 = bf16[1,1024,1024]{2,1,0:T(8,128)(2,1)S(1)} copy-done((bf16[1,1024,1024]{2,1,0:T(8,128)(2,1)S(1)}, bf16[1,1024,1024]{2,1,0:T(8,128)(2,1)}, u32[]{:S(2)}) %copy-start.3) | copy-done | bytes 2097176
  4.3 1.0 copy-done.9
  5.4 2.1 %shard_map.77.refs_2_ = bf16[8,256,128]{2,1,0:T(8,128)(2,1)S(1)} custom-call(bf16[256,1024]{1,0:T(8,128)(2,1)S(1)} %bitcast.30, bf16[8,128,1024]{2,1,0:T(8,128)(2,1)S(1)} %bitcast.18), custom_call_target="tpu_custom_call" | custom-call | flops 3449999872 | bytes 2097152 | tf_op jit(solution)/shard_map/pallas_call | solution.py:42
  7.5 0.8 copy-done.5
  8.3 6.3 %collective-permute-done.refs_0_.refs_4_ = bf16[256,1024]{1,0:T(8,128)(2,1)S(1)} collective-permute-done((bf16[256,1024]{1,0:T(8,128)(2,1)}, bf16[256,1024]{1,0:T(8,128)(2,1)S(1)}, u32[]{:S(2)}, u32[]{:S(2)}) %collective-permute-start) | collective-permute-done | bytes 524320 | tf_op jit(solution)/shard_map/ppermute | solution.py:312
  14.8 0.5 copy-done.11
  15.4 0.8 copy-done.13
  16.2 1.9 %shard_map.78 = (bf16[128,1024]{1,0:T(8,128)(2,1)}, bf16[128,1024]{1,0:T(8,128)(2,1)}) custom-call(bf16[256,1024]{1,0:T(8,128)(2,1)} %copy-done.11, bf16[256,1024]{1,0:T(8,128)(2,1)} %copy-done.13, bf16[8,256,128]{2,1,0:T(8,128)(2,1)} %copy-done.5), custom_call_target="tpu_custom_call" | custom-call | tf_op jit(solution)/shard_map/pallas_call | solution.py:204
  18.0 1.0 collective-permute-start.3
  19.0 1.5 %collective-permute-start.2 = (bf16[128,1024]{1,0:T(8,128)(2,1)}, bf16[128,1024]{1,0:T(8,128)(2,1)S(1)}, u32[]{:S(2)}, u32[]{:S(2)}) collective-permute-start(bf16[128,1024]{1,0:T(8,128)(2,1)} %get-tuple-element.6), channel_id=1, source_target_pairs={{0,4},{1,5},{2,6},{3,7},{4,0},{5,1},{6,2},{7,3},{8,12},{9,13},{10,... | collective-permute-start | bytes 786440 | tf_op jit(solution)/shard_map/ppermute | solution.py:312
  20.6 0.5 collective-permute-start.8
  21.1 4.5 %all-to-all-start = ((bf16[8,256,128]{2,1,0:T(8,128)(2,1)}), bf16[8,256,128]{2,1,0:T(8,128)(2,1)S(1)}, u32[]{:S(2)}, u32[]{:S(2)}) async-start(bf16[8,256,128]{2,1,0:T(8,128)(2,1)} %copy-done.5), calls=%async_computation | async-start | bytes 1048576 | tf_op jit(solution)/shard_map/all_to_all | solution.py:325
  25.8 0.3 collective-permute-start.9
  26.2 1.2 %constant_dynamic-slice_fusion = bf16[3,1,128,1024]{3,2,1,0:T(8,128)(2,1)S(1)} fusion(bf16[3,8,128,1024]{3,2,1,0:T(8,128)(2,1)} %bitcast.16, s32[]{:T(128)S(6)} %select_n.4), kind=kLoop, calls=%fused_computation.1 | loop fusion | bytes 1572868 | tf_op jit(solution)/shard_map/jit(dynamic_index_in_dim)/dynamic_slice | solution.py:381
  27.4 6.4 %all-to-all-done.refs_2_ = bf16[8,256,128]{2,1,0:T(8,128)(2,1)S(1)} async-done(((bf16[8,256,128]{2,1,0:T(8,128)(2,1)}), bf16[8,256,128]{2,1,0:T(8,128)(2,1)S(1)}, u32[]{:S(2)}, u32[]{:S(2)}) %all-to-all-start) | async-done | bytes 524320 | tf_op jit(solution)/shard_map/all_to_all | solution.py:325
  33.8 1.0 shard_map.79.refs_14_.refs_3_
  34.8 1.5 %collective-permute-start.4 = (bf16[256,1024]{1,0:T(8,128)(2,1)}, bf16[256,1024]{1,0:T(8,128)(2,1)}, u32[]{:S(2)}, u32[]{:S(2)}) collective-permute-start(bf16[256,1024]{1,0:T(8,128)(2,1)} %shard_map.79.refs_14_.refs_3_), channel_id=1, source_target_pairs={{0,2},{1,3},{2,0},{3,1},{4,6},{5,7},{6,4},{7,5},{8,10},{9,11},{10,... | collective-permute-start | bytes 1572872 | tf_op jit(solution)/shard_map/ppermute | solution.py:312
  36.3 0.5 collective-permute-start.5
  36.9 1.0 copy-done.14
  37.9 11.8 %shard_map.80 = bf16[16,128,384]{2,1,0:T(8,128)(2,1)} custom-call(s32[16]{0:T(128)S(1)} %copy-done.16, s32[3]{0:T(128)S(1)} %pad_add_fusion.refs_1_, bf16[384,1024]{1,0:T(8,128)(2,1)S(1)} %bitcast.23, bf16[256,1024]{1,0:T(8,128)(2,1)S(1)} %bitcast.28, bf16[256,1024]{1,0:T(8,128)(2,1)S(1)} %copy-done.12, bf16[256,1024]{1,0:T(8,128)(2,1)S(1)} %copy-done.14, ...), custom_call_target="tpu_custom_call" | custom-call | flops 13799999488 | bytes 7340032 | tf_op jit(solution)/shard_map/pallas_call | solution.py:42
  49.8 1.8 %shard_map.81 = (bf16[128,1024]{1,0:T(8,128)(2,1)}, bf16[128,1024]{1,0:T(8,128)(2,1)}) custom-call(bf16[256,1024]{1,0:T(8,128)(2,1)} %collective-permute-done.4.refs_0_.refs_4_, bf16[256,1024]{1,0:T(8,128)(2,1)} %collective-permute-done.5.refs_1_.refs_5_, bf16[8,256,384]{2,1,0:T(8,128)(2,1)} %bitcast.8.refs_2_.refs_13_), custom_call_target="tpu_custom_call" | custom-call | tf_op jit(solution)/shard_map/pallas_call | solution.py:204
  51.6 1.6 %collective-permute-start.11 = (bf16[128,1024]{1,0:T(8,128)(2,1)}, bf16[128,1024]{1,0:T(8,128)(2,1)S(1)}, u32[]{:S(2)}, u32[]{:S(2)}) collective-permute-start(bf16[128,1024]{1,0:T(8,128)(2,1)} %get-tuple-element.8), channel_id=1, source_target_pairs={{0,4},{1,5},{2,6},{3,7},{4,0},{5,1},{6,2},{7,3},{8,12},{9,13},{10,... | collective-permute-start | bytes 786440 | tf_op jit(solution)/shard_map/ppermute | solution.py:312
  53.2 0.6 collective-permute-start.12
  53.7 0.5 collective-permute-start.15
  54.2 5.0 %all-to-all-start.1 = ((bf16[8,256,384]{2,1,0:T(8,128)(2,1)}), bf16[8,256,384]{2,1,0:T(8,128)(2,1)S(1)}, u32[]{:S(2)}, u32[]{:S(2)}) async-start(bf16[8,256,384]{2,1,0:T(8,128)(2,1)} %bitcast.8.refs_2_.refs_13_), calls=%async_computation.1 | async-start | bytes 3145728 | tf_op jit(solution)/shard_map/all_to_all | solution.py:325
  59.2 1.4 %collective-permute-done.11.refs_6_ = bf16[128,1024]{1,0:T(8,128)(2,1)S(1)} collective-permute-done((bf16[128,1024]{1,0:T(8,128)(2,1)}, bf16[128,1024]{1,0:T(8,128)(2,1)S(1)}, u32[]{:S(2)}, u32[]{:S(2)}) %collective-permute-start.11) | collective-permute-done | bytes 262176 | tf_op jit(solution)/shard_map/ppermute | solution.py:312
  60.6 1.9 %collective-permute-done.12.refs_7_ = bf16[128,1024]{1,0:T(8,128)(2,1)S(1)} collective-permute-done((bf16[128,1024]{1,0:T(8,128)(2,1)}, bf16[128,1024]{1,0:T(8,128)(2,1)S(1)}, u32[]{:S(2)}, u32[]{:S(2)}) %collective-permute-start.12) | collective-permute-done | bytes 262176 | tf_op jit(solution)/shard_map/ppermute | solution.py:312
  62.5 1.5 %collective-permute-done.17.refs_12_ = bf16[128,1024]{1,0:T(8,128)(2,1)S(1)} collective-permute-done((bf16[128,1024]{1,0:T(8,128)(2,1)S(1)}, bf16[128,1024]{1,0:T(8,128)(2,1)S(1)}, u32[]{:S(2)}, u32[]{:S(2)}) %collective-permute-start.17) | collective-permute-done | bytes 262176 | tf_op jit(solution)/shard_map/ppermute | solution.py:312
  64.0 8.3 %shard_map.82 = bf16[16,128,128]{2,1,0:T(8,128)(2,1)S(1)} custom-call(s32[16]{0:T(128)S(1)} %copy-done.16, s32[3]{0:T(128)S(1)} %pad_add_fusion.refs_1_, bf16[384,1024]{1,0:T(8,128)(2,1)S(1)} %bitcast.24, bf16[256,1024]{1,0:T(8,128)(2,1)} %shard_map.79.refs_14_.refs_3_, bf16[256,1024]{1,0:T(8,128)(2,1)} %collective-permute-done.4.refs_0_.refs_4_, ...), custom_call_target="tpu_custom_call" | custom-call | flops 9200000000 | bytes 5242880 | tf_op jit(solution)/shard_map/pallas_call | solution.py:42
  72.3 0.8 copy-done.15
  73.1 5.6 %all-to-all-done.1.refs_1_.grad_ref = bf16[8,256,384]{2,1,0:T(8,128)(2,1)S(1)} async-done(((bf16[8,256,384]{2,1,0:T(8,128)(2,1)}), bf16[8,256,384]{2,1,0:T(8,128)(2,1)S(1)}, u32[]{:S(2)}, u32[]{:S(2)}) %all-to-all-start.1) | async-done | bytes 1572896 | tf_op jit(solution)/shard_map/all_to_all | solution.py:325
  78.7 1.2 %copy-done = bf16[8,256,384]{2,1,0:T(8,128)(2,1)} copy-done((bf16[8,256,384]{2,1,0:T(8,128)(2,1)}, bf16[8,256,384]{2,1,0:T(8,128)(2,1)S(1)}, u32[]{:S(2)}) %copy-start) | copy-done | bytes 1572888
  79.9 1.8 %shard_map.83 = bf16[8,256,128]{2,1,0:T(8,128)(2,1)} custom-call(bf16[8,256,128]{2,1,0:T(8,128)(2,1)} %bitcast.32, bf16[8,256,384]{2,1,0:T(8,128)(2,1)} %copy-done), custom_call_target="tpu_custom_call" | custom-call | tf_op jit(solution)/shard_map/pallas_call | solution.py:204
  81.8 4.9 %all-to-all-start.2 = ((bf16[8,256,128]{2,1,0:T(8,128)(2,1)}), bf16[8,256,128]{2,1,0:T(8,128)(2,1)S(1)}, u32[]{:S(2)}, u32[]{:S(2)}) async-start(bf16[8,256,128]{2,1,0:T(8,128)(2,1)} %shard_map.83), calls=%async_computation.2 | async-start | bytes 1048576 | tf_op jit(solution)/shard_map/all_to_all | solution.py:325
  86.7 1.4 %copy-done.1 = bf16[8,256,384]{2,1,0:T(8,128)(2,1)S(1)} copy-done((bf16[8,256,384]{2,1,0:T(8,128)(2,1)S(1)}, bf16[8,256,384]{2,1,0:T(8,128)(2,1)}, u32[]{:S(2)}) %copy-start.1) | copy-done | bytes 1572888
  88.1 2.8 %copy-done.2 = bf16[1,3072,1024]{2,1,0:T(8,128)(2,1)S(1)} copy-done((bf16[1,3072,1024]{2,1,0:T(8,128)(2,1)S(1)}, bf16[1,3072,1024]{2,1,0:T(8,128)(2,1)}, u32[]{:S(2)}) %copy-start.2) | copy-done | bytes 6291480
  90.9 1.0 copy-done.8
  91.9 1.0 copy-done.10
  93.0 2.8 %shard_map.85 = bf16[256,1024]{1,0:T(8,128)(2,1)} custom-call(bf16[8,256,384]{2,1,0:T(8,128)(2,1)S(1)} %copy-done.1, bf16[256,1024]{1,0:T(8,128)(2,1)S(1)} %bitcast.29, bf16[256,1024]{1,0:T(8,128)(2,1)S(1)} %bitcast.31, bf16[3072,1024]{1,0:T(8,128)(2,1)S(1)} %bitcast.17), custom_call_target="tpu_custom_call" | custom-call | flops 1610612736 | bytes 6291456 | tf_op jit(solution)/shard_map/pallas_call | solution.py:42
  95.8 2.4 %collective-permute-start.19 = (bf16[256,1024]{1,0:T(8,128)(2,1)}, bf16[256,1024]{1,0:T(8,128)(2,1)}, u32[]{:S(2)}, u32[]{:S(2)}) collective-permute-start(bf16[256,1024]{1,0:T(8,128)(2,1)} %shard_map.85), channel_id=1, source_target_pairs={{8,0},{16,8},{24,16},{9,1},{17,9},{25,17},{10,2},{18,10},{26,18},{... | collective-permute-start | bytes 1572872 | tf_op jit(solution)/shard_map/ppermute | solution.py:355
  98.2 0.7 shard_map.84
  98.9 4.3 %collective-permute-start.18 = (bf16[256,1024]{1,0:T(8,128)(2,1)S(1)}, bf16[256,1024]{1,0:T(8,128)(2,1)S(1)}, u32[]{:S(2)}, u32[]{:S(2)}) collective-permute-start(bf16[256,1024]{1,0:T(8,128)(2,1)S(1)} %shard_map.84), channel_id=1, source_target_pairs={{0,8},{8,16},{16,24},{1,9},{9,17},{17,25},{2,10},{10,18},{18,26},{... | collective-permute-start | bytes 1572872 | tf_op jit(solution)/shard_map/ppermute | solution.py:355
  103.2 8.8 %collective-permute-done.19 = bf16[256,1024]{1,0:T(8,128)(2,1)} collective-permute-done((bf16[256,1024]{1,0:T(8,128)(2,1)}, bf16[256,1024]{1,0:T(8,128)(2,1)}, u32[]{:S(2)}, u32[]{:S(2)}) %collective-permute-start.19) | collective-permute-done | bytes 524320 | tf_op jit(solution)/shard_map/ppermute | solution.py:355
  112.0 2.5 %collective-permute-done.18 = bf16[256,1024]{1,0:T(8,128)(2,1)S(1)} collective-permute-done((bf16[256,1024]{1,0:T(8,128)(2,1)S(1)}, bf16[256,1024]{1,0:T(8,128)(2,1)S(1)}, u32[]{:S(2)}, u32[]{:S(2)}) %collective-permute-start.18) | collective-permute-done | bytes 524320 | tf_op jit(solution)/shard_map/ppermute | solution.py:355
  114.5 0.8 copy.12
  115.3 1.9 %copy.13 = bf16[1,256,1024]{2,1,0:T(8,128)(2,1)} copy(bf16[1,256,1024]{2,1,0:T(8,128)(2,1)} %bitcast.13) | data formatting | bytes 1048576
  (45 shorter events, 0.7 us)
Async XLA Ops:
  0.6 13.9 %collective-permute-start = (bf16[256,1024]{1,0:T(8,128)(2,1)}, bf16[256,1024]{1,0:T(8,128)(2,1)S(1)}, u32[]{:S(2)}, u32[]{:S(2)}) collective-permute-start(bf16[256,1024]{1,0:T(8,128)(2,1)} %bitcast.25), channel_id=1, source_target_pairs={{0,2},{1,3},{2,0},{3,1},{4,6},{5,7},{6,4},{7,5},{8,10},{9,11},{10,... | collective-permute-start | bytes 1572872 | tf_op jit(solution)/shard_map/ppermute | solution.py:312
  1.2 13.6 %collective-permute-start.1 = (bf16[256,1024]{1,0:T(8,128)(2,1)}, bf16[256,1024]{1,0:T(8,128)(2,1)S(1)}, u32[]{:S(2)}, u32[]{:S(2)}) collective-permute-start(bf16[256,1024]{1,0:T(8,128)(2,1)} %bitcast.26), channel_id=1, source_target_pairs={{0,4},{1,5},{2,6},{3,7},{4,0},{5,1},{6,2},{7,3},{8,12},{9,13},{10,... | collective-permute-start | bytes 1572872 | tf_op jit(solution)/shard_map/ppermute | solution.py:312
  2.7 32.1 %collective-permute-start.6 = (bf16[256,1024]{1,0:T(8,128)(2,1)}, bf16[256,1024]{1,0:T(8,128)(2,1)}, u32[]{:S(2)}, u32[]{:S(2)}) collective-permute-start(bf16[256,1024]{1,0:T(8,128)(2,1)} %bitcast.27), channel_id=1, source_target_pairs={{0,1},{1,0},{2,3},{3,2},{4,5},{5,4},{6,7},{7,6},{8,9},{9,8},{10,11... | collective-permute-start | bytes 1572872 | tf_op jit(solution)/shard_map/ppermute | solution.py:312
  2.8 1.6 %copy-start.3 = (bf16[1,1024,1024]{2,1,0:T(8,128)(2,1)S(1)}, bf16[1,1024,1024]{2,1,0:T(8,128)(2,1)}, u32[]{:S(2)}) copy-start(bf16[1,1024,1024]{2,1,0:T(8,128)(2,1)} %param.10) | copy-start | bytes 6291460
  4.3 1.0 copy-start.9
  7.5 0.8 copy-start.5
  8.3 25.6 %copy-start.6 = (bf16[1,256,1024]{2,1,0:T(8,128)(2,1)S(1)}, bf16[1,256,1024]{2,1,0:T(8,128)(2,1)}, u32[]{:S(2)}) copy-start(bf16[1,256,1024]{2,1,0:T(8,128)(2,1)} %param.6) | copy-start | bytes 1572868
  14.6 0.8 copy-start.11
  15.4 0.8 copy-start.13
  18.0 7.5 %collective-permute-start.3 = (bf16[128,1024]{1,0:T(8,128)(2,1)}, bf16[128,1024]{1,0:T(8,128)(2,1)S(1)}, u32[]{:S(2)}, u32[]{:S(2)}) collective-permute-start(bf16[128,1024]{1,0:T(8,128)(2,1)} %get-tuple-element.7), channel_id=1, source_target_pairs={{0,2},{1,3},{2,0},{3,1},{4,6},{5,7},{6,4},{7,5},{8,10},{9,11},{10,... | collective-permute-start | bytes 786440 | tf_op jit(solution)/shard_map/ppermute | solution.py:312
  19.0 6.8 %collective-permute-start.2 = (bf16[128,1024]{1,0:T(8,128)(2,1)}, bf16[128,1024]{1,0:T(8,128)(2,1)S(1)}, u32[]{:S(2)}, u32[]{:S(2)}) collective-permute-start(bf16[128,1024]{1,0:T(8,128)(2,1)} %get-tuple-element.6), channel_id=1, source_target_pairs={{0,4},{1,5},{2,6},{3,7},{4,0},{5,1},{6,2},{7,3},{8,12},{9,13},{10,... | collective-permute-start | bytes 786440 | tf_op jit(solution)/shard_map/ppermute | solution.py:312
  20.6 16.3 %collective-permute-start.7 = (bf16[256,1024]{1,0:T(8,128)(2,1)}, bf16[256,1024]{1,0:T(8,128)(2,1)}, u32[]{:S(2)}, u32[]{:S(2)}) collective-permute-start(bf16[256,1024]{1,0:T(8,128)(2,1)} %copy-done.11), channel_id=1, source_target_pairs={{0,1},{1,0},{2,3},{3,2},{4,5},{5,4},{6,7},{7,6},{8,9},{9,8},{10,11... | collective-permute-start | bytes 1572872 | tf_op jit(solution)/shard_map/ppermute | solution.py:312
  20.6 16.3 %collective-permute-start.8 = (bf16[256,1024]{1,0:T(8,128)(2,1)}, bf16[256,1024]{1,0:T(8,128)(2,1)}, u32[]{:S(2)}, u32[]{:S(2)}) collective-permute-start(bf16[256,1024]{1,0:T(8,128)(2,1)} %copy-done.13), channel_id=1, source_target_pairs={{0,1},{1,0},{2,3},{3,2},{4,5},{5,4},{6,7},{7,6},{8,9},{9,8},{10,11... | collective-permute-start | bytes 1572872 | tf_op jit(solution)/shard_map/ppermute | solution.py:312
  21.1 12.8 %all-to-all-start = ((bf16[8,256,128]{2,1,0:T(8,128)(2,1)}), bf16[8,256,128]{2,1,0:T(8,128)(2,1)S(1)}, u32[]{:S(2)}, u32[]{:S(2)}) async-start(bf16[8,256,128]{2,1,0:T(8,128)(2,1)} %copy-done.5), calls=%async_computation | async-start | bytes 1048576 | tf_op jit(solution)/shard_map/all_to_all | solution.py:325
  25.5 11.3 %copy-start.7 = (bf16[1,256,1024]{2,1,0:T(8,128)(2,1)S(1)}, bf16[1,256,1024]{2,1,0:T(8,128)(2,1)}, u32[]{:S(2)}) copy-start(bf16[1,256,1024]{2,1,0:T(8,128)(2,1)} %param.7) | copy-start | bytes 1572868
  25.5 11.3 %copy-start.12 = (bf16[256,1024]{1,0:T(8,128)(2,1)S(1)}, bf16[256,1024]{1,0:T(8,128)(2,1)}, u32[]{:S(2)}) copy-start(bf16[256,1024]{1,0:T(8,128)(2,1)} %copy-done.11) | copy-start | bytes 1572868
  25.5 11.3 %copy-start.16 = (s32[16]{0:T(128)S(1)}, s32[16]{0:T(128)}, u32[]{:S(2)}) copy-start(s32[16]{0:T(128)} %refs_0_.3) | copy-start | bytes 196
  25.6 10.7 %collective-permute-start.10 = (bf16[128,1024]{1,0:T(8,128)(2,1)S(1)}, bf16[128,1024]{1,0:T(8,128)(2,1)}, u32[]{:S(2)}, u32[]{:S(2)}) collective-permute-start(bf16[128,1024]{1,0:T(8,128)(2,1)S(1)} %collective-permute-done.3.refs_1_.refs_7_), channel_id=1, source_target_pairs={{0,1},{1,0},{2,3},{3,2},{4,5},{5,4},{6,7},{7,6},{8,9},{9,8},{10,11... | collective-permute-start | bytes 786440 | tf_op jit(solution)/shard_map/ppermute | solution.py:312
  25.8 11.0 %collective-permute-start.9 = (bf16[128,1024]{1,0:T(8,128)(2,1)S(1)}, bf16[128,1024]{1,0:T(8,128)(2,1)}, u32[]{:S(2)}, u32[]{:S(2)}) collective-permute-start(bf16[128,1024]{1,0:T(8,128)(2,1)S(1)} %collective-permute-done.2.refs_0_.refs_6_), channel_id=1, source_target_pairs={{0,1},{1,0},{2,3},{3,2},{4,5},{5,4},{6,7},{7,6},{8,9},{9,8},{10,11... | collective-permute-start | bytes 786440 | tf_op jit(solution)/shard_map/ppermute | solution.py:312
  34.8 14.9 %collective-permute-start.4 = (bf16[256,1024]{1,0:T(8,128)(2,1)}, bf16[256,1024]{1,0:T(8,128)(2,1)}, u32[]{:S(2)}, u32[]{:S(2)}) collective-permute-start(bf16[256,1024]{1,0:T(8,128)(2,1)} %shard_map.79.refs_14_.refs_3_), channel_id=1, source_target_pairs={{0,2},{1,3},{2,0},{3,1},{4,6},{5,7},{6,4},{7,5},{8,10},{9,11},{10,... | collective-permute-start | bytes 1572872 | tf_op jit(solution)/shard_map/ppermute | solution.py:312
  36.3 13.4 %collective-permute-start.5 = (bf16[256,1024]{1,0:T(8,128)(2,1)}, bf16[256,1024]{1,0:T(8,128)(2,1)}, u32[]{:S(2)}, u32[]{:S(2)}) collective-permute-start(bf16[256,1024]{1,0:T(8,128)(2,1)} %shard_map.79.refs_14_.refs_3_), channel_id=1, source_target_pairs={{0,4},{1,5},{2,6},{3,7},{4,0},{5,1},{6,2},{7,3},{8,12},{9,13},{10,... | collective-permute-start | bytes 1572872 | tf_op jit(solution)/shard_map/ppermute | solution.py:312
  36.9 25.7 %collective-permute-start.13 = (bf16[256,1024]{1,0:T(8,128)(2,1)}, bf16[256,1024]{1,0:T(8,128)(2,1)}, u32[]{:S(2)}, u32[]{:S(2)}) collective-permute-start(bf16[256,1024]{1,0:T(8,128)(2,1)} %shard_map.79.refs_14_.refs_3_), channel_id=1, source_target_pairs={{0,1},{1,0},{2,3},{3,2},{4,5},{5,4},{6,7},{7,6},{8,9},{9,8},{10,11... | collective-permute-start | bytes 1572872 | tf_op jit(solution)/shard_map/ppermute | solution.py:312
  36.9 1.0 copy-start.14
  51.6 9.0 %collective-permute-start.11 = (bf16[128,1024]{1,0:T(8,128)(2,1)}, bf16[128,1024]{1,0:T(8,128)(2,1)S(1)}, u32[]{:S(2)}, u32[]{:S(2)}) collective-permute-start(bf16[128,1024]{1,0:T(8,128)(2,1)} %get-tuple-element.8), channel_id=1, source_target_pairs={{0,4},{1,5},{2,6},{3,7},{4,0},{5,1},{6,2},{7,3},{8,12},{9,13},{10,... | collective-permute-start | bytes 786440 | tf_op jit(solution)/shard_map/ppermute | solution.py:312
  53.2 9.3 %collective-permute-start.12 = (bf16[128,1024]{1,0:T(8,128)(2,1)}, bf16[128,1024]{1,0:T(8,128)(2,1)S(1)}, u32[]{:S(2)}, u32[]{:S(2)}) collective-permute-start(bf16[128,1024]{1,0:T(8,128)(2,1)} %get-tuple-element.9), channel_id=1, source_target_pairs={{0,2},{1,3},{2,0},{3,1},{4,6},{5,7},{6,4},{7,5},{8,10},{9,11},{10,... | collective-permute-start | bytes 786440 | tf_op jit(solution)/shard_map/ppermute | solution.py:312
  53.7 10.3 %collective-permute-start.14 = (bf16[256,1024]{1,0:T(8,128)(2,1)}, bf16[256,1024]{1,0:T(8,128)(2,1)}, u32[]{:S(2)}, u32[]{:S(2)}) collective-permute-start(bf16[256,1024]{1,0:T(8,128)(2,1)} %collective-permute-done.4.refs_0_.refs_4_), channel_id=1, source_target_pairs={{0,1},{1,0},{2,3},{3,2},{4,5},{5,4},{6,7},{7,6},{8,9},{9,8},{10,11... | collective-permute-start | bytes 1572872 | tf_op jit(solution)/shard_map/ppermute | solution.py:312
  53.7 10.3 %collective-permute-start.15 = (bf16[256,1024]{1,0:T(8,128)(2,1)}, bf16[256,1024]{1,0:T(8,128)(2,1)}, u32[]{:S(2)}, u32[]{:S(2)}) collective-permute-start(bf16[256,1024]{1,0:T(8,128)(2,1)} %collective-permute-done.5.refs_1_.refs_5_), channel_id=1, source_target_pairs={{0,1},{1,0},{2,3},{3,2},{4,5},{5,4},{6,7},{7,6},{8,9},{9,8},{10,11... | collective-permute-start | bytes 1572872 | tf_op jit(solution)/shard_map/ppermute | solution.py:312
  54.2 24.5 %all-to-all-start.1 = ((bf16[8,256,384]{2,1,0:T(8,128)(2,1)}), bf16[8,256,384]{2,1,0:T(8,128)(2,1)S(1)}, u32[]{:S(2)}, u32[]{:S(2)}) async-start(bf16[8,256,384]{2,1,0:T(8,128)(2,1)} %bitcast.8.refs_2_.refs_13_), calls=%async_computation.1 | async-start | bytes 3145728 | tf_op jit(solution)/shard_map/all_to_all | solution.py:325
  60.6 1.9 %collective-permute-start.16 = (bf16[128,1024]{1,0:T(8,128)(2,1)S(1)}, bf16[128,1024]{1,0:T(8,128)(2,1)S(1)}, u32[]{:S(2)}, u32[]{:S(2)}) collective-permute-start(bf16[128,1024]{1,0:T(8,128)(2,1)S(1)} %collective-permute-done.11.refs_6_), channel_id=1, source_target_pairs={{0,1},{1,0},{2,3},{3,2},{4,5},{5,4},{6,7},{7,6},{8,9},{9,8},{10,11... | collective-permute-start | bytes 786440 | tf_op jit(solution)/shard_map/ppermute | solution.py:312
  62.5 1.5 %collective-permute-start.17 = (bf16[128,1024]{1,0:T(8,128)(2,1)S(1)}, bf16[128,1024]{1,0:T(8,128)(2,1)S(1)}, u32[]{:S(2)}, u32[]{:S(2)}) collective-permute-start(bf16[128,1024]{1,0:T(8,128)(2,1)S(1)} %collective-permute-done.12.refs_7_), channel_id=1, source_target_pairs={{0,1},{1,0},{2,3},{3,2},{4,5},{5,4},{6,7},{7,6},{8,9},{9,8},{10,11... | collective-permute-start | bytes 786440 | tf_op jit(solution)/shard_map/ppermute | solution.py:312
  72.3 0.8 copy-start.15
  78.7 1.2 %copy-start = (bf16[8,256,384]{2,1,0:T(8,128)(2,1)}, bf16[8,256,384]{2,1,0:T(8,128)(2,1)S(1)}, u32[]{:S(2)}) copy-start(bf16[8,256,384]{2,1,0:T(8,128)(2,1)S(1)} %all-to-all-done.1.refs_1_.grad_ref) | copy-start | bytes 4718596
  81.8 16.4 %all-to-all-start.2 = ((bf16[8,256,128]{2,1,0:T(8,128)(2,1)}), bf16[8,256,128]{2,1,0:T(8,128)(2,1)S(1)}, u32[]{:S(2)}, u32[]{:S(2)}) async-start(bf16[8,256,128]{2,1,0:T(8,128)(2,1)} %shard_map.83), calls=%async_computation.2 | async-start | bytes 1048576 | tf_op jit(solution)/shard_map/all_to_all | solution.py:325
  86.7 1.4 %copy-start.1 = (bf16[8,256,384]{2,1,0:T(8,128)(2,1)S(1)}, bf16[8,256,384]{2,1,0:T(8,128)(2,1)}, u32[]{:S(2)}) copy-start(bf16[8,256,384]{2,1,0:T(8,128)(2,1)} %copy-done) | copy-start | bytes 4718596
  88.1 2.8 %copy-start.2 = (bf16[1,3072,1024]{2,1,0:T(8,128)(2,1)S(1)}, bf16[1,3072,1024]{2,1,0:T(8,128)(2,1)}, u32[]{:S(2)}) copy-start(bf16[1,3072,1024]{2,1,0:T(8,128)(2,1)} %param.9) | copy-start | bytes 18874372
  90.9 1.0 copy-start.8
  91.9 1.0 copy-start.10
  93.0 5.2 %copy-start.4 = (bf16[1,1024,1024]{2,1,0:T(8,128)(2,1)S(1)}, bf16[1,1024,1024]{2,1,0:T(8,128)(2,1)}, u32[]{:S(2)}) copy-start(bf16[1,1024,1024]{2,1,0:T(8,128)(2,1)} %param.10) | copy-start | bytes 6291460
  95.8 16.2 %collective-permute-start.19 = (bf16[256,1024]{1,0:T(8,128)(2,1)}, bf16[256,1024]{1,0:T(8,128)(2,1)}, u32[]{:S(2)}, u32[]{:S(2)}) collective-permute-start(bf16[256,1024]{1,0:T(8,128)(2,1)} %shard_map.85), channel_id=1, source_target_pairs={{8,0},{16,8},{24,16},{9,1},{17,9},{25,17},{10,2},{18,10},{26,18},{... | collective-permute-start | bytes 1572872 | tf_op jit(solution)/shard_map/ppermute | solution.py:355
  98.9 15.6 %collective-permute-start.18 = (bf16[256,1024]{1,0:T(8,128)(2,1)S(1)}, bf16[256,1024]{1,0:T(8,128)(2,1)S(1)}, u32[]{:S(2)}, u32[]{:S(2)}) collective-permute-start(bf16[256,1024]{1,0:T(8,128)(2,1)S(1)} %shard_map.84), channel_id=1, source_target_pairs={{0,8},{8,16},{16,24},{1,9},{9,17},{17,25},{2,10},{10,18},{18,26},{... | collective-permute-start | bytes 1572872 | tf_op jit(solution)/shard_map/ppermute | solution.py:355

commit v7 on v6

--- a/solution.py
+++ b/solution.py
@@ -42,7 +42,7 @@
     return pl.pallas_call(
         kernel,
         in_specs=in_specs,
-        out_specs=VMEM,
+        out_specs=[VMEM] * len(out_shape) if isinstance(out_shape, list) else VMEM,
         out_shape=out_shape,
         scratch_shapes=scratch,
         compiler_params=pltpu.CompilerParams(vmem_limit_bytes=grant),
@@ -97,7 +97,8 @@
         results.append(low(scale(c) * (rounded - unit * mean)))
     for c, result in zip((2, 1, 0), results):
         for i, t in enumerate(tiles):
-            out[t, :, c * HD : (c + 1) * HD] = result[i * TILE : (i + 1) * TILE]
+            half = pl.ds(t % 2 * TILE, TILE)
+            out[t // 2, half, c * HD : (c + 1) * HD] = result[i * TILE : (i + 1) * TILE]
 
 
 def head_kernel(back, unread, pieces, spacing, *refs):
@@ -106,9 +107,11 @@
     refs = refs[3 + len(pieces) :]
     if back:
         grads, refs = refs[0], refs[1:]
-    out, kept, count, member = refs[unread : unread + 4]
+    refs = refs[unread:]
     if back:
-        scales = refs[unread + 4]
+        out, kept, count, member, scales = refs
+    else:
+        out_refs, (kept, count, member, out) = refs[:HEADS], refs[HEADS:]
     flip, residue = info_ref[0], info_ref[2]
     tiles = kept.shape[0]
     clusters = count.shape[0]
@@ -158,6 +161,9 @@
         return carry
 
     lax.fori_loop(0, clusters, visit, 0)
+    if not back:
+        for k in range(HEADS):
+            out_refs[k][...] = out[pl.ds(2 * (flip ^ k), 2)].reshape(out_refs[k].shape)
 
 
 def head_work(info, tile_cluster, pieces, weights, spacing, grads=None, earlier=()):
@@ -176,18 +182,20 @@
     ]
     if back:
         scratch.append(pltpu.VMEM((tiles, TILE, 2 * HD), jnp.float32))
+        shape = jax.ShapeDtypeStruct((HEADS, 2 * TILE, wide), jnp.bfloat16)
+    else:
+        scratch.append(pltpu.VMEM((tiles, TILE, HD), jnp.bfloat16))
+        shape = [jax.ShapeDtypeStruct((2 * TILE, HD), jnp.bfloat16) for _ in range(HEADS)]
     shapes = tuple((k, start, array.shape[0]) for k, start, array in pieces)
-    out = call(
+    return call(
         functools.partial(head_kernel, back, len(earlier), shapes, spacing),
         operands + list(earlier),
         [SMEM, SMEM] + [VMEM] * (len(operands) - 2) + [HBM] * len(earlier),
-        jax.ShapeDtypeStruct((tiles, TILE, wide), jnp.bfloat16),
+        shape,
         scratch,
         MICROSECOND * (12 if back else 8),
         2 * tokens * (width + 2 * wide),
     )
-    return out.reshape(HEADS, 2 * TILE, wide)
-
 
 def copy_kernel(starts, *refs):
     count = len(starts)
@@ -201,12 +209,15 @@
 
 
 def rows_after(arrays, starts, rows, earlier):
+    rows = [rows] * len(arrays) if isinstance(rows, int) else rows
     return pl.pallas_call(
         functools.partial(copy_kernel, starts),
         in_specs=[HBM] * (len(arrays) + len(earlier)),
         out_specs=[VMEM] * len(arrays),
-        out_shape=[jax.ShapeDtypeStruct((rows, *a.shape[1:]), a.dtype) for a in arrays],
+        out_shape=[jax.ShapeDtypeStruct((n, *a.shape[1:]), a.dtype) for n, a in zip(rows, arrays)],
         scratch_shapes=[pltpu.SemaphoreType.DMA((len(arrays),))],
+        compiler_params=pltpu.CompilerParams(vmem_limit_bytes=24 * MIB),
+        cost_estimate=pl.CostEstimate(flops=MICROSECOND, bytes_accessed=0, transcendentals=0),
     )(*arrays, *earlier)
 
 
@@ -255,20 +266,23 @@
     )
 
 
-def finish_kernel(att_ref, x_ref, w_ref, out_ref):
-    att = jnp.concatenate([att_ref[k] for k in range(HEADS)], axis=1)
+def finish_kernel(info_ref, *refs):
+    att_refs, (x_ref, w_ref, out_ref) = refs[:HEADS], refs[HEADS:]
+    flip = info_ref[0]
+    att = jnp.concatenate([ref[...] for ref in att_refs], axis=1)
     block = 256
     for start in range(0, x_ref.shape[1], block):
         columns = slice(start, start + block)
-        out_ref[:, columns] = low(high(x_ref[:, columns]) + dot(att, w_ref[:, columns], NN))
-
-
-def finish(attention, current, w_fin):
+        w = jnp.concatenate([w_ref[flip ^ k, :, columns] for k in range(HEADS)], axis=0)
+        out_ref[:, columns] = low(high(x_ref[:, columns]) + dot(att, w, NN))
+
+
+def finish(info, attention, current, w_fin):
     tokens, width = current.shape
     return call(
         finish_kernel,
-        [attention, current, w_fin],
-        [VMEM] * 3,
+        [info, *attention, current, w_fin.reshape(HEADS, HD, width)],
+        [SMEM] + [VMEM] * (HEADS + 2),
         jax.ShapeDtypeStruct((tokens, width), jnp.bfloat16),
         [],
         2 * tokens * width * HEADS * HD,
@@ -315,10 +329,18 @@
 def gather_rows(x, earlier):
     half = x.shape[0] // 2
     over_x, over_y = partner(x, 2), partner(x, 4)
-    top, bottom = rows_after([over_x, over_y], [0, half], half, earlier)
+    if earlier:
+        top, bottom = rows_after([over_x, over_y], [0, half], half, earlier)
+    else:
+        top, bottom = over_x[:half], over_y[half:]
     top, bottom = partner(top, 4), partner(bottom, 2)
     pieces = [(0, 0, x), (2, 0, over_x), (4, 0, over_y), (6, 0, top), (6, half, bottom)]
     return pieces + [(k + 1, start, partner(block, 1)) for k, start, block in pieces]
+
+
+def swap(blocks):
+    moved = {k: partner(blocks[k], k) for k in (2, 4, 6, 3, 5, 7, 1)}
+    return [blocks[0]] + [moved[k] for k in range(1, HEADS)]
 
 
 def all_swap(blocks):
@@ -363,7 +385,7 @@
     own = lax.axis_index("seq").astype(jnp.int32)
     if spacing == 1:
         info = jnp.stack([own, own, jnp.zeros_like(own)])
-        gather, spread, collect = gather_rows, all_swap, all_swap
+        gather, spread, collect, collect_each = gather_rows, all_swap, all_swap, swap
     else:
         info = jnp.stack([jnp.zeros_like(own), own // spacing, own % spacing])
 
@@ -376,12 +398,15 @@
 
         def collect(blocks):
             return to_tokens(blocks, own, spacing, tokens)
+
+        def collect_each(blocks):
+            return list(collect(jnp.stack(blocks)))
 
     own_head = w_rows.reshape(3, HEADS, HD, -1)
     own_head = lax.dynamic_index_in_dim(own_head, info[1], 1, keepdims=False)
     own_head = own_head.reshape(3 * HD, -1)
     spreading = spread_grads(upstream, w_fin)
-    stored_pieces = gather(stored, [spreading])
+    stored_pieces = gather(stored, [])
     grad_attention = spread(spreading)
     earlier = [block for k, _, block in stored_pieces if k == HEADS - 2]
     normed = norm_after(current, [*earlier, grad_attention])
@@ -393,11 +418,12 @@
     outputs = head_work(
         info, tile_cluster, current_pieces, own_head, spacing, earlier=[grads]
     )
-    outputs = rows_after([outputs], [0], HEADS, [returned_grads])[0]
-    returned = collect(outputs)
-    grad_self = finish_back(returned_grads, stored, upstream, w_rows)
+    returned = collect_each(outputs)
+    near = [stored, upstream, w_rows]
+    near = rows_after(near, [0] * 3, [a.shape[0] for a in near], outputs[:1])
+    grad_self = finish_back(returned_grads, *near)
     grad_input = passed_along(grad_self, "pipe", -1)
-    result = finish(returned, current, w_fin)
+    result = finish(info, returned, current, w_fin)
     next_input = passed_along(result, "pipe", 1)
     return (next_input[None], grad_input[None])
 

time: 119 us -> 121 us (1.017)
  waiting for transfers between devices: 34.9 us -> 41.6 us
  local copies, waits for them, and re-layouts: 17.9 us -> 14.3 us
  Pallas kernels: 32.2 us -> 30.1 us
    ppermute x18 -> x25, waiting for transfers between devices: 11.5 us -> 21.5 us  [partner(): return lax.ppermute(block, 'seq', route)]
    ppermute x18 -> x25, starting transfers between devices: 10.3 us -> 16 us  [partner(): return lax.ppermute(block, 'seq', route)]
    all_to_all x3 -> x2, waiting for transfers between devices: 12 us -> 6.52 us  [all_swap(): lax.all_to_all(blocks, 'seq', split_axis=0, concat_axis=0, tiled=True)]
    all_to_all x3 -> x2, starting transfers between devices: 14.3 us -> 9.76 us  [all_swap(): lax.all_to_all(blocks, 'seq', split_axis=0, concat_axis=0, tiled=True)]
    unnamed x36 -> x34, local copies, waits for them, and re-layouts: 16.7 us -> 12.2 us
    pallas_call x3 -> x2, Pallas kernels: 5.54 us -> 2.36 us  [rows_after(): pl.pallas_call(functools.partial(copy_kernel, starts), in_specs=[HBM] * (...]
    ppermute x2, waiting for transfers between devices: 11.3 us -> 13.5 us  [passed_along(): return lax.ppermute(block, axis, route)]
  transfers between devices with their start and end apart: 23 -> 29, of which waited for: 9 -> 11; matrix products, arithmetic and copies ran while one was open for 1% -> 2% of each run, Pallas kernels for 26% -> 25%
where the time goes in v7:
time: 121 us; the launch traced here: 119 us
  waiting for transfers between devices  41.6 us (34%)
  starting transfers between devices  31.6 us (26%)
  Pallas kernels  30.1 us (25%)
  local copies, waits for them, and re-layouts  14.3 us (12%)
    pallas_call x6, Pallas kernels, call(): pl.pallas_call(kernel, in_specs=in_specs, out_specs=[VMEM] * len(out_shap...  27.7 us
    ppermute x25, waiting for transfers between devices, partner(): return lax.ppermute(block, 'seq', route)  21.5 us
    ppermute x25, starting transfers between devices, partner(): return lax.ppermute(block, 'seq', route)  16 us
    ppermute x2, waiting for transfers between devices, passed_along(): return lax.ppermute(block, axis, route)  13.5 us
    unnamed x34, local copies, waits for them, and re-layouts  12.2 us
    all_to_all x2, starting transfers between devices, all_swap(): lax.all_to_all(blocks, 'seq', split_axis=0, concat_axis=0, tiled=True)  9.76 us
    all_to_all x2, waiting for transfers between devices, all_swap(): lax.all_to_all(blocks, 'seq', split_axis=0, concat_axis=0, tiled=True)  6.52 us
    ppermute x2, starting transfers between devices, passed_along(): return lax.ppermute(block, axis, route)  5.84 us
  transfers between devices with their start and end apart: 29, of which 11 were waited for; matrix products, arithmetic and copies ran while one was open for 2% of the time, Pallas kernels for 25%

profile of v7, /device:TPU:18, one launch (start us, length us, event | category | flops | bytes accessed | tf_op | source)
XLA Modules:
  0.0 118.5 jit_solution(17484347945484621312)
XLA Ops:
  0.6 1.6 %collective-permute-start.2 = (bf16[256,1024]{1,0:T(8,128)(2,1)}, bf16[256,1024]{1,0:T(8,128)(2,1)S(1)}, u32[]{:S(2)}, u32[]{:S(2)}) collective-permute-start(bf16[256,1024]{1,0:T(8,128)(2,1)} %bitcast.24), channel_id=1, source_target_pairs={{0,4},{1,5},{2,6},{3,7},{4,0},{5,1},{6,2},{7,3},{8,12},{9,13},{10,... | collective-permute-start | bytes 1572872 | tf_op jit(solution)/shard_map/ppermute | solution.py:326
  2.2 0.5 collective-permute-start
  2.8 11.8 %collective-permute-done.2.refs_5_ = bf16[256,1024]{1,0:T(8,128)(2,1)S(1)} collective-permute-done((bf16[256,1024]{1,0:T(8,128)(2,1)}, bf16[256,1024]{1,0:T(8,128)(2,1)S(1)}, u32[]{:S(2)}, u32[]{:S(2)}) %collective-permute-start.2) | collective-permute-done | bytes 524320 | tf_op jit(solution)/shard_map/ppermute | solution.py:326
  14.6 0.6 collective-permute-start.3
  15.2 0.7 collective-permute-done.refs_4_
  15.9 1.0 slice.8
  16.9 0.9 collective-permute-start.1
  17.8 0.5 collective-permute-start.7
  18.3 1.6 %copy-done.2 = bf16[1,1024,1024]{2,1,0:T(8,128)(2,1)S(1)} copy-done((bf16[1,1024,1024]{2,1,0:T(8,128)(2,1)S(1)}, bf16[1,1024,1024]{2,1,0:T(8,128)(2,1)}, u32[]{:S(2)}) %copy-start.2) | copy-done | bytes 2097176
  19.9 1.0 copy-done.9
  20.9 2.8 %shard_map.77 = bf16[8,256,128]{2,1,0:T(8,128)(2,1)} custom-call(bf16[256,1024]{1,0:T(8,128)(2,1)S(1)} %bitcast.29, bf16[8,128,1024]{2,1,0:T(8,128)(2,1)S(1)} %bitcast.17), custom_call_target="tpu_custom_call" | custom-call | flops 3449999872 | bytes 2097152 | tf_op jit(solution)/shard_map/pallas_call | solution.py:42
  23.7 4.9 %all-to-all-start = ((bf16[8,256,128]{2,1,0:T(8,128)(2,1)}), bf16[8,256,128]{2,1,0:T(8,128)(2,1)S(1)}, u32[]{:S(2)}, u32[]{:S(2)}) async-start(bf16[8,256,128]{2,1,0:T(8,128)(2,1)} %shard_map.77), calls=%async_computation | async-start | bytes 1048576 | tf_op jit(solution)/shard_map/all_to_all | solution.py:347
  28.8 0.4 collective-permute-start.9
  29.2 1.2 %constant_dynamic-slice_fusion = bf16[3,1,128,1024]{3,2,1,0:T(8,128)(2,1)S(1)} fusion(bf16[3,8,128,1024]{3,2,1,0:T(8,128)(2,1)} %bitcast.13, s32[]{:T(128)S(6)} %select_n.4), kind=kLoop, calls=%fused_computation.1 | loop fusion | bytes 1572868 | tf_op jit(solution)/shard_map/jit(dynamic_index_in_dim)/dynamic_slice | solution.py:406
  30.4 6.5 %all-to-all-done.refs_2_ = bf16[8,256,128]{2,1,0:T(8,128)(2,1)S(1)} async-done(((bf16[8,256,128]{2,1,0:T(8,128)(2,1)}), bf16[8,256,128]{2,1,0:T(8,128)(2,1)S(1)}, u32[]{:S(2)}, u32[]{:S(2)}) %all-to-all-start) | async-done | bytes 524320 | tf_op jit(solution)/shard_map/all_to_all | solution.py:347
  36.9 1.0 shard_map.78.refs_14_.refs_3_
  38.0 0.6 collective-permute-start.5
  38.6 1.4 %collective-permute-start.4 = (bf16[256,1024]{1,0:T(8,128)(2,1)}, bf16[256,1024]{1,0:T(8,128)(2,1)}, u32[]{:S(2)}, u32[]{:S(2)}) collective-permute-start(bf16[256,1024]{1,0:T(8,128)(2,1)} %shard_map.78.refs_14_.refs_3_), channel_id=1, source_target_pairs={{0,2},{1,3},{2,0},{3,1},{4,6},{5,7},{6,4},{7,5},{8,10},{9,11},{10,... | collective-permute-start | bytes 1572872 | tf_op jit(solution)/shard_map/ppermute | solution.py:326
  40.0 10.7 %shard_map.79.refs_2_.refs_13_ = bf16[8,256,384]{2,1,0:T(8,128)(2,1)S(1)} custom-call(s32[16]{0:T(128)S(1)} %copy-done.13, s32[3]{0:T(128)S(1)} %pad_add_fusion.refs_1_.info_ref, bf16[384,1024]{1,0:T(8,128)(2,1)S(1)} %bitcast.22, bf16[256,1024]{1,0:T(8,128)(2,1)S(1)} %bitcast.27, bf16[256,1024]{1,0:T(8,128)(2,1)} %collective-permute-done.refs_4_, ...), custom_call_target="tpu_custom_call" | custom-call | flops 13799999488 | bytes 7340032 | tf_op jit(solution)/shard_map/pallas_call | solution.py:42
  50.8 1.8 %collective-permute-done.5.refs_1_.refs_5_ = bf16[256,1024]{1,0:T(8,128)(2,1)} collective-permute-done((bf16[256,1024]{1,0:T(8,128)(2,1)}, bf16[256,1024]{1,0:T(8,128)(2,1)}, u32[]{:S(2)}, u32[]{:S(2)}) %collective-permute-start.5) | collective-permute-done | bytes 524320 | tf_op jit(solution)/shard_map/ppermute | solution.py:326
  52.9 1.8 %shard_map.80 = (bf16[128,1024]{1,0:T(8,128)(2,1)}, bf16[128,1024]{1,0:T(8,128)(2,1)}) custom-call(bf16[256,1024]{1,0:T(8,128)(2,1)} %collective-permute-done.4.refs_0_.refs_4_, bf16[256,1024]{1,0:T(8,128)(2,1)} %collective-permute-done.5.refs_1_.refs_5_, bf16[8,256,384]{2,1,0:T(8,128)(2,1)S(1)} %shard_map.79.refs_2_.refs_13_), custom_call_target="tpu_custom_call" | custom-call | flops 1150000000 | tf_op jit(solution)/shard_map/pallas_call | solution.py:213
  54.7 1.5 %collective-permute-start.11 = (bf16[128,1024]{1,0:T(8,128)(2,1)}, bf16[128,1024]{1,0:T(8,128)(2,1)}, u32[]{:S(2)}, u32[]{:S(2)}) collective-permute-start(bf16[128,1024]{1,0:T(8,128)(2,1)} %get-tuple-element.15), channel_id=1, source_target_pairs={{0,4},{1,5},{2,6},{3,7},{4,0},{5,1},{6,2},{7,3},{8,12},{9,13},{10,... | collective-permute-start | bytes 786440 | tf_op jit(solution)/shard_map/ppermute | solution.py:326
  56.3 0.5 collective-permute-start.14
  56.8 1.5 %collective-permute-start.12 = (bf16[128,1024]{1,0:T(8,128)(2,1)}, bf16[128,1024]{1,0:T(8,128)(2,1)}, u32[]{:S(2)}, u32[]{:S(2)}) collective-permute-start(bf16[128,1024]{1,0:T(8,128)(2,1)} %get-tuple-element.16), channel_id=1, source_target_pairs={{0,2},{1,3},{2,0},{3,1},{4,6},{5,7},{6,4},{7,5},{8,10},{9,11},{10,... | collective-permute-start | bytes 786440 | tf_op jit(solution)/shard_map/ppermute | solution.py:326
  58.3 4.9 %all-to-all-start.1 = ((bf16[8,256,384]{2,1,0:T(8,128)(2,1)}), bf16[8,256,384]{2,1,0:T(8,128)(2,1)}, u32[]{:S(2)}, u32[]{:S(2)}) async-start(bf16[8,256,384]{2,1,0:T(8,128)(2,1)} %copy-done.5), calls=%async_computation.1 | async-start | bytes 3145728 | tf_op jit(solution)/shard_map/all_to_all | solution.py:347
  63.3 2.4 %collective-permute-done.12.refs_7_ = bf16[128,1024]{1,0:T(8,128)(2,1)} collective-permute-done((bf16[128,1024]{1,0:T(8,128)(2,1)}, bf16[128,1024]{1,0:T(8,128)(2,1)}, u32[]{:S(2)}, u32[]{:S(2)}) %collective-permute-start.12) | collective-permute-done | bytes 262176 | tf_op jit(solution)/shard_map/ppermute | solution.py:326
  65.8 1.7 %collective-permute-done.17.refs_12_ = bf16[128,1024]{1,0:T(8,128)(2,1)S(1)} collective-permute-done((bf16[128,1024]{1,0:T(8,128)(2,1)}, bf16[128,1024]{1,0:T(8,128)(2,1)S(1)}, u32[]{:S(2)}, u32[]{:S(2)}) %collective-permute-start.17) | collective-permute-done | bytes 262176 | tf_op jit(solution)/shard_map/ppermute | solution.py:326
  67.5 1.4 %copy-done.6 = bf16[8,256,384]{2,1,0:T(8,128)(2,1)S(1)} copy-done((bf16[8,256,384]{2,1,0:T(8,128)(2,1)S(1)}, bf16[8,256,384]{2,1,0:T(8,128)(2,1)}, u32[]{:S(2)}) %copy-start.6) | copy-done | bytes 1572888
  68.9 8.5 %shard_map.81 = (bf16[256,128]{1,0:T(8,128)(2,1)S(1)}, bf16[256,128]{1,0:T(8,128)(2,1)S(1)}, bf16[256,128]{1,0:T(8,128)(2,1)S(1)}, bf16[256,128]{1,0:T(8,128)(2,...) custom-call(s32[16]{0:T(128)S(1)} %copy-done.13, ...), custom_call_target="tpu_custom_call" | custom-call | flops 9200000000 | bytes 5242880 | tf_op jit(solution)/shard_map/pallas_call | solution.py:42
  77.7 1.3 %collective-permute-start.19 = (bf16[256,128]{1,0:T(8,128)(2,1)S(1)}, bf16[256,128]{1,0:T(8,128)(2,1)S(1)}, u32[]{:S(2)}, u32[]{:S(2)}) collective-permute-start(bf16[256,128]{1,0:T(8,128)(2,1)S(1)} %get-tuple-element.19), channel_id=1, source_target_pairs={{0,2},{1,3},{2,0},{3,1},{4,6},{5,7},{6,4},{7,5},{8,10},{9,11},{10,... | collective-permute-start | bytes 196616 | tf_op jit(solution)/shard_map/ppermute | solution.py:326
  79.0 0.4 collective-permute-start.20
  79.5 1.7 %collective-permute-start.22 = (bf16[256,128]{1,0:T(8,128)(2,1)S(1)}, bf16[256,128]{1,0:T(8,128)(2,1)S(1)}, u32[]{:S(2)}, u32[]{:S(2)}) collective-permute-start(bf16[256,128]{1,0:T(8,128)(2,1)S(1)} %get-tuple-element.22), channel_id=1, source_target_pairs={{0,5},{1,4},{2,7},{3,6},{4,1},{5,0},{6,3},{7,2},{8,13},{9,12},{10,... | collective-permute-start | bytes 196616 | tf_op jit(solution)/shard_map/ppermute | solution.py:326
  81.2 1.0 collective-permute-start.23
  82.2 1.8 %collective-permute-done.19.refs_2_ = bf16[256,128]{1,0:T(8,128)(2,1)S(1)} collective-permute-done((bf16[256,128]{1,0:T(8,128)(2,1)S(1)}, bf16[256,128]{1,0:T(8,128)(2,1)S(1)}, u32[]{:S(2)}, u32[]{:S(2)}) %collective-permute-start.19) | collective-permute-done | bytes 65568 | tf_op jit(solution)/shard_map/ppermute | solution.py:326
  84.0 0.8 collective-permute-start.24
  84.8 0.5 shard_map.83
  85.4 2.7 %copy-done = bf16[3072,1024]{1,0:T(8,128)(2,1)} copy-done((bf16[3072,1024]{1,0:T(8,128)(2,1)}, bf16[3072,1024]{1,0:T(8,128)(2,1)S(1)}, u32[]{:S(2)}) %copy-start) | copy-done | bytes 6291480
  88.1 0.9 collective-permute-done.24.refs_7_
  89.0 1.3 %shard_map.82 = bf16[256,1024]{1,0:T(8,128)(2,1)S(1)} custom-call(s32[3]{0:T(128)S(1)} %pad_add_fusion.refs_1_.info_ref, bf16[256,128]{1,0:T(8,128)(2,1)S(1)} %get-tuple-element.17.refs_0_.refs_3_, bf16[256,128]{1,0:T(8,128)(2,1)S(1)} %collective-permute-done.18.refs_1_, bf16[256,128]{1,0:T(8,128)(2,1)S(1)} %collective-permute-done.19.refs_2_, ...), custom_call_target="tpu_custom_call" | custom-call | flops 536870912 | bytes 2097152 | tf_op jit(solution)/shard_map/pallas_call | solution.py:42
  90.3 3.5 %collective-permute-start.25 = (bf16[256,1024]{1,0:T(8,128)(2,1)S(1)}, bf16[256,1024]{1,0:T(8,128)(2,1)S(1)}, u32[]{:S(2)}, u32[]{:S(2)}) collective-permute-start(bf16[256,1024]{1,0:T(8,128)(2,1)S(1)} %shard_map.82), channel_id=1, source_target_pairs={{0,8},{8,16},{16,24},{1,9},{9,17},{17,25},{2,10},{10,18},{18,26},{... | collective-permute-start | bytes 1572872 | tf_op jit(solution)/shard_map/ppermute | solution.py:377
  93.8 2.8 %copy-done.1 = bf16[3072,1024]{1,0:T(8,128)(2,1)S(1)} copy-done((bf16[3072,1024]{1,0:T(8,128)(2,1)S(1)}, bf16[3072,1024]{1,0:T(8,128)(2,1)}, u32[]{:S(2)}) %copy-start.1) | copy-done | bytes 6291480
  96.5 1.0 copy-done.12
  97.6 3.4 %shard_map.84 = bf16[256,1024]{1,0:T(8,128)(2,1)S(1)} custom-call(bf16[8,256,384]{2,1,0:T(8,128)(2,1)} %all-to-all-done.1.grad_ref, bf16[256,1024]{1,0:T(8,128)(2,1)S(1)} %get-tuple-element.25.x_ref, bf16[256,1024]{1,0:T(8,128)(2,1)S(1)} %copy-done.12, bf16[3072,1024]{1,0:T(8,128)(2,1)S(1)} %copy-done.1), custom_call_target="tpu_custom_call" | custom-call | flops 1610612736 | bytes 6291456 | tf_op jit(solution)/shard_map/pallas_call | solution.py:42
  101.0 2.4 %collective-permute-start.26 = (bf16[256,1024]{1,0:T(8,128)(2,1)S(1)}, bf16[256,1024]{1,0:T(8,128)(2,1)S(1)}, u32[]{:S(2)}, u32[]{:S(2)}) collective-permute-start(bf16[256,1024]{1,0:T(8,128)(2,1)S(1)} %shard_map.84), channel_id=1, source_target_pairs={{8,0},{16,8},{24,16},{9,1},{17,9},{25,17},{10,2},{18,10},{26,18},{... | collective-permute-start | bytes 1572872 | tf_op jit(solution)/shard_map/ppermute | solution.py:377
  103.4 3.1 %collective-permute-done.25 = bf16[256,1024]{1,0:T(8,128)(2,1)S(1)} collective-permute-done((bf16[256,1024]{1,0:T(8,128)(2,1)S(1)}, bf16[256,1024]{1,0:T(8,128)(2,1)S(1)}, u32[]{:S(2)}, u32[]{:S(2)}) %collective-permute-start.25) | collective-permute-done | bytes 524320 | tf_op jit(solution)/shard_map/ppermute | solution.py:377
  106.4 10.5 %collective-permute-done.26 = bf16[256,1024]{1,0:T(8,128)(2,1)S(1)} collective-permute-done((bf16[256,1024]{1,0:T(8,128)(2,1)S(1)}, bf16[256,1024]{1,0:T(8,128)(2,1)S(1)}, u32[]{:S(2)}, u32[]{:S(2)}) %collective-permute-start.26) | collective-permute-done | bytes 524320 | tf_op jit(solution)/shard_map/ppermute | solution.py:377
  116.9 0.8 copy.12
  117.7 0.8 copy.13
  (57 shorter events, 1.2 us)
Async XLA Ops:
  0.6 13.9 %collective-permute-start.2 = (bf16[256,1024]{1,0:T(8,128)(2,1)}, bf16[256,1024]{1,0:T(8,128)(2,1)S(1)}, u32[]{:S(2)}, u32[]{:S(2)}) collective-permute-start(bf16[256,1024]{1,0:T(8,128)(2,1)} %bitcast.24), channel_id=1, source_target_pairs={{0,4},{1,5},{2,6},{3,7},{4,0},{5,1},{6,2},{7,3},{8,12},{9,13},{10,... | collective-permute-start | bytes 1572872 | tf_op jit(solution)/shard_map/ppermute | solution.py:326
  2.2 13.7 %collective-permute-start = (bf16[256,1024]{1,0:T(8,128)(2,1)}, bf16[256,1024]{1,0:T(8,128)(2,1)}, u32[]{:S(2)}, u32[]{:S(2)}) collective-permute-start(bf16[256,1024]{1,0:T(8,128)(2,1)} %bitcast.25), channel_id=1, source_target_pairs={{0,2},{1,3},{2,0},{3,1},{4,6},{5,7},{6,4},{7,5},{8,10},{9,11},{10,... | collective-permute-start | bytes 1572872 | tf_op jit(solution)/shard_map/ppermute | solution.py:326
  2.7 35.2 %collective-permute-start.6 = (bf16[256,1024]{1,0:T(8,128)(2,1)}, bf16[256,1024]{1,0:T(8,128)(2,1)}, u32[]{:S(2)}, u32[]{:S(2)}) collective-permute-start(bf16[256,1024]{1,0:T(8,128)(2,1)} %bitcast.26), channel_id=1, source_target_pairs={{0,1},{1,0},{2,3},{3,2},{4,5},{5,4},{6,7},{7,6},{8,9},{9,8},{10,11... | collective-permute-start | bytes 1572872 | tf_op jit(solution)/shard_map/ppermute | solution.py:326
  14.6 14.1 %collective-permute-start.3 = (bf16[128,1024]{1,0:T(8,128)(2,1)S(1)}, bf16[128,1024]{1,0:T(8,128)(2,1)S(1)}, u32[]{:S(2)}, u32[]{:S(2)}) collective-permute-start(bf16[128,1024]{1,0:T(8,128)(2,1)S(1)} %slice.9), channel_id=1, source_target_pairs={{0,2},{1,3},{2,0},{3,1},{4,6},{5,7},{6,4},{7,5},{8,10},{9,11},{10,... | collective-permute-start | bytes 786440 | tf_op jit(solution)/shard_map/ppermute | solution.py:326
  16.9 11.9 %collective-permute-start.1 = (bf16[128,1024]{1,0:T(8,128)(2,1)S(1)}, bf16[128,1024]{1,0:T(8,128)(2,1)S(1)}, u32[]{:S(2)}, u32[]{:S(2)}) collective-permute-start(bf16[128,1024]{1,0:T(8,128)(2,1)S(1)} %slice.8), channel_id=1, source_target_pairs={{0,4},{1,5},{2,6},{3,7},{4,0},{5,1},{6,2},{7,3},{8,12},{9,13},{10,... | collective-permute-start | bytes 786440 | tf_op jit(solution)/shard_map/ppermute | solution.py:326
  17.8 20.8 %collective-permute-start.8 = (bf16[256,1024]{1,0:T(8,128)(2,1)S(1)}, bf16[256,1024]{1,0:T(8,128)(2,1)}, u32[]{:S(2)}, u32[]{:S(2)}) collective-permute-start(bf16[256,1024]{1,0:T(8,128)(2,1)S(1)} %collective-permute-done.2.refs_5_), channel_id=1, source_target_pairs={{0,1},{1,0},{2,3},{3,2},{4,5},{5,4},{6,7},{7,6},{8,9},{9,8},{10,11... | collective-permute-start | bytes 1572872 | tf_op jit(solution)/shard_map/ppermute | solution.py:326
  17.8 22.3 %collective-permute-start.7 = (bf16[256,1024]{1,0:T(8,128)(2,1)}, bf16[256,1024]{1,0:T(8,128)(2,1)}, u32[]{:S(2)}, u32[]{:S(2)}) collective-permute-start(bf16[256,1024]{1,0:T(8,128)(2,1)} %collective-permute-done.refs_4_), channel_id=1, source_target_pairs={{0,1},{1,0},{2,3},{3,2},{4,5},{5,4},{6,7},{7,6},{8,9},{9,8},{10,11... | collective-permute-start | bytes 1572872 | tf_op jit(solution)/shard_map/ppermute | solution.py:326
  18.3 1.6 %copy-start.2 = (bf16[1,1024,1024]{2,1,0:T(8,128)(2,1)S(1)}, bf16[1,1024,1024]{2,1,0:T(8,128)(2,1)}, u32[]{:S(2)}) copy-start(bf16[1,1024,1024]{2,1,0:T(8,128)(2,1)} %param.10) | copy-start | bytes 6291460
  19.9 1.0 copy-start.9
  20.9 16.1 %copy-start.4 = (bf16[1,256,1024]{2,1,0:T(8,128)(2,1)S(1)}, bf16[1,256,1024]{2,1,0:T(8,128)(2,1)}, u32[]{:S(2)}) copy-start(bf16[1,256,1024]{2,1,0:T(8,128)(2,1)} %param.6) | copy-start | bytes 1572868
  20.9 19.1 %copy-start.7 = (bf16[1,256,1024]{2,1,0:T(8,128)(2,1)S(1)}, bf16[1,256,1024]{2,1,0:T(8,128)(2,1)}, u32[]{:S(2)}) copy-start(bf16[1,256,1024]{2,1,0:T(8,128)(2,1)} %param.7) | copy-start | bytes 1572868
  20.9 19.1 %copy-start.13 = (s32[16]{0:T(128)S(1)}, s32[16]{0:T(128)}, u32[]{:S(2)}) copy-start(s32[16]{0:T(128)} %refs_0_.3) | copy-start | bytes 196
  23.7 13.2 %all-to-all-start = ((bf16[8,256,128]{2,1,0:T(8,128)(2,1)}), bf16[8,256,128]{2,1,0:T(8,128)(2,1)S(1)}, u32[]{:S(2)}, u32[]{:S(2)}) async-start(bf16[8,256,128]{2,1,0:T(8,128)(2,1)} %shard_map.77), calls=%async_computation | async-start | bytes 1048576 | tf_op jit(solution)/shard_map/all_to_all | solution.py:347
  28.7 9.4 %collective-permute-start.10 = (bf16[128,1024]{1,0:T(8,128)(2,1)S(1)}, bf16[128,1024]{1,0:T(8,128)(2,1)}, u32[]{:S(2)}, u32[]{:S(2)}) collective-permute-start(bf16[128,1024]{1,0:T(8,128)(2,1)S(1)} %collective-permute-done.3.refs_1_.refs_7_), channel_id=1, source_target_pairs={{0,1},{1,0},{2,3},{3,2},{4,5},{5,4},{6,7},{7,6},{8,9},{9,8},{10,11... | collective-permute-start | bytes 786440 | tf_op jit(solution)/shard_map/ppermute | solution.py:326
  28.8 11.2 %collective-permute-start.9 = (bf16[128,1024]{1,0:T(8,128)(2,1)S(1)}, bf16[128,1024]{1,0:T(8,128)(2,1)}, u32[]{:S(2)}, u32[]{:S(2)}) collective-permute-start(bf16[128,1024]{1,0:T(8,128)(2,1)S(1)} %collective-permute-done.1.refs_0_.refs_6_), channel_id=1, source_target_pairs={{0,1},{1,0},{2,3},{3,2},{4,5},{5,4},{6,7},{7,6},{8,9},{9,8},{10,11... | collective-permute-start | bytes 786440 | tf_op jit(solution)/shard_map/ppermute | solution.py:326
  37.9 27.8 %collective-permute-start.13 = (bf16[256,1024]{1,0:T(8,128)(2,1)}, bf16[256,1024]{1,0:T(8,128)(2,1)}, u32[]{:S(2)}, u32[]{:S(2)}) collective-permute-start(bf16[256,1024]{1,0:T(8,128)(2,1)} %shard_map.78.refs_14_.refs_3_), channel_id=1, source_target_pairs={{0,1},{1,0},{2,3},{3,2},{4,5},{5,4},{6,7},{7,6},{8,9},{9,8},{10,11... | collective-permute-start | bytes 1572872 | tf_op jit(solution)/shard_map/ppermute | solution.py:326
  38.0 14.6 %collective-permute-start.5 = (bf16[256,1024]{1,0:T(8,128)(2,1)}, bf16[256,1024]{1,0:T(8,128)(2,1)}, u32[]{:S(2)}, u32[]{:S(2)}) collective-permute-start(bf16[256,1024]{1,0:T(8,128)(2,1)} %shard_map.78.refs_14_.refs_3_), channel_id=1, source_target_pairs={{0,4},{1,5},{2,6},{3,7},{4,0},{5,1},{6,2},{7,3},{8,12},{9,13},{10,... | collective-permute-start | bytes 1572872 | tf_op jit(solution)/shard_map/ppermute | solution.py:326
  38.6 14.3 %collective-permute-start.4 = (bf16[256,1024]{1,0:T(8,128)(2,1)}, bf16[256,1024]{1,0:T(8,128)(2,1)}, u32[]{:S(2)}, u32[]{:S(2)}) collective-permute-start(bf16[256,1024]{1,0:T(8,128)(2,1)} %shard_map.78.refs_14_.refs_3_), channel_id=1, source_target_pairs={{0,2},{1,3},{2,0},{3,1},{4,6},{5,7},{6,4},{7,5},{8,10},{9,11},{10,... | collective-permute-start | bytes 1572872 | tf_op jit(solution)/shard_map/ppermute | solution.py:326
  50.8 6.0 %copy-start.5 = (bf16[8,256,384]{2,1,0:T(8,128)(2,1)}, bf16[8,256,384]{2,1,0:T(8,128)(2,1)S(1)}, u32[]{:S(2)}) copy-start(bf16[8,256,384]{2,1,0:T(8,128)(2,1)S(1)} %shard_map.79.refs_2_.refs_13_) | copy-start | bytes 4718596
  54.7 8.4 %collective-permute-start.11 = (bf16[128,1024]{1,0:T(8,128)(2,1)}, bf16[128,1024]{1,0:T(8,128)(2,1)}, u32[]{:S(2)}, u32[]{:S(2)}) collective-permute-start(bf16[128,1024]{1,0:T(8,128)(2,1)} %get-tuple-element.15), channel_id=1, source_target_pairs={{0,4},{1,5},{2,6},{3,7},{4,0},{5,1},{6,2},{7,3},{8,12},{9,13},{10,... | collective-permute-start | bytes 786440 | tf_op jit(solution)/shard_map/ppermute | solution.py:326
  56.3 9.5 %collective-permute-start.15 = (bf16[256,1024]{1,0:T(8,128)(2,1)}, bf16[256,1024]{1,0:T(8,128)(2,1)}, u32[]{:S(2)}, u32[]{:S(2)}) collective-permute-start(bf16[256,1024]{1,0:T(8,128)(2,1)} %collective-permute-done.5.refs_1_.refs_5_), channel_id=1, source_target_pairs={{0,1},{1,0},{2,3},{3,2},{4,5},{5,4},{6,7},{7,6},{8,9},{9,8},{10,11... | collective-permute-start | bytes 1572872 | tf_op jit(solution)/shard_map/ppermute | solution.py:326
  56.3 9.5 %collective-permute-start.14 = (bf16[256,1024]{1,0:T(8,128)(2,1)}, bf16[256,1024]{1,0:T(8,128)(2,1)}, u32[]{:S(2)}, u32[]{:S(2)}) collective-permute-start(bf16[256,1024]{1,0:T(8,128)(2,1)} %collective-permute-done.4.refs_0_.refs_4_), channel_id=1, source_target_pairs={{0,1},{1,0},{2,3},{3,2},{4,5},{5,4},{6,7},{7,6},{8,9},{9,8},{10,11... | collective-permute-start | bytes 1572872 | tf_op jit(solution)/shard_map/ppermute | solution.py:326
  56.8 9.0 %collective-permute-start.12 = (bf16[128,1024]{1,0:T(8,128)(2,1)}, bf16[128,1024]{1,0:T(8,128)(2,1)}, u32[]{:S(2)}, u32[]{:S(2)}) collective-permute-start(bf16[128,1024]{1,0:T(8,128)(2,1)} %get-tuple-element.16), channel_id=1, source_target_pairs={{0,2},{1,3},{2,0},{3,1},{4,6},{5,7},{6,4},{7,5},{8,10},{9,11},{10,... | collective-permute-start | bytes 786440 | tf_op jit(solution)/shard_map/ppermute | solution.py:326
  58.2 26.6 %slice-start = ((s8[6291456]{0:T(1024)(128)(4,1)}), s8[2097152]{0:T(1024)(128)(4,1)S(1)}, s32[]{:S(2)}) async-start(s8[6291456]{0:T(1024)(128)(4,1)} %bitcast.14), calls=%async_computation.2 | async-start | bytes 4194304
  58.3 35.5 %all-to-all-start.1 = ((bf16[8,256,384]{2,1,0:T(8,128)(2,1)}), bf16[8,256,384]{2,1,0:T(8,128)(2,1)}, u32[]{:S(2)}, u32[]{:S(2)}) async-start(bf16[8,256,384]{2,1,0:T(8,128)(2,1)} %copy-done.5), calls=%async_computation.1 | async-start | bytes 3145728 | tf_op jit(solution)/shard_map/all_to_all | solution.py:347
  63.1 21.7 %slice-start.1 = ((s8[6291456]{0:T(1024)(128)(4,1)}), s8[4194304]{0:T(1024)(128)(4,1)S(1)}, s32[]{:S(2)}) async-start(s8[6291456]{0:T(1024)(128)(4,1)} %bitcast.14), calls=%async_computation.3 | async-start | bytes 8388608
  63.1 2.7 %collective-permute-start.16 = (bf16[128,1024]{1,0:T(8,128)(2,1)}, bf16[128,1024]{1,0:T(8,128)(2,1)S(1)}, u32[]{:S(2)}, u32[]{:S(2)}) collective-permute-start(bf16[128,1024]{1,0:T(8,128)(2,1)} %collective-permute-done.11.refs_6_), channel_id=1, source_target_pairs={{0,1},{1,0},{2,3},{3,2},{4,5},{5,4},{6,7},{7,6},{8,9},{9,8},{10,11... | collective-permute-start | bytes 786440 | tf_op jit(solution)/shard_map/ppermute | solution.py:326
  65.8 1.7 %collective-permute-start.17 = (bf16[128,1024]{1,0:T(8,128)(2,1)}, bf16[128,1024]{1,0:T(8,128)(2,1)S(1)}, u32[]{:S(2)}, u32[]{:S(2)}) collective-permute-start(bf16[128,1024]{1,0:T(8,128)(2,1)} %collective-permute-done.12.refs_7_), channel_id=1, source_target_pairs={{0,1},{1,0},{2,3},{3,2},{4,5},{5,4},{6,7},{7,6},{8,9},{9,8},{10,11... | collective-permute-start | bytes 786440 | tf_op jit(solution)/shard_map/ppermute | solution.py:326
  67.5 1.4 %copy-start.6 = (bf16[8,256,384]{2,1,0:T(8,128)(2,1)S(1)}, bf16[8,256,384]{2,1,0:T(8,128)(2,1)}, u32[]{:S(2)}) copy-start(bf16[8,256,384]{2,1,0:T(8,128)(2,1)} %copy-done.5) | copy-start | bytes 4718596
  68.9 15.9 %copy-start.8 = (bf16[1,256,1024]{2,1,0:T(8,128)(2,1)S(1)}, bf16[1,256,1024]{2,1,0:T(8,128)(2,1)}, u32[]{:S(2)}) copy-start(bf16[1,256,1024]{2,1,0:T(8,128)(2,1)} %param.7) | copy-start | bytes 1572868
  68.9 15.9 %copy-start.10 = (bf16[1,256,1024]{2,1,0:T(8,128)(2,1)S(1)}, bf16[1,256,1024]{2,1,0:T(8,128)(2,1)}, u32[]{:S(2)}) copy-start(bf16[1,256,1024]{2,1,0:T(8,128)(2,1)} %param.8) | copy-start | bytes 1572868
  77.5 11.5 %copy-start.3 = (bf16[1,1024,1024]{2,1,0:T(8,128)(2,1)S(1)}, bf16[1,1024,1024]{2,1,0:T(8,128)(2,1)}, u32[]{:S(2)}) copy-start(bf16[1,1024,1024]{2,1,0:T(8,128)(2,1)} %param.10) | copy-start | bytes 6291460
  77.5 3.7 %collective-permute-start.18 = (bf16[256,128]{1,0:T(8,128)(2,1)S(1)}, bf16[256,128]{1,0:T(8,128)(2,1)S(1)}, u32[]{:S(2)}, u32[]{:S(2)}) collective-permute-start(bf16[256,128]{1,0:T(8,128)(2,1)S(1)} %get-tuple-element.18), channel_id=1, source_target_pairs={{0,1},{1,0},{2,3},{3,2},{4,5},{5,4},{6,7},{7,6},{8,9},{9,8},{10,11... | collective-permute-start | bytes 196616 | tf_op jit(solution)/shard_map/ppermute | solution.py:326
  77.7 6.3 %collective-permute-start.19 = (bf16[256,128]{1,0:T(8,128)(2,1)S(1)}, bf16[256,128]{1,0:T(8,128)(2,1)S(1)}, u32[]{:S(2)}, u32[]{:S(2)}) collective-permute-start(bf16[256,128]{1,0:T(8,128)(2,1)S(1)} %get-tuple-element.19), channel_id=1, source_target_pairs={{0,2},{1,3},{2,0},{3,1},{4,6},{5,7},{6,4},{7,5},{8,10},{9,11},{10,... | collective-permute-start | bytes 196616 | tf_op jit(solution)/shard_map/ppermute | solution.py:326
  79.0 9.1 %collective-permute-start.20 = (bf16[256,128]{1,0:T(8,128)(2,1)S(1)}, bf16[256,128]{1,0:T(8,128)(2,1)S(1)}, u32[]{:S(2)}, u32[]{:S(2)}) collective-permute-start(bf16[256,128]{1,0:T(8,128)(2,1)S(1)} %get-tuple-element.20), channel_id=1, source_target_pairs={{0,3},{1,2},{2,1},{3,0},{4,7},{5,6},{6,5},{7,4},{8,11},{9,10},{10,... | collective-permute-start | bytes 196616 | tf_op jit(solution)/shard_map/ppermute | solution.py:326
  79.4 8.6 %collective-permute-start.21 = (bf16[256,128]{1,0:T(8,128)(2,1)S(1)}, bf16[256,128]{1,0:T(8,128)(2,1)S(1)}, u32[]{:S(2)}, u32[]{:S(2)}) collective-permute-start(bf16[256,128]{1,0:T(8,128)(2,1)S(1)} %get-tuple-element.21), channel_id=1, source_target_pairs={{0,4},{1,5},{2,6},{3,7},{4,0},{5,1},{6,2},{7,3},{8,12},{9,13},{10,... | collective-permute-start | bytes 196616 | tf_op jit(solution)/shard_map/ppermute | solution.py:326
  79.5 8.5 %collective-permute-start.22 = (bf16[256,128]{1,0:T(8,128)(2,1)S(1)}, bf16[256,128]{1,0:T(8,128)(2,1)S(1)}, u32[]{:S(2)}, u32[]{:S(2)}) collective-permute-start(bf16[256,128]{1,0:T(8,128)(2,1)S(1)} %get-tuple-element.22), channel_id=1, source_target_pairs={{0,5},{1,4},{2,7},{3,6},{4,1},{5,0},{6,3},{7,2},{8,13},{9,12},{10,... | collective-permute-start | bytes 196616 | tf_op jit(solution)/shard_map/ppermute | solution.py:326
  81.2 6.8 %collective-permute-start.23 = (bf16[256,128]{1,0:T(8,128)(2,1)S(1)}, bf16[256,128]{1,0:T(8,128)(2,1)S(1)}, u32[]{:S(2)}, u32[]{:S(2)}) collective-permute-start(bf16[256,128]{1,0:T(8,128)(2,1)S(1)} %get-tuple-element.23), channel_id=1, source_target_pairs={{0,6},{1,7},{2,4},{3,5},{4,2},{5,3},{6,0},{7,1},{8,14},{9,15},{10,... | collective-permute-start | bytes 196616 | tf_op jit(solution)/shard_map/ppermute | solution.py:326
  84.0 5.0 %collective-permute-start.24 = (bf16[256,128]{1,0:T(8,128)(2,1)S(1)}, bf16[256,128]{1,0:T(8,128)(2,1)S(1)}, u32[]{:S(2)}, u32[]{:S(2)}) collective-permute-start(bf16[256,128]{1,0:T(8,128)(2,1)S(1)} %get-tuple-element.24), channel_id=1, source_target_pairs={{0,7},{1,6},{2,5},{3,4},{4,3},{5,2},{6,1},{7,0},{8,15},{9,14},{10,... | collective-permute-start | bytes 196616 | tf_op jit(solution)/shard_map/ppermute | solution.py:326
  85.4 2.7 %copy-start = (bf16[3072,1024]{1,0:T(8,128)(2,1)}, bf16[3072,1024]{1,0:T(8,128)(2,1)S(1)}, u32[]{:S(2)}) copy-start(bf16[3072,1024]{1,0:T(8,128)(2,1)S(1)} %get-tuple-element.27.w_ref) | copy-start | bytes 18874372
  88.0 2.2 %copy-start.11 = (bf16[256,1024]{1,0:T(8,128)(2,1)}, bf16[256,1024]{1,0:T(8,128)(2,1)S(1)}, u32[]{:S(2)}) copy-start(bf16[256,1024]{1,0:T(8,128)(2,1)S(1)} %get-tuple-element.26.up_ref) | copy-start | bytes 1572868
  90.3 16.2 %collective-permute-start.25 = (bf16[256,1024]{1,0:T(8,128)(2,1)S(1)}, bf16[256,1024]{1,0:T(8,128)(2,1)S(1)}, u32[]{:S(2)}, u32[]{:S(2)}) collective-permute-start(bf16[256,1024]{1,0:T(8,128)(2,1)S(1)} %shard_map.82), channel_id=1, source_target_pairs={{0,8},{8,16},{16,24},{1,9},{9,17},{17,25},{2,10},{10,18},{18,26},{... | collective-permute-start | bytes 1572872 | tf_op jit(solution)/shard_map/ppermute | solution.py:377
  93.8 2.8 %copy-start.1 = (bf16[3072,1024]{1,0:T(8,128)(2,1)S(1)}, bf16[3072,1024]{1,0:T(8,128)(2,1)}, u32[]{:S(2)}) copy-start(bf16[3072,1024]{1,0:T(8,128)(2,1)} %copy-done) | copy-start | bytes 18874372
  96.5 1.0 copy-start.12
  101.0 15.9 %collective-permute-start.26 = (bf16[256,1024]{1,0:T(8,128)(2,1)S(1)}, bf16[256,1024]{1,0:T(8,128)(2,1)S(1)}, u32[]{:S(2)}, u32[]{:S(2)}) collective-permute-start(bf16[256,1024]{1,0:T(8,128)(2,1)S(1)} %shard_map.84), channel_id=1, source_target_pairs={{8,0},{16,8},{24,16},{9,1},{17,9},{25,17},{10,2},{18,10},{26,18},{... | collective-permute-start | bytes 1572872 | tf_op jit(solution)/shard_map/ppermute | solution.py:377

commit v8 on v7

--- a/solution.py
+++ b/solution.py
@@ -209,12 +209,11 @@
 
 
 def rows_after(arrays, starts, rows, earlier):
-    rows = [rows] * len(arrays) if isinstance(rows, int) else rows
     return pl.pallas_call(
         functools.partial(copy_kernel, starts),
         in_specs=[HBM] * (len(arrays) + len(earlier)),
         out_specs=[VMEM] * len(arrays),
-        out_shape=[jax.ShapeDtypeStruct((n, *a.shape[1:]), a.dtype) for n, a in zip(rows, arrays)],
+        out_shape=[jax.ShapeDtypeStruct((rows, *a.shape[1:]), a.dtype) for a in arrays],
         scratch_shapes=[pltpu.SemaphoreType.DMA((len(arrays),))],
         compiler_params=pltpu.CompilerParams(vmem_limit_bytes=24 * MIB),
         cost_estimate=pl.CostEstimate(flops=MICROSECOND, bytes_accessed=0, transcendentals=0),
@@ -290,34 +289,56 @@
     )
 
 
-def finish_back_kernel(grad_ref, x_ref, up_ref, w_ref, out_ref, total):
-    for c in range(3):
-        grads = jnp.concatenate(
-            [grad_ref[k, :, c * HD : (c + 1) * HD] for k in range(HEADS)], axis=1
-        )
-        product = dot(grads, w_ref[c * HEADS * HD : (c + 1) * HEADS * HD], NN)
-        if c == 0:
+def finish_back_kernel(grad_ref, x_ref, up_ref, w_ref, out_ref, grads, x, up, rows, total, sems):
+    chunks = rows.shape[0]
+    depth = rows.shape[1]
+    held = depth // HD
+    copies = [fetch(grad_ref, grads, sems.at[0])]
+    copies += [
+        fetch(w_ref.at[pl.ds(i * depth, depth)], rows.at[i], sems.at[1 + i]) for i in range(chunks)
+    ]
+    copies.append(fetch(x_ref, x, sems.at[1 + chunks]))
+    copies.append(fetch(up_ref, up, sems.at[2 + chunks]))
+    copies[0].wait()
+    for i in range(chunks):
+        c, first = i * held // HEADS, i * held % HEADS
+        columns = slice(c * HD, (c + 1) * HD)
+        block = jnp.concatenate([grads[first + j, :, columns] for j in range(held)], axis=1)
+        copies[1 + i].wait()
+        product = dot(block, rows[i], NN)
+        if i == 0:
             total[...] = product
         else:
             total[...] += product
-    x = high(x_ref[...])
-    scale = rows_rsqrt(x)
-    unit = x * scale
+    copies[1 + chunks].wait()
+    copies[2 + chunks].wait()
+    stored = high(x[...])
+    scale = rows_rsqrt(stored)
+    unit = stored * scale
     g = total[...]
     pulled = scale * (g - unit * jnp.mean(unit * g, axis=1, keepdims=True))
-    out_ref[...] = low(high(up_ref[...]) + pulled)
+    out_ref[...] = low(high(up[...]) + pulled)
 
 
 def finish_back(grads, stored, upstream, w_qkv):
     tokens, width = stored.shape
+    chunks = 6
     return call(
         finish_back_kernel,
         [grads, stored, upstream, w_qkv],
-        [VMEM] * 4,
+        [HBM] * 4,
         jax.ShapeDtypeStruct((tokens, width), jnp.bfloat16),
-        [pltpu.VMEM((tokens, width), jnp.float32)],
-        2 * tokens * width * 3 * HEADS * HD,
+        [
+            pltpu.VMEM(grads.shape, jnp.bfloat16),
+            pltpu.VMEM((tokens, width), jnp.bfloat16),
+            pltpu.VMEM((tokens, width), jnp.bfloat16),
+            pltpu.VMEM((chunks, w_qkv.shape[0] // chunks, width), jnp.bfloat16),
+            pltpu.VMEM((tokens, width), jnp.float32),
+            pltpu.SemaphoreType.DMA((chunks + 3,)),
+        ],
+        MICROSECOND * 5,
         6 * width * HEADS * HD,
+        grant=58 * MIB,
     )
 
 
@@ -328,13 +349,15 @@
 
 def gather_rows(x, earlier):
     half = x.shape[0] // 2
-    over_x, over_y = partner(x, 2), partner(x, 4)
+    top, bottom = x[:half], x[half:]
+    x_top, y_bottom = partner(top, 2), partner(bottom, 4)
+    x_bottom, y_top = partner(bottom, 2), partner(top, 4)
+    relay_top, relay_bottom = x_top, y_bottom
     if earlier:
-        top, bottom = rows_after([over_x, over_y], [0, half], half, earlier)
-    else:
-        top, bottom = over_x[:half], over_y[half:]
-    top, bottom = partner(top, 4), partner(bottom, 2)
-    pieces = [(0, 0, x), (2, 0, over_x), (4, 0, over_y), (6, 0, top), (6, half, bottom)]
+        relay_top, relay_bottom = rows_after([x_top, y_bottom], [0, 0], half, earlier)
+    far_top, far_bottom = partner(relay_top, 4), partner(relay_bottom, 2)
+    pieces = [(0, 0, x), (2, 0, x_top), (4, half, y_bottom), (2, half, x_bottom)]
+    pieces += [(4, 0, y_top), (6, 0, far_top), (6, half, far_bottom)]
     return pieces + [(k + 1, start, partner(block, 1)) for k, start, block in pieces]
 
 
@@ -419,9 +442,7 @@
         info, tile_cluster, current_pieces, own_head, spacing, earlier=[grads]
     )
     returned = collect_each(outputs)
-    near = [stored, upstream, w_rows]
-    near = rows_after(near, [0] * 3, [a.shape[0] for a in near], outputs[:1])
-    grad_self = finish_back(returned_grads, *near)
+    grad_self = finish_back(returned_grads, stored, upstream, w_rows)
     grad_input = passed_along(grad_self, "pipe", -1)
     result = finish(info, returned, current, w_fin)
     next_input = passed_along(result, "pipe", 1)

time: 121 us -> 114 us (0.942)
  the two profiles are of different devices: /device:TPU:18 before, /device:TPU:0 now
where the time goes in v8:
time: 114 us; the launch traced here: 113 us
  starting transfers between devices  36.1 us (32%)
  waiting for transfers between devices  32.4 us (28%)
  Pallas kernels  31.8 us (28%)
  local copies, waits for them, and re-layouts  12.2 us (11%)
    pallas_call x6, Pallas kernels, call(): pl.pallas_call(kernel, in_specs=in_specs, out_specs=[VMEM] * len(out_shap...  30 us
    ppermute x33, starting transfers between devices, partner(): return lax.ppermute(block, 'seq', route)  22.5 us
    ppermute x33, waiting for transfers between devices, partner(): return lax.ppermute(block, 'seq', route)  17.9 us
    ppermute x2, waiting for transfers between devices, passed_along(): return lax.ppermute(block, axis, route)  14.5 us
    unnamed x38, local copies, waits for them, and re-layouts  9.86 us
    all_to_all x2, starting transfers between devices, all_swap(): lax.all_to_all(blocks, 'seq', split_axis=0, concat_axis=0, tiled=True)  8.76 us
    ppermute x2, starting transfers between devices, passed_along(): return lax.ppermute(block, axis, route)  4.81 us
  transfers between devices with their start and end apart: 37, of which 12 were waited for; matrix products, arithmetic and copies ran while one was open for 1% of the time, Pallas kernels for 28%

profile of v8, /device:TPU:0, one launch (start us, length us, event | category | flops | bytes accessed | tf_op | source)
XLA Modules:
  0.0 113.3 jit_solution(9018334368040614291)
XLA Ops:
  0.6 1.1 slice_bitcast_fusion
  1.7 3.0 %collective-permute-start.2 = (bf16[128,1024]{1,0:T(8,128)(2,1)S(1)}, bf16[128,1024]{1,0:T(8,128)(2,1)S(1)}, u32[]{:S(2)}, u32[]{:S(2)}) collective-permute-start(bf16[128,1024]{1,0:T(8,128)(2,1)S(1)} %get-tuple-element.24), channel_id=1, source_target_pairs={{0,4},{1,5},{2,6},{3,7},{4,0},{5,1},{6,2},{7,3},{8,12},{9,13},{10,... | collective-permute-start | bytes 786440 | tf_op jit(solution)/shard_map/ppermute | solution.py:347
  4.7 1.5 %collective-permute-start.8 = (bf16[128,1024]{1,0:T(8,128)(2,1)S(1)}, bf16[128,1024]{1,0:T(8,128)(2,1)}, u32[]{:S(2)}, u32[]{:S(2)}) collective-permute-start(bf16[128,1024]{1,0:T(8,128)(2,1)S(1)} %get-tuple-element.24), channel_id=1, source_target_pairs={{0,2},{1,3},{2,0},{3,1},{4,6},{5,7},{6,4},{7,5},{8,10},{9,11},{10,... | collective-permute-start | bytes 786440 | tf_op jit(solution)/shard_map/ppermute | solution.py:347
  6.2 0.5 collective-permute-start
  6.8 1.6 %copy-done = bf16[1,1024,1024]{2,1,0:T(8,128)(2,1)S(1)} copy-done((bf16[1,1024,1024]{2,1,0:T(8,128)(2,1)S(1)}, bf16[1,1024,1024]{2,1,0:T(8,128)(2,1)}, u32[]{:S(2)}) %copy-start) | copy-done | bytes 2097176
  8.4 1.0 copy-done.4
  9.5 2.8 %shard_map.77 = bf16[8,256,128]{2,1,0:T(8,128)(2,1)} custom-call(bf16[256,1024]{1,0:T(8,128)(2,1)S(1)} %bitcast.28, bf16[8,128,1024]{2,1,0:T(8,128)(2,1)S(1)} %bitcast.17), custom_call_target="tpu_custom_call" | custom-call | flops 3449999872 | bytes 2097152 | tf_op jit(solution)/shard_map/pallas_call | solution.py:42
  12.3 4.3 %all-to-all-start = ((bf16[8,256,128]{2,1,0:T(8,128)(2,1)}), bf16[8,256,128]{2,1,0:T(8,128)(2,1)S(1)}, u32[]{:S(2)}, u32[]{:S(2)}) async-start(bf16[8,256,128]{2,1,0:T(8,128)(2,1)} %shard_map.77), calls=%async_computation | async-start | bytes 1048576 | tf_op jit(solution)/shard_map/all_to_all | solution.py:370
  16.6 1.5 %collective-permute-done.refs_4_ = bf16[128,1024]{1,0:T(8,128)(2,1)S(1)} collective-permute-done((bf16[128,1024]{1,0:T(8,128)(2,1)S(1)}, bf16[128,1024]{1,0:T(8,128)(2,1)S(1)}, u32[]{:S(2)}, u32[]{:S(2)}) %collective-permute-start) | collective-permute-done | bytes 262176 | tf_op jit(solution)/shard_map/ppermute | solution.py:347
  18.1 0.6 collective-permute-start.1
  18.7 1.5 %collective-permute-start.3 = (bf16[128,1024]{1,0:T(8,128)(2,1)S(1)}, bf16[128,1024]{1,0:T(8,128)(2,1)S(1)}, u32[]{:S(2)}, u32[]{:S(2)}) collective-permute-start(bf16[128,1024]{1,0:T(8,128)(2,1)S(1)} %collective-permute-done.2.refs_5_), channel_id=1, source_target_pairs={{0,2},{1,3},{2,0},{3,1},{4,6},{5,7},{6,4},{7,5},{8,10},{9,11},{10,... | collective-permute-start | bytes 786440 | tf_op jit(solution)/shard_map/ppermute | solution.py:347
  20.2 0.5 collective-permute-start.12
  20.8 0.6 copy-done.9
  21.4 1.2 %constant_dynamic-slice_fusion = bf16[3,1,128,1024]{3,2,1,0:T(8,128)(2,1)S(1)} fusion(bf16[3,8,128,1024]{3,2,1,0:T(8,128)(2,1)} %bitcast.31, s32[]{:T(128)S(6)} %select_n.4), kind=kLoop, calls=%fused_computation.3 | loop fusion | bytes 1572868 | tf_op jit(solution)/shard_map/jit(dynamic_index_in_dim)/dynamic_slice | solution.py:429
  22.6 8.5 %collective-permute-done.1.refs_0_.refs_8_ = bf16[128,1024]{1,0:T(8,128)(2,1)S(1)} collective-permute-done((bf16[128,1024]{1,0:T(8,128)(2,1)S(1)}, bf16[128,1024]{1,0:T(8,128)(2,1)S(1)}, u32[]{:S(2)}, u32[]{:S(2)}) %collective-permute-start.1) | collective-permute-done | bytes 262176 | tf_op jit(solution)/shard_map/ppermute | solution.py:347
  33.0 0.6 collective-permute-start.5
  33.6 1.2 %collective-permute-start.6 = (bf16[128,1024]{1,0:T(8,128)(2,1)S(1)}, bf16[128,1024]{1,0:T(8,128)(2,1)}, u32[]{:S(2)}, u32[]{:S(2)}) collective-permute-start(bf16[128,1024]{1,0:T(8,128)(2,1)S(1)} %get-tuple-element.22), channel_id=1, source_target_pairs={{0,2},{1,3},{2,0},{3,1},{4,6},{5,7},{6,4},{7,5},{8,10},{9,11},{10,... | collective-permute-start | bytes 786440 | tf_op jit(solution)/shard_map/ppermute | solution.py:347
  34.8 0.8 collective-permute-start.4
  35.6 1.4 %collective-permute-start.7 = (bf16[128,1024]{1,0:T(8,128)(2,1)S(1)}, bf16[128,1024]{1,0:T(8,128)(2,1)}, u32[]{:S(2)}, u32[]{:S(2)}) collective-permute-start(bf16[128,1024]{1,0:T(8,128)(2,1)S(1)} %get-tuple-element.23), channel_id=1, source_target_pairs={{0,4},{1,5},{2,6},{3,7},{4,0},{5,1},{6,2},{7,3},{8,12},{9,13},{10,... | collective-permute-start | bytes 786440 | tf_op jit(solution)/shard_map/ppermute | solution.py:347
  37.1 12.3 %shard_map.79.refs_2_.refs_17_ = bf16[8,256,384]{2,1,0:T(8,128)(2,1)} custom-call(s32[16]{0:T(128)S(1)} %copy-done.17, s32[3]{0:T(128)S(1)} %pad_add_fusion.refs_1_.info_ref, bf16[384,1024]{1,0:T(8,128)(2,1)S(1)} %bitcast.22, bf16[256,1024]{1,0:T(8,128)(2,1)S(1)} %bitcast.26, bf16[128,1024]{1,0:T(8,128)(2,1)S(1)} %copy-done.8, ...), custom_call_target="tpu_custom_call" | custom-call | flops 13799999488 | bytes 7340032 | tf_op jit(solution)/shard_map/pallas_call | solution.py:42
  49.3 1.7 %shard_map.80 = (bf16[128,1024]{1,0:T(8,128)(2,1)}, bf16[128,1024]{1,0:T(8,128)(2,1)S(1)}) custom-call(bf16[128,1024]{1,0:T(8,128)(2,1)} %collective-permute-done.4.refs_0_.refs_4_, bf16[128,1024]{1,0:T(8,128)(2,1)} %collective-permute-done.5.refs_1_.refs_5_, bf16[8,256,384]{2,1,0:T(8,128)(2,1)} %shard_map.79.refs_2_.refs_17_), custom_call_target="tpu_custom_call" | custom-call | flops 1150000000 | tf_op jit(solution)/shard_map/pallas_call | solution.py:212
  51.1 0.7 collective-permute-start.17
  51.8 1.2 %collective-permute-start.18 = (bf16[128,1024]{1,0:T(8,128)(2,1)S(1)}, bf16[128,1024]{1,0:T(8,128)(2,1)S(1)}, u32[]{:S(2)}, u32[]{:S(2)}) collective-permute-start(bf16[128,1024]{1,0:T(8,128)(2,1)S(1)} %get-tuple-element.13), channel_id=1, source_target_pairs={{0,2},{1,3},{2,0},{3,1},{4,6},{5,7},{6,4},{7,5},{8,10},{9,11},{10,... | collective-permute-start | bytes 786440 | tf_op jit(solution)/shard_map/ppermute | solution.py:347
  53.5 4.5 %all-to-all-start.1 = ((bf16[8,256,384]{2,1,0:T(8,128)(2,1)}), bf16[8,256,384]{2,1,0:T(8,128)(2,1)}, u32[]{:S(2)}, u32[]{:S(2)}) async-start(bf16[8,256,384]{2,1,0:T(8,128)(2,1)} %shard_map.79.refs_2_.refs_17_), calls=%async_computation.1 | async-start | bytes 3145728 | tf_op jit(solution)/shard_map/all_to_all | solution.py:370
  58.0 2.1 %collective-permute-done.17.refs_8_ = bf16[128,1024]{1,0:T(8,128)(2,1)S(1)} collective-permute-done((bf16[128,1024]{1,0:T(8,128)(2,1)}, bf16[128,1024]{1,0:T(8,128)(2,1)S(1)}, u32[]{:S(2)}, u32[]{:S(2)}) %collective-permute-start.17) | collective-permute-done | bytes 262176 | tf_op jit(solution)/shard_map/ppermute | solution.py:347
  60.6 0.7 copy-done.13
  61.4 0.7 copy-done.15
  62.5 0.7 copy-done.11
  63.7 0.9 copy-done.12
  64.6 0.9 copy-done.14
  65.6 0.9 copy-done.16
  66.5 8.3 %shard_map.81 = (bf16[256,128]{1,0:T(8,128)(2,1)S(1)}, bf16[256,128]{1,0:T(8,128)(2,1)S(1)}, bf16[256,128]{1,0:T(8,128)(2,1)S(1)}, bf16[256,128]{1,0:T(8,128)(2,...) custom-call(s32[16]{0:T(128)S(1)} %copy-done.17, ...), custom_call_target="tpu_custom_call" | custom-call | flops 9200000000 | bytes 5242880 | tf_op jit(solution)/shard_map/pallas_call | solution.py:42
  75.3 1.5 %collective-permute-start.27 = (bf16[256,128]{1,0:T(8,128)(2,1)S(1)}, bf16[256,128]{1,0:T(8,128)(2,1)S(1)}, u32[]{:S(2)}, u32[]{:S(2)}) collective-permute-start(bf16[256,128]{1,0:T(8,128)(2,1)S(1)} %get-tuple-element.16), channel_id=1, source_target_pairs={{0,2},{1,3},{2,0},{3,1},{4,6},{5,7},{6,4},{7,5},{8,10},{9,11},{10,... | collective-permute-start | bytes 196616 | tf_op jit(solution)/shard_map/ppermute | solution.py:347
  76.8 1.4 %collective-permute-start.29 = (bf16[256,128]{1,0:T(8,128)(2,1)S(1)}, bf16[256,128]{1,0:T(8,128)(2,1)S(1)}, u32[]{:S(2)}, u32[]{:S(2)}) collective-permute-start(bf16[256,128]{1,0:T(8,128)(2,1)S(1)} %get-tuple-element.18), channel_id=1, source_target_pairs={{0,4},{1,5},{2,6},{3,7},{4,0},{5,1},{6,2},{7,3},{8,12},{9,13},{10,... | collective-permute-start | bytes 196616 | tf_op jit(solution)/shard_map/ppermute | solution.py:347
  78.2 0.6 collective-permute-start.30
  78.8 2.1 %collective-permute-start.31 = (bf16[256,128]{1,0:T(8,128)(2,1)S(1)}, bf16[256,128]{1,0:T(8,128)(2,1)S(1)}, u32[]{:S(2)}, u32[]{:S(2)}) collective-permute-start(bf16[256,128]{1,0:T(8,128)(2,1)S(1)} %get-tuple-element.20), channel_id=1, source_target_pairs={{0,6},{1,7},{2,4},{3,5},{4,2},{5,3},{6,0},{7,1},{8,14},{9,15},{10,... | collective-permute-start | bytes 196616 | tf_op jit(solution)/shard_map/ppermute | solution.py:347
  81.2 0.5 collective-permute-done.29.refs_4_
  81.8 0.8 collective-permute-done.30.refs_5_
  82.6 1.5 %collective-permute-done.31.refs_6_ = bf16[256,128]{1,0:T(8,128)(2,1)S(1)} collective-permute-done((bf16[256,128]{1,0:T(8,128)(2,1)S(1)}, bf16[256,128]{1,0:T(8,128)(2,1)S(1)}, u32[]{:S(2)}, u32[]{:S(2)}) %collective-permute-start.31) | collective-permute-done | bytes 65568 | tf_op jit(solution)/shard_map/ppermute | solution.py:347
  84.0 2.0 %collective-permute-done.32.refs_7_ = bf16[256,128]{1,0:T(8,128)(2,1)S(1)} collective-permute-done((bf16[256,128]{1,0:T(8,128)(2,1)S(1)}, bf16[256,128]{1,0:T(8,128)(2,1)S(1)}, u32[]{:S(2)}, u32[]{:S(2)}) %collective-permute-start.32) | collective-permute-done | bytes 65568 | tf_op jit(solution)/shard_map/ppermute | solution.py:347
  86.0 1.3 %shard_map.82 = bf16[256,1024]{1,0:T(8,128)(2,1)S(1)} custom-call(s32[3]{0:T(128)S(1)} %pad_add_fusion.refs_1_.info_ref, bf16[256,128]{1,0:T(8,128)(2,1)S(1)} %get-tuple-element.14.refs_0_, bf16[256,128]{1,0:T(8,128)(2,1)S(1)} %collective-permute-done.26.refs_1_, bf16[256,128]{1,0:T(8,128)(2,1)S(1)} %collective-permute-done.27.refs_2_, ...), custom_call_target="tpu_custom_call" | custom-call | flops 536870912 | bytes 2097152 | tf_op jit(solution)/shard_map/pallas_call | solution.py:42
  87.3 3.5 %collective-permute-start.33 = (bf16[256,1024]{1,0:T(8,128)(2,1)S(1)}, bf16[256,1024]{1,0:T(8,128)(2,1)S(1)}, u32[]{:S(2)}, u32[]{:S(2)}) collective-permute-start(bf16[256,1024]{1,0:T(8,128)(2,1)S(1)} %shard_map.82), channel_id=1, source_target_pairs={{0,8},{8,16},{16,24},{1,9},{9,17},{17,25},{2,10},{10,18},{18,26},{... | collective-permute-start | bytes 1572872 | tf_op jit(solution)/shard_map/ppermute | solution.py:400
  90.8 5.1 %shard_map.83 = bf16[256,1024]{1,0:T(8,128)(2,1)} custom-call(bf16[8,256,384]{2,1,0:T(8,128)(2,1)} %all-to-all-done.1.grad_ref, bf16[256,1024]{1,0:T(8,128)(2,1)} %bitcast.24, bf16[256,1024]{1,0:T(8,128)(2,1)} %bitcast.27, bf16[3072,1024]{1,0:T(8,128)(2,1)} %bitcast.32), custom_call_target="tpu_custom_call" | custom-call | flops 5750000128 | bytes 6291456 | tf_op jit(solution)/shard_map/pallas_call | solution.py:42
  96.0 1.3 %collective-permute-start.34 = (bf16[256,1024]{1,0:T(8,128)(2,1)}, bf16[256,1024]{1,0:T(8,128)(2,1)S(1)}, u32[]{:S(2)}, u32[]{:S(2)}) collective-permute-start(bf16[256,1024]{1,0:T(8,128)(2,1)} %shard_map.83), channel_id=1, source_target_pairs={{8,0},{16,8},{24,16},{9,1},{17,9},{25,17},{10,2},{18,10},{26,18},{... | collective-permute-start | bytes 1572872 | tf_op jit(solution)/shard_map/ppermute | solution.py:400
  97.3 5.0 %collective-permute-done.33 = bf16[256,1024]{1,0:T(8,128)(2,1)S(1)} collective-permute-done((bf16[256,1024]{1,0:T(8,128)(2,1)S(1)}, bf16[256,1024]{1,0:T(8,128)(2,1)S(1)}, u32[]{:S(2)}, u32[]{:S(2)}) %collective-permute-start.33) | collective-permute-done | bytes 524320 | tf_op jit(solution)/shard_map/ppermute | solution.py:400
  102.2 9.5 %collective-permute-done.34 = bf16[256,1024]{1,0:T(8,128)(2,1)S(1)} collective-permute-done((bf16[256,1024]{1,0:T(8,128)(2,1)}, bf16[256,1024]{1,0:T(8,128)(2,1)S(1)}, u32[]{:S(2)}, u32[]{:S(2)}) %collective-permute-start.34) | collective-permute-done | bytes 524320 | tf_op jit(solution)/shard_map/ppermute | solution.py:400
  111.7 0.8 copy.12
  112.5 0.8 copy.13
  (75 shorter events, 4.8 us)
Async XLA Ops:
  1.7 17.0 %collective-permute-start.2 = (bf16[128,1024]{1,0:T(8,128)(2,1)S(1)}, bf16[128,1024]{1,0:T(8,128)(2,1)S(1)}, u32[]{:S(2)}, u32[]{:S(2)}) collective-permute-start(bf16[128,1024]{1,0:T(8,128)(2,1)S(1)} %get-tuple-element.24), channel_id=1, source_target_pairs={{0,4},{1,5},{2,6},{3,7},{4,0},{5,1},{6,2},{7,3},{8,12},{9,13},{10,... | collective-permute-start | bytes 786440 | tf_op jit(solution)/shard_map/ppermute | solution.py:347
  4.7 15.5 %collective-permute-start.8 = (bf16[128,1024]{1,0:T(8,128)(2,1)S(1)}, bf16[128,1024]{1,0:T(8,128)(2,1)}, u32[]{:S(2)}, u32[]{:S(2)}) collective-permute-start(bf16[128,1024]{1,0:T(8,128)(2,1)S(1)} %get-tuple-element.24), channel_id=1, source_target_pairs={{0,2},{1,3},{2,0},{3,1},{4,6},{5,7},{6,4},{7,5},{8,10},{9,11},{10,... | collective-permute-start | bytes 786440 | tf_op jit(solution)/shard_map/ppermute | solution.py:347
  6.2 11.9 %collective-permute-start = (bf16[128,1024]{1,0:T(8,128)(2,1)S(1)}, bf16[128,1024]{1,0:T(8,128)(2,1)S(1)}, u32[]{:S(2)}, u32[]{:S(2)}) collective-permute-start(bf16[128,1024]{1,0:T(8,128)(2,1)S(1)} %get-tuple-element.25), channel_id=1, source_target_pairs={{0,2},{1,3},{2,0},{3,1},{4,6},{5,7},{6,4},{7,5},{8,10},{9,11},{10,... | collective-permute-start | bytes 786440 | tf_op jit(solution)/shard_map/ppermute | solution.py:347
  6.8 14.0 %collective-permute-start.9 = (bf16[128,1024]{1,0:T(8,128)(2,1)S(1)}, bf16[128,1024]{1,0:T(8,128)(2,1)S(1)}, u32[]{:S(2)}, u32[]{:S(2)}) collective-permute-start(bf16[128,1024]{1,0:T(8,128)(2,1)S(1)} %get-tuple-element.25), channel_id=1, source_target_pairs={{0,4},{1,5},{2,6},{3,7},{4,0},{5,1},{6,2},{7,3},{8,12},{9,13},{10,... | collective-permute-start | bytes 786440 | tf_op jit(solution)/shard_map/ppermute | solution.py:347
  6.8 1.6 %copy-start = (bf16[1,1024,1024]{2,1,0:T(8,128)(2,1)S(1)}, bf16[1,1024,1024]{2,1,0:T(8,128)(2,1)}, u32[]{:S(2)}) copy-start(bf16[1,1024,1024]{2,1,0:T(8,128)(2,1)} %param.10) | copy-start | bytes 6291460
  8.4 1.0 copy-start.4
  9.5 11.2 %copy-start.3 = (bf16[1,256,1024]{2,1,0:T(8,128)(2,1)S(1)}, bf16[1,256,1024]{2,1,0:T(8,128)(2,1)}, u32[]{:S(2)}) copy-start(bf16[1,256,1024]{2,1,0:T(8,128)(2,1)} %param.7) | copy-start | bytes 1572868
  12.3 19.9 %copy-start.2 = (bf16[1,256,1024]{2,1,0:T(8,128)(2,1)S(1)}, bf16[1,256,1024]{2,1,0:T(8,128)(2,1)}, u32[]{:S(2)}) copy-start(bf16[1,256,1024]{2,1,0:T(8,128)(2,1)} %param.6) | copy-start | bytes 1572868
  12.3 19.9 %all-to-all-start = ((bf16[8,256,128]{2,1,0:T(8,128)(2,1)}), bf16[8,256,128]{2,1,0:T(8,128)(2,1)S(1)}, u32[]{:S(2)}, u32[]{:S(2)}) async-start(bf16[8,256,128]{2,1,0:T(8,128)(2,1)} %shard_map.77), calls=%async_computation | async-start | bytes 1048576 | tf_op jit(solution)/shard_map/all_to_all | solution.py:370
  18.1 14.1 %copy-start.7 = (bf16[128,1024]{1,0:T(8,128)(2,1)}, bf16[128,1024]{1,0:T(8,128)(2,1)S(1)}, u32[]{:S(2)}) copy-start(bf16[128,1024]{1,0:T(8,128)(2,1)S(1)} %collective-permute-done.refs_4_) | copy-start | bytes 786436
  18.1 13.0 %collective-permute-start.1 = (bf16[128,1024]{1,0:T(8,128)(2,1)S(1)}, bf16[128,1024]{1,0:T(8,128)(2,1)S(1)}, u32[]{:S(2)}, u32[]{:S(2)}) collective-permute-start(bf16[128,1024]{1,0:T(8,128)(2,1)S(1)} %collective-permute-done.refs_4_), channel_id=1, source_target_pairs={{0,4},{1,5},{2,6},{3,7},{4,0},{5,1},{6,2},{7,3},{8,12},{9,13},{10,... | collective-permute-start | bytes 786440 | tf_op jit(solution)/shard_map/ppermute | solution.py:347
  18.7 13.5 %copy-start.5 = (bf16[128,1024]{1,0:T(8,128)(2,1)}, bf16[128,1024]{1,0:T(8,128)(2,1)S(1)}, u32[]{:S(2)}) copy-start(bf16[128,1024]{1,0:T(8,128)(2,1)S(1)} %collective-permute-done.2.refs_5_) | copy-start | bytes 786436
  18.7 12.4 %collective-permute-start.3 = (bf16[128,1024]{1,0:T(8,128)(2,1)S(1)}, bf16[128,1024]{1,0:T(8,128)(2,1)S(1)}, u32[]{:S(2)}, u32[]{:S(2)}) collective-permute-start(bf16[128,1024]{1,0:T(8,128)(2,1)S(1)} %collective-permute-done.2.refs_5_), channel_id=1, source_target_pairs={{0,2},{1,3},{2,0},{3,1},{4,6},{5,7},{6,4},{7,5},{8,10},{9,11},{10,... | collective-permute-start | bytes 786440 | tf_op jit(solution)/shard_map/ppermute | solution.py:347
  20.2 11.4 %collective-permute-start.11 = (bf16[128,1024]{1,0:T(8,128)(2,1)S(1)}, bf16[128,1024]{1,0:T(8,128)(2,1)}, u32[]{:S(2)}, u32[]{:S(2)}) collective-permute-start(bf16[128,1024]{1,0:T(8,128)(2,1)S(1)} %collective-permute-done.refs_4_), channel_id=1, source_target_pairs={{0,1},{1,0},{2,3},{3,2},{4,5},{5,4},{6,7},{7,6},{8,9},{9,8},{10,11... | collective-permute-start | bytes 786440 | tf_op jit(solution)/shard_map/ppermute | solution.py:347
  20.2 11.5 %collective-permute-start.12 = (bf16[128,1024]{1,0:T(8,128)(2,1)S(1)}, bf16[128,1024]{1,0:T(8,128)(2,1)}, u32[]{:S(2)}, u32[]{:S(2)}) collective-permute-start(bf16[128,1024]{1,0:T(8,128)(2,1)S(1)} %collective-permute-done.2.refs_5_), channel_id=1, source_target_pairs={{0,1},{1,0},{2,3},{3,2},{4,5},{5,4},{6,7},{7,6},{8,9},{9,8},{10,11... | collective-permute-start | bytes 786440 | tf_op jit(solution)/shard_map/ppermute | solution.py:347
  20.7 14.1 %collective-permute-start.10 = (bf16[256,1024]{1,0:T(8,128)(2,1)S(1)}, bf16[256,1024]{1,0:T(8,128)(2,1)}, u32[]{:S(2)}, u32[]{:S(2)}) collective-permute-start(bf16[256,1024]{1,0:T(8,128)(2,1)S(1)} %bitcast.25), channel_id=1, source_target_pairs={{0,1},{1,0},{2,3},{3,2},{4,5},{5,4},{6,7},{7,6},{8,9},{9,8},{10,11... | collective-permute-start | bytes 1572872 | tf_op jit(solution)/shard_map/ppermute | solution.py:347
  21.4 15.6 %copy-start.17 = (s32[16]{0:T(128)S(1)}, s32[16]{0:T(128)}, u32[]{:S(2)}) copy-start(s32[16]{0:T(128)} %refs_0_.3) | copy-start | bytes 196
  31.1 1.9 %collective-permute-start.13 = (bf16[128,1024]{1,0:T(8,128)(2,1)}, bf16[128,1024]{1,0:T(8,128)(2,1)}, u32[]{:S(2)}, u32[]{:S(2)}) collective-permute-start(bf16[128,1024]{1,0:T(8,128)(2,1)} %collective-permute-done.8.refs_6_), channel_id=1, source_target_pairs={{0,1},{1,0},{2,3},{3,2},{4,5},{5,4},{6,7},{7,6},{8,9},{9,8},{10,11... | collective-permute-start | bytes 786440 | tf_op jit(solution)/shard_map/ppermute | solution.py:347
  31.1 2.5 %collective-permute-start.14 = (bf16[128,1024]{1,0:T(8,128)(2,1)}, bf16[128,1024]{1,0:T(8,128)(2,1)}, u32[]{:S(2)}, u32[]{:S(2)}) collective-permute-start(bf16[128,1024]{1,0:T(8,128)(2,1)} %copy-done.9), channel_id=1, source_target_pairs={{0,1},{1,0},{2,3},{3,2},{4,5},{5,4},{6,7},{7,6},{8,9},{9,8},{10,11... | collective-permute-start | bytes 786440 | tf_op jit(solution)/shard_map/ppermute | solution.py:347
  31.6 4.0 %collective-permute-start.15 = (bf16[128,1024]{1,0:T(8,128)(2,1)S(1)}, bf16[128,1024]{1,0:T(8,128)(2,1)}, u32[]{:S(2)}, u32[]{:S(2)}) collective-permute-start(bf16[128,1024]{1,0:T(8,128)(2,1)S(1)} %collective-permute-done.1.refs_0_.refs_8_), channel_id=1, source_target_pairs={{0,1},{1,0},{2,3},{3,2},{4,5},{5,4},{6,7},{7,6},{8,9},{9,8},{10,11... | collective-permute-start | bytes 786440 | tf_op jit(solution)/shard_map/ppermute | solution.py:347
  31.7 5.4 %collective-permute-start.16 = (bf16[128,1024]{1,0:T(8,128)(2,1)S(1)}, bf16[128,1024]{1,0:T(8,128)(2,1)}, u32[]{:S(2)}, u32[]{:S(2)}) collective-permute-start(bf16[128,1024]{1,0:T(8,128)(2,1)S(1)} %collective-permute-done.3.refs_1_.refs_9_), channel_id=1, source_target_pairs={{0,1},{1,0},{2,3},{3,2},{4,5},{5,4},{6,7},{7,6},{8,9},{9,8},{10,11... | collective-permute-start | bytes 786440 | tf_op jit(solution)/shard_map/ppermute | solution.py:347
  32.2 4.8 %copy-start.10 = (bf16[128,1024]{1,0:T(8,128)(2,1)S(1)}, bf16[128,1024]{1,0:T(8,128)(2,1)}, u32[]{:S(2)}) copy-start(bf16[128,1024]{1,0:T(8,128)(2,1)} %copy-done.9) | copy-start | bytes 786436
  32.2 4.8 %copy-start.6 = (bf16[128,1024]{1,0:T(8,128)(2,1)S(1)}, bf16[128,1024]{1,0:T(8,128)(2,1)}, u32[]{:S(2)}) copy-start(bf16[128,1024]{1,0:T(8,128)(2,1)} %copy-done.5) | copy-start | bytes 786436
  32.2 4.8 %copy-start.8 = (bf16[128,1024]{1,0:T(8,128)(2,1)S(1)}, bf16[128,1024]{1,0:T(8,128)(2,1)}, u32[]{:S(2)}) copy-start(bf16[128,1024]{1,0:T(8,128)(2,1)} %copy-done.7) | copy-start | bytes 786436
  33.0 16.4 %collective-permute-start.5 = (bf16[128,1024]{1,0:T(8,128)(2,1)S(1)}, bf16[128,1024]{1,0:T(8,128)(2,1)}, u32[]{:S(2)}, u32[]{:S(2)}) collective-permute-start(bf16[128,1024]{1,0:T(8,128)(2,1)S(1)} %get-tuple-element.22), channel_id=1, source_target_pairs={{0,4},{1,5},{2,6},{3,7},{4,0},{5,1},{6,2},{7,3},{8,12},{9,13},{10,... | collective-permute-start | bytes 786440 | tf_op jit(solution)/shard_map/ppermute | solution.py:347
  33.6 19.4 %collective-permute-start.6 = (bf16[128,1024]{1,0:T(8,128)(2,1)S(1)}, bf16[128,1024]{1,0:T(8,128)(2,1)}, u32[]{:S(2)}, u32[]{:S(2)}) collective-permute-start(bf16[128,1024]{1,0:T(8,128)(2,1)S(1)} %get-tuple-element.22), channel_id=1, source_target_pairs={{0,2},{1,3},{2,0},{3,1},{4,6},{5,7},{6,4},{7,5},{8,10},{9,11},{10,... | collective-permute-start | bytes 786440 | tf_op jit(solution)/shard_map/ppermute | solution.py:347
  34.8 14.5 %collective-permute-start.4 = (bf16[128,1024]{1,0:T(8,128)(2,1)S(1)}, bf16[128,1024]{1,0:T(8,128)(2,1)}, u32[]{:S(2)}, u32[]{:S(2)}) collective-permute-start(bf16[128,1024]{1,0:T(8,128)(2,1)S(1)} %get-tuple-element.23), channel_id=1, source_target_pairs={{0,2},{1,3},{2,0},{3,1},{4,6},{5,7},{6,4},{7,5},{8,10},{9,11},{10,... | collective-permute-start | bytes 786440 | tf_op jit(solution)/shard_map/ppermute | solution.py:347
  35.6 17.4 %collective-permute-start.7 = (bf16[128,1024]{1,0:T(8,128)(2,1)S(1)}, bf16[128,1024]{1,0:T(8,128)(2,1)}, u32[]{:S(2)}, u32[]{:S(2)}) collective-permute-start(bf16[128,1024]{1,0:T(8,128)(2,1)S(1)} %get-tuple-element.23), channel_id=1, source_target_pairs={{0,4},{1,5},{2,6},{3,7},{4,0},{5,1},{6,2},{7,3},{8,12},{9,13},{10,... | collective-permute-start | bytes 786440 | tf_op jit(solution)/shard_map/ppermute | solution.py:347
  37.0 26.2 %collective-permute-start.19 = (bf16[256,1024]{1,0:T(8,128)(2,1)S(1)}, bf16[256,1024]{1,0:T(8,128)(2,1)}, u32[]{:S(2)}, u32[]{:S(2)}) collective-permute-start(bf16[256,1024]{1,0:T(8,128)(2,1)S(1)} %shard_map.78.refs_18_.refs_3_), channel_id=1, source_target_pairs={{0,1},{1,0},{2,3},{3,2},{4,5},{5,4},{6,7},{7,6},{8,9},{9,8},{10,11... | collective-permute-start | bytes 1572872 | tf_op jit(solution)/shard_map/ppermute | solution.py:347
  51.1 9.0 %collective-permute-start.17 = (bf16[128,1024]{1,0:T(8,128)(2,1)}, bf16[128,1024]{1,0:T(8,128)(2,1)S(1)}, u32[]{:S(2)}, u32[]{:S(2)}) collective-permute-start(bf16[128,1024]{1,0:T(8,128)(2,1)} %get-tuple-element.12), channel_id=1, source_target_pairs={{0,4},{1,5},{2,6},{3,7},{4,0},{5,1},{6,2},{7,3},{8,12},{9,13},{10,... | collective-permute-start | bytes 786440 | tf_op jit(solution)/shard_map/ppermute | solution.py:347
  51.8 8.4 %collective-permute-start.18 = (bf16[128,1024]{1,0:T(8,128)(2,1)S(1)}, bf16[128,1024]{1,0:T(8,128)(2,1)S(1)}, u32[]{:S(2)}, u32[]{:S(2)}) collective-permute-start(bf16[128,1024]{1,0:T(8,128)(2,1)S(1)} %get-tuple-element.13), channel_id=1, source_target_pairs={{0,2},{1,3},{2,0},{3,1},{4,6},{5,7},{6,4},{7,5},{8,10},{9,11},{10,... | collective-permute-start | bytes 786440 | tf_op jit(solution)/shard_map/ppermute | solution.py:347
  53.0 7.6 %collective-permute-start.20 = (bf16[128,1024]{1,0:T(8,128)(2,1)}, bf16[128,1024]{1,0:T(8,128)(2,1)S(1)}, u32[]{:S(2)}, u32[]{:S(2)}) collective-permute-start(bf16[128,1024]{1,0:T(8,128)(2,1)} %collective-permute-done.4.refs_0_.refs_4_), channel_id=1, source_target_pairs={{0,1},{1,0},{2,3},{3,2},{4,5},{5,4},{6,7},{7,6},{8,9},{9,8},{10,11... | collective-permute-start | bytes 786440 | tf_op jit(solution)/shard_map/ppermute | solution.py:347
  53.0 8.4 %collective-permute-start.21 = (bf16[128,1024]{1,0:T(8,128)(2,1)}, bf16[128,1024]{1,0:T(8,128)(2,1)S(1)}, u32[]{:S(2)}, u32[]{:S(2)}) collective-permute-start(bf16[128,1024]{1,0:T(8,128)(2,1)} %collective-permute-done.5.refs_1_.refs_5_), channel_id=1, source_target_pairs={{0,1},{1,0},{2,3},{3,2},{4,5},{5,4},{6,7},{7,6},{8,9},{9,8},{10,11... | collective-permute-start | bytes 786440 | tf_op jit(solution)/shard_map/ppermute | solution.py:347
  53.5 37.3 %all-to-all-start.1 = ((bf16[8,256,384]{2,1,0:T(8,128)(2,1)}), bf16[8,256,384]{2,1,0:T(8,128)(2,1)}, u32[]{:S(2)}, u32[]{:S(2)}) async-start(bf16[8,256,384]{2,1,0:T(8,128)(2,1)} %shard_map.79.refs_2_.refs_17_), calls=%async_computation.1 | async-start | bytes 3145728 | tf_op jit(solution)/shard_map/all_to_all | solution.py:370
  58.0 28.0 %copy-start.1 = (bf16[1,1024,1024]{2,1,0:T(8,128)(2,1)S(1)}, bf16[1,1024,1024]{2,1,0:T(8,128)(2,1)}, u32[]{:S(2)}) copy-start(bf16[1,1024,1024]{2,1,0:T(8,128)(2,1)} %param.10) | copy-start | bytes 6291460
  60.1 3.2 %collective-permute-start.22 = (bf16[128,1024]{1,0:T(8,128)(2,1)}, bf16[128,1024]{1,0:T(8,128)(2,1)S(1)}, u32[]{:S(2)}, u32[]{:S(2)}) collective-permute-start(bf16[128,1024]{1,0:T(8,128)(2,1)} %collective-permute-done.6.refs_6_), channel_id=1, source_target_pairs={{0,1},{1,0},{2,3},{3,2},{4,5},{5,4},{6,7},{7,6},{8,9},{9,8},{10,11... | collective-permute-start | bytes 786440 | tf_op jit(solution)/shard_map/ppermute | solution.py:347
  60.2 3.0 %collective-permute-start.23 = (bf16[128,1024]{1,0:T(8,128)(2,1)}, bf16[128,1024]{1,0:T(8,128)(2,1)S(1)}, u32[]{:S(2)}, u32[]{:S(2)}) collective-permute-start(bf16[128,1024]{1,0:T(8,128)(2,1)} %collective-permute-done.7.refs_7_), channel_id=1, source_target_pairs={{0,1},{1,0},{2,3},{3,2},{4,5},{5,4},{6,7},{7,6},{8,9},{9,8},{10,11... | collective-permute-start | bytes 786440 | tf_op jit(solution)/shard_map/ppermute | solution.py:347
  61.3 2.0 %collective-permute-start.24 = (bf16[128,1024]{1,0:T(8,128)(2,1)S(1)}, bf16[128,1024]{1,0:T(8,128)(2,1)S(1)}, u32[]{:S(2)}, u32[]{:S(2)}) collective-permute-start(bf16[128,1024]{1,0:T(8,128)(2,1)S(1)} %collective-permute-done.17.refs_8_), channel_id=1, source_target_pairs={{0,1},{1,0},{2,3},{3,2},{4,5},{5,4},{6,7},{7,6},{8,9},{9,8},{10,11... | collective-permute-start | bytes 786440 | tf_op jit(solution)/shard_map/ppermute | solution.py:347
  62.2 1.5 %collective-permute-start.25 = (bf16[128,1024]{1,0:T(8,128)(2,1)S(1)}, bf16[128,1024]{1,0:T(8,128)(2,1)S(1)}, u32[]{:S(2)}, u32[]{:S(2)}) collective-permute-start(bf16[128,1024]{1,0:T(8,128)(2,1)S(1)} %collective-permute-done.18.refs_9_), channel_id=1, source_target_pairs={{0,1},{1,0},{2,3},{3,2},{4,5},{5,4},{6,7},{7,6},{8,9},{9,8},{10,11... | collective-permute-start | bytes 786440 | tf_op jit(solution)/shard_map/ppermute | solution.py:347
  74.9 3.9 %collective-permute-start.26 = (bf16[256,128]{1,0:T(8,128)(2,1)S(1)}, bf16[256,128]{1,0:T(8,128)(2,1)S(1)}, u32[]{:S(2)}, u32[]{:S(2)}) collective-permute-start(bf16[256,128]{1,0:T(8,128)(2,1)S(1)} %get-tuple-element.15), channel_id=1, source_target_pairs={{0,1},{1,0},{2,3},{3,2},{4,5},{5,4},{6,7},{7,6},{8,9},{9,8},{10,11... | collective-permute-start | bytes 196616 | tf_op jit(solution)/shard_map/ppermute | solution.py:347
  75.3 5.6 %collective-permute-start.27 = (bf16[256,128]{1,0:T(8,128)(2,1)S(1)}, bf16[256,128]{1,0:T(8,128)(2,1)S(1)}, u32[]{:S(2)}, u32[]{:S(2)}) collective-permute-start(bf16[256,128]{1,0:T(8,128)(2,1)S(1)} %get-tuple-element.16), channel_id=1, source_target_pairs={{0,2},{1,3},{2,0},{3,1},{4,6},{5,7},{6,4},{7,5},{8,10},{9,11},{10,... | collective-permute-start | bytes 196616 | tf_op jit(solution)/shard_map/ppermute | solution.py:347
  76.8 4.5 %collective-permute-start.28 = (bf16[256,128]{1,0:T(8,128)(2,1)S(1)}, bf16[256,128]{1,0:T(8,128)(2,1)S(1)}, u32[]{:S(2)}, u32[]{:S(2)}) collective-permute-start(bf16[256,128]{1,0:T(8,128)(2,1)S(1)} %get-tuple-element.17), channel_id=1, source_target_pairs={{0,3},{1,2},{2,1},{3,0},{4,7},{5,6},{6,5},{7,4},{8,11},{9,10},{10,... | collective-permute-start | bytes 196616 | tf_op jit(solution)/shard_map/ppermute | solution.py:347
  76.8 4.9 %collective-permute-start.29 = (bf16[256,128]{1,0:T(8,128)(2,1)S(1)}, bf16[256,128]{1,0:T(8,128)(2,1)S(1)}, u32[]{:S(2)}, u32[]{:S(2)}) collective-permute-start(bf16[256,128]{1,0:T(8,128)(2,1)S(1)} %get-tuple-element.18), channel_id=1, source_target_pairs={{0,4},{1,5},{2,6},{3,7},{4,0},{5,1},{6,2},{7,3},{8,12},{9,13},{10,... | collective-permute-start | bytes 196616 | tf_op jit(solution)/shard_map/ppermute | solution.py:347
  78.2 4.4 %collective-permute-start.30 = (bf16[256,128]{1,0:T(8,128)(2,1)S(1)}, bf16[256,128]{1,0:T(8,128)(2,1)S(1)}, u32[]{:S(2)}, u32[]{:S(2)}) collective-permute-start(bf16[256,128]{1,0:T(8,128)(2,1)S(1)} %get-tuple-element.19), channel_id=1, source_target_pairs={{0,5},{1,4},{2,7},{3,6},{4,1},{5,0},{6,3},{7,2},{8,13},{9,12},{10,... | collective-permute-start | bytes 196616 | tf_op jit(solution)/shard_map/ppermute | solution.py:347
  78.8 5.2 %collective-permute-start.31 = (bf16[256,128]{1,0:T(8,128)(2,1)S(1)}, bf16[256,128]{1,0:T(8,128)(2,1)S(1)}, u32[]{:S(2)}, u32[]{:S(2)}) collective-permute-start(bf16[256,128]{1,0:T(8,128)(2,1)S(1)} %get-tuple-element.20), channel_id=1, source_target_pairs={{0,6},{1,7},{2,4},{3,5},{4,2},{5,3},{6,0},{7,1},{8,14},{9,15},{10,... | collective-permute-start | bytes 196616 | tf_op jit(solution)/shard_map/ppermute | solution.py:347
  81.0 5.0 %collective-permute-start.32 = (bf16[256,128]{1,0:T(8,128)(2,1)S(1)}, bf16[256,128]{1,0:T(8,128)(2,1)S(1)}, u32[]{:S(2)}, u32[]{:S(2)}) collective-permute-start(bf16[256,128]{1,0:T(8,128)(2,1)S(1)} %get-tuple-element.21), channel_id=1, source_target_pairs={{0,7},{1,6},{2,5},{3,4},{4,3},{5,2},{6,1},{7,0},{8,15},{9,14},{10,... | collective-permute-start | bytes 196616 | tf_op jit(solution)/shard_map/ppermute | solution.py:347
  87.3 14.9 %collective-permute-start.33 = (bf16[256,1024]{1,0:T(8,128)(2,1)S(1)}, bf16[256,1024]{1,0:T(8,128)(2,1)S(1)}, u32[]{:S(2)}, u32[]{:S(2)}) collective-permute-start(bf16[256,1024]{1,0:T(8,128)(2,1)S(1)} %shard_map.82), channel_id=1, source_target_pairs={{0,8},{8,16},{16,24},{1,9},{9,17},{17,25},{2,10},{10,18},{18,26},{... | collective-permute-start | bytes 1572872 | tf_op jit(solution)/shard_map/ppermute | solution.py:400
  96.0 15.8 %collective-permute-start.34 = (bf16[256,1024]{1,0:T(8,128)(2,1)}, bf16[256,1024]{1,0:T(8,128)(2,1)S(1)}, u32[]{:S(2)}, u32[]{:S(2)}) collective-permute-start(bf16[256,1024]{1,0:T(8,128)(2,1)} %shard_map.83), channel_id=1, source_target_pairs={{8,0},{16,8},{24,16},{9,1},{17,9},{25,17},{10,2},{18,10},{26,18},{... | collective-permute-start | bytes 1572872 | tf_op jit(solution)/shard_map/ppermute | solution.py:400
  (7 other events, 5.7 us)

commit v9 on v6

--- a/solution.py
+++ b/solution.py
@@ -42,7 +42,7 @@
     return pl.pallas_call(
         kernel,
         in_specs=in_specs,
-        out_specs=VMEM,
+        out_specs=[VMEM] * len(out_shape) if isinstance(out_shape, list) else VMEM,
         out_shape=out_shape,
         scratch_shapes=scratch,
         compiler_params=pltpu.CompilerParams(vmem_limit_bytes=grant),
@@ -106,9 +106,10 @@
     refs = refs[3 + len(pieces) :]
     if back:
         grads, refs = refs[0], refs[1:]
-    out, kept, count, member = refs[unread : unread + 4]
+    refs = refs[unread:]
+    out_refs, (kept, out, count, member) = refs[:HEADS], refs[HEADS : HEADS + 4]
     if back:
-        scales = refs[unread + 4]
+        scales = refs[HEADS + 4]
     flip, residue = info_ref[0], info_ref[2]
     tiles = kept.shape[0]
     clusters = count.shape[0]
@@ -158,6 +159,8 @@
         return carry
 
     lax.fori_loop(0, clusters, visit, 0)
+    for k in range(HEADS):
+        out_refs[k][...] = out[pl.ds(2 * (flip ^ k), 2)].reshape(out_refs[k].shape)
 
 
 def head_work(info, tile_cluster, pieces, weights, spacing, grads=None, earlier=()):
@@ -171,23 +174,22 @@
         operands.append(grads.reshape(tiles, TILE, HD))
     scratch = [
         pltpu.VMEM((tiles, TILE, 3 * HD), jnp.bfloat16),
+        pltpu.VMEM((tiles, TILE, wide), jnp.bfloat16),
         pltpu.SMEM((tiles // 2,), jnp.int32),
         pltpu.SMEM((tiles // 2 * CAPACITY,), jnp.int32),
     ]
     if back:
         scratch.append(pltpu.VMEM((tiles, TILE, 2 * HD), jnp.float32))
     shapes = tuple((k, start, array.shape[0]) for k, start, array in pieces)
-    out = call(
+    return call(
         functools.partial(head_kernel, back, len(earlier), shapes, spacing),
         operands + list(earlier),
         [SMEM, SMEM] + [VMEM] * (len(operands) - 2) + [HBM] * len(earlier),
-        jax.ShapeDtypeStruct((tiles, TILE, wide), jnp.bfloat16),
+        [jax.ShapeDtypeStruct((2 * TILE, wide), jnp.bfloat16) for _ in range(HEADS)],
         scratch,
         MICROSECOND * (12 if back else 8),
         2 * tokens * (width + 2 * wide),
     )
-    return out.reshape(HEADS, 2 * TILE, wide)
-
 
 def copy_kernel(starts, *refs):
     count = len(starts)
@@ -207,6 +209,8 @@
         out_specs=[VMEM] * len(arrays),
         out_shape=[jax.ShapeDtypeStruct((rows, *a.shape[1:]), a.dtype) for a in arrays],
         scratch_shapes=[pltpu.SemaphoreType.DMA((len(arrays),))],
+        compiler_params=pltpu.CompilerParams(vmem_limit_bytes=24 * MIB),
+        cost_estimate=pl.CostEstimate(flops=MICROSECOND, bytes_accessed=0, transcendentals=0),
     )(*arrays, *earlier)
 
 
@@ -255,33 +259,41 @@
     )
 
 
-def finish_kernel(att_ref, x_ref, w_ref, out_ref):
-    att = jnp.concatenate([att_ref[k] for k in range(HEADS)], axis=1)
+def finish_kernel(unread, info_ref, *refs):
+    att_refs, refs = refs[:HEADS], refs[HEADS:]
+    x_ref, w_ref, (out_ref, att) = refs[0], refs[1], refs[2 + unread :]
+    flip = info_ref[0]
+    for k in range(HEADS):
+        att[flip ^ k] = att_refs[k][...]
+    whole = jnp.concatenate([att[k] for k in range(HEADS)], axis=1)
     block = 256
     for start in range(0, x_ref.shape[1], block):
         columns = slice(start, start + block)
-        out_ref[:, columns] = low(high(x_ref[:, columns]) + dot(att, w_ref[:, columns], NN))
-
-
-def finish(attention, current, w_fin):
+        out_ref[:, columns] = low(high(x_ref[:, columns]) + dot(whole, w_ref[:, columns], NN))
+
+
+def finish(info, attention, current, w_fin, earlier):
     tokens, width = current.shape
     return call(
-        finish_kernel,
-        [attention, current, w_fin],
-        [VMEM] * 3,
+        functools.partial(finish_kernel, len(earlier)),
+        [info, *attention, current, w_fin, *earlier],
+        [SMEM] + [VMEM] * (HEADS + 2) + [HBM] * len(earlier),
         jax.ShapeDtypeStruct((tokens, width), jnp.bfloat16),
-        [],
-        2 * tokens * width * HEADS * HD,
+        [pltpu.VMEM((HEADS, tokens, HD), jnp.bfloat16)],
+        MICROSECOND,
         2 * width * HEADS * HD,
     )
 
 
-def finish_back_kernel(grad_ref, x_ref, up_ref, w_ref, out_ref, total):
+def finish_back_kernel(info_ref, *refs):
+    grad_refs, (x_ref, up_ref, w_ref, out_ref, grads, total) = refs[:HEADS], refs[HEADS:]
+    flip = info_ref[0]
+    for k in range(HEADS):
+        grads[flip ^ k] = grad_refs[k][...]
     for c in range(3):
-        grads = jnp.concatenate(
-            [grad_ref[k, :, c * HD : (c + 1) * HD] for k in range(HEADS)], axis=1
-        )
-        product = dot(grads, w_ref[c * HEADS * HD : (c + 1) * HEADS * HD], NN)
+        columns = slice(c * HD, (c + 1) * HD)
+        block = jnp.concatenate([grads[k, :, columns] for k in range(HEADS)], axis=1)
+        product = dot(block, w_ref[c * HEADS * HD : (c + 1) * HEADS * HD], NN)
         if c == 0:
             total[...] = product
         else:
@@ -294,15 +306,18 @@
     out_ref[...] = low(high(up_ref[...]) + pulled)
 
 
-def finish_back(grads, stored, upstream, w_qkv):
+def finish_back(info, grads, stored, upstream, w_qkv):
     tokens, width = stored.shape
     return call(
         finish_back_kernel,
-        [grads, stored, upstream, w_qkv],
-        [VMEM] * 4,
+        [info, *grads, stored, upstream, w_qkv],
+        [SMEM] + [VMEM] * (HEADS + 3),
         jax.ShapeDtypeStruct((tokens, width), jnp.bfloat16),
-        [pltpu.VMEM((tokens, width), jnp.float32)],
-        2 * tokens * width * 3 * HEADS * HD,
+        [
+            pltpu.VMEM((HEADS, tokens, 3 * HD), jnp.bfloat16),
+            pltpu.VMEM((tokens, width), jnp.float32),
+        ],
+        MICROSECOND * 3,
         6 * width * HEADS * HD,
     )
 
@@ -314,11 +329,23 @@
 
 def gather_rows(x, earlier):
     half = x.shape[0] // 2
-    over_x, over_y = partner(x, 2), partner(x, 4)
-    top, bottom = rows_after([over_x, over_y], [0, half], half, earlier)
-    top, bottom = partner(top, 4), partner(bottom, 2)
-    pieces = [(0, 0, x), (2, 0, over_x), (4, 0, over_y), (6, 0, top), (6, half, bottom)]
+    if earlier:
+        over_x, over_y = partner(x, 2), partner(x, 4)
+        relay_top, relay_bottom = rows_after([over_x, over_y], [0, half], half, earlier)
+        pieces = [(0, 0, x), (2, 0, over_x), (4, 0, over_y)]
+    else:
+        top, bottom = x[:half], x[half:]
+        relay_top, relay_bottom = partner(top, 2), partner(bottom, 4)
+        pieces = [(0, 0, x), (2, 0, relay_top), (4, half, relay_bottom)]
+        pieces += [(2, half, partner(bottom, 2)), (4, 0, partner(top, 4))]
+    far_top, far_bottom = partner(relay_top, 4), partner(relay_bottom, 2)
+    pieces += [(6, 0, far_top), (6, half, far_bottom)]
     return pieces + [(k + 1, start, partner(block, 1)) for k, start, block in pieces]
+
+
+def swap(blocks):
+    moved = {k: partner(blocks[k], k) for k in (2, 4, 6, 3, 5, 7, 1)}
+    return [blocks[0]] + [moved[k] for k in range(1, HEADS)]
 
 
 def all_swap(blocks):
@@ -363,7 +390,7 @@
     own = lax.axis_index("seq").astype(jnp.int32)
     if spacing == 1:
         info = jnp.stack([own, own, jnp.zeros_like(own)])
-        gather, spread, collect = gather_rows, all_swap, all_swap
+        gather, spread, collect = gather_rows, all_swap, swap
     else:
         info = jnp.stack([jnp.zeros_like(own), own // spacing, own % spacing])
 
@@ -375,29 +402,28 @@
             return to_heads(blocks, own, spacing)
 
         def collect(blocks):
-            return to_tokens(blocks, own, spacing, tokens)
+            return list(to_tokens(jnp.stack(blocks), own, spacing, tokens))
 
     own_head = w_rows.reshape(3, HEADS, HD, -1)
     own_head = lax.dynamic_index_in_dim(own_head, info[1], 1, keepdims=False)
     own_head = own_head.reshape(3 * HD, -1)
     spreading = spread_grads(upstream, w_fin)
-    stored_pieces = gather(stored, [spreading])
+    stored_pieces = gather(stored, [])
     grad_attention = spread(spreading)
     earlier = [block for k, _, block in stored_pieces if k == HEADS - 2]
     normed = norm_after(current, [*earlier, grad_attention])
     grads = head_work(
         info, tile_cluster, stored_pieces, own_head, spacing, grad_attention, [normed]
     )
-    current_pieces = gather(normed, [grads])
+    current_pieces = gather(normed, grads[:1])
     returned_grads = collect(grads)
     outputs = head_work(
-        info, tile_cluster, current_pieces, own_head, spacing, earlier=[grads]
-    )
-    outputs = rows_after([outputs], [0], HEADS, [returned_grads])[0]
+        info, tile_cluster, current_pieces, own_head, spacing, earlier=grads[:1]
+    )
     returned = collect(outputs)
-    grad_self = finish_back(returned_grads, stored, upstream, w_rows)
+    grad_self = finish_back(info, returned_grads, stored, upstream, w_rows)
     grad_input = passed_along(grad_self, "pipe", -1)
-    result = finish(returned, current, w_fin)
+    result = finish(info, returned, current, w_fin, [grad_self])
     next_input = passed_along(result, "pipe", 1)
     return (next_input[None], grad_input[None])
 

time: 119 us -> 119 us (level)
  waiting for transfers between devices: 34.9 us -> 46.1 us
  local copies, waits for them, and re-layouts: 17.9 us -> 10.1 us
  Pallas kernels: 32.2 us -> 25.5 us
  starting transfers between devices: 31.3 us -> 35.1 us
    ppermute x18 -> x36, waiting for transfers between devices: 11.5 us -> 28.8 us  [partner(): return lax.ppermute(block, 'seq', route)]
    ppermute x18 -> x36, starting transfers between devices: 10.3 us -> 24.8 us  [partner(): return lax.ppermute(block, 'seq', route)]
    all_to_all x3 -> x1, starting transfers between devices: 14.3 us -> 4.38 us  [all_swap(): lax.all_to_all(blocks, 'seq', split_axis=0, concat_axis=0, tiled=True)]
    unnamed x36 -> x32, local copies, waits for them, and re-layouts: 16.7 us -> 7.83 us
    all_to_all x3 -> x1, waiting for transfers between devices: 12 us -> 5.25 us  [all_swap(): lax.all_to_all(blocks, 'seq', split_axis=0, concat_axis=0, tiled=True)]
    pallas_call x3 -> x1, Pallas kernels: 5.54 us -> 0.06 us  [rows_after(): pl.pallas_call(functools.partial(copy_kernel, starts), in_specs=[HBM] * (...]
    pallas_call x6, Pallas kernels: 26.7 us -> 25.4 us  [call(): pl.pallas_call(kernel, in_specs=in_specs, out_specs=[VMEM] * len(out_shap...]
  transfers between devices with their start and end apart: 23 -> 39, of which waited for: 9 -> 11; matrix products, arithmetic and copies ran while one was open for 1% -> 1% of each run, Pallas kernels for 26% -> 22%
where the time goes in v9:
time: 119 us; the launch traced here: 118 us
  waiting for transfers between devices  46.1 us (39%)
  starting transfers between devices  35.1 us (29%)
  Pallas kernels  25.5 us (21%)
  local copies, waits for them, and re-layouts  10.1 us (8%)
    ppermute x36, waiting for transfers between devices, partner(): return lax.ppermute(block, 'seq', route)  28.8 us
    pallas_call x6, Pallas kernels, call(): pl.pallas_call(kernel, in_specs=in_specs, out_specs=[VMEM] * len(out_shap...  25.4 us
    ppermute x36, starting transfers between devices, partner(): return lax.ppermute(block, 'seq', route)  24.8 us
    ppermute x2, waiting for transfers between devices, passed_along(): return lax.ppermute(block, axis, route)  12.1 us
    unnamed x32, local copies, waits for them, and re-layouts  7.83 us
    ppermute x2, starting transfers between devices, passed_along(): return lax.ppermute(block, axis, route)  5.87 us
    all_to_all x1, waiting for transfers between devices, all_swap(): lax.all_to_all(blocks, 'seq', split_axis=0, concat_axis=0, tiled=True)  5.25 us
    all_to_all x1, starting transfers between devices, all_swap(): lax.all_to_all(blocks, 'seq', split_axis=0, concat_axis=0, tiled=True)  4.38 us
  transfers between devices with their start and end apart: 39, of which 11 were waited for; matrix products, arithmetic and copies ran while one was open for 1% of the time, Pallas kernels for 22%

profile of v9, /device:TPU:18, one launch (start us, length us, event | category | flops | bytes accessed | tf_op | source)
XLA Modules:
  0.0 117.7 jit_solution(9770926317043677879)
XLA Ops:
  0.6 1.1 slice_bitcast_fusion
  1.7 1.6 %collective-permute-start.2 = (bf16[128,1024]{1,0:T(8,128)(2,1)S(1)}, bf16[128,1024]{1,0:T(8,128)(2,1)S(1)}, u32[]{:S(2)}, u32[]{:S(2)}) collective-permute-start(bf16[128,1024]{1,0:T(8,128)(2,1)S(1)} %get-tuple-element.38), channel_id=1, source_target_pairs={{0,4},{1,5},{2,6},{3,7},{4,0},{5,1},{6,2},{7,3},{8,12},{9,13},{10,... | collective-permute-start | bytes 786440 | tf_op jit(solution)/shard_map/ppermute | solution.py:327
  3.3 0.5 collective-permute-start
  3.8 1.5 %collective-permute-start.6 = (bf16[128,1024]{1,0:T(8,128)(2,1)S(1)}, bf16[128,1024]{1,0:T(8,128)(2,1)}, u32[]{:S(2)}, u32[]{:S(2)}) collective-permute-start(bf16[128,1024]{1,0:T(8,128)(2,1)S(1)} %get-tuple-element.38), channel_id=1, source_target_pairs={{0,2},{1,3},{2,0},{3,1},{4,6},{5,7},{6,4},{7,5},{8,10},{9,11},{10,... | collective-permute-start | bytes 786440 | tf_op jit(solution)/shard_map/ppermute | solution.py:327
  5.3 0.5 collective-permute-start.7
  5.8 5.1 %collective-permute-done.2.refs_5_ = bf16[128,1024]{1,0:T(8,128)(2,1)S(1)} collective-permute-done((bf16[128,1024]{1,0:T(8,128)(2,1)S(1)}, bf16[128,1024]{1,0:T(8,128)(2,1)S(1)}, u32[]{:S(2)}, u32[]{:S(2)}) %collective-permute-start.2) | collective-permute-done | bytes 262176 | tf_op jit(solution)/shard_map/ppermute | solution.py:327
  11.0 0.5 collective-permute-start.3
  11.5 1.0 collective-permute-done.refs_4_
  12.5 5.7 %collective-permute-done.6.refs_6_ = bf16[128,1024]{1,0:T(8,128)(2,1)} collective-permute-done((bf16[128,1024]{1,0:T(8,128)(2,1)S(1)}, bf16[128,1024]{1,0:T(8,128)(2,1)}, u32[]{:S(2)}, u32[]{:S(2)}) %collective-permute-start.6) | collective-permute-done | bytes 262176 | tf_op jit(solution)/shard_map/ppermute | solution.py:327
  18.8 1.6 %copy-done.2 = bf16[1,1024,1024]{2,1,0:T(8,128)(2,1)S(1)} copy-done((bf16[1,1024,1024]{2,1,0:T(8,128)(2,1)S(1)}, bf16[1,1024,1024]{2,1,0:T(8,128)(2,1)}, u32[]{:S(2)}) %copy-start.2) | copy-done | bytes 2097176
  20.3 1.0 copy-done.4
  21.4 2.8 %shard_map.77 = bf16[8,256,128]{2,1,0:T(8,128)(2,1)} custom-call(bf16[256,1024]{1,0:T(8,128)(2,1)S(1)} %bitcast.32, bf16[8,128,1024]{2,1,0:T(8,128)(2,1)S(1)} %bitcast.30), custom_call_target="tpu_custom_call" | custom-call | flops 3449999872 | bytes 2097152 | tf_op jit(solution)/shard_map/pallas_call | solution.py:42
  24.3 4.4 %all-to-all-start = ((bf16[8,256,128]{2,1,0:T(8,128)(2,1)}), bf16[8,256,128]{2,1,0:T(8,128)(2,1)S(1)}, u32[]{:S(2)}, u32[]{:S(2)}) async-start(bf16[8,256,128]{2,1,0:T(8,128)(2,1)} %shard_map.77), calls=%async_computation | async-start | bytes 1048576 | tf_op jit(solution)/shard_map/all_to_all | solution.py:352
  29.2 0.7 copy-done.10
  30.5 1.2 %constant_dynamic-slice_fusion = bf16[3,1,128,1024]{3,2,1,0:T(8,128)(2,1)S(1)} fusion(bf16[3,8,128,1024]{3,2,1,0:T(8,128)(2,1)} %bitcast.26, s32[]{:T(128)S(6)} %select_n.4), kind=kLoop, calls=%fused_computation.3 | loop fusion | bytes 1572868 | tf_op jit(solution)/shard_map/jit(dynamic_index_in_dim)/dynamic_slice | solution.py:408
  31.7 5.2 %all-to-all-done.refs_2_ = bf16[8,256,128]{2,1,0:T(8,128)(2,1)S(1)} async-done(((bf16[8,256,128]{2,1,0:T(8,128)(2,1)}), bf16[8,256,128]{2,1,0:T(8,128)(2,1)S(1)}, u32[]{:S(2)}, u32[]{:S(2)}) %all-to-all-start) | async-done | bytes 524320 | tf_op jit(solution)/shard_map/all_to_all | solution.py:352
  37.1 1.5 %collective-permute-start.4 = (bf16[256,1024]{1,0:T(8,128)(2,1)S(1)}, bf16[256,1024]{1,0:T(8,128)(2,1)S(1)}, u32[]{:S(2)}, u32[]{:S(2)}) collective-permute-start(bf16[256,1024]{1,0:T(8,128)(2,1)S(1)} %shard_map.78.refs_18_.refs_3_), channel_id=1, source_target_pairs={{0,2},{1,3},{2,0},{3,1},{4,6},{5,7},{6,4},{7,5},{8,10},{9,11},{10,... | collective-permute-start | bytes 1572872 | tf_op jit(solution)/shard_map/ppermute | solution.py:327
  38.7 0.6 collective-permute-start.5
  39.3 0.9 copy-done.7
  40.2 0.9 copy-done.9
  41.2 0.9 copy-done.11
  42.1 11.2 %shard_map.79 = (bf16[256,384]{1,0:T(8,128)(2,1)S(1)}, bf16[256,384]{1,0:T(8,128)(2,1)S(1)}, bf16[256,384]{1,0:T(8,128)(2,1)S(1)}, bf16[256,384]{1,0:T(8,128)(2,...) custom-call(s32[16]{0:T(128)S(1)} %copy-done.12, ...), custom_call_target="tpu_custom_call" | custom-call | flops 13799999488 | bytes 7340032 | tf_op jit(solution)/shard_map/pallas_call | solution.py:42
  53.4 0.6 collective-permute-start.30
  54.8 1.5 %collective-permute-start.15 = (bf16[128,1024]{1,0:T(8,128)(2,1)S(1)}, bf16[128,1024]{1,0:T(8,128)(2,1)S(1)}, u32[]{:S(2)}, u32[]{:S(2)}) collective-permute-start(bf16[128,1024]{1,0:T(8,128)(2,1)S(1)} %get-tuple-element.21), channel_id=1, source_target_pairs={{0,4},{1,5},{2,6},{3,7},{4,0},{5,1},{6,2},{7,3},{8,12},{9,13},{10,... | collective-permute-start | bytes 786440 | tf_op jit(solution)/shard_map/ppermute | solution.py:327
  56.3 4.4 %collective-permute-done.30.refs_2_ = bf16[256,384]{1,0:T(8,128)(2,1)S(1)} collective-permute-done((bf16[256,384]{1,0:T(8,128)(2,1)S(1)}, bf16[256,384]{1,0:T(8,128)(2,1)S(1)}, u32[]{:S(2)}, u32[]{:S(2)}) %collective-permute-start.30) | collective-permute-done | bytes 196640 | tf_op jit(solution)/shard_map/ppermute | solution.py:327
  60.7 0.6 collective-permute-start.16
  61.2 2.1 %collective-permute-done.15.refs_6_ = bf16[128,1024]{1,0:T(8,128)(2,1)S(1)} collective-permute-done((bf16[128,1024]{1,0:T(8,128)(2,1)S(1)}, bf16[128,1024]{1,0:T(8,128)(2,1)S(1)}, u32[]{:S(2)}, u32[]{:S(2)}) %collective-permute-start.15) | collective-permute-done | bytes 262176 | tf_op jit(solution)/shard_map/ppermute | solution.py:327
  63.4 5.2 %collective-permute-done.16.refs_7_ = bf16[128,1024]{1,0:T(8,128)(2,1)S(1)} collective-permute-done((bf16[128,1024]{1,0:T(8,128)(2,1)S(1)}, bf16[128,1024]{1,0:T(8,128)(2,1)S(1)}, u32[]{:S(2)}, u32[]{:S(2)}) %collective-permute-start.16) | collective-permute-done | bytes 262176 | tf_op jit(solution)/shard_map/ppermute | solution.py:327
  68.5 0.7 collective-permute-start.31
  69.2 1.5 %collective-permute-start.32 = (bf16[256,384]{1,0:T(8,128)(2,1)S(1)}, bf16[256,384]{1,0:T(8,128)(2,1)S(1)}, u32[]{:S(2)}, u32[]{:S(2)}) collective-permute-start(bf16[256,384]{1,0:T(8,128)(2,1)S(1)} %get-tuple-element.34), channel_id=1, source_target_pairs={{0,4},{1,5},{2,6},{3,7},{4,0},{5,1},{6,2},{7,3},{8,12},{9,13},{10,... | collective-permute-start | bytes 589832 | tf_op jit(solution)/shard_map/ppermute | solution.py:327
  70.7 2.3 %collective-permute-start.34 = (bf16[256,384]{1,0:T(8,128)(2,1)S(1)}, bf16[256,384]{1,0:T(8,128)(2,1)S(1)}, u32[]{:S(2)}, u32[]{:S(2)}) collective-permute-start(bf16[256,384]{1,0:T(8,128)(2,1)S(1)} %get-tuple-element.36), channel_id=1, source_target_pairs={{0,6},{1,7},{2,4},{3,5},{4,2},{5,3},{6,0},{7,1},{8,14},{9,15},{10,... | collective-permute-start | bytes 589832 | tf_op jit(solution)/shard_map/ppermute | solution.py:327
  73.0 0.7 collective-permute-start.35
  73.7 7.2 %shard_map.81 = (bf16[256,128]{1,0:T(8,128)(2,1)S(1)}, bf16[256,128]{1,0:T(8,128)(2,1)S(1)}, bf16[256,128]{1,0:T(8,128)(2,1)S(1)}, bf16[256,128]{1,0:T(8,128)(2,...) custom-call(s32[16]{0:T(128)S(1)} %copy-done.12, ...), custom_call_target="tpu_custom_call" | custom-call | flops 9200000000 | bytes 5242880 | tf_op jit(solution)/shard_map/pallas_call | solution.py:42
  81.2 4.2 %collective-permute-done.32.refs_4_ = bf16[256,384]{1,0:T(8,128)(2,1)S(1)} collective-permute-done((bf16[256,384]{1,0:T(8,128)(2,1)S(1)}, bf16[256,384]{1,0:T(8,128)(2,1)S(1)}, u32[]{:S(2)}, u32[]{:S(2)}) %collective-permute-start.32) | collective-permute-done | bytes 196640 | tf_op jit(solution)/shard_map/ppermute | solution.py:327
  85.4 1.5 %collective-permute-start.23 = (bf16[256,128]{1,0:T(8,128)(2,1)S(1)}, bf16[256,128]{1,0:T(8,128)(2,1)S(1)}, u32[]{:S(2)}, u32[]{:S(2)}) collective-permute-start(bf16[256,128]{1,0:T(8,128)(2,1)S(1)} %get-tuple-element.25), channel_id=1, source_target_pairs={{0,2},{1,3},{2,0},{3,1},{4,6},{5,7},{6,4},{7,5},{8,10},{9,11},{10,... | collective-permute-start | bytes 196616 | tf_op jit(solution)/shard_map/ppermute | solution.py:327
  86.9 0.8 collective-permute-done.33.refs_5_
  87.7 1.8 %collective-permute-start.24 = (bf16[256,128]{1,0:T(8,128)(2,1)S(1)}, bf16[256,128]{1,0:T(8,128)(2,1)S(1)}, u32[]{:S(2)}, u32[]{:S(2)}) collective-permute-start(bf16[256,128]{1,0:T(8,128)(2,1)S(1)} %get-tuple-element.26), channel_id=1, source_target_pairs={{0,3},{1,2},{2,1},{3,0},{4,7},{5,6},{6,5},{7,4},{8,11},{9,10},{10,... | collective-permute-start | bytes 196616 | tf_op jit(solution)/shard_map/ppermute | solution.py:327
  89.6 1.5 %collective-permute-start.25 = (bf16[256,128]{1,0:T(8,128)(2,1)S(1)}, bf16[256,128]{1,0:T(8,128)(2,1)S(1)}, u32[]{:S(2)}, u32[]{:S(2)}) collective-permute-start(bf16[256,128]{1,0:T(8,128)(2,1)S(1)} %get-tuple-element.27), channel_id=1, source_target_pairs={{0,4},{1,5},{2,6},{3,7},{4,0},{5,1},{6,2},{7,3},{8,12},{9,13},{10,... | collective-permute-start | bytes 196616 | tf_op jit(solution)/shard_map/ppermute | solution.py:327
  91.1 1.2 %collective-permute-start.27 = (bf16[256,128]{1,0:T(8,128)(2,1)S(1)}, bf16[256,128]{1,0:T(8,128)(2,1)S(1)}, u32[]{:S(2)}, u32[]{:S(2)}) collective-permute-start(bf16[256,128]{1,0:T(8,128)(2,1)S(1)} %get-tuple-element.29), channel_id=1, source_target_pairs={{0,6},{1,7},{2,4},{3,5},{4,2},{5,3},{6,0},{7,1},{8,14},{9,15},{10,... | collective-permute-start | bytes 196616 | tf_op jit(solution)/shard_map/ppermute | solution.py:327
  92.2 1.7 %collective-permute-start.28 = (bf16[256,128]{1,0:T(8,128)(2,1)S(1)}, bf16[256,128]{1,0:T(8,128)(2,1)S(1)}, u32[]{:S(2)}, u32[]{:S(2)}) collective-permute-start(bf16[256,128]{1,0:T(8,128)(2,1)S(1)} %get-tuple-element.30), channel_id=1, source_target_pairs={{0,7},{1,6},{2,5},{3,4},{4,3},{5,2},{6,1},{7,0},{8,15},{9,14},{10,... | collective-permute-start | bytes 196616 | tf_op jit(solution)/shard_map/ppermute | solution.py:327
  94.0 2.8 %shard_map.82.refs_10_ = bf16[256,1024]{1,0:T(8,128)(2,1)S(1)} custom-call(s32[3]{0:T(128)S(1)} %pad_add_fusion.refs_1_.info_ref, bf16[256,384]{1,0:T(8,128)(2,1)S(1)} %get-tuple-element.20.refs_2_.refs_13_.refs_0_, bf16[256,384]{1,0:T(8,128)(2,1)S(1)} %collective-permute-done.29.refs_1_, bf16[256,384]{1,0:T(8,128)(2,1)S(1)} %collective-permute-done.30.refs_2_, ...), custom_call_target="tpu_custom_call" | custom-call | flops 3449999872 | bytes 6291456 | tf_op jit(solution)/shard_map/pallas_call | solution.py:42
  96.8 2.4 %collective-permute-start.37 = (bf16[256,1024]{1,0:T(8,128)(2,1)S(1)}, bf16[256,1024]{1,0:T(8,128)(2,1)S(1)}, u32[]{:S(2)}, u32[]{:S(2)}) collective-permute-start(bf16[256,1024]{1,0:T(8,128)(2,1)S(1)} %shard_map.82.refs_10_), channel_id=1, source_target_pairs={{8,0},{16,8},{24,16},{9,1},{17,9},{25,17},{10,2},{18,10},{26,18},{... | collective-permute-start | bytes 1572872 | tf_op jit(solution)/shard_map/ppermute | solution.py:382
  99.2 1.3 %shard_map.83 = bf16[256,1024]{1,0:T(8,128)(2,1)S(1)} custom-call(s32[3]{0:T(128)S(1)} %pad_add_fusion.refs_1_.info_ref, bf16[256,128]{1,0:T(8,128)(2,1)S(1)} %get-tuple-element.23.refs_0_, bf16[256,128]{1,0:T(8,128)(2,1)S(1)} %collective-permute-done.22.refs_1_, bf16[256,128]{1,0:T(8,128)(2,1)S(1)} %collective-permute-done.23.refs_2_, ...), custom_call_target="tpu_custom_call" | custom-call | flops 1150000000 | bytes 2097152 | tf_op jit(solution)/shard_map/pallas_call | solution.py:42
  100.5 3.5 %collective-permute-start.36 = (bf16[256,1024]{1,0:T(8,128)(2,1)S(1)}, bf16[256,1024]{1,0:T(8,128)(2,1)S(1)}, u32[]{:S(2)}, u32[]{:S(2)}) collective-permute-start(bf16[256,1024]{1,0:T(8,128)(2,1)S(1)} %shard_map.83), channel_id=1, source_target_pairs={{0,8},{8,16},{16,24},{1,9},{9,17},{17,25},{2,10},{10,18},{18,26},{... | collective-permute-start | bytes 1572872 | tf_op jit(solution)/shard_map/ppermute | solution.py:382
  104.0 8.7 %collective-permute-done.37 = bf16[256,1024]{1,0:T(8,128)(2,1)S(1)} collective-permute-done((bf16[256,1024]{1,0:T(8,128)(2,1)S(1)}, bf16[256,1024]{1,0:T(8,128)(2,1)S(1)}, u32[]{:S(2)}, u32[]{:S(2)}) %collective-permute-start.37) | collective-permute-done | bytes 524320 | tf_op jit(solution)/shard_map/ppermute | solution.py:382
  112.7 3.4 %collective-permute-done.36 = bf16[256,1024]{1,0:T(8,128)(2,1)S(1)} collective-permute-done((bf16[256,1024]{1,0:T(8,128)(2,1)S(1)}, bf16[256,1024]{1,0:T(8,128)(2,1)S(1)}, u32[]{:S(2)}, u32[]{:S(2)}) %collective-permute-start.36) | collective-permute-done | bytes 524320 | tf_op jit(solution)/shard_map/ppermute | solution.py:382
  116.1 0.8 copy.12
  116.9 0.8 copy.13
  (73 shorter events, 3.0 us)
Async XLA Ops:
  1.7 9.3 %collective-permute-start.2 = (bf16[128,1024]{1,0:T(8,128)(2,1)S(1)}, bf16[128,1024]{1,0:T(8,128)(2,1)S(1)}, u32[]{:S(2)}, u32[]{:S(2)}) collective-permute-start(bf16[128,1024]{1,0:T(8,128)(2,1)S(1)} %get-tuple-element.38), channel_id=1, source_target_pairs={{0,4},{1,5},{2,6},{3,7},{4,0},{5,1},{6,2},{7,3},{8,12},{9,13},{10,... | collective-permute-start | bytes 786440 | tf_op jit(solution)/shard_map/ppermute | solution.py:327
  3.3 9.2 %collective-permute-start = (bf16[128,1024]{1,0:T(8,128)(2,1)S(1)}, bf16[128,1024]{1,0:T(8,128)(2,1)S(1)}, u32[]{:S(2)}, u32[]{:S(2)}) collective-permute-start(bf16[128,1024]{1,0:T(8,128)(2,1)S(1)} %get-tuple-element.39), channel_id=1, source_target_pairs={{0,2},{1,3},{2,0},{3,1},{4,6},{5,7},{6,4},{7,5},{8,10},{9,11},{10,... | collective-permute-start | bytes 786440 | tf_op jit(solution)/shard_map/ppermute | solution.py:327
  3.8 14.4 %collective-permute-start.6 = (bf16[128,1024]{1,0:T(8,128)(2,1)S(1)}, bf16[128,1024]{1,0:T(8,128)(2,1)}, u32[]{:S(2)}, u32[]{:S(2)}) collective-permute-start(bf16[128,1024]{1,0:T(8,128)(2,1)S(1)} %get-tuple-element.38), channel_id=1, source_target_pairs={{0,2},{1,3},{2,0},{3,1},{4,6},{5,7},{6,4},{7,5},{8,10},{9,11},{10,... | collective-permute-start | bytes 786440 | tf_op jit(solution)/shard_map/ppermute | solution.py:327
  5.3 13.4 %collective-permute-start.7 = (bf16[128,1024]{1,0:T(8,128)(2,1)S(1)}, bf16[128,1024]{1,0:T(8,128)(2,1)}, u32[]{:S(2)}, u32[]{:S(2)}) collective-permute-start(bf16[128,1024]{1,0:T(8,128)(2,1)S(1)} %get-tuple-element.39), channel_id=1, source_target_pairs={{0,4},{1,5},{2,6},{3,7},{4,0},{5,1},{6,2},{7,3},{8,12},{9,13},{10,... | collective-permute-start | bytes 786440 | tf_op jit(solution)/shard_map/ppermute | solution.py:327
  5.8 33.4 %collective-permute-start.8 = (bf16[256,1024]{1,0:T(8,128)(2,1)}, bf16[256,1024]{1,0:T(8,128)(2,1)S(1)}, u32[]{:S(2)}, u32[]{:S(2)}) collective-permute-start(bf16[256,1024]{1,0:T(8,128)(2,1)} %bitcast.21), channel_id=1, source_target_pairs={{0,1},{1,0},{2,3},{3,2},{4,5},{5,4},{6,7},{7,6},{8,9},{9,8},{10,11... | collective-permute-start | bytes 1572872 | tf_op jit(solution)/shard_map/ppermute | solution.py:327
  11.0 13.3 %copy-start.6 = (bf16[128,1024]{1,0:T(8,128)(2,1)}, bf16[128,1024]{1,0:T(8,128)(2,1)S(1)}, u32[]{:S(2)}) copy-start(bf16[128,1024]{1,0:T(8,128)(2,1)S(1)} %collective-permute-done.2.refs_5_) | copy-start | bytes 786436
  11.0 17.8 %collective-permute-start.3 = (bf16[128,1024]{1,0:T(8,128)(2,1)S(1)}, bf16[128,1024]{1,0:T(8,128)(2,1)S(1)}, u32[]{:S(2)}, u32[]{:S(2)}) collective-permute-start(bf16[128,1024]{1,0:T(8,128)(2,1)S(1)} %collective-permute-done.2.refs_5_), channel_id=1, source_target_pairs={{0,2},{1,3},{2,0},{3,1},{4,6},{5,7},{6,4},{7,5},{8,10},{9,11},{10,... | collective-permute-start | bytes 786440 | tf_op jit(solution)/shard_map/ppermute | solution.py:327
  12.5 11.7 %copy-start.8 = (bf16[128,1024]{1,0:T(8,128)(2,1)}, bf16[128,1024]{1,0:T(8,128)(2,1)S(1)}, u32[]{:S(2)}) copy-start(bf16[128,1024]{1,0:T(8,128)(2,1)S(1)} %collective-permute-done.refs_4_) | copy-start | bytes 786436
  12.5 16.6 %collective-permute-start.10 = (bf16[128,1024]{1,0:T(8,128)(2,1)S(1)}, bf16[128,1024]{1,0:T(8,128)(2,1)S(1)}, u32[]{:S(2)}, u32[]{:S(2)}) collective-permute-start(bf16[128,1024]{1,0:T(8,128)(2,1)S(1)} %collective-permute-done.2.refs_5_), channel_id=1, source_target_pairs={{0,1},{1,0},{2,3},{3,2},{4,5},{5,4},{6,7},{7,6},{8,9},{9,8},{10,11... | collective-permute-start | bytes 786440 | tf_op jit(solution)/shard_map/ppermute | solution.py:327
  18.2 10.4 %collective-permute-start.1 = (bf16[128,1024]{1,0:T(8,128)(2,1)S(1)}, bf16[128,1024]{1,0:T(8,128)(2,1)S(1)}, u32[]{:S(2)}, u32[]{:S(2)}) collective-permute-start(bf16[128,1024]{1,0:T(8,128)(2,1)S(1)} %collective-permute-done.refs_4_), channel_id=1, source_target_pairs={{0,4},{1,5},{2,6},{3,7},{4,0},{5,1},{6,2},{7,3},{8,12},{9,13},{10,... | collective-permute-start | bytes 786440 | tf_op jit(solution)/shard_map/ppermute | solution.py:327
  18.7 11.3 %collective-permute-start.9 = (bf16[128,1024]{1,0:T(8,128)(2,1)S(1)}, bf16[128,1024]{1,0:T(8,128)(2,1)}, u32[]{:S(2)}, u32[]{:S(2)}) collective-permute-start(bf16[128,1024]{1,0:T(8,128)(2,1)S(1)} %collective-permute-done.refs_4_), channel_id=1, source_target_pairs={{0,1},{1,0},{2,3},{3,2},{4,5},{5,4},{6,7},{7,6},{8,9},{9,8},{10,11... | collective-permute-start | bytes 786440 | tf_op jit(solution)/shard_map/ppermute | solution.py:327
  21.4 15.5 %copy-start.1 = (bf16[1,256,1024]{2,1,0:T(8,128)(2,1)S(1)}, bf16[1,256,1024]{2,1,0:T(8,128)(2,1)}, u32[]{:S(2)}) copy-start(bf16[1,256,1024]{2,1,0:T(8,128)(2,1)} %param.6) | copy-start | bytes 1572868
  21.4 17.8 %copy-start = (bf16[1,256,1024]{2,1,0:T(8,128)(2,1)S(1)}, bf16[1,256,1024]{2,1,0:T(8,128)(2,1)}, u32[]{:S(2)}) copy-start(bf16[1,256,1024]{2,1,0:T(8,128)(2,1)} %param.7) | copy-start | bytes 1572868
  21.4 17.9 %copy-start.12 = (s32[16]{0:T(128)S(1)}, s32[16]{0:T(128)}, u32[]{:S(2)}) copy-start(s32[16]{0:T(128)} %refs_0_.3) | copy-start | bytes 196
  24.3 12.7 %all-to-all-start = ((bf16[8,256,128]{2,1,0:T(8,128)(2,1)}), bf16[8,256,128]{2,1,0:T(8,128)(2,1)S(1)}, u32[]{:S(2)}, u32[]{:S(2)}) async-start(bf16[8,256,128]{2,1,0:T(8,128)(2,1)} %shard_map.77), calls=%async_computation | async-start | bytes 1048576 | tf_op jit(solution)/shard_map/all_to_all | solution.py:352
  28.6 8.5 %collective-permute-start.11 = (bf16[128,1024]{1,0:T(8,128)(2,1)}, bf16[128,1024]{1,0:T(8,128)(2,1)}, u32[]{:S(2)}, u32[]{:S(2)}) collective-permute-start(bf16[128,1024]{1,0:T(8,128)(2,1)} %collective-permute-done.6.refs_6_), channel_id=1, source_target_pairs={{0,1},{1,0},{2,3},{3,2},{4,5},{5,4},{6,7},{7,6},{8,9},{9,8},{10,11... | collective-permute-start | bytes 786440 | tf_op jit(solution)/shard_map/ppermute | solution.py:327
  28.8 9.9 %collective-permute-start.12 = (bf16[128,1024]{1,0:T(8,128)(2,1)}, bf16[128,1024]{1,0:T(8,128)(2,1)}, u32[]{:S(2)}, u32[]{:S(2)}) collective-permute-start(bf16[128,1024]{1,0:T(8,128)(2,1)} %collective-permute-done.7.refs_7_), channel_id=1, source_target_pairs={{0,1},{1,0},{2,3},{3,2},{4,5},{5,4},{6,7},{7,6},{8,9},{9,8},{10,11... | collective-permute-start | bytes 786440 | tf_op jit(solution)/shard_map/ppermute | solution.py:327
  29.9 9.3 %collective-permute-start.13 = (bf16[128,1024]{1,0:T(8,128)(2,1)S(1)}, bf16[128,1024]{1,0:T(8,128)(2,1)}, u32[]{:S(2)}, u32[]{:S(2)}) collective-permute-start(bf16[128,1024]{1,0:T(8,128)(2,1)S(1)} %collective-permute-done.1.refs_0_.refs_8_), channel_id=1, source_target_pairs={{0,1},{1,0},{2,3},{3,2},{4,5},{5,4},{6,7},{7,6},{8,9},{9,8},{10,11... | collective-permute-start | bytes 786440 | tf_op jit(solution)/shard_map/ppermute | solution.py:327
  30.0 9.2 %collective-permute-start.14 = (bf16[128,1024]{1,0:T(8,128)(2,1)S(1)}, bf16[128,1024]{1,0:T(8,128)(2,1)}, u32[]{:S(2)}, u32[]{:S(2)}) collective-permute-start(bf16[128,1024]{1,0:T(8,128)(2,1)S(1)} %collective-permute-done.3.refs_1_.refs_9_), channel_id=1, source_target_pairs={{0,1},{1,0},{2,3},{3,2},{4,5},{5,4},{6,7},{7,6},{8,9},{9,8},{10,11... | collective-permute-start | bytes 786440 | tf_op jit(solution)/shard_map/ppermute | solution.py:327
  37.1 17.0 %collective-permute-start.4 = (bf16[256,1024]{1,0:T(8,128)(2,1)S(1)}, bf16[256,1024]{1,0:T(8,128)(2,1)S(1)}, u32[]{:S(2)}, u32[]{:S(2)}) collective-permute-start(bf16[256,1024]{1,0:T(8,128)(2,1)S(1)} %shard_map.78.refs_18_.refs_3_), channel_id=1, source_target_pairs={{0,2},{1,3},{2,0},{3,1},{4,6},{5,7},{6,4},{7,5},{8,10},{9,11},{10,... | collective-permute-start | bytes 1572872 | tf_op jit(solution)/shard_map/ppermute | solution.py:327
  38.7 15.8 %collective-permute-start.5 = (bf16[256,1024]{1,0:T(8,128)(2,1)S(1)}, bf16[256,1024]{1,0:T(8,128)(2,1)S(1)}, u32[]{:S(2)}, u32[]{:S(2)}) collective-permute-start(bf16[256,1024]{1,0:T(8,128)(2,1)S(1)} %shard_map.78.refs_18_.refs_3_), channel_id=1, source_target_pairs={{0,4},{1,5},{2,6},{3,7},{4,0},{5,1},{6,2},{7,3},{8,12},{9,13},{10,... | collective-permute-start | bytes 1572872 | tf_op jit(solution)/shard_map/ppermute | solution.py:327
  53.3 1.5 %collective-permute-start.29 = (bf16[256,384]{1,0:T(8,128)(2,1)S(1)}, bf16[256,384]{1,0:T(8,128)(2,1)S(1)}, u32[]{:S(2)}, u32[]{:S(2)}) collective-permute-start(bf16[256,384]{1,0:T(8,128)(2,1)S(1)} %get-tuple-element.31), channel_id=1, source_target_pairs={{0,1},{1,0},{2,3},{3,2},{4,5},{5,4},{6,7},{7,6},{8,9},{9,8},{10,11... | collective-permute-start | bytes 589832 | tf_op jit(solution)/shard_map/ppermute | solution.py:327
  53.4 7.3 %collective-permute-start.30 = (bf16[256,384]{1,0:T(8,128)(2,1)S(1)}, bf16[256,384]{1,0:T(8,128)(2,1)S(1)}, u32[]{:S(2)}, u32[]{:S(2)}) collective-permute-start(bf16[256,384]{1,0:T(8,128)(2,1)S(1)} %get-tuple-element.32), channel_id=1, source_target_pairs={{0,2},{1,3},{2,0},{3,1},{4,6},{5,7},{6,4},{7,5},{8,10},{9,11},{10,... | collective-permute-start | bytes 589832 | tf_op jit(solution)/shard_map/ppermute | solution.py:327
  54.0 14.6 %collective-permute-start.17 = (bf16[256,1024]{1,0:T(8,128)(2,1)S(1)}, bf16[256,1024]{1,0:T(8,128)(2,1)S(1)}, u32[]{:S(2)}, u32[]{:S(2)}) collective-permute-start(bf16[256,1024]{1,0:T(8,128)(2,1)S(1)} %shard_map.78.refs_18_.refs_3_), channel_id=1, source_target_pairs={{0,1},{1,0},{2,3},{3,2},{4,5},{5,4},{6,7},{7,6},{8,9},{9,8},{10,11... | collective-permute-start | bytes 1572872 | tf_op jit(solution)/shard_map/ppermute | solution.py:327
  54.2 15.1 %collective-permute-start.18 = (bf16[256,1024]{1,0:T(8,128)(2,1)S(1)}, bf16[256,1024]{1,0:T(8,128)(2,1)S(1)}, u32[]{:S(2)}, u32[]{:S(2)}) collective-permute-start(bf16[256,1024]{1,0:T(8,128)(2,1)S(1)} %collective-permute-done.4.refs_0_.refs_4_), channel_id=1, source_target_pairs={{0,1},{1,0},{2,3},{3,2},{4,5},{5,4},{6,7},{7,6},{8,9},{9,8},{10,11... | collective-permute-start | bytes 1572872 | tf_op jit(solution)/shard_map/ppermute | solution.py:327
  54.5 16.2 %collective-permute-start.19 = (bf16[256,1024]{1,0:T(8,128)(2,1)S(1)}, bf16[256,1024]{1,0:T(8,128)(2,1)S(1)}, u32[]{:S(2)}, u32[]{:S(2)}) collective-permute-start(bf16[256,1024]{1,0:T(8,128)(2,1)S(1)} %collective-permute-done.5.refs_1_.refs_5_), channel_id=1, source_target_pairs={{0,1},{1,0},{2,3},{3,2},{4,5},{5,4},{6,7},{7,6},{8,9},{9,8},{10,11... | collective-permute-start | bytes 1572872 | tf_op jit(solution)/shard_map/ppermute | solution.py:327
  54.8 8.6 %collective-permute-start.15 = (bf16[128,1024]{1,0:T(8,128)(2,1)S(1)}, bf16[128,1024]{1,0:T(8,128)(2,1)S(1)}, u32[]{:S(2)}, u32[]{:S(2)}) collective-permute-start(bf16[128,1024]{1,0:T(8,128)(2,1)S(1)} %get-tuple-element.21), channel_id=1, source_target_pairs={{0,4},{1,5},{2,6},{3,7},{4,0},{5,1},{6,2},{7,3},{8,12},{9,13},{10,... | collective-permute-start | bytes 786440 | tf_op jit(solution)/shard_map/ppermute | solution.py:327
  60.7 7.9 %collective-permute-start.16 = (bf16[128,1024]{1,0:T(8,128)(2,1)S(1)}, bf16[128,1024]{1,0:T(8,128)(2,1)S(1)}, u32[]{:S(2)}, u32[]{:S(2)}) collective-permute-start(bf16[128,1024]{1,0:T(8,128)(2,1)S(1)} %get-tuple-element.22), channel_id=1, source_target_pairs={{0,2},{1,3},{2,0},{3,1},{4,6},{5,7},{6,4},{7,5},{8,10},{9,11},{10,... | collective-permute-start | bytes 786440 | tf_op jit(solution)/shard_map/ppermute | solution.py:327
  63.4 7.3 %collective-permute-start.20 = (bf16[128,1024]{1,0:T(8,128)(2,1)S(1)}, bf16[128,1024]{1,0:T(8,128)(2,1)S(1)}, u32[]{:S(2)}, u32[]{:S(2)}) collective-permute-start(bf16[128,1024]{1,0:T(8,128)(2,1)S(1)} %collective-permute-done.15.refs_6_), channel_id=1, source_target_pairs={{0,1},{1,0},{2,3},{3,2},{4,5},{5,4},{6,7},{7,6},{8,9},{9,8},{10,11... | collective-permute-start | bytes 786440 | tf_op jit(solution)/shard_map/ppermute | solution.py:327
  68.5 4.4 %collective-permute-start.21 = (bf16[128,1024]{1,0:T(8,128)(2,1)S(1)}, bf16[128,1024]{1,0:T(8,128)(2,1)S(1)}, u32[]{:S(2)}, u32[]{:S(2)}) collective-permute-start(bf16[128,1024]{1,0:T(8,128)(2,1)S(1)} %collective-permute-done.16.refs_7_), channel_id=1, source_target_pairs={{0,1},{1,0},{2,3},{3,2},{4,5},{5,4},{6,7},{7,6},{8,9},{9,8},{10,11... | collective-permute-start | bytes 786440 | tf_op jit(solution)/shard_map/ppermute | solution.py:327
  68.5 12.4 %collective-permute-start.31 = (bf16[256,384]{1,0:T(8,128)(2,1)S(1)}, bf16[256,384]{1,0:T(8,128)(2,1)S(1)}, u32[]{:S(2)}, u32[]{:S(2)}) collective-permute-start(bf16[256,384]{1,0:T(8,128)(2,1)S(1)} %get-tuple-element.33), channel_id=1, source_target_pairs={{0,3},{1,2},{2,1},{3,0},{4,7},{5,6},{6,5},{7,4},{8,11},{9,10},{10,... | collective-permute-start | bytes 589832 | tf_op jit(solution)/shard_map/ppermute | solution.py:327
  69.2 16.2 %collective-permute-start.32 = (bf16[256,384]{1,0:T(8,128)(2,1)S(1)}, bf16[256,384]{1,0:T(8,128)(2,1)S(1)}, u32[]{:S(2)}, u32[]{:S(2)}) collective-permute-start(bf16[256,384]{1,0:T(8,128)(2,1)S(1)} %get-tuple-element.34), channel_id=1, source_target_pairs={{0,4},{1,5},{2,6},{3,7},{4,0},{5,1},{6,2},{7,3},{8,12},{9,13},{10,... | collective-permute-start | bytes 589832 | tf_op jit(solution)/shard_map/ppermute | solution.py:327
  70.7 17.0 %collective-permute-start.33 = (bf16[256,384]{1,0:T(8,128)(2,1)S(1)}, bf16[256,384]{1,0:T(8,128)(2,1)S(1)}, u32[]{:S(2)}, u32[]{:S(2)}) collective-permute-start(bf16[256,384]{1,0:T(8,128)(2,1)S(1)} %get-tuple-element.35), channel_id=1, source_target_pairs={{0,5},{1,4},{2,7},{3,6},{4,1},{5,0},{6,3},{7,2},{8,13},{9,12},{10,... | collective-permute-start | bytes 589832 | tf_op jit(solution)/shard_map/ppermute | solution.py:327
  70.7 18.9 %collective-permute-start.34 = (bf16[256,384]{1,0:T(8,128)(2,1)S(1)}, bf16[256,384]{1,0:T(8,128)(2,1)S(1)}, u32[]{:S(2)}, u32[]{:S(2)}) collective-permute-start(bf16[256,384]{1,0:T(8,128)(2,1)S(1)} %get-tuple-element.36), channel_id=1, source_target_pairs={{0,6},{1,7},{2,4},{3,5},{4,2},{5,3},{6,0},{7,1},{8,14},{9,15},{10,... | collective-permute-start | bytes 589832 | tf_op jit(solution)/shard_map/ppermute | solution.py:327
  73.0 21.0 %slice-start = ((s8[6291456]{0:T(1024)(128)(4,1)}), s8[4194304]{0:T(1024)(128)(4,1)S(1)}, s32[]{:S(2)}) async-start(s8[6291456]{0:T(1024)(128)(4,1)} %bitcast.27), calls=%async_computation.1 | async-start | bytes 8388608
  73.0 21.0 %slice-start.1 = ((s8[6291456]{0:T(1024)(128)(4,1)}), s8[2097152]{0:T(1024)(128)(4,1)S(1)}, s32[]{:S(2)}) async-start(s8[6291456]{0:T(1024)(128)(4,1)} %bitcast.27), calls=%async_computation.2 | async-start | bytes 4194304
  73.0 21.0 %copy-start.5 = (bf16[1,256,1024]{2,1,0:T(8,128)(2,1)S(1)}, bf16[1,256,1024]{2,1,0:T(8,128)(2,1)}, u32[]{:S(2)}) copy-start(bf16[1,256,1024]{2,1,0:T(8,128)(2,1)} %param.8) | copy-start | bytes 1572868
  73.0 18.1 %collective-permute-start.35 = (bf16[256,384]{1,0:T(8,128)(2,1)S(1)}, bf16[256,384]{1,0:T(8,128)(2,1)S(1)}, u32[]{:S(2)}, u32[]{:S(2)}) collective-permute-start(bf16[256,384]{1,0:T(8,128)(2,1)S(1)} %get-tuple-element.37), channel_id=1, source_target_pairs={{0,7},{1,6},{2,5},{3,4},{4,3},{5,2},{6,1},{7,0},{8,15},{9,14},{10,... | collective-permute-start | bytes 589832 | tf_op jit(solution)/shard_map/ppermute | solution.py:327
  80.9 10.1 %collective-permute-start.22 = (bf16[256,128]{1,0:T(8,128)(2,1)S(1)}, bf16[256,128]{1,0:T(8,128)(2,1)S(1)}, u32[]{:S(2)}, u32[]{:S(2)}) collective-permute-start(bf16[256,128]{1,0:T(8,128)(2,1)S(1)} %get-tuple-element.24), channel_id=1, source_target_pairs={{0,1},{1,0},{2,3},{3,2},{4,5},{5,4},{6,7},{7,6},{8,9},{9,8},{10,11... | collective-permute-start | bytes 196616 | tf_op jit(solution)/shard_map/ppermute | solution.py:327
  85.4 6.8 %collective-permute-start.23 = (bf16[256,128]{1,0:T(8,128)(2,1)S(1)}, bf16[256,128]{1,0:T(8,128)(2,1)S(1)}, u32[]{:S(2)}, u32[]{:S(2)}) collective-permute-start(bf16[256,128]{1,0:T(8,128)(2,1)S(1)} %get-tuple-element.25), channel_id=1, source_target_pairs={{0,2},{1,3},{2,0},{3,1},{4,6},{5,7},{6,4},{7,5},{8,10},{9,11},{10,... | collective-permute-start | bytes 196616 | tf_op jit(solution)/shard_map/ppermute | solution.py:327
  87.7 9.0 %collective-permute-start.24 = (bf16[256,128]{1,0:T(8,128)(2,1)S(1)}, bf16[256,128]{1,0:T(8,128)(2,1)S(1)}, u32[]{:S(2)}, u32[]{:S(2)}) collective-permute-start(bf16[256,128]{1,0:T(8,128)(2,1)S(1)} %get-tuple-element.26), channel_id=1, source_target_pairs={{0,3},{1,2},{2,1},{3,0},{4,7},{5,6},{6,5},{7,4},{8,11},{9,10},{10,... | collective-permute-start | bytes 196616 | tf_op jit(solution)/shard_map/ppermute | solution.py:327
  89.6 9.6 %collective-permute-start.25 = (bf16[256,128]{1,0:T(8,128)(2,1)S(1)}, bf16[256,128]{1,0:T(8,128)(2,1)S(1)}, u32[]{:S(2)}, u32[]{:S(2)}) collective-permute-start(bf16[256,128]{1,0:T(8,128)(2,1)S(1)} %get-tuple-element.27), channel_id=1, source_target_pairs={{0,4},{1,5},{2,6},{3,7},{4,0},{5,1},{6,2},{7,3},{8,12},{9,13},{10,... | collective-permute-start | bytes 196616 | tf_op jit(solution)/shard_map/ppermute | solution.py:327
  91.0 8.1 %collective-permute-start.26 = (bf16[256,128]{1,0:T(8,128)(2,1)S(1)}, bf16[256,128]{1,0:T(8,128)(2,1)S(1)}, u32[]{:S(2)}, u32[]{:S(2)}) collective-permute-start(bf16[256,128]{1,0:T(8,128)(2,1)S(1)} %get-tuple-element.28), channel_id=1, source_target_pairs={{0,5},{1,4},{2,7},{3,6},{4,1},{5,0},{6,3},{7,2},{8,13},{9,12},{10,... | collective-permute-start | bytes 196616 | tf_op jit(solution)/shard_map/ppermute | solution.py:327
  91.1 8.1 %collective-permute-start.27 = (bf16[256,128]{1,0:T(8,128)(2,1)S(1)}, bf16[256,128]{1,0:T(8,128)(2,1)S(1)}, u32[]{:S(2)}, u32[]{:S(2)}) collective-permute-start(bf16[256,128]{1,0:T(8,128)(2,1)S(1)} %get-tuple-element.29), channel_id=1, source_target_pairs={{0,6},{1,7},{2,4},{3,5},{4,2},{5,3},{6,0},{7,1},{8,14},{9,15},{10,... | collective-permute-start | bytes 196616 | tf_op jit(solution)/shard_map/ppermute | solution.py:327
  92.2 6.9 %collective-permute-start.28 = (bf16[256,128]{1,0:T(8,128)(2,1)S(1)}, bf16[256,128]{1,0:T(8,128)(2,1)S(1)}, u32[]{:S(2)}, u32[]{:S(2)}) collective-permute-start(bf16[256,128]{1,0:T(8,128)(2,1)S(1)} %get-tuple-element.30), channel_id=1, source_target_pairs={{0,7},{1,6},{2,5},{3,4},{4,3},{5,2},{6,1},{7,0},{8,15},{9,14},{10,... | collective-permute-start | bytes 196616 | tf_op jit(solution)/shard_map/ppermute | solution.py:327
  94.0 5.2 %copy-start.3 = (bf16[1,1024,1024]{2,1,0:T(8,128)(2,1)S(1)}, bf16[1,1024,1024]{2,1,0:T(8,128)(2,1)}, u32[]{:S(2)}) copy-start(bf16[1,1024,1024]{2,1,0:T(8,128)(2,1)} %param.10) | copy-start | bytes 6291460
  96.8 15.9 %collective-permute-start.37 = (bf16[256,1024]{1,0:T(8,128)(2,1)S(1)}, bf16[256,1024]{1,0:T(8,128)(2,1)S(1)}, u32[]{:S(2)}, u32[]{:S(2)}) collective-permute-start(bf16[256,1024]{1,0:T(8,128)(2,1)S(1)} %shard_map.82.refs_10_), channel_id=1, source_target_pairs={{8,0},{16,8},{24,16},{9,1},{17,9},{25,17},{10,2},{18,10},{26,18},{... | collective-permute-start | bytes 1572872 | tf_op jit(solution)/shard_map/ppermute | solution.py:382
  100.5 15.6 %collective-permute-start.36 = (bf16[256,1024]{1,0:T(8,128)(2,1)S(1)}, bf16[256,1024]{1,0:T(8,128)(2,1)S(1)}, u32[]{:S(2)}, u32[]{:S(2)}) collective-permute-start(bf16[256,1024]{1,0:T(8,128)(2,1)S(1)} %shard_map.83), channel_id=1, source_target_pairs={{0,8},{8,16},{16,24},{1,9},{9,17},{17,25},{2,10},{10,18},{18,26},{... | collective-permute-start | bytes 1572872 | tf_op jit(solution)/shard_map/ppermute | solution.py:382
  (6 other events, 6.2 us)

commit v10 on v8

--- a/solution.py
+++ b/solution.py
@@ -74,7 +74,8 @@
         return jnp.concatenate([kept[t, :, c * HD : (c + 1) * HD] for t in tiles], axis=0)
 
     def scale(c):
-        return jnp.concatenate([scales[t, :, c * HD : (c + 1) * HD] for t in tiles], axis=0)
+        column = c * HD // 2
+        return jnp.concatenate([scales[t, :, column : column + 1] for t in tiles], axis=0)
 
     q, k, v = load(0), load(1), load(2)
     g = jnp.concatenate([grads[t] for t in tiles], axis=0)
@@ -97,36 +98,10 @@
         results.append(low(scale(c) * (rounded - unit * mean)))
     for c, result in zip((2, 1, 0), results):
         for i, t in enumerate(tiles):
-            half = pl.ds(t % 2 * TILE, TILE)
-            out[t // 2, half, c * HD : (c + 1) * HD] = result[i * TILE : (i + 1) * TILE]
-
-
-def head_kernel(back, unread, pieces, spacing, *refs):
-    cluster_ref, info_ref, w_ref = refs[:3]
-    x_refs = refs[3 : 3 + len(pieces)]
-    refs = refs[3 + len(pieces) :]
-    if back:
-        grads, refs = refs[0], refs[1:]
-    refs = refs[unread:]
-    if back:
-        out, kept, count, member, scales = refs
-    else:
-        out_refs, (kept, count, member, out) = refs[:HEADS], refs[HEADS:]
-    flip, residue = info_ref[0], info_ref[2]
-    tiles = kept.shape[0]
-    clusters = count.shape[0]
-    for c in range(clusters):
-        count[c] = 0
-
-    def enter(t, carry):
-        c = cluster_ref[t * spacing + residue] // spacing
-        place = count[c]
-        member[c * CAPACITY + place] = t
-        count[c] = place + 1
-        return carry
-
-    lax.fori_loop(0, tiles, enter, 0)
-
+            out[t, :, c * HD : (c + 1) * HD] = result[i * TILE : (i + 1) * TILE]
+
+
+def project_rows(back, flip, pieces, x_refs, w_ref, kept, scales):
     weights = w_ref[...]
     for (slot, start, rows), x_ref in zip(pieces, x_refs):
         normed = x_ref[...]
@@ -134,68 +109,132 @@
             x = high(normed)
             normed = low(x * rows_rsqrt(x))
         mixed = dot(normed, weights, NT)
+        q, k, v = (mixed[:, c * HD : (c + 1) * HD] for c in range(3))
+        q_scale, k_scale = rows_rsqrt(q), rows_rsqrt(k)
+        whole = low(jnp.concatenate([q * q_scale, k * k_scale, v], axis=1))
+        if back:
+            lane = lax.broadcasted_iota(jnp.int32, q.shape, 1)
+            both = jnp.where(lane < HD // 2, q_scale, k_scale)
         place = 2 * (flip ^ slot) + start // TILE
-        for c in range(3):
-            u = mixed[:, c * HD : (c + 1) * HD]
-            if c < 2:
-                scale = rows_rsqrt(u)
-                u = u * scale
-            for j in range(rows // TILE):
-                kept[place + j, :, c * HD : (c + 1) * HD] = low(u[j * TILE : (j + 1) * TILE])
-                if back and c < 2:
-                    scales[place + j, :, c * HD : (c + 1) * HD] = jnp.broadcast_to(
-                        scale[j * TILE : (j + 1) * TILE], (TILE, HD)
-                    )
+        for j in range(rows // TILE):
+            kept[place + j] = whole[j * TILE : (j + 1) * TILE]
+            if back:
+                scales[place + j] = both[j * TILE : (j + 1) * TILE]
+
+
+def visit_clusters(cluster_ref, residue, spacing, count, member, body):
+    clusters = count.shape[0]
+    for c in range(clusters):
+        count[c] = 0
+
+    def enter(t, carry):
+        c = cluster_ref[t * spacing + residue] // spacing
+        place = count[c]
+        member[c * CAPACITY + place] = t
+        count[c] = place + 1
+        return carry
+
+    lax.fori_loop(0, 2 * clusters, enter, 0)
 
     def visit(c, carry):
         for n in range(1, CAPACITY + 1):
 
             @pl.when(count[c] == n)
             def _():
-                held = [member[c * CAPACITY + i] for i in range(n)]
-                if back:
-                    backward_cluster(held, kept, out, scales, grads)
-                else:
-                    forward_cluster(held, kept, out)
+                body([member[c * CAPACITY + i] for i in range(n)])
 
         return carry
 
     lax.fori_loop(0, clusters, visit, 0)
-    if not back:
-        for k in range(HEADS):
-            out_refs[k][...] = out[pl.ds(2 * (flip ^ k), 2)].reshape(out_refs[k].shape)
-
-
-def head_work(info, tile_cluster, pieces, weights, spacing, grads=None, earlier=()):
-    back = grads is not None
-    width = weights.shape[1]
-    tiles = 2 * HEADS
-    wide = 3 * HD if back else HD
-    tokens = tiles * TILE
-    operands = [tile_cluster, info, weights] + [array for _, _, array in pieces]
-    if back:
-        operands.append(grads.reshape(tiles, TILE, HD))
-    scratch = [
-        pltpu.VMEM((tiles, TILE, 3 * HD), jnp.bfloat16),
+
+
+def forward_kernel(pieces, unread, spacing, cluster_ref, info_ref, w_ref, *refs):
+    x_refs, refs = refs[: len(pieces)], refs[len(pieces) + unread :]
+    out_refs, (kept, out, count, member) = refs[:HEADS], refs[HEADS:]
+    flip, residue = info_ref[0], info_ref[2]
+    project_rows(False, flip, pieces, x_refs, w_ref, kept, None)
+    visit_clusters(
+        cluster_ref, residue, spacing, count, member, lambda held: forward_cluster(held, kept, out)
+    )
+    for k in range(HEADS):
+        out_refs[k][...] = out[pl.ds(2 * (flip ^ k), 2)].reshape(out_refs[k].shape)
+
+
+def project_kernel(pieces, unread, info_ref, w_ref, *refs):
+    x_refs, (kept, scales) = refs[: len(pieces)], refs[len(pieces) + unread :]
+    project_rows(True, info_ref[0], pieces, x_refs, w_ref, kept, scales)
+
+
+def backward_kernel(spacing, cluster_ref, info_ref, kept, scales, grads, out, count, member):
+    visit_clusters(
+        cluster_ref,
+        info_ref[2],
+        spacing,
+        count,
+        member,
+        lambda held: backward_cluster(held, kept, out, scales, grads),
+    )
+
+
+def tables(tiles):
+    return [
         pltpu.SMEM((tiles // 2,), jnp.int32),
         pltpu.SMEM((tiles // 2 * CAPACITY,), jnp.int32),
     ]
-    if back:
-        scratch.append(pltpu.VMEM((tiles, TILE, 2 * HD), jnp.float32))
-        shape = jax.ShapeDtypeStruct((HEADS, 2 * TILE, wide), jnp.bfloat16)
-    else:
-        scratch.append(pltpu.VMEM((tiles, TILE, HD), jnp.bfloat16))
-        shape = [jax.ShapeDtypeStruct((2 * TILE, HD), jnp.bfloat16) for _ in range(HEADS)]
+
+
+def head_forward(info, tile_cluster, pieces, weights, spacing, earlier):
+    width = weights.shape[1]
+    tiles = 2 * HEADS
+    arrays = [array for _, _, array in pieces]
     shapes = tuple((k, start, array.shape[0]) for k, start, array in pieces)
     return call(
-        functools.partial(head_kernel, back, len(earlier), shapes, spacing),
-        operands + list(earlier),
-        [SMEM, SMEM] + [VMEM] * (len(operands) - 2) + [HBM] * len(earlier),
-        shape,
-        scratch,
-        MICROSECOND * (12 if back else 8),
-        2 * tokens * (width + 2 * wide),
-    )
+        functools.partial(forward_kernel, shapes, len(earlier), spacing),
+        [tile_cluster, info, weights, *arrays, *earlier],
+        [SMEM, SMEM] + [VMEM] * (1 + len(arrays)) + [HBM] * len(earlier),
+        [jax.ShapeDtypeStruct((2 * TILE, HD), jnp.bfloat16) for _ in range(HEADS)],
+        [
+            pltpu.VMEM((tiles, TILE, 3 * HD), jnp.bfloat16),
+            pltpu.VMEM((tiles, TILE, HD), jnp.bfloat16),
+            *tables(tiles),
+        ],
+        MICROSECOND * 8,
+        2 * tiles * TILE * width,
+    )
+
+
+def head_project(info, pieces, weights, earlier):
+    width = weights.shape[1]
+    tiles = 2 * HEADS
+    arrays = [array for _, _, array in pieces]
+    shapes = tuple((k, start, array.shape[0]) for k, start, array in pieces)
+    return call(
+        functools.partial(project_kernel, shapes, len(earlier)),
+        [info, weights, *arrays, *earlier],
+        [SMEM] + [VMEM] * (1 + len(arrays)) + [HBM] * len(earlier),
+        [
+            jax.ShapeDtypeStruct((tiles, TILE, 3 * HD), jnp.bfloat16),
+            jax.ShapeDtypeStruct((tiles, TILE, HD), jnp.float32),
+        ],
+        [],
+        MICROSECOND * 5,
+        2 * tiles * TILE * width,
+    )
+
+
+def head_backward(info, tile_cluster, kept, scales, grads, spacing):
+    tiles = kept.shape[0]
+    out = call(
+        functools.partial(backward_kernel, spacing),
+        [tile_cluster, info, kept, scales, grads.reshape(tiles, TILE, HD)],
+        [SMEM, SMEM] + [VMEM] * 3,
+        jax.ShapeDtypeStruct((tiles, TILE, 3 * HD), jnp.bfloat16),
+        tables(tiles),
+        MICROSECOND * 7,
+        2 * tiles * TILE * 8 * HD,
+    )
+    return out.reshape(HEADS, 2 * TILE, 3 * HD)
+
 
 def copy_kernel(starts, *refs):
     count = len(starts)
@@ -265,26 +304,28 @@
     )
 
 
-def finish_kernel(info_ref, *refs):
-    att_refs, (x_ref, w_ref, out_ref) = refs[:HEADS], refs[HEADS:]
+def finish_kernel(unread, info_ref, *refs):
+    att_refs, refs = refs[:HEADS], refs[HEADS:]
+    x_ref, w_ref, (out_ref, att) = refs[0], refs[1], refs[2 + unread :]
     flip = info_ref[0]
-    att = jnp.concatenate([ref[...] for ref in att_refs], axis=1)
+    for k in range(HEADS):
+        att[flip ^ k] = att_refs[k][...]
+    whole = jnp.concatenate([att[k] for k in range(HEADS)], axis=1)
     block = 256
     for start in range(0, x_ref.shape[1], block):
         columns = slice(start, start + block)
-        w = jnp.concatenate([w_ref[flip ^ k, :, columns] for k in range(HEADS)], axis=0)
-        out_ref[:, columns] = low(high(x_ref[:, columns]) + dot(att, w, NN))
-
-
-def finish(info, attention, current, w_fin):
+        out_ref[:, columns] = low(high(x_ref[:, columns]) + dot(whole, w_ref[:, columns], NN))
+
+
+def finish(info, attention, current, w_fin, earlier):
     tokens, width = current.shape
     return call(
-        finish_kernel,
-        [info, *attention, current, w_fin.reshape(HEADS, HD, width)],
-        [SMEM] + [VMEM] * (HEADS + 2),
+        functools.partial(finish_kernel, len(earlier)),
+        [info, *attention, current, w_fin, *earlier],
+        [SMEM] + [VMEM] * (HEADS + 2) + [HBM] * len(earlier),
         jax.ShapeDtypeStruct((tokens, width), jnp.bfloat16),
-        [],
-        2 * tokens * width * HEADS * HD,
+        [pltpu.VMEM((HEADS, tokens, HD), jnp.bfloat16)],
+        MICROSECOND,
         2 * width * HEADS * HD,
     )
 
@@ -347,17 +388,18 @@
     return lax.ppermute(block, "seq", route)
 
 
-def gather_rows(x, earlier):
+def gather_rows(x, top_after, bottom_after):
     half = x.shape[0] // 2
     top, bottom = x[:half], x[half:]
-    x_top, y_bottom = partner(top, 2), partner(bottom, 4)
-    x_bottom, y_top = partner(bottom, 2), partner(top, 4)
-    relay_top, relay_bottom = x_top, y_bottom
-    if earlier:
-        relay_top, relay_bottom = rows_after([x_top, y_bottom], [0, 0], half, earlier)
+    relay_top, relay_bottom = partner(top, 2), partner(bottom, 4)
+    pieces = [(0, 0, x), (2, 0, relay_top), (4, half, relay_bottom)]
+    pieces += [(2, half, partner(bottom, 2)), (4, 0, partner(top, 4))]
+    if top_after:
+        relay_top, relay_bottom = rows_after([relay_top, relay_bottom], [0, 0], half, top_after)
+    else:
+        relay_bottom = rows_after([relay_bottom], [0], half, bottom_after)[0]
     far_top, far_bottom = partner(relay_top, 4), partner(relay_bottom, 2)
-    pieces = [(0, 0, x), (2, 0, x_top), (4, half, y_bottom), (2, half, x_bottom)]
-    pieces += [(4, 0, y_top), (6, 0, far_top), (6, half, far_bottom)]
+    pieces += [(6, 0, far_top), (6, half, far_bottom)]
     return pieces + [(k + 1, start, partner(block, 1)) for k, start, block in pieces]
 
 
@@ -408,11 +450,11 @@
     own = lax.axis_index("seq").astype(jnp.int32)
     if spacing == 1:
         info = jnp.stack([own, own, jnp.zeros_like(own)])
-        gather, spread, collect, collect_each = gather_rows, all_swap, all_swap, swap
+        gather, spread, collect, collect_grads = gather_rows, all_swap, swap, all_swap
     else:
         info = jnp.stack([jnp.zeros_like(own), own // spacing, own % spacing])
 
-        def gather(x, earlier):
+        def gather(x, top_after, bottom_after):
             copies = jnp.broadcast_to(x, (HEADS, *x.shape))
             return [(k, 0, block) for k, block in enumerate(to_heads(copies, own, spacing))]
 
@@ -420,31 +462,27 @@
             return to_heads(blocks, own, spacing)
 
         def collect(blocks):
+            return list(to_tokens(jnp.stack(blocks), own, spacing, tokens))
+
+        def collect_grads(blocks):
             return to_tokens(blocks, own, spacing, tokens)
-
-        def collect_each(blocks):
-            return list(collect(jnp.stack(blocks)))
 
     own_head = w_rows.reshape(3, HEADS, HD, -1)
     own_head = lax.dynamic_index_in_dim(own_head, info[1], 1, keepdims=False)
     own_head = own_head.reshape(3 * HD, -1)
-    spreading = spread_grads(upstream, w_fin)
-    stored_pieces = gather(stored, [])
-    grad_attention = spread(spreading)
+    grad_attention = spread(spread_grads(upstream, w_fin))
+    stored_pieces = gather(stored, [], [grad_attention])
     earlier = [block for k, _, block in stored_pieces if k == HEADS - 2]
     normed = norm_after(current, [*earlier, grad_attention])
-    grads = head_work(
-        info, tile_cluster, stored_pieces, own_head, spacing, grad_attention, [normed]
-    )
-    current_pieces = gather(normed, [grads])
-    returned_grads = collect(grads)
-    outputs = head_work(
-        info, tile_cluster, current_pieces, own_head, spacing, earlier=[grads]
-    )
-    returned = collect_each(outputs)
+    kept, scales = head_project(info, stored_pieces, own_head, [normed])
+    current_pieces = gather(normed, [scales], [])
+    grads = head_backward(info, tile_cluster, kept, scales, grad_attention, spacing)
+    returned_grads = collect_grads(grads)
+    outputs = head_forward(info, tile_cluster, current_pieces, own_head, spacing, [grads])
+    returned = collect(outputs)
     grad_self = finish_back(returned_grads, stored, upstream, w_rows)
     grad_input = passed_along(grad_self, "pipe", -1)
-    result = finish(info, returned, current, w_fin)
+    result = finish(info, returned, current, w_fin, [grad_self])
     next_input = passed_along(result, "pipe", 1)
     return (next_input[None], grad_input[None])
 

time: 114 us -> 124 us (1.088)
  the two profiles are of different devices: /device:TPU:0 before, /device:TPU:18 now
where the time goes in v10:
time: 124 us; the launch traced here: 122 us
  starting transfers between devices  37.7 us (30%)
  waiting for transfers between devices  37.7 us (30%)
  Pallas kernels  34.2 us (28%)
  local copies, waits for them, and re-layouts  11 us (9%)
    pallas_call x7, Pallas kernels, call(): pl.pallas_call(kernel, in_specs=in_specs, out_specs=[VMEM] * len(out_shap...  31.5 us
    ppermute x33, waiting for transfers between devices, partner(): return lax.ppermute(block, 'seq', route)  23.5 us
    ppermute x33, starting transfers between devices, partner(): return lax.ppermute(block, 'seq', route)  22.6 us
    ppermute x2, waiting for transfers between devices, passed_along(): return lax.ppermute(block, axis, route)  14.2 us
    all_to_all x2, starting transfers between devices, all_swap(): lax.all_to_all(blocks, 'seq', split_axis=0, concat_axis=0, tiled=True)  9.28 us
    unnamed x48, local copies, waits for them, and re-layouts  8.26 us
    ppermute x2, starting transfers between devices, passed_along(): return lax.ppermute(block, axis, route)  5.84 us
    pallas_call x2, Pallas kernels, rows_after(): pl.pallas_call(functools.partial(copy_kernel, starts), in_specs=[HBM] * (...  2.63 us
  transfers between devices with their start and end apart: 37, of which 10 were waited for; matrix products, arithmetic and copies ran while one was open for 2% of the time, Pallas kernels for 25%

profile of v10, /device:TPU:18, one launch (start us, length us, event | category | flops | bytes accessed | tf_op | source)
XLA Modules:
  0.0 121.6 jit_solution(8968311875833924553)
XLA Ops:
  0.6 1.6 %copy-done.2 = bf16[1,1024,1024]{2,1,0:T(8,128)(2,1)S(1)} copy-done((bf16[1,1024,1024]{2,1,0:T(8,128)(2,1)S(1)}, bf16[1,1024,1024]{2,1,0:T(8,128)(2,1)}, u32[]{:S(2)}) %copy-start.2) | copy-done | bytes 2097176
  2.2 1.0 copy-done.4
  3.3 2.9 %shard_map.77 = bf16[8,256,128]{2,1,0:T(8,128)(2,1)} custom-call(bf16[256,1024]{1,0:T(8,128)(2,1)S(1)} %bitcast.30, bf16[8,128,1024]{2,1,0:T(8,128)(2,1)S(1)} %bitcast.27), custom_call_target="tpu_custom_call" | custom-call | flops 3449999872 | bytes 2097152 | tf_op jit(solution)/shard_map/pallas_call | solution.py:42
  6.1 4.3 %all-to-all-start = ((bf16[8,256,128]{2,1,0:T(8,128)(2,1)}), bf16[8,256,128]{2,1,0:T(8,128)(2,1)S(1)}, u32[]{:S(2)}, u32[]{:S(2)}) async-start(bf16[8,256,128]{2,1,0:T(8,128)(2,1)} %shard_map.77), calls=%async_computation | async-start | bytes 1048576 | tf_op jit(solution)/shard_map/all_to_all | solution.py:412
  10.4 0.7 slice_bitcast_fusion
  11.1 2.0 %collective-permute-start.2 = (bf16[128,1024]{1,0:T(8,128)(2,1)S(1)}, bf16[128,1024]{1,0:T(8,128)(2,1)S(1)}, u32[]{:S(2)}, u32[]{:S(2)}) collective-permute-start(bf16[128,1024]{1,0:T(8,128)(2,1)S(1)} %get-tuple-element.28), channel_id=1, source_target_pairs={{0,4},{1,5},{2,6},{3,7},{4,0},{5,1},{6,2},{7,3},{8,12},{9,13},{10,... | collective-permute-start | bytes 786440 | tf_op jit(solution)/shard_map/ppermute | solution.py:388
  13.2 1.5 %collective-permute-start.8 = (bf16[128,1024]{1,0:T(8,128)(2,1)S(1)}, bf16[128,1024]{1,0:T(8,128)(2,1)S(1)}, u32[]{:S(2)}, u32[]{:S(2)}) collective-permute-start(bf16[128,1024]{1,0:T(8,128)(2,1)S(1)} %get-tuple-element.28), channel_id=1, source_target_pairs={{0,2},{1,3},{2,0},{3,1},{4,6},{5,7},{6,4},{7,5},{8,10},{9,11},{10,... | collective-permute-start | bytes 786440 | tf_op jit(solution)/shard_map/ppermute | solution.py:388
  15.2 8.2 %collective-permute-done.refs_1_ = bf16[128,1024]{1,0:T(8,128)(2,1)S(1)} collective-permute-done((bf16[128,1024]{1,0:T(8,128)(2,1)}, bf16[128,1024]{1,0:T(8,128)(2,1)S(1)}, u32[]{:S(2)}, u32[]{:S(2)}) %collective-permute-start) | collective-permute-done | bytes 262176 | tf_op jit(solution)/shard_map/ppermute | solution.py:388
  23.4 1.9 %collective-permute-start.1 = (bf16[128,1024]{1,0:T(8,128)(2,1)S(1)}, bf16[128,1024]{1,0:T(8,128)(2,1)S(1)}, u32[]{:S(2)}, u32[]{:S(2)}) collective-permute-start(bf16[128,1024]{1,0:T(8,128)(2,1)S(1)} %collective-permute-done.refs_1_), channel_id=1, source_target_pairs={{0,4},{1,5},{2,6},{3,7},{4,0},{5,1},{6,2},{7,3},{8,12},{9,13},{10,... | collective-permute-start | bytes 786440 | tf_op jit(solution)/shard_map/ppermute | solution.py:388
  25.9 0.7 shard_map.78
  26.6 2.2 %collective-permute-done.8.refs_3_ = bf16[128,1024]{1,0:T(8,128)(2,1)S(1)} collective-permute-done((bf16[128,1024]{1,0:T(8,128)(2,1)S(1)}, bf16[128,1024]{1,0:T(8,128)(2,1)S(1)}, u32[]{:S(2)}, u32[]{:S(2)}) %collective-permute-start.8) | collective-permute-done | bytes 262176 | tf_op jit(solution)/shard_map/ppermute | solution.py:388
  28.9 1.6 %collective-permute-start.3 = (bf16[128,1024]{1,0:T(8,128)(2,1)}, bf16[128,1024]{1,0:T(8,128)(2,1)S(1)}, u32[]{:S(2)}, u32[]{:S(2)}) collective-permute-start(bf16[128,1024]{1,0:T(8,128)(2,1)} %shard_map.78), channel_id=1, source_target_pairs={{0,2},{1,3},{2,0},{3,1},{4,6},{5,7},{6,4},{7,5},{8,10},{9,11},{10,... | collective-permute-start | bytes 786440 | tf_op jit(solution)/shard_map/ppermute | solution.py:388
  30.5 0.7 copy-done.16
  31.2 1.3 %constant_dynamic-slice_fusion = bf16[3,1,128,1024]{3,2,1,0:T(8,128)(2,1)S(1)} fusion(bf16[3,8,128,1024]{3,2,1,0:T(8,128)(2,1)} %bitcast.33, s32[]{:T(128)S(6)} %select_n.4), kind=kLoop, calls=%fused_computation.3 | loop fusion | bytes 1572868 | tf_op jit(solution)/shard_map/jit(dynamic_index_in_dim)/dynamic_slice | solution.py:471
  32.5 3.1 %collective-permute-done.1.refs_0_.refs_5_ = bf16[128,1024]{1,0:T(8,128)(2,1)S(1)} collective-permute-done((bf16[128,1024]{1,0:T(8,128)(2,1)S(1)}, bf16[128,1024]{1,0:T(8,128)(2,1)S(1)}, u32[]{:S(2)}, u32[]{:S(2)}) %collective-permute-start.1) | collective-permute-done | bytes 262176 | tf_op jit(solution)/shard_map/ppermute | solution.py:388
  36.1 1.1 collective-permute-done.3.refs_1_.refs_6_
  37.5 0.7 fusion
  38.2 1.3 %collective-permute-start.5 = (bf16[128,1024]{1,0:T(8,128)(2,1)S(1)}, bf16[128,1024]{1,0:T(8,128)(2,1)S(1)}, u32[]{:S(2)}, u32[]{:S(2)}) collective-permute-start(bf16[128,1024]{1,0:T(8,128)(2,1)S(1)} %get-tuple-element.26), channel_id=1, source_target_pairs={{0,4},{1,5},{2,6},{3,7},{4,0},{5,1},{6,2},{7,3},{8,12},{9,13},{10,... | collective-permute-start | bytes 786440 | tf_op jit(solution)/shard_map/ppermute | solution.py:388
  39.6 1.5 %collective-permute-start.6 = (bf16[128,1024]{1,0:T(8,128)(2,1)S(1)}, bf16[128,1024]{1,0:T(8,128)(2,1)S(1)}, u32[]{:S(2)}, u32[]{:S(2)}) collective-permute-start(bf16[128,1024]{1,0:T(8,128)(2,1)S(1)} %get-tuple-element.26), channel_id=1, source_target_pairs={{0,2},{1,3},{2,0},{3,1},{4,6},{5,7},{6,4},{7,5},{8,10},{9,11},{10,... | collective-permute-start | bytes 786440 | tf_op jit(solution)/shard_map/ppermute | solution.py:388
  41.0 0.6 collective-permute-start.4
  41.6 0.7 collective-permute-start.7
  42.3 5.1 %shard_map.80 = (bf16[16,128,384]{2,1,0:T(8,128)(2,1)S(1)}, f32[16,128,128]{2,1,0:T(8,128)S(1)}) custom-call(s32[3]{0:T(128)S(1)} %pad_add_fusion.info_ref, bf16[384,1024]{1,0:T(8,128)(2,1)S(1)} %bitcast.20, bf16[256,1024]{1,0:T(8,128)(2,1)S(1)} %bitcast.24, bf16[128,1024]{1,0:T(8,128)(2,1)S(1)} %copy-done.9, bf16[128,1024]{1,0:T(8,128)(2,1)S(1)} %copy-done.11, ...), custom_call_target="tpu_custom_call" | custom-call | flops 5750000128 | bytes 4194304 | tf_op jit(solution)/shard_map/pallas_call | solution.py:42
  47.5 6.3 %collective-permute-done.4.refs_0_.refs_1_ = bf16[128,1024]{1,0:T(8,128)(2,1)} collective-permute-done((bf16[128,1024]{1,0:T(8,128)(2,1)}, bf16[128,1024]{1,0:T(8,128)(2,1)}, u32[]{:S(2)}, u32[]{:S(2)}) %collective-permute-start.4) | collective-permute-done | bytes 262176 | tf_op jit(solution)/shard_map/ppermute | solution.py:388
  53.7 1.9 %shard_map.81 = (bf16[128,1024]{1,0:T(8,128)(2,1)}, bf16[128,1024]{1,0:T(8,128)(2,1)}) custom-call(bf16[128,1024]{1,0:T(8,128)(2,1)} %collective-permute-done.4.refs_0_.refs_1_, bf16[128,1024]{1,0:T(8,128)(2,1)S(1)} %collective-permute-done.5.refs_1_.refs_2_, f32[16,128,128]{2,1,0:T(8,128)S(1)} %get-tuple-element.14.refs_2_.scales), custom_call_target="tpu_custom_call" | custom-call | flops 1150000000 | tf_op jit(solution)/shard_map/pallas_call | solution.py:251
  55.7 0.8 collective-permute-start.17
  56.4 1.3 %collective-permute-start.18 = (bf16[128,1024]{1,0:T(8,128)(2,1)}, bf16[128,1024]{1,0:T(8,128)(2,1)S(1)}, u32[]{:S(2)}, u32[]{:S(2)}) collective-permute-start(bf16[128,1024]{1,0:T(8,128)(2,1)} %get-tuple-element.16), channel_id=1, source_target_pairs={{0,2},{1,3},{2,0},{3,1},{4,6},{5,7},{6,4},{7,5},{8,10},{9,11},{10,... | collective-permute-start | bytes 786440 | tf_op jit(solution)/shard_map/ppermute | solution.py:388
  57.8 7.7 %shard_map.82 = bf16[16,128,384]{2,1,0:T(8,128)(2,1)} custom-call(s32[16]{0:T(128)S(1)} %copy-done.20, s32[3]{0:T(128)S(1)} %pad_add_fusion.info_ref, bf16[16,128,384]{2,1,0:T(8,128)(2,1)S(1)} %get-tuple-element.17.kept, f32[16,128,128]{2,1,0:T(8,128)S(1)} %get-tuple-element.14.refs_2_.scales, bf16[16,128,128]{2,1,0:T(8,128)(2,1)S(1)} %bitcast.19), custom_call_target="tpu_custom_call" | custom-call | flops 8049999872 | bytes 4194304 | tf_op jit(solution)/shard_map/pallas_call | solution.py:42
  65.5 5.0 %all-to-all-start.1 = ((bf16[8,256,384]{2,1,0:T(8,128)(2,1)}), bf16[8,256,384]{2,1,0:T(8,128)(2,1)}, u32[]{:S(2)}, u32[]{:S(2)}) async-start(bf16[8,256,384]{2,1,0:T(8,128)(2,1)} %bitcast.10.refs_14_), calls=%async_computation.1 | async-start | bytes 3145728 | tf_op jit(solution)/shard_map/all_to_all | solution.py:412
  71.6 0.7 copy-done.18
  72.5 1.0 collective-permute-done.23.refs_11_
  73.9 0.9 copy-done.19
  74.8 9.0 %shard_map.83 = (bf16[256,128]{1,0:T(8,128)(2,1)S(1)}, bf16[256,128]{1,0:T(8,128)(2,1)S(1)}, bf16[256,128]{1,0:T(8,128)(2,1)S(1)}, bf16[256,128]{1,0:T(8,128)(2,...) custom-call(s32[16]{0:T(128)S(1)} %copy-done.20, ...), custom_call_target="tpu_custom_call" | custom-call | flops 9200000000 | bytes 4194304 | tf_op jit(solution)/shard_map/pallas_call | solution.py:42
  83.9 0.6 copy-done.21
  84.7 0.6 collective-permute-start.27
  85.3 1.1 collective-permute-start.28
  86.4 1.5 %collective-permute-start.29 = (bf16[256,128]{1,0:T(8,128)(2,1)}, bf16[256,128]{1,0:T(8,128)(2,1)S(1)}, u32[]{:S(2)}, u32[]{:S(2)}) collective-permute-start(bf16[256,128]{1,0:T(8,128)(2,1)} %get-tuple-element.22), channel_id=1, source_target_pairs={{0,4},{1,5},{2,6},{3,7},{4,0},{5,1},{6,2},{7,3},{8,12},{9,13},{10,... | collective-permute-start | bytes 196616 | tf_op jit(solution)/shard_map/ppermute | solution.py:388
  88.2 1.5 %collective-permute-start.31 = (bf16[256,128]{1,0:T(8,128)(2,1)S(1)}, bf16[256,128]{1,0:T(8,128)(2,1)S(1)}, u32[]{:S(2)}, u32[]{:S(2)}) collective-permute-start(bf16[256,128]{1,0:T(8,128)(2,1)S(1)} %get-tuple-element.24), channel_id=1, source_target_pairs={{0,6},{1,7},{2,4},{3,5},{4,2},{5,3},{6,0},{7,1},{8,14},{9,15},{10,... | collective-permute-start | bytes 196616 | tf_op jit(solution)/shard_map/ppermute | solution.py:388
  89.7 1.2 collective-permute-done.27.refs_2_
  90.8 1.4 %collective-permute-start.32 = (bf16[256,128]{1,0:T(8,128)(2,1)S(1)}, bf16[256,128]{1,0:T(8,128)(2,1)S(1)}, u32[]{:S(2)}, u32[]{:S(2)}) collective-permute-start(bf16[256,128]{1,0:T(8,128)(2,1)S(1)} %get-tuple-element.25), channel_id=1, source_target_pairs={{0,7},{1,6},{2,5},{3,4},{4,3},{5,2},{6,1},{7,0},{8,15},{9,14},{10,... | collective-permute-start | bytes 196616 | tf_op jit(solution)/shard_map/ppermute | solution.py:388
  92.2 5.3 %shard_map.84.refs_10_ = bf16[256,1024]{1,0:T(8,128)(2,1)} custom-call(bf16[8,256,384]{2,1,0:T(8,128)(2,1)} %all-to-all-done.1.grad_ref, bf16[256,1024]{1,0:T(8,128)(2,1)} %bitcast.22, bf16[256,1024]{1,0:T(8,128)(2,1)} %bitcast.29, bf16[3072,1024]{1,0:T(8,128)(2,1)} %bitcast.34), custom_call_target="tpu_custom_call" | custom-call | flops 5750000128 | bytes 6291456 | tf_op jit(solution)/shard_map/pallas_call | solution.py:42
  97.6 1.0 copy-done.5
  98.7 1.3 %shard_map.85 = bf16[256,1024]{1,0:T(8,128)(2,1)S(1)} custom-call(s32[3]{0:T(128)S(1)} %pad_add_fusion.info_ref, bf16[256,128]{1,0:T(8,128)(2,1)S(1)} %copy-done.22, bf16[256,128]{1,0:T(8,128)(2,1)S(1)} %collective-permute-done.26.refs_1_, bf16[256,128]{1,0:T(8,128)(2,1)S(1)} %collective-permute-done.27.refs_2_, ...), custom_call_target="tpu_custom_call" | custom-call | flops 1150000000 | bytes 2097152 | tf_op jit(solution)/shard_map/pallas_call | solution.py:42
  99.9 3.5 %collective-permute-start.33 = (bf16[256,1024]{1,0:T(8,128)(2,1)S(1)}, bf16[256,1024]{1,0:T(8,128)(2,1)S(1)}, u32[]{:S(2)}, u32[]{:S(2)}) collective-permute-start(bf16[256,1024]{1,0:T(8,128)(2,1)S(1)} %shard_map.85), channel_id=1, source_target_pairs={{0,8},{8,16},{16,24},{1,9},{9,17},{17,25},{2,10},{10,18},{18,26},{... | collective-permute-start | bytes 1572872 | tf_op jit(solution)/shard_map/ppermute | solution.py:442
  103.4 2.4 %collective-permute-start.34 = (bf16[256,1024]{1,0:T(8,128)(2,1)S(1)}, bf16[256,1024]{1,0:T(8,128)(2,1)S(1)}, u32[]{:S(2)}, u32[]{:S(2)}) collective-permute-start(bf16[256,1024]{1,0:T(8,128)(2,1)S(1)} %copy-done.5), channel_id=1, source_target_pairs={{8,0},{16,8},{24,16},{9,1},{17,9},{25,17},{10,2},{18,10},{26,18},{... | collective-permute-start | bytes 1572872 | tf_op jit(solution)/shard_map/ppermute | solution.py:442
  105.8 10.5 %collective-permute-done.33 = bf16[256,1024]{1,0:T(8,128)(2,1)S(1)} collective-permute-done((bf16[256,1024]{1,0:T(8,128)(2,1)S(1)}, bf16[256,1024]{1,0:T(8,128)(2,1)S(1)}, u32[]{:S(2)}, u32[]{:S(2)}) %collective-permute-start.33) | collective-permute-done | bytes 524320 | tf_op jit(solution)/shard_map/ppermute | solution.py:442
  116.3 3.7 %collective-permute-done.34 = bf16[256,1024]{1,0:T(8,128)(2,1)S(1)} collective-permute-done((bf16[256,1024]{1,0:T(8,128)(2,1)S(1)}, bf16[256,1024]{1,0:T(8,128)(2,1)S(1)}, u32[]{:S(2)}, u32[]{:S(2)}) %collective-permute-start.34) | collective-permute-done | bytes 524320 | tf_op jit(solution)/shard_map/ppermute | solution.py:442
  120.0 0.8 copy.12
  120.8 0.8 copy.13
  (87 shorter events, 4.2 us)
Async XLA Ops:
  3.3 7.1 %copy-start = (bf16[1,256,1024]{2,1,0:T(8,128)(2,1)S(1)}, bf16[1,256,1024]{2,1,0:T(8,128)(2,1)}, u32[]{:S(2)}) copy-start(bf16[1,256,1024]{2,1,0:T(8,128)(2,1)} %param.7) | copy-start | bytes 1572868
  6.1 19.7 %all-to-all-start = ((bf16[8,256,128]{2,1,0:T(8,128)(2,1)}), bf16[8,256,128]{2,1,0:T(8,128)(2,1)S(1)}, u32[]{:S(2)}, u32[]{:S(2)}) async-start(bf16[8,256,128]{2,1,0:T(8,128)(2,1)} %shard_map.77), calls=%async_computation | async-start | bytes 1048576 | tf_op jit(solution)/shard_map/all_to_all | solution.py:412
  11.1 12.3 %collective-permute-start = (bf16[128,1024]{1,0:T(8,128)(2,1)}, bf16[128,1024]{1,0:T(8,128)(2,1)S(1)}, u32[]{:S(2)}, u32[]{:S(2)}) collective-permute-start(bf16[128,1024]{1,0:T(8,128)(2,1)} %get-tuple-element.29), channel_id=1, source_target_pairs={{0,2},{1,3},{2,0},{3,1},{4,6},{5,7},{6,4},{7,5},{8,10},{9,11},{10,... | collective-permute-start | bytes 786440 | tf_op jit(solution)/shard_map/ppermute | solution.py:388
  11.1 26.1 %copy-start.1 = (bf16[1,256,1024]{2,1,0:T(8,128)(2,1)S(1)}, bf16[1,256,1024]{2,1,0:T(8,128)(2,1)}, u32[]{:S(2)}) copy-start(bf16[1,256,1024]{2,1,0:T(8,128)(2,1)} %param.6) | copy-start | bytes 1572868
  11.1 14.2 %collective-permute-start.2 = (bf16[128,1024]{1,0:T(8,128)(2,1)S(1)}, bf16[128,1024]{1,0:T(8,128)(2,1)S(1)}, u32[]{:S(2)}, u32[]{:S(2)}) collective-permute-start(bf16[128,1024]{1,0:T(8,128)(2,1)S(1)} %get-tuple-element.28), channel_id=1, source_target_pairs={{0,4},{1,5},{2,6},{3,7},{4,0},{5,1},{6,2},{7,3},{8,12},{9,13},{10,... | collective-permute-start | bytes 786440 | tf_op jit(solution)/shard_map/ppermute | solution.py:388
  13.2 15.7 %collective-permute-start.8 = (bf16[128,1024]{1,0:T(8,128)(2,1)S(1)}, bf16[128,1024]{1,0:T(8,128)(2,1)S(1)}, u32[]{:S(2)}, u32[]{:S(2)}) collective-permute-start(bf16[128,1024]{1,0:T(8,128)(2,1)S(1)} %get-tuple-element.28), channel_id=1, source_target_pairs={{0,2},{1,3},{2,0},{3,1},{4,6},{5,7},{6,4},{7,5},{8,10},{9,11},{10,... | collective-permute-start | bytes 786440 | tf_op jit(solution)/shard_map/ppermute | solution.py:388
  14.6 15.9 %collective-permute-start.9 = (bf16[128,1024]{1,0:T(8,128)(2,1)}, bf16[128,1024]{1,0:T(8,128)(2,1)S(1)}, u32[]{:S(2)}, u32[]{:S(2)}) collective-permute-start(bf16[128,1024]{1,0:T(8,128)(2,1)} %get-tuple-element.29), channel_id=1, source_target_pairs={{0,4},{1,5},{2,6},{3,7},{4,0},{5,1},{6,2},{7,3},{8,12},{9,13},{10,... | collective-permute-start | bytes 786440 | tf_op jit(solution)/shard_map/ppermute | solution.py:388
  23.4 12.1 %collective-permute-start.1 = (bf16[128,1024]{1,0:T(8,128)(2,1)S(1)}, bf16[128,1024]{1,0:T(8,128)(2,1)S(1)}, u32[]{:S(2)}, u32[]{:S(2)}) collective-permute-start(bf16[128,1024]{1,0:T(8,128)(2,1)S(1)} %collective-permute-done.refs_1_), channel_id=1, source_target_pairs={{0,4},{1,5},{2,6},{3,7},{4,0},{5,1},{6,2},{7,3},{8,12},{9,13},{10,... | collective-permute-start | bytes 786440 | tf_op jit(solution)/shard_map/ppermute | solution.py:388
  25.3 10.3 %collective-permute-start.11 = (bf16[128,1024]{1,0:T(8,128)(2,1)S(1)}, bf16[128,1024]{1,0:T(8,128)(2,1)}, u32[]{:S(2)}, u32[]{:S(2)}) collective-permute-start(bf16[128,1024]{1,0:T(8,128)(2,1)S(1)} %collective-permute-done.refs_1_), channel_id=1, source_target_pairs={{0,1},{1,0},{2,3},{3,2},{4,5},{5,4},{6,7},{7,6},{8,9},{9,8},{10,11... | collective-permute-start | bytes 786440 | tf_op jit(solution)/shard_map/ppermute | solution.py:388
  25.4 10.7 %collective-permute-start.12 = (bf16[128,1024]{1,0:T(8,128)(2,1)S(1)}, bf16[128,1024]{1,0:T(8,128)(2,1)}, u32[]{:S(2)}, u32[]{:S(2)}) collective-permute-start(bf16[128,1024]{1,0:T(8,128)(2,1)S(1)} %collective-permute-done.2.refs_0_.refs_2_), channel_id=1, source_target_pairs={{0,1},{1,0},{2,3},{3,2},{4,5},{5,4},{6,7},{7,6},{8,9},{9,8},{10,11... | collective-permute-start | bytes 786440 | tf_op jit(solution)/shard_map/ppermute | solution.py:388
  28.9 8.4 %collective-permute-start.3 = (bf16[128,1024]{1,0:T(8,128)(2,1)}, bf16[128,1024]{1,0:T(8,128)(2,1)S(1)}, u32[]{:S(2)}, u32[]{:S(2)}) collective-permute-start(bf16[128,1024]{1,0:T(8,128)(2,1)} %shard_map.78), channel_id=1, source_target_pairs={{0,2},{1,3},{2,0},{3,1},{4,6},{5,7},{6,4},{7,5},{8,10},{9,11},{10,... | collective-permute-start | bytes 786440 | tf_op jit(solution)/shard_map/ppermute | solution.py:388
  30.5 10.5 %collective-permute-start.10 = (bf16[256,1024]{1,0:T(8,128)(2,1)S(1)}, bf16[256,1024]{1,0:T(8,128)(2,1)}, u32[]{:S(2)}, u32[]{:S(2)}) collective-permute-start(bf16[256,1024]{1,0:T(8,128)(2,1)S(1)} %bitcast.23), channel_id=1, source_target_pairs={{0,1},{1,0},{2,3},{3,2},{4,5},{5,4},{6,7},{7,6},{8,9},{9,8},{10,11... | collective-permute-start | bytes 1572872 | tf_op jit(solution)/shard_map/ppermute | solution.py:388
  31.2 11.1 %copy-start.9 = (bf16[128,1024]{1,0:T(8,128)(2,1)S(1)}, bf16[128,1024]{1,0:T(8,128)(2,1)}, u32[]{:S(2)}) copy-start(bf16[128,1024]{1,0:T(8,128)(2,1)} %copy-done.8) | copy-start | bytes 786436
  31.2 11.1 %copy-start.11 = (bf16[128,1024]{1,0:T(8,128)(2,1)S(1)}, bf16[128,1024]{1,0:T(8,128)(2,1)}, u32[]{:S(2)}) copy-start(bf16[128,1024]{1,0:T(8,128)(2,1)} %copy-done.10) | copy-start | bytes 786436
  31.2 11.1 %copy-start.15 = (bf16[128,1024]{1,0:T(8,128)(2,1)S(1)}, bf16[128,1024]{1,0:T(8,128)(2,1)}, u32[]{:S(2)}) copy-start(bf16[128,1024]{1,0:T(8,128)(2,1)} %copy-done.14) | copy-start | bytes 786436
  31.2 11.1 %copy-start.17 = (bf16[128,1024]{1,0:T(8,128)(2,1)S(1)}, bf16[128,1024]{1,0:T(8,128)(2,1)}, u32[]{:S(2)}) copy-start(bf16[128,1024]{1,0:T(8,128)(2,1)} %copy-done.16) | copy-start | bytes 786436
  35.5 2.7 %collective-permute-start.13 = (bf16[128,1024]{1,0:T(8,128)(2,1)}, bf16[128,1024]{1,0:T(8,128)(2,1)S(1)}, u32[]{:S(2)}, u32[]{:S(2)}) collective-permute-start(bf16[128,1024]{1,0:T(8,128)(2,1)} %copy-done.14), channel_id=1, source_target_pairs={{0,1},{1,0},{2,3},{3,2},{4,5},{5,4},{6,7},{7,6},{8,9},{9,8},{10,11... | collective-permute-start | bytes 786440 | tf_op jit(solution)/shard_map/ppermute | solution.py:388
  35.6 4.0 %collective-permute-start.14 = (bf16[128,1024]{1,0:T(8,128)(2,1)}, bf16[128,1024]{1,0:T(8,128)(2,1)S(1)}, u32[]{:S(2)}, u32[]{:S(2)}) collective-permute-start(bf16[128,1024]{1,0:T(8,128)(2,1)} %copy-done.16), channel_id=1, source_target_pairs={{0,1},{1,0},{2,3},{3,2},{4,5},{5,4},{6,7},{7,6},{8,9},{9,8},{10,11... | collective-permute-start | bytes 786440 | tf_op jit(solution)/shard_map/ppermute | solution.py:388
  36.1 5.5 %collective-permute-start.15 = (bf16[128,1024]{1,0:T(8,128)(2,1)S(1)}, bf16[128,1024]{1,0:T(8,128)(2,1)S(1)}, u32[]{:S(2)}, u32[]{:S(2)}) collective-permute-start(bf16[128,1024]{1,0:T(8,128)(2,1)S(1)} %collective-permute-done.1.refs_0_.refs_5_), channel_id=1, source_target_pairs={{0,1},{1,0},{2,3},{3,2},{4,5},{5,4},{6,7},{7,6},{8,9},{9,8},{10,11... | collective-permute-start | bytes 786440 | tf_op jit(solution)/shard_map/ppermute | solution.py:388
  37.2 5.1 %collective-permute-start.16 = (bf16[128,1024]{1,0:T(8,128)(2,1)S(1)}, bf16[128,1024]{1,0:T(8,128)(2,1)S(1)}, u32[]{:S(2)}, u32[]{:S(2)}) collective-permute-start(bf16[128,1024]{1,0:T(8,128)(2,1)S(1)} %collective-permute-done.3.refs_1_.refs_6_), channel_id=1, source_target_pairs={{0,1},{1,0},{2,3},{3,2},{4,5},{5,4},{6,7},{7,6},{8,9},{9,8},{10,11... | collective-permute-start | bytes 786440 | tf_op jit(solution)/shard_map/ppermute | solution.py:388
  38.2 15.5 %collective-permute-start.5 = (bf16[128,1024]{1,0:T(8,128)(2,1)S(1)}, bf16[128,1024]{1,0:T(8,128)(2,1)S(1)}, u32[]{:S(2)}, u32[]{:S(2)}) collective-permute-start(bf16[128,1024]{1,0:T(8,128)(2,1)S(1)} %get-tuple-element.26), channel_id=1, source_target_pairs={{0,4},{1,5},{2,6},{3,7},{4,0},{5,1},{6,2},{7,3},{8,12},{9,13},{10,... | collective-permute-start | bytes 786440 | tf_op jit(solution)/shard_map/ppermute | solution.py:388
  39.6 18.2 %collective-permute-start.6 = (bf16[128,1024]{1,0:T(8,128)(2,1)S(1)}, bf16[128,1024]{1,0:T(8,128)(2,1)S(1)}, u32[]{:S(2)}, u32[]{:S(2)}) collective-permute-start(bf16[128,1024]{1,0:T(8,128)(2,1)S(1)} %get-tuple-element.26), channel_id=1, source_target_pairs={{0,2},{1,3},{2,0},{3,1},{4,6},{5,7},{6,4},{7,5},{8,10},{9,11},{10,... | collective-permute-start | bytes 786440 | tf_op jit(solution)/shard_map/ppermute | solution.py:388
  41.0 12.7 %collective-permute-start.4 = (bf16[128,1024]{1,0:T(8,128)(2,1)}, bf16[128,1024]{1,0:T(8,128)(2,1)}, u32[]{:S(2)}, u32[]{:S(2)}) collective-permute-start(bf16[128,1024]{1,0:T(8,128)(2,1)} %get-tuple-element.27), channel_id=1, source_target_pairs={{0,2},{1,3},{2,0},{3,1},{4,6},{5,7},{6,4},{7,5},{8,10},{9,11},{10,... | collective-permute-start | bytes 786440 | tf_op jit(solution)/shard_map/ppermute | solution.py:388
  41.6 28.9 %collective-permute-start.7 = (bf16[128,1024]{1,0:T(8,128)(2,1)}, bf16[128,1024]{1,0:T(8,128)(2,1)}, u32[]{:S(2)}, u32[]{:S(2)}) collective-permute-start(bf16[128,1024]{1,0:T(8,128)(2,1)} %get-tuple-element.27), channel_id=1, source_target_pairs={{0,4},{1,5},{2,6},{3,7},{4,0},{5,1},{6,2},{7,3},{8,12},{9,13},{10,... | collective-permute-start | bytes 786440 | tf_op jit(solution)/shard_map/ppermute | solution.py:388
  42.3 28.5 %collective-permute-start.19 = (bf16[256,1024]{1,0:T(8,128)(2,1)S(1)}, bf16[256,1024]{1,0:T(8,128)(2,1)}, u32[]{:S(2)}, u32[]{:S(2)}) collective-permute-start(bf16[256,1024]{1,0:T(8,128)(2,1)S(1)} %shard_map.79.refs_14_.refs_0_), channel_id=1, source_target_pairs={{0,1},{1,0},{2,3},{3,2},{4,5},{5,4},{6,7},{7,6},{8,9},{9,8},{10,11... | collective-permute-start | bytes 1572872 | tf_op jit(solution)/shard_map/ppermute | solution.py:388
  55.7 15.5 %collective-permute-start.17 = (bf16[128,1024]{1,0:T(8,128)(2,1)}, bf16[128,1024]{1,0:T(8,128)(2,1)S(1)}, u32[]{:S(2)}, u32[]{:S(2)}) collective-permute-start(bf16[128,1024]{1,0:T(8,128)(2,1)} %get-tuple-element.15), channel_id=1, source_target_pairs={{0,4},{1,5},{2,6},{3,7},{4,0},{5,1},{6,2},{7,3},{8,12},{9,13},{10,... | collective-permute-start | bytes 786440 | tf_op jit(solution)/shard_map/ppermute | solution.py:388
  56.4 14.9 %collective-permute-start.18 = (bf16[128,1024]{1,0:T(8,128)(2,1)}, bf16[128,1024]{1,0:T(8,128)(2,1)S(1)}, u32[]{:S(2)}, u32[]{:S(2)}) collective-permute-start(bf16[128,1024]{1,0:T(8,128)(2,1)} %get-tuple-element.16), channel_id=1, source_target_pairs={{0,2},{1,3},{2,0},{3,1},{4,6},{5,7},{6,4},{7,5},{8,10},{9,11},{10,... | collective-permute-start | bytes 786440 | tf_op jit(solution)/shard_map/ppermute | solution.py:388
  57.8 7.8 %copy-start.12 = (bf16[128,1024]{1,0:T(8,128)(2,1)}, bf16[128,1024]{1,0:T(8,128)(2,1)S(1)}, u32[]{:S(2)}) copy-start(bf16[128,1024]{1,0:T(8,128)(2,1)S(1)} %collective-permute-done.6.refs_3_) | copy-start | bytes 786436
  57.8 13.9 %collective-permute-start.20 = (bf16[128,1024]{1,0:T(8,128)(2,1)}, bf16[128,1024]{1,0:T(8,128)(2,1)S(1)}, u32[]{:S(2)}, u32[]{:S(2)}) collective-permute-start(bf16[128,1024]{1,0:T(8,128)(2,1)} %collective-permute-done.4.refs_0_.refs_1_), channel_id=1, source_target_pairs={{0,1},{1,0},{2,3},{3,2},{4,5},{5,4},{6,7},{7,6},{8,9},{9,8},{10,11... | collective-permute-start | bytes 786440 | tf_op jit(solution)/shard_map/ppermute | solution.py:388
  65.5 5.0 %copy-start.7 = (bf16[128,1024]{1,0:T(8,128)(2,1)S(1)}, bf16[128,1024]{1,0:T(8,128)(2,1)}, u32[]{:S(2)}) copy-start(bf16[128,1024]{1,0:T(8,128)(2,1)} %copy-done.6) | copy-start | bytes 786436
  65.5 5.3 %copy-start.13 = (bf16[128,1024]{1,0:T(8,128)(2,1)S(1)}, bf16[128,1024]{1,0:T(8,128)(2,1)}, u32[]{:S(2)}) copy-start(bf16[128,1024]{1,0:T(8,128)(2,1)} %copy-done.12) | copy-start | bytes 786436
  65.5 26.7 %all-to-all-start.1 = ((bf16[8,256,384]{2,1,0:T(8,128)(2,1)}), bf16[8,256,384]{2,1,0:T(8,128)(2,1)}, u32[]{:S(2)}, u32[]{:S(2)}) async-start(bf16[8,256,384]{2,1,0:T(8,128)(2,1)} %bitcast.10.refs_14_), calls=%async_computation.1 | async-start | bytes 3145728 | tf_op jit(solution)/shard_map/all_to_all | solution.py:412
  70.5 2.0 %collective-permute-start.21 = (bf16[128,1024]{1,0:T(8,128)(2,1)S(1)}, bf16[128,1024]{1,0:T(8,128)(2,1)S(1)}, u32[]{:S(2)}, u32[]{:S(2)}) collective-permute-start(bf16[128,1024]{1,0:T(8,128)(2,1)S(1)} %copy-done.7), channel_id=1, source_target_pairs={{0,1},{1,0},{2,3},{3,2},{4,5},{5,4},{6,7},{7,6},{8,9},{9,8},{10,11... | collective-permute-start | bytes 786440 | tf_op jit(solution)/shard_map/ppermute | solution.py:388
  70.8 1.8 %collective-permute-start.22 = (bf16[128,1024]{1,0:T(8,128)(2,1)S(1)}, bf16[128,1024]{1,0:T(8,128)(2,1)S(1)}, u32[]{:S(2)}, u32[]{:S(2)}) collective-permute-start(bf16[128,1024]{1,0:T(8,128)(2,1)S(1)} %copy-done.13), channel_id=1, source_target_pairs={{0,1},{1,0},{2,3},{3,2},{4,5},{5,4},{6,7},{7,6},{8,9},{9,8},{10,11... | collective-permute-start | bytes 786440 | tf_op jit(solution)/shard_map/ppermute | solution.py:388
  71.1 2.3 %collective-permute-start.23 = (bf16[128,1024]{1,0:T(8,128)(2,1)}, bf16[128,1024]{1,0:T(8,128)(2,1)S(1)}, u32[]{:S(2)}, u32[]{:S(2)}) collective-permute-start(bf16[128,1024]{1,0:T(8,128)(2,1)} %collective-permute-done.7.refs_4_), channel_id=1, source_target_pairs={{0,1},{1,0},{2,3},{3,2},{4,5},{5,4},{6,7},{7,6},{8,9},{9,8},{10,11... | collective-permute-start | bytes 786440 | tf_op jit(solution)/shard_map/ppermute | solution.py:388
  71.3 2.2 %collective-permute-start.24 = (bf16[128,1024]{1,0:T(8,128)(2,1)S(1)}, bf16[128,1024]{1,0:T(8,128)(2,1)S(1)}, u32[]{:S(2)}, u32[]{:S(2)}) collective-permute-start(bf16[128,1024]{1,0:T(8,128)(2,1)S(1)} %collective-permute-done.17.refs_5_), channel_id=1, source_target_pairs={{0,1},{1,0},{2,3},{3,2},{4,5},{5,4},{6,7},{7,6},{8,9},{9,8},{10,11... | collective-permute-start | bytes 786440 | tf_op jit(solution)/shard_map/ppermute | solution.py:388
  72.3 1.5 %collective-permute-start.25 = (bf16[128,1024]{1,0:T(8,128)(2,1)S(1)}, bf16[128,1024]{1,0:T(8,128)(2,1)S(1)}, u32[]{:S(2)}, u32[]{:S(2)}) collective-permute-start(bf16[128,1024]{1,0:T(8,128)(2,1)S(1)} %collective-permute-done.18.refs_6_), channel_id=1, source_target_pairs={{0,1},{1,0},{2,3},{3,2},{4,5},{5,4},{6,7},{7,6},{8,9},{9,8},{10,11... | collective-permute-start | bytes 786440 | tf_op jit(solution)/shard_map/ppermute | solution.py:388
  84.5 3.7 %collective-permute-start.26 = (bf16[256,128]{1,0:T(8,128)(2,1)S(1)}, bf16[256,128]{1,0:T(8,128)(2,1)S(1)}, u32[]{:S(2)}, u32[]{:S(2)}) collective-permute-start(bf16[256,128]{1,0:T(8,128)(2,1)S(1)} %get-tuple-element.19), channel_id=1, source_target_pairs={{0,1},{1,0},{2,3},{3,2},{4,5},{5,4},{6,7},{7,6},{8,9},{9,8},{10,11... | collective-permute-start | bytes 196616 | tf_op jit(solution)/shard_map/ppermute | solution.py:388
  84.7 6.2 %collective-permute-start.27 = (bf16[256,128]{1,0:T(8,128)(2,1)S(1)}, bf16[256,128]{1,0:T(8,128)(2,1)S(1)}, u32[]{:S(2)}, u32[]{:S(2)}) collective-permute-start(bf16[256,128]{1,0:T(8,128)(2,1)S(1)} %get-tuple-element.20), channel_id=1, source_target_pairs={{0,2},{1,3},{2,0},{3,1},{4,6},{5,7},{6,4},{7,5},{8,10},{9,11},{10,... | collective-permute-start | bytes 196616 | tf_op jit(solution)/shard_map/ppermute | solution.py:388
  85.3 12.3 %collective-permute-start.28 = (bf16[256,128]{1,0:T(8,128)(2,1)}, bf16[256,128]{1,0:T(8,128)(2,1)S(1)}, u32[]{:S(2)}, u32[]{:S(2)}) collective-permute-start(bf16[256,128]{1,0:T(8,128)(2,1)} %get-tuple-element.21), channel_id=1, source_target_pairs={{0,3},{1,2},{2,1},{3,0},{4,7},{5,6},{6,5},{7,4},{8,11},{9,10},{10,... | collective-permute-start | bytes 196616 | tf_op jit(solution)/shard_map/ppermute | solution.py:388
  86.4 11.2 %collective-permute-start.29 = (bf16[256,128]{1,0:T(8,128)(2,1)}, bf16[256,128]{1,0:T(8,128)(2,1)S(1)}, u32[]{:S(2)}, u32[]{:S(2)}) collective-permute-start(bf16[256,128]{1,0:T(8,128)(2,1)} %get-tuple-element.22), channel_id=1, source_target_pairs={{0,4},{1,5},{2,6},{3,7},{4,0},{5,1},{6,2},{7,3},{8,12},{9,13},{10,... | collective-permute-start | bytes 196616 | tf_op jit(solution)/shard_map/ppermute | solution.py:388
  87.9 9.7 %collective-permute-start.30 = (bf16[256,128]{1,0:T(8,128)(2,1)}, bf16[256,128]{1,0:T(8,128)(2,1)S(1)}, u32[]{:S(2)}, u32[]{:S(2)}) collective-permute-start(bf16[256,128]{1,0:T(8,128)(2,1)} %get-tuple-element.23), channel_id=1, source_target_pairs={{0,5},{1,4},{2,7},{3,6},{4,1},{5,0},{6,3},{7,2},{8,13},{9,12},{10,... | collective-permute-start | bytes 196616 | tf_op jit(solution)/shard_map/ppermute | solution.py:388
  88.2 9.4 %collective-permute-start.31 = (bf16[256,128]{1,0:T(8,128)(2,1)S(1)}, bf16[256,128]{1,0:T(8,128)(2,1)S(1)}, u32[]{:S(2)}, u32[]{:S(2)}) collective-permute-start(bf16[256,128]{1,0:T(8,128)(2,1)S(1)} %get-tuple-element.24), channel_id=1, source_target_pairs={{0,6},{1,7},{2,4},{3,5},{4,2},{5,3},{6,0},{7,1},{8,14},{9,15},{10,... | collective-permute-start | bytes 196616 | tf_op jit(solution)/shard_map/ppermute | solution.py:388
  90.8 6.7 %collective-permute-start.32 = (bf16[256,128]{1,0:T(8,128)(2,1)S(1)}, bf16[256,128]{1,0:T(8,128)(2,1)S(1)}, u32[]{:S(2)}, u32[]{:S(2)}) collective-permute-start(bf16[256,128]{1,0:T(8,128)(2,1)S(1)} %get-tuple-element.25), channel_id=1, source_target_pairs={{0,7},{1,6},{2,5},{3,4},{4,3},{5,2},{6,1},{7,0},{8,15},{9,14},{10,... | collective-permute-start | bytes 196616 | tf_op jit(solution)/shard_map/ppermute | solution.py:388
  92.2 5.4 %copy-start.3 = (bf16[1,1024,1024]{2,1,0:T(8,128)(2,1)S(1)}, bf16[1,1024,1024]{2,1,0:T(8,128)(2,1)}, u32[]{:S(2)}) copy-start(bf16[1,1024,1024]{2,1,0:T(8,128)(2,1)} %param.10) | copy-start | bytes 6291460
  92.2 5.4 %copy-start.22 = (bf16[256,128]{1,0:T(8,128)(2,1)S(1)}, bf16[256,128]{1,0:T(8,128)(2,1)}, u32[]{:S(2)}) copy-start(bf16[256,128]{1,0:T(8,128)(2,1)} %copy-done.21) | copy-start | bytes 196612
  99.9 16.4 %collective-permute-start.33 = (bf16[256,1024]{1,0:T(8,128)(2,1)S(1)}, bf16[256,1024]{1,0:T(8,128)(2,1)S(1)}, u32[]{:S(2)}, u32[]{:S(2)}) collective-permute-start(bf16[256,1024]{1,0:T(8,128)(2,1)S(1)} %shard_map.85), channel_id=1, source_target_pairs={{0,8},{8,16},{16,24},{1,9},{9,17},{17,25},{2,10},{10,18},{18,26},{... | collective-permute-start | bytes 1572872 | tf_op jit(solution)/shard_map/ppermute | solution.py:442
  103.4 16.6 %collective-permute-start.34 = (bf16[256,1024]{1,0:T(8,128)(2,1)S(1)}, bf16[256,1024]{1,0:T(8,128)(2,1)S(1)}, u32[]{:S(2)}, u32[]{:S(2)}) collective-permute-start(bf16[256,1024]{1,0:T(8,128)(2,1)S(1)} %copy-done.5), channel_id=1, source_target_pairs={{8,0},{16,8},{24,16},{9,1},{17,9},{25,17},{10,2},{18,10},{26,18},{... | collective-permute-start | bytes 1572872 | tf_op jit(solution)/shard_map/ppermute | solution.py:442
  (12 other events, 18.7 us)

commit v11 on v8

--- a/solution.py
+++ b/solution.py
@@ -233,7 +233,7 @@
         [VMEM] + [HBM] * len(earlier),
         jax.ShapeDtypeStruct(x.shape, jnp.bfloat16),
         [],
-        4 * x.size,
+        MICROSECOND * 10,
         4 * x.size,
     )
 
@@ -266,7 +266,7 @@
 
 
 def finish_kernel(info_ref, *refs):
-    att_refs, (x_ref, w_ref, out_ref) = refs[:HEADS], refs[HEADS:]
+    att_refs, (x_ref, w_ref, _, out_ref) = refs[:HEADS], refs[HEADS:]
     flip = info_ref[0]
     att = jnp.concatenate([ref[...] for ref in att_refs], axis=1)
     block = 256
@@ -276,12 +276,12 @@
         out_ref[:, columns] = low(high(x_ref[:, columns]) + dot(att, w, NN))
 
 
-def finish(info, attention, current, w_fin):
+def finish(info, attention, current, w_fin, earlier):
     tokens, width = current.shape
     return call(
         finish_kernel,
-        [info, *attention, current, w_fin.reshape(HEADS, HD, width)],
-        [SMEM] + [VMEM] * (HEADS + 2),
+        [info, *attention, current, w_fin.reshape(HEADS, HD, width), earlier],
+        [SMEM] + [VMEM] * (HEADS + 2) + [HBM],
         jax.ShapeDtypeStruct((tokens, width), jnp.bfloat16),
         [],
         2 * tokens * width * HEADS * HD,
@@ -349,15 +349,10 @@
 
 def gather_rows(x, earlier):
     half = x.shape[0] // 2
-    top, bottom = x[:half], x[half:]
-    x_top, y_bottom = partner(top, 2), partner(bottom, 4)
-    x_bottom, y_top = partner(bottom, 2), partner(top, 4)
-    relay_top, relay_bottom = x_top, y_bottom
-    if earlier:
-        relay_top, relay_bottom = rows_after([x_top, y_bottom], [0, 0], half, earlier)
+    over_x, over_y = partner(x, 2), partner(x, 4)
+    relay_top, relay_bottom = rows_after([over_x, over_y], [0, half], half, earlier)
     far_top, far_bottom = partner(relay_top, 4), partner(relay_bottom, 2)
-    pieces = [(0, 0, x), (2, 0, x_top), (4, half, y_bottom), (2, half, x_bottom)]
-    pieces += [(4, 0, y_top), (6, 0, far_top), (6, half, far_bottom)]
+    pieces = [(0, 0, x), (2, 0, over_x), (4, 0, over_y), (6, 0, far_top), (6, half, far_bottom)]
     return pieces + [(k + 1, start, partner(block, 1)) for k, start, block in pieces]
 
 
@@ -429,7 +424,7 @@
     own_head = lax.dynamic_index_in_dim(own_head, info[1], 1, keepdims=False)
     own_head = own_head.reshape(3 * HD, -1)
     spreading = spread_grads(upstream, w_fin)
-    stored_pieces = gather(stored, [])
+    stored_pieces = gather(stored, [spreading])
     grad_attention = spread(spreading)
     earlier = [block for k, _, block in stored_pieces if k == HEADS - 2]
     normed = norm_after(current, [*earlier, grad_attention])
@@ -444,7 +439,7 @@
     returned = collect_each(outputs)
     grad_self = finish_back(returned_grads, stored, upstream, w_rows)
     grad_input = passed_along(grad_self, "pipe", -1)
-    result = finish(info, returned, current, w_fin)
+    result = finish(info, returned, current, w_fin, grad_self)
     next_input = passed_along(result, "pipe", 1)
     return (next_input[None], grad_input[None])
 

time: 114 us -> 105 us (0.921)
  the two profiles are of different devices: /device:TPU:0 before, /device:TPU:18 now
where the time goes in v11:
time: 105 us; the launch traced here: 103 us
  starting transfers between devices  36 us (34%)
  Pallas kernels  32.2 us (31%)
  waiting for transfers between devices  27.9 us (27%)
  local copies, waits for them, and re-layouts  6.46 us (6%)
    pallas_call x6, Pallas kernels, call(): pl.pallas_call(kernel, in_specs=in_specs, out_specs=[VMEM] * len(out_shap...  29.3 us
    ppermute x25, starting transfers between devices, partner(): return lax.ppermute(block, 'seq', route)  20.5 us
    ppermute x2, waiting for transfers between devices, passed_along(): return lax.ppermute(block, axis, route)  14.2 us
    ppermute x25, waiting for transfers between devices, partner(): return lax.ppermute(block, 'seq', route)  13.6 us
    all_to_all x2, starting transfers between devices, all_swap(): lax.all_to_all(blocks, 'seq', split_axis=0, concat_axis=0, tiled=True)  9.63 us
    ppermute x2, starting transfers between devices, passed_along(): return lax.ppermute(block, axis, route)  5.84 us
    unnamed x16, local copies, waits for them, and re-layouts  5.27 us
    pallas_call x2, Pallas kernels, rows_after(): pl.pallas_call(functools.partial(copy_kernel, starts), in_specs=[HBM] * (...  2.82 us
  transfers between devices with their start and end apart: 29, of which 12 were waited for; matrix products, arithmetic and copies ran while one was open for 1% of the time, Pallas kernels for 30%

profile of v11, /device:TPU:18, one launch (start us, length us, event | category | flops | bytes accessed | tf_op | source)
XLA Modules:
  0.0 103.4 jit_solution(4019906577323450093)
XLA Ops:
  0.6 0.6 collective-permute-start
  1.2 1.5 %collective-permute-start.1 = (bf16[256,1024]{1,0:T(8,128)(2,1)}, bf16[256,1024]{1,0:T(8,128)(2,1)}, u32[]{:S(2)}, u32[]{:S(2)}) collective-permute-start(bf16[256,1024]{1,0:T(8,128)(2,1)} %bitcast.21), channel_id=1, source_target_pairs={{0,4},{1,5},{2,6},{3,7},{4,0},{5,1},{6,2},{7,3},{8,12},{9,13},{10,... | collective-permute-start | bytes 1572872 | tf_op jit(solution)/shard_map/ppermute | solution.py:347
  2.8 1.6 %copy-done = bf16[1,1024,1024]{2,1,0:T(8,128)(2,1)S(1)} copy-done((bf16[1,1024,1024]{2,1,0:T(8,128)(2,1)S(1)}, bf16[1,1024,1024]{2,1,0:T(8,128)(2,1)}, u32[]{:S(2)}) %copy-start) | copy-done | bytes 2097176
  4.3 1.0 %copy-done.5 = bf16[1,256,1024]{2,1,0:T(8,128)(2,1)S(1)} copy-done((bf16[1,256,1024]{2,1,0:T(8,128)(2,1)S(1)}, bf16[1,256,1024]{2,1,0:T(8,128)(2,1)}, u32[]{:S(2)}) %copy-start.5) | copy-done | bytes 524312
  5.4 2.8 %shard_map.77.refs_2_ = bf16[8,256,128]{2,1,0:T(8,128)(2,1)} custom-call(bf16[256,1024]{1,0:T(8,128)(2,1)S(1)} %bitcast.26, bf16[8,128,1024]{2,1,0:T(8,128)(2,1)S(1)} %bitcast.13), custom_call_target="tpu_custom_call" | custom-call | flops 3449999872 | bytes 2097152 | tf_op jit(solution)/shard_map/pallas_call | solution.py:42
  8.2 4.9 %all-to-all-start = ((bf16[8,256,128]{2,1,0:T(8,128)(2,1)}), bf16[8,256,128]{2,1,0:T(8,128)(2,1)S(1)}, u32[]{:S(2)}, u32[]{:S(2)}) async-start(bf16[8,256,128]{2,1,0:T(8,128)(2,1)} %shard_map.77.refs_2_), calls=%async_computation | async-start | bytes 1048576 | tf_op jit(solution)/shard_map/all_to_all | solution.py:365
  13.1 1.4 %collective-permute-done.refs_0_.refs_4_ = bf16[256,1024]{1,0:T(8,128)(2,1)S(1)} collective-permute-done((bf16[256,1024]{1,0:T(8,128)(2,1)}, bf16[256,1024]{1,0:T(8,128)(2,1)S(1)}, u32[]{:S(2)}, u32[]{:S(2)}) %collective-permute-start) | collective-permute-done | bytes 524320 | tf_op jit(solution)/shard_map/ppermute | solution.py:347
  14.6 0.4 collective-permute-done.1.refs_1_.refs_5_
  14.9 1.0 shard_map.78
  15.9 1.7 %collective-permute-start.3 = (bf16[128,1024]{1,0:T(8,128)(2,1)S(1)}, bf16[128,1024]{1,0:T(8,128)(2,1)}, u32[]{:S(2)}, u32[]{:S(2)}) collective-permute-start(bf16[128,1024]{1,0:T(8,128)(2,1)S(1)} %get-tuple-element.15), channel_id=1, source_target_pairs={{0,2},{1,3},{2,0},{3,1},{4,6},{5,7},{6,4},{7,5},{8,10},{9,11},{10,... | collective-permute-start | bytes 786440 | tf_op jit(solution)/shard_map/ppermute | solution.py:347
  17.6 2.5 %collective-permute-start.2 = (bf16[128,1024]{1,0:T(8,128)(2,1)S(1)}, bf16[128,1024]{1,0:T(8,128)(2,1)}, u32[]{:S(2)}, u32[]{:S(2)}) collective-permute-start(bf16[128,1024]{1,0:T(8,128)(2,1)S(1)} %get-tuple-element.14), channel_id=1, source_target_pairs={{0,4},{1,5},{2,6},{3,7},{4,0},{5,1},{6,2},{7,3},{8,12},{9,13},{10,... | collective-permute-start | bytes 786440 | tf_op jit(solution)/shard_map/ppermute | solution.py:347
  20.3 1.2 %constant_dynamic-slice_fusion = bf16[3,1,128,1024]{3,2,1,0:T(8,128)(2,1)S(1)} fusion(bf16[3,8,128,1024]{3,2,1,0:T(8,128)(2,1)} %bitcast.29, s32[]{:T(128)S(6)} %select_n.4), kind=kLoop, calls=%fused_computation.1 | loop fusion | bytes 1572868 | tf_op jit(solution)/shard_map/jit(dynamic_index_in_dim)/dynamic_slice | solution.py:424
  21.5 0.6 collective-permute-start.7
  22.1 4.0 %collective-permute-done.3.refs_1_.refs_7_ = bf16[128,1024]{1,0:T(8,128)(2,1)} collective-permute-done((bf16[128,1024]{1,0:T(8,128)(2,1)S(1)}, bf16[128,1024]{1,0:T(8,128)(2,1)}, u32[]{:S(2)}, u32[]{:S(2)}) %collective-permute-start.3) | collective-permute-done | bytes 262176 | tf_op jit(solution)/shard_map/ppermute | solution.py:347
  26.1 1.1 %collective-permute-done.2.refs_0_.refs_6_ = bf16[128,1024]{1,0:T(8,128)(2,1)} collective-permute-done((bf16[128,1024]{1,0:T(8,128)(2,1)S(1)}, bf16[128,1024]{1,0:T(8,128)(2,1)}, u32[]{:S(2)}, u32[]{:S(2)}) %collective-permute-start.2) | collective-permute-done | bytes 262176 | tf_op jit(solution)/shard_map/ppermute | solution.py:347
  27.2 0.2 shard_map.79.refs_14_.refs_3_
  27.4 1.1 %collective-permute-start.4 = (bf16[256,1024]{1,0:T(8,128)(2,1)S(1)}, bf16[256,1024]{1,0:T(8,128)(2,1)}, u32[]{:S(2)}, u32[]{:S(2)}) collective-permute-start(bf16[256,1024]{1,0:T(8,128)(2,1)S(1)} %shard_map.79.refs_14_.refs_3_), channel_id=1, source_target_pairs={{0,2},{1,3},{2,0},{3,1},{4,6},{5,7},{6,4},{7,5},{8,10},{9,11},{10,... | collective-permute-start | bytes 1572872 | tf_op jit(solution)/shard_map/ppermute | solution.py:347
  28.5 1.5 %collective-permute-start.5 = (bf16[256,1024]{1,0:T(8,128)(2,1)S(1)}, bf16[256,1024]{1,0:T(8,128)(2,1)}, u32[]{:S(2)}, u32[]{:S(2)}) collective-permute-start(bf16[256,1024]{1,0:T(8,128)(2,1)S(1)} %shard_map.79.refs_14_.refs_3_), channel_id=1, source_target_pairs={{0,4},{1,5},{2,6},{3,7},{4,0},{5,1},{6,2},{7,3},{8,12},{9,13},{10,... | collective-permute-start | bytes 1572872 | tf_op jit(solution)/shard_map/ppermute | solution.py:347
  30.0 12.0 %shard_map.80.refs_2_.refs_13_ = bf16[8,256,384]{2,1,0:T(8,128)(2,1)} custom-call(s32[16]{0:T(128)S(1)} %copy-done.6, s32[3]{0:T(128)S(1)} %pad_add_fusion.refs_1_.info_ref, bf16[384,1024]{1,0:T(8,128)(2,1)S(1)} %bitcast.15, bf16[256,1024]{1,0:T(8,128)(2,1)S(1)} %bitcast.24, bf16[256,1024]{1,0:T(8,128)(2,1)S(1)} %collective-permute-done.refs_0_.refs_4_, ...), custom_call_target="tpu_custom_call" | custom-call | flops 13799999488 | bytes 7340032 | tf_op jit(solution)/shard_map/pallas_call | solution.py:42
  42.0 0.2 collective-permute-done.5.refs_1_.refs_5_
  42.2 1.8 %shard_map.81 = (bf16[128,1024]{1,0:T(8,128)(2,1)}, bf16[128,1024]{1,0:T(8,128)(2,1)}) custom-call(bf16[256,1024]{1,0:T(8,128)(2,1)} %collective-permute-done.4.refs_0_.refs_4_, bf16[256,1024]{1,0:T(8,128)(2,1)} %collective-permute-done.5.refs_1_.refs_5_, bf16[8,256,384]{2,1,0:T(8,128)(2,1)} %shard_map.80.refs_2_.refs_13_), custom_call_target="tpu_custom_call" | custom-call | flops 1150000000 | tf_op jit(solution)/shard_map/pallas_call | solution.py:212
  44.0 1.6 %collective-permute-start.11 = (bf16[128,1024]{1,0:T(8,128)(2,1)}, bf16[128,1024]{1,0:T(8,128)(2,1)S(1)}, u32[]{:S(2)}, u32[]{:S(2)}) collective-permute-start(bf16[128,1024]{1,0:T(8,128)(2,1)} %get-tuple-element.16), channel_id=1, source_target_pairs={{0,4},{1,5},{2,6},{3,7},{4,0},{5,1},{6,2},{7,3},{8,12},{9,13},{10,... | collective-permute-start | bytes 786440 | tf_op jit(solution)/shard_map/ppermute | solution.py:347
  45.6 1.5 %collective-permute-start.12 = (bf16[128,1024]{1,0:T(8,128)(2,1)}, bf16[128,1024]{1,0:T(8,128)(2,1)}, u32[]{:S(2)}, u32[]{:S(2)}) collective-permute-start(bf16[128,1024]{1,0:T(8,128)(2,1)} %get-tuple-element.17), channel_id=1, source_target_pairs={{0,2},{1,3},{2,0},{3,1},{4,6},{5,7},{6,4},{7,5},{8,10},{9,11},{10,... | collective-permute-start | bytes 786440 | tf_op jit(solution)/shard_map/ppermute | solution.py:347
  47.1 0.5 collective-permute-start.15
  47.6 4.7 %all-to-all-start.1 = ((bf16[8,256,384]{2,1,0:T(8,128)(2,1)}), bf16[8,256,384]{2,1,0:T(8,128)(2,1)}, u32[]{:S(2)}, u32[]{:S(2)}) async-start(bf16[8,256,384]{2,1,0:T(8,128)(2,1)} %shard_map.80.refs_2_.refs_13_), calls=%async_computation.1 | async-start | bytes 3145728 | tf_op jit(solution)/shard_map/all_to_all | solution.py:365
  52.3 0.5 collective-permute-done.11.refs_6_
  52.8 0.4 collective-permute-done.12.refs_7_
  53.2 0.1 collective-permute-start.17
  53.3 1.0 collective-permute-done.16.refs_11_
  54.3 0.6 collective-permute-done.17.refs_12_
  55.0 7.8 %shard_map.82 = (bf16[256,128]{1,0:T(8,128)(2,1)S(1)}, bf16[256,128]{1,0:T(8,128)(2,1)S(1)}, bf16[256,128]{1,0:T(8,128)(2,1)S(1)}, bf16[256,128]{1,0:T(8,128)(2,...) custom-call(s32[16]{0:T(128)S(1)} %copy-done.6, ...), custom_call_target="tpu_custom_call" | custom-call | flops 9200000000 | bytes 5242880 | tf_op jit(solution)/shard_map/pallas_call | solution.py:42
  62.8 0.2 collective-permute-start.18
  63.0 1.4 %collective-permute-start.19 = (bf16[256,128]{1,0:T(8,128)(2,1)S(1)}, bf16[256,128]{1,0:T(8,128)(2,1)S(1)}, u32[]{:S(2)}, u32[]{:S(2)}) collective-permute-start(bf16[256,128]{1,0:T(8,128)(2,1)S(1)} %get-tuple-element.20), channel_id=1, source_target_pairs={{0,2},{1,3},{2,0},{3,1},{4,6},{5,7},{6,4},{7,5},{8,10},{9,11},{10,... | collective-permute-start | bytes 196616 | tf_op jit(solution)/shard_map/ppermute | solution.py:347
  64.4 0.3 collective-permute-start.20
  64.7 1.5 %collective-permute-start.21 = (bf16[256,128]{1,0:T(8,128)(2,1)S(1)}, bf16[256,128]{1,0:T(8,128)(2,1)S(1)}, u32[]{:S(2)}, u32[]{:S(2)}) collective-permute-start(bf16[256,128]{1,0:T(8,128)(2,1)S(1)} %get-tuple-element.22), channel_id=1, source_target_pairs={{0,4},{1,5},{2,6},{3,7},{4,0},{5,1},{6,2},{7,3},{8,12},{9,13},{10,... | collective-permute-start | bytes 196616 | tf_op jit(solution)/shard_map/ppermute | solution.py:347
  66.2 0.3 collective-permute-start.22
  66.5 2.0 %collective-permute-start.23 = (bf16[256,128]{1,0:T(8,128)(2,1)S(1)}, bf16[256,128]{1,0:T(8,128)(2,1)S(1)}, u32[]{:S(2)}, u32[]{:S(2)}) collective-permute-start(bf16[256,128]{1,0:T(8,128)(2,1)S(1)} %get-tuple-element.24), channel_id=1, source_target_pairs={{0,6},{1,7},{2,4},{3,5},{4,2},{5,3},{6,0},{7,1},{8,14},{9,15},{10,... | collective-permute-start | bytes 196616 | tf_op jit(solution)/shard_map/ppermute | solution.py:347
  68.5 4.0 %collective-permute-done.19.refs_2_ = bf16[256,128]{1,0:T(8,128)(2,1)S(1)} collective-permute-done((bf16[256,128]{1,0:T(8,128)(2,1)S(1)}, bf16[256,128]{1,0:T(8,128)(2,1)S(1)}, u32[]{:S(2)}, u32[]{:S(2)}) %collective-permute-start.19) | collective-permute-done | bytes 65568 | tf_op jit(solution)/shard_map/ppermute | solution.py:347
  72.5 1.5 %collective-permute-start.24 = (bf16[256,128]{1,0:T(8,128)(2,1)S(1)}, bf16[256,128]{1,0:T(8,128)(2,1)S(1)}, u32[]{:S(2)}, u32[]{:S(2)}) collective-permute-start(bf16[256,128]{1,0:T(8,128)(2,1)S(1)} %get-tuple-element.25), channel_id=1, source_target_pairs={{0,7},{1,6},{2,5},{3,4},{4,3},{5,2},{6,1},{7,0},{8,15},{9,14},{10,... | collective-permute-start | bytes 196616 | tf_op jit(solution)/shard_map/ppermute | solution.py:347
  74.0 5.3 %shard_map.83.refs_10_ = bf16[256,1024]{1,0:T(8,128)(2,1)} custom-call(bf16[8,256,384]{2,1,0:T(8,128)(2,1)} %all-to-all-done.1.grad_ref, bf16[256,1024]{1,0:T(8,128)(2,1)} %bitcast.22, bf16[256,1024]{1,0:T(8,128)(2,1)} %bitcast.25, bf16[3072,1024]{1,0:T(8,128)(2,1)} %bitcast.30), custom_call_target="tpu_custom_call" | custom-call | flops 5750000128 | bytes 6291456 | tf_op jit(solution)/shard_map/pallas_call | solution.py:42
  79.4 1.0 copy-done.3
  80.4 1.3 %shard_map.84 = bf16[256,1024]{1,0:T(8,128)(2,1)S(1)} custom-call(s32[3]{0:T(128)S(1)} %pad_add_fusion.refs_1_.info_ref, bf16[256,128]{1,0:T(8,128)(2,1)S(1)} %get-tuple-element.18.refs_0_, bf16[256,128]{1,0:T(8,128)(2,1)S(1)} %collective-permute-done.18.refs_1_, bf16[256,128]{1,0:T(8,128)(2,1)S(1)} %collective-permute-done.19.refs_2_, ...), custom_call_target="tpu_custom_call" | custom-call | flops 536870912 | bytes 2097152 | tf_op jit(solution)/shard_map/pallas_call | solution.py:42
  81.7 3.5 %collective-permute-start.25 = (bf16[256,1024]{1,0:T(8,128)(2,1)S(1)}, bf16[256,1024]{1,0:T(8,128)(2,1)S(1)}, u32[]{:S(2)}, u32[]{:S(2)}) collective-permute-start(bf16[256,1024]{1,0:T(8,128)(2,1)S(1)} %shard_map.84), channel_id=1, source_target_pairs={{0,8},{8,16},{16,24},{1,9},{9,17},{17,25},{2,10},{10,18},{18,26},{... | collective-permute-start | bytes 1572872 | tf_op jit(solution)/shard_map/ppermute | solution.py:395
  85.2 2.4 %collective-permute-start.26 = (bf16[256,1024]{1,0:T(8,128)(2,1)S(1)}, bf16[256,1024]{1,0:T(8,128)(2,1)S(1)}, u32[]{:S(2)}, u32[]{:S(2)}) collective-permute-start(bf16[256,1024]{1,0:T(8,128)(2,1)S(1)} %copy-done.3), channel_id=1, source_target_pairs={{8,0},{16,8},{24,16},{9,1},{17,9},{25,17},{10,2},{18,10},{26,18},{... | collective-permute-start | bytes 1572872 | tf_op jit(solution)/shard_map/ppermute | solution.py:395
  87.6 10.5 %collective-permute-done.25 = bf16[256,1024]{1,0:T(8,128)(2,1)S(1)} collective-permute-done((bf16[256,1024]{1,0:T(8,128)(2,1)S(1)}, bf16[256,1024]{1,0:T(8,128)(2,1)S(1)}, u32[]{:S(2)}, u32[]{:S(2)}) %collective-permute-start.25) | collective-permute-done | bytes 524320 | tf_op jit(solution)/shard_map/ppermute | solution.py:395
  98.1 3.7 %collective-permute-done.26 = bf16[256,1024]{1,0:T(8,128)(2,1)S(1)} collective-permute-done((bf16[256,1024]{1,0:T(8,128)(2,1)S(1)}, bf16[256,1024]{1,0:T(8,128)(2,1)S(1)}, u32[]{:S(2)}, u32[]{:S(2)}) %collective-permute-start.26) | collective-permute-done | bytes 524320 | tf_op jit(solution)/shard_map/ppermute | solution.py:395
  101.8 0.8 copy.12
  102.6 0.8 copy.13
  (36 shorter events, 0.2 us)
Async XLA Ops:
  0.6 13.9 %collective-permute-start = (bf16[256,1024]{1,0:T(8,128)(2,1)}, bf16[256,1024]{1,0:T(8,128)(2,1)S(1)}, u32[]{:S(2)}, u32[]{:S(2)}) collective-permute-start(bf16[256,1024]{1,0:T(8,128)(2,1)} %bitcast.20), channel_id=1, source_target_pairs={{0,2},{1,3},{2,0},{3,1},{4,6},{5,7},{6,4},{7,5},{8,10},{9,11},{10,... | collective-permute-start | bytes 1572872 | tf_op jit(solution)/shard_map/ppermute | solution.py:347
  1.2 13.7 %collective-permute-start.1 = (bf16[256,1024]{1,0:T(8,128)(2,1)}, bf16[256,1024]{1,0:T(8,128)(2,1)}, u32[]{:S(2)}, u32[]{:S(2)}) collective-permute-start(bf16[256,1024]{1,0:T(8,128)(2,1)} %bitcast.21), channel_id=1, source_target_pairs={{0,4},{1,5},{2,6},{3,7},{4,0},{5,1},{6,2},{7,3},{8,12},{9,13},{10,... | collective-permute-start | bytes 1572872 | tf_op jit(solution)/shard_map/ppermute | solution.py:347
  2.7 1.6 %copy-start = (bf16[1,1024,1024]{2,1,0:T(8,128)(2,1)S(1)}, bf16[1,1024,1024]{2,1,0:T(8,128)(2,1)}, u32[]{:S(2)}) copy-start(bf16[1,1024,1024]{2,1,0:T(8,128)(2,1)} %param.10) | copy-start | bytes 6291460
  4.3 1.0 %copy-start.5 = (bf16[1,256,1024]{2,1,0:T(8,128)(2,1)S(1)}, bf16[1,256,1024]{2,1,0:T(8,128)(2,1)}, u32[]{:S(2)}) copy-start(bf16[1,256,1024]{2,1,0:T(8,128)(2,1)} %param.8) | copy-start | bytes 1572868
  8.2 18.9 %all-to-all-start = ((bf16[8,256,128]{2,1,0:T(8,128)(2,1)}), bf16[8,256,128]{2,1,0:T(8,128)(2,1)S(1)}, u32[]{:S(2)}, u32[]{:S(2)}) async-start(bf16[8,256,128]{2,1,0:T(8,128)(2,1)} %shard_map.77.refs_2_), calls=%async_computation | async-start | bytes 1048576 | tf_op jit(solution)/shard_map/all_to_all | solution.py:365
  13.1 7.1 %copy-start.4 = (bf16[1,256,1024]{2,1,0:T(8,128)(2,1)S(1)}, bf16[1,256,1024]{2,1,0:T(8,128)(2,1)}, u32[]{:S(2)}) copy-start(bf16[1,256,1024]{2,1,0:T(8,128)(2,1)} %param.7) | copy-start | bytes 1572868
  13.1 14.0 %copy-start.2 = (bf16[1,256,1024]{2,1,0:T(8,128)(2,1)S(1)}, bf16[1,256,1024]{2,1,0:T(8,128)(2,1)}, u32[]{:S(2)}) copy-start(bf16[1,256,1024]{2,1,0:T(8,128)(2,1)} %param.6) | copy-start | bytes 1572868
  15.9 10.2 %collective-permute-start.3 = (bf16[128,1024]{1,0:T(8,128)(2,1)S(1)}, bf16[128,1024]{1,0:T(8,128)(2,1)}, u32[]{:S(2)}, u32[]{:S(2)}) collective-permute-start(bf16[128,1024]{1,0:T(8,128)(2,1)S(1)} %get-tuple-element.15), channel_id=1, source_target_pairs={{0,2},{1,3},{2,0},{3,1},{4,6},{5,7},{6,4},{7,5},{8,10},{9,11},{10,... | collective-permute-start | bytes 786440 | tf_op jit(solution)/shard_map/ppermute | solution.py:347
  17.6 9.5 %collective-permute-start.2 = (bf16[128,1024]{1,0:T(8,128)(2,1)S(1)}, bf16[128,1024]{1,0:T(8,128)(2,1)}, u32[]{:S(2)}, u32[]{:S(2)}) collective-permute-start(bf16[128,1024]{1,0:T(8,128)(2,1)S(1)} %get-tuple-element.14), channel_id=1, source_target_pairs={{0,4},{1,5},{2,6},{3,7},{4,0},{5,1},{6,2},{7,3},{8,12},{9,13},{10,... | collective-permute-start | bytes 786440 | tf_op jit(solution)/shard_map/ppermute | solution.py:347
  20.2 7.2 %collective-permute-start.6 = (bf16[256,1024]{1,0:T(8,128)(2,1)S(1)}, bf16[256,1024]{1,0:T(8,128)(2,1)}, u32[]{:S(2)}, u32[]{:S(2)}) collective-permute-start(bf16[256,1024]{1,0:T(8,128)(2,1)S(1)} %bitcast.23), channel_id=1, source_target_pairs={{0,1},{1,0},{2,3},{3,2},{4,5},{5,4},{6,7},{7,6},{8,9},{9,8},{10,11... | collective-permute-start | bytes 1572872 | tf_op jit(solution)/shard_map/ppermute | solution.py:347
  21.5 8.5 %collective-permute-start.7 = (bf16[256,1024]{1,0:T(8,128)(2,1)S(1)}, bf16[256,1024]{1,0:T(8,128)(2,1)}, u32[]{:S(2)}, u32[]{:S(2)}) collective-permute-start(bf16[256,1024]{1,0:T(8,128)(2,1)S(1)} %collective-permute-done.refs_0_.refs_4_), channel_id=1, source_target_pairs={{0,1},{1,0},{2,3},{3,2},{4,5},{5,4},{6,7},{7,6},{8,9},{9,8},{10,11... | collective-permute-start | bytes 1572872 | tf_op jit(solution)/shard_map/ppermute | solution.py:347
  22.0 8.0 %collective-permute-start.8 = (bf16[256,1024]{1,0:T(8,128)(2,1)}, bf16[256,1024]{1,0:T(8,128)(2,1)}, u32[]{:S(2)}, u32[]{:S(2)}) collective-permute-start(bf16[256,1024]{1,0:T(8,128)(2,1)} %collective-permute-done.1.refs_1_.refs_5_), channel_id=1, source_target_pairs={{0,1},{1,0},{2,3},{3,2},{4,5},{5,4},{6,7},{7,6},{8,9},{9,8},{10,11... | collective-permute-start | bytes 1572872 | tf_op jit(solution)/shard_map/ppermute | solution.py:347
  26.1 2.4 %collective-permute-start.10 = (bf16[128,1024]{1,0:T(8,128)(2,1)}, bf16[128,1024]{1,0:T(8,128)(2,1)}, u32[]{:S(2)}, u32[]{:S(2)}) collective-permute-start(bf16[128,1024]{1,0:T(8,128)(2,1)} %collective-permute-done.3.refs_1_.refs_7_), channel_id=1, source_target_pairs={{0,1},{1,0},{2,3},{3,2},{4,5},{5,4},{6,7},{7,6},{8,9},{9,8},{10,11... | collective-permute-start | bytes 786440 | tf_op jit(solution)/shard_map/ppermute | solution.py:347
  27.2 2.8 %collective-permute-start.9 = (bf16[128,1024]{1,0:T(8,128)(2,1)}, bf16[128,1024]{1,0:T(8,128)(2,1)}, u32[]{:S(2)}, u32[]{:S(2)}) collective-permute-start(bf16[128,1024]{1,0:T(8,128)(2,1)} %collective-permute-done.2.refs_0_.refs_6_), channel_id=1, source_target_pairs={{0,1},{1,0},{2,3},{3,2},{4,5},{5,4},{6,7},{7,6},{8,9},{9,8},{10,11... | collective-permute-start | bytes 786440 | tf_op jit(solution)/shard_map/ppermute | solution.py:347
  27.2 2.9 %copy-start.6 = (s32[16]{0:T(128)S(1)}, s32[16]{0:T(128)}, u32[]{:S(2)}) copy-start(s32[16]{0:T(128)} %refs_0_.3) | copy-start | bytes 196
  27.4 14.6 %collective-permute-start.4 = (bf16[256,1024]{1,0:T(8,128)(2,1)S(1)}, bf16[256,1024]{1,0:T(8,128)(2,1)}, u32[]{:S(2)}, u32[]{:S(2)}) collective-permute-start(bf16[256,1024]{1,0:T(8,128)(2,1)S(1)} %shard_map.79.refs_14_.refs_3_), channel_id=1, source_target_pairs={{0,2},{1,3},{2,0},{3,1},{4,6},{5,7},{6,4},{7,5},{8,10},{9,11},{10,... | collective-permute-start | bytes 1572872 | tf_op jit(solution)/shard_map/ppermute | solution.py:347
  28.5 13.7 %collective-permute-start.5 = (bf16[256,1024]{1,0:T(8,128)(2,1)S(1)}, bf16[256,1024]{1,0:T(8,128)(2,1)}, u32[]{:S(2)}, u32[]{:S(2)}) collective-permute-start(bf16[256,1024]{1,0:T(8,128)(2,1)S(1)} %shard_map.79.refs_14_.refs_3_), channel_id=1, source_target_pairs={{0,4},{1,5},{2,6},{3,7},{4,0},{5,1},{6,2},{7,3},{8,12},{9,13},{10,... | collective-permute-start | bytes 1572872 | tf_op jit(solution)/shard_map/ppermute | solution.py:347
  30.0 23.3 %collective-permute-start.13 = (bf16[256,1024]{1,0:T(8,128)(2,1)S(1)}, bf16[256,1024]{1,0:T(8,128)(2,1)}, u32[]{:S(2)}, u32[]{:S(2)}) collective-permute-start(bf16[256,1024]{1,0:T(8,128)(2,1)S(1)} %shard_map.79.refs_14_.refs_3_), channel_id=1, source_target_pairs={{0,1},{1,0},{2,3},{3,2},{4,5},{5,4},{6,7},{7,6},{8,9},{9,8},{10,11... | collective-permute-start | bytes 1572872 | tf_op jit(solution)/shard_map/ppermute | solution.py:347
  44.0 8.8 %collective-permute-start.11 = (bf16[128,1024]{1,0:T(8,128)(2,1)}, bf16[128,1024]{1,0:T(8,128)(2,1)S(1)}, u32[]{:S(2)}, u32[]{:S(2)}) collective-permute-start(bf16[128,1024]{1,0:T(8,128)(2,1)} %get-tuple-element.16), channel_id=1, source_target_pairs={{0,4},{1,5},{2,6},{3,7},{4,0},{5,1},{6,2},{7,3},{8,12},{9,13},{10,... | collective-permute-start | bytes 786440 | tf_op jit(solution)/shard_map/ppermute | solution.py:347
  45.6 7.6 %collective-permute-start.12 = (bf16[128,1024]{1,0:T(8,128)(2,1)}, bf16[128,1024]{1,0:T(8,128)(2,1)}, u32[]{:S(2)}, u32[]{:S(2)}) collective-permute-start(bf16[128,1024]{1,0:T(8,128)(2,1)} %get-tuple-element.17), channel_id=1, source_target_pairs={{0,2},{1,3},{2,0},{3,1},{4,6},{5,7},{6,4},{7,5},{8,10},{9,11},{10,... | collective-permute-start | bytes 786440 | tf_op jit(solution)/shard_map/ppermute | solution.py:347
  47.0 7.9 %collective-permute-start.14 = (bf16[256,1024]{1,0:T(8,128)(2,1)}, bf16[256,1024]{1,0:T(8,128)(2,1)S(1)}, u32[]{:S(2)}, u32[]{:S(2)}) collective-permute-start(bf16[256,1024]{1,0:T(8,128)(2,1)} %collective-permute-done.4.refs_0_.refs_4_), channel_id=1, source_target_pairs={{0,1},{1,0},{2,3},{3,2},{4,5},{5,4},{6,7},{7,6},{8,9},{9,8},{10,11... | collective-permute-start | bytes 1572872 | tf_op jit(solution)/shard_map/ppermute | solution.py:347
  47.1 7.9 %collective-permute-start.15 = (bf16[256,1024]{1,0:T(8,128)(2,1)}, bf16[256,1024]{1,0:T(8,128)(2,1)S(1)}, u32[]{:S(2)}, u32[]{:S(2)}) collective-permute-start(bf16[256,1024]{1,0:T(8,128)(2,1)} %collective-permute-done.5.refs_1_.refs_5_), channel_id=1, source_target_pairs={{0,1},{1,0},{2,3},{3,2},{4,5},{5,4},{6,7},{7,6},{8,9},{9,8},{10,11... | collective-permute-start | bytes 1572872 | tf_op jit(solution)/shard_map/ppermute | solution.py:347
  47.6 26.5 %all-to-all-start.1 = ((bf16[8,256,384]{2,1,0:T(8,128)(2,1)}), bf16[8,256,384]{2,1,0:T(8,128)(2,1)}, u32[]{:S(2)}, u32[]{:S(2)}) async-start(bf16[8,256,384]{2,1,0:T(8,128)(2,1)} %shard_map.80.refs_2_.refs_13_), calls=%async_computation.1 | async-start | bytes 3145728 | tf_op jit(solution)/shard_map/all_to_all | solution.py:365
  52.8 1.5 %collective-permute-start.16 = (bf16[128,1024]{1,0:T(8,128)(2,1)S(1)}, bf16[128,1024]{1,0:T(8,128)(2,1)S(1)}, u32[]{:S(2)}, u32[]{:S(2)}) collective-permute-start(bf16[128,1024]{1,0:T(8,128)(2,1)S(1)} %collective-permute-done.11.refs_6_), channel_id=1, source_target_pairs={{0,1},{1,0},{2,3},{3,2},{4,5},{5,4},{6,7},{7,6},{8,9},{9,8},{10,11... | collective-permute-start | bytes 786440 | tf_op jit(solution)/shard_map/ppermute | solution.py:347
  53.2 1.7 %collective-permute-start.17 = (bf16[128,1024]{1,0:T(8,128)(2,1)}, bf16[128,1024]{1,0:T(8,128)(2,1)S(1)}, u32[]{:S(2)}, u32[]{:S(2)}) collective-permute-start(bf16[128,1024]{1,0:T(8,128)(2,1)} %collective-permute-done.12.refs_7_), channel_id=1, source_target_pairs={{0,1},{1,0},{2,3},{3,2},{4,5},{5,4},{6,7},{7,6},{8,9},{9,8},{10,11... | collective-permute-start | bytes 786440 | tf_op jit(solution)/shard_map/ppermute | solution.py:347
  62.8 3.7 %collective-permute-start.18 = (bf16[256,128]{1,0:T(8,128)(2,1)S(1)}, bf16[256,128]{1,0:T(8,128)(2,1)S(1)}, u32[]{:S(2)}, u32[]{:S(2)}) collective-permute-start(bf16[256,128]{1,0:T(8,128)(2,1)S(1)} %get-tuple-element.19), channel_id=1, source_target_pairs={{0,1},{1,0},{2,3},{3,2},{4,5},{5,4},{6,7},{7,6},{8,9},{9,8},{10,11... | collective-permute-start | bytes 196616 | tf_op jit(solution)/shard_map/ppermute | solution.py:347
  63.0 9.5 %collective-permute-start.19 = (bf16[256,128]{1,0:T(8,128)(2,1)S(1)}, bf16[256,128]{1,0:T(8,128)(2,1)S(1)}, u32[]{:S(2)}, u32[]{:S(2)}) collective-permute-start(bf16[256,128]{1,0:T(8,128)(2,1)S(1)} %get-tuple-element.20), channel_id=1, source_target_pairs={{0,2},{1,3},{2,0},{3,1},{4,6},{5,7},{6,4},{7,5},{8,10},{9,11},{10,... | collective-permute-start | bytes 196616 | tf_op jit(solution)/shard_map/ppermute | solution.py:347
  64.4 14.9 %collective-permute-start.20 = (bf16[256,128]{1,0:T(8,128)(2,1)S(1)}, bf16[256,128]{1,0:T(8,128)(2,1)S(1)}, u32[]{:S(2)}, u32[]{:S(2)}) collective-permute-start(bf16[256,128]{1,0:T(8,128)(2,1)S(1)} %get-tuple-element.21), channel_id=1, source_target_pairs={{0,3},{1,2},{2,1},{3,0},{4,7},{5,6},{6,5},{7,4},{8,11},{9,10},{10,... | collective-permute-start | bytes 196616 | tf_op jit(solution)/shard_map/ppermute | solution.py:347
  64.7 14.6 %collective-permute-start.21 = (bf16[256,128]{1,0:T(8,128)(2,1)S(1)}, bf16[256,128]{1,0:T(8,128)(2,1)S(1)}, u32[]{:S(2)}, u32[]{:S(2)}) collective-permute-start(bf16[256,128]{1,0:T(8,128)(2,1)S(1)} %get-tuple-element.22), channel_id=1, source_target_pairs={{0,4},{1,5},{2,6},{3,7},{4,0},{5,1},{6,2},{7,3},{8,12},{9,13},{10,... | collective-permute-start | bytes 196616 | tf_op jit(solution)/shard_map/ppermute | solution.py:347
  66.2 13.2 %collective-permute-start.22 = (bf16[256,128]{1,0:T(8,128)(2,1)S(1)}, bf16[256,128]{1,0:T(8,128)(2,1)S(1)}, u32[]{:S(2)}, u32[]{:S(2)}) collective-permute-start(bf16[256,128]{1,0:T(8,128)(2,1)S(1)} %get-tuple-element.23), channel_id=1, source_target_pairs={{0,5},{1,4},{2,7},{3,6},{4,1},{5,0},{6,3},{7,2},{8,13},{9,12},{10,... | collective-permute-start | bytes 196616 | tf_op jit(solution)/shard_map/ppermute | solution.py:347
  66.5 12.9 %collective-permute-start.23 = (bf16[256,128]{1,0:T(8,128)(2,1)S(1)}, bf16[256,128]{1,0:T(8,128)(2,1)S(1)}, u32[]{:S(2)}, u32[]{:S(2)}) collective-permute-start(bf16[256,128]{1,0:T(8,128)(2,1)S(1)} %get-tuple-element.24), channel_id=1, source_target_pairs={{0,6},{1,7},{2,4},{3,5},{4,2},{5,3},{6,0},{7,1},{8,14},{9,15},{10,... | collective-permute-start | bytes 196616 | tf_op jit(solution)/shard_map/ppermute | solution.py:347
  72.5 6.9 %collective-permute-start.24 = (bf16[256,128]{1,0:T(8,128)(2,1)S(1)}, bf16[256,128]{1,0:T(8,128)(2,1)S(1)}, u32[]{:S(2)}, u32[]{:S(2)}) collective-permute-start(bf16[256,128]{1,0:T(8,128)(2,1)S(1)} %get-tuple-element.25), channel_id=1, source_target_pairs={{0,7},{1,6},{2,5},{3,4},{4,3},{5,2},{6,1},{7,0},{8,15},{9,14},{10,... | collective-permute-start | bytes 196616 | tf_op jit(solution)/shard_map/ppermute | solution.py:347
  74.0 5.3 %copy-start.1 = (bf16[1,1024,1024]{2,1,0:T(8,128)(2,1)S(1)}, bf16[1,1024,1024]{2,1,0:T(8,128)(2,1)}, u32[]{:S(2)}) copy-start(bf16[1,1024,1024]{2,1,0:T(8,128)(2,1)} %param.10) | copy-start | bytes 6291460
  79.4 1.0 %copy-start.3 = (bf16[256,1024]{1,0:T(8,128)(2,1)S(1)}, bf16[256,1024]{1,0:T(8,128)(2,1)}, u32[]{:S(2)}) copy-start(bf16[256,1024]{1,0:T(8,128)(2,1)} %shard_map.83.refs_10_) | copy-start | bytes 1572868
  81.7 16.4 %collective-permute-start.25 = (bf16[256,1024]{1,0:T(8,128)(2,1)S(1)}, bf16[256,1024]{1,0:T(8,128)(2,1)S(1)}, u32[]{:S(2)}, u32[]{:S(2)}) collective-permute-start(bf16[256,1024]{1,0:T(8,128)(2,1)S(1)} %shard_map.84), channel_id=1, source_target_pairs={{0,8},{8,16},{16,24},{1,9},{9,17},{17,25},{2,10},{10,18},{18,26},{... | collective-permute-start | bytes 1572872 | tf_op jit(solution)/shard_map/ppermute | solution.py:395
  85.2 16.6 %collective-permute-start.26 = (bf16[256,1024]{1,0:T(8,128)(2,1)S(1)}, bf16[256,1024]{1,0:T(8,128)(2,1)S(1)}, u32[]{:S(2)}, u32[]{:S(2)}) collective-permute-start(bf16[256,1024]{1,0:T(8,128)(2,1)S(1)} %copy-done.3), channel_id=1, source_target_pairs={{8,0},{16,8},{24,16},{9,1},{17,9},{25,17},{10,2},{18,10},{26,18},{... | collective-permute-start | bytes 1572872 | tf_op jit(solution)/shard_map/ppermute | solution.py:395

commit v12 on v11

--- a/solution.py
+++ b/solution.py
@@ -266,25 +266,31 @@
 
 
 def finish_kernel(info_ref, *refs):
-    att_refs, (x_ref, w_ref, _, out_ref) = refs[:HEADS], refs[HEADS:]
-    flip = info_ref[0]
+    att_refs, refs = refs[:HEADS], refs[HEADS:]
+    x_ref, w_ref, grad_ref, first_ref, second_ref, x, sem = refs
+    flip, odd = info_ref[0], info_ref[3]
+    x_copy = fetch(x_ref, x, sem)
     att = jnp.concatenate([ref[...] for ref in att_refs], axis=1)
+    x_copy.wait()
     block = 256
     for start in range(0, x_ref.shape[1], block):
         columns = slice(start, start + block)
         w = jnp.concatenate([w_ref[flip ^ k, :, columns] for k in range(HEADS)], axis=0)
-        out_ref[:, columns] = low(high(x_ref[:, columns]) + dot(att, w, NN))
-
-
-def finish(info, attention, current, w_fin, earlier):
+        result = low(high(x[:, columns]) + dot(att, w, NN))
+        grad = grad_ref[:, columns]
+        first_ref[:, columns] = jnp.where(odd == 0, result, grad)
+        second_ref[:, columns] = jnp.where(odd == 0, grad, result)
+
+
+def finish(info, attention, current, w_fin, grad_self):
     tokens, width = current.shape
     return call(
         finish_kernel,
-        [info, *attention, current, w_fin.reshape(HEADS, HD, width), earlier],
-        [SMEM] + [VMEM] * (HEADS + 2) + [HBM],
-        jax.ShapeDtypeStruct((tokens, width), jnp.bfloat16),
-        [],
-        2 * tokens * width * HEADS * HD,
+        [info, *attention, current, w_fin.reshape(HEADS, HD, width), grad_self],
+        [SMEM] + [VMEM] * HEADS + [HBM] + [VMEM] * 2,
+        [jax.ShapeDtypeStruct((tokens, width), jnp.bfloat16)] * 2,
+        [pltpu.VMEM((tokens, width), jnp.bfloat16), pltpu.SemaphoreType.DMA],
+        MICROSECOND,
         2 * width * HEADS * HD,
     )
 
@@ -389,10 +395,12 @@
     return lax.dynamic_index_in_dim(returned, own % places, 1, keepdims=False)
 
 
-def passed_along(block, axis, distance):
-    devices = range(lax.axis_size(axis))
-    route = [(i - distance, i) for i in devices if i - distance in devices]
-    return lax.ppermute(block, axis, route)
+def swapped(block, first):
+    planes = lax.axis_size("pipe")
+    route = []
+    for i in range(first, planes - 1, 2):
+        route += [(i, i + 1), (i + 1, i)]
+    return lax.ppermute(block, "pipe", route)
 
 
 def per_device(section_input, saved_input, grad_output, w_qkv, w_out, tile_cluster):
@@ -401,11 +409,12 @@
     tokens = current.shape[0]
     spacing = lax.axis_size("seq") // HEADS
     own = lax.axis_index("seq").astype(jnp.int32)
+    odd = lax.axis_index("pipe").astype(jnp.int32) % 2
     if spacing == 1:
-        info = jnp.stack([own, own, jnp.zeros_like(own)])
+        info = jnp.stack([own, own, jnp.zeros_like(own), odd])
         gather, spread, collect, collect_each = gather_rows, all_swap, all_swap, swap
     else:
-        info = jnp.stack([jnp.zeros_like(own), own // spacing, own % spacing])
+        info = jnp.stack([jnp.zeros_like(own), own // spacing, own % spacing, odd])
 
         def gather(x, earlier):
             copies = jnp.broadcast_to(x, (HEADS, *x.shape))
@@ -438,9 +447,10 @@
     )
     returned = collect_each(outputs)
     grad_self = finish_back(returned_grads, stored, upstream, w_rows)
-    grad_input = passed_along(grad_self, "pipe", -1)
-    result = finish(info, returned, current, w_fin, grad_self)
-    next_input = passed_along(result, "pipe", 1)
+    first, second = finish(info, returned, current, w_fin, grad_self)
+    first, second = swapped(first, 0), swapped(second, 1)
+    next_input = jnp.where(odd == 1, first, second)
+    grad_input = jnp.where(odd == 1, second, first)
     return (next_input[None], grad_input[None])
 
 

time: 105 us -> 102 us (0.971)
  starting transfers between devices: 36 us -> 33.5 us
  local copies, waits for them, and re-layouts: 6.46 us -> 4.87 us
    ppermute x2, starting transfers between devices: 5.84 us -> 3.55 us  [swapped(): return lax.ppermute(block, 'pipe', route)]
    unnamed x16 -> x14, local copies, waits for them, and re-layouts: 5.27 us -> 3.69 us
    pallas_call x6, Pallas kernels: 29.3 us -> 30.4 us  [call(): pl.pallas_call(kernel, in_specs=in_specs, out_specs=[VMEM] * len(out_shap...]
  transfers between devices with their start and end apart: 29 -> 29, of which waited for: 12 -> 13; matrix products, arithmetic and copies ran while one was open for 1% -> 1% of each run, Pallas kernels for 30% -> 31%
where the time goes in v12:
time: 102 us; the launch traced here: 101 us
  starting transfers between devices  33.5 us (33%)
  Pallas kernels  32.3 us (32%)
  waiting for transfers between devices  28.6 us (28%)
  local copies, waits for them, and re-layouts  4.87 us (5%)
  other arithmetic  1.11 us (1%)
    pallas_call x6, Pallas kernels, call(): pl.pallas_call(kernel, in_specs=in_specs, out_specs=[VMEM] * len(out_shap...  30.4 us
    ppermute x25, starting transfers between devices, partner(): return lax.ppermute(block, 'seq', route)  19.6 us
    ppermute x2, waiting for transfers between devices, swapped(): return lax.ppermute(block, 'pipe', route)  14.7 us
    ppermute x25, waiting for transfers between devices, partner(): return lax.ppermute(block, 'seq', route)  14 us
    all_to_all x2, starting transfers between devices, all_swap(): lax.all_to_all(blocks, 'seq', split_axis=0, concat_axis=0, tiled=True)  10.4 us
    unnamed x14, local copies, waits for them, and re-layouts  3.69 us
    ppermute x2, starting transfers between devices, swapped(): return lax.ppermute(block, 'pipe', route)  3.55 us
  transfers between devices with their start and end apart: 29, of which 13 were waited for; matrix products, arithmetic and copies ran while one was open for 1% of the time, Pallas kernels for 31%

profile of v12, /device:TPU:18, one launch (start us, length us, event | category | flops | bytes accessed | tf_op | source)
XLA Modules:
  0.0 101.3 jit_solution(10714987077781617001)
XLA Ops:
  0.6 0.6 collective-permute-start
  1.2 1.5 %collective-permute-start.1 = (bf16[256,1024]{1,0:T(8,128)(2,1)}, bf16[256,1024]{1,0:T(8,128)(2,1)S(1)}, u32[]{:S(2)}, u32[]{:S(2)}) collective-permute-start(bf16[256,1024]{1,0:T(8,128)(2,1)} %bitcast.22), channel_id=1, source_target_pairs={{0,4},{1,5},{2,6},{3,7},{4,0},{5,1},{6,2},{7,3},{8,12},{9,13},{10,... | collective-permute-start | bytes 1572872 | tf_op jit(solution)/shard_map/ppermute | solution.py:353
  2.8 1.6 %copy-done = bf16[1,1024,1024]{2,1,0:T(8,128)(2,1)S(1)} copy-done((bf16[1,1024,1024]{2,1,0:T(8,128)(2,1)S(1)}, bf16[1,1024,1024]{2,1,0:T(8,128)(2,1)}, u32[]{:S(2)}) %copy-start) | copy-done | bytes 2097176
  4.3 1.0 %copy-done.3 = bf16[1,256,1024]{2,1,0:T(8,128)(2,1)S(1)} copy-done((bf16[1,256,1024]{2,1,0:T(8,128)(2,1)S(1)}, bf16[1,256,1024]{2,1,0:T(8,128)(2,1)}, u32[]{:S(2)}) %copy-start.3) | copy-done | bytes 524312
  5.4 2.8 %shard_map.77.refs_2_ = bf16[8,256,128]{2,1,0:T(8,128)(2,1)} custom-call(bf16[256,1024]{1,0:T(8,128)(2,1)S(1)} %bitcast.27, bf16[8,128,1024]{2,1,0:T(8,128)(2,1)S(1)} %bitcast.19), custom_call_target="tpu_custom_call" | custom-call | flops 3449999872 | bytes 2097152 | tf_op jit(solution)/shard_map/pallas_call | solution.py:42
  8.2 4.9 %all-to-all-start = ((bf16[8,256,128]{2,1,0:T(8,128)(2,1)}), bf16[8,256,128]{2,1,0:T(8,128)(2,1)S(1)}, u32[]{:S(2)}, u32[]{:S(2)}) async-start(bf16[8,256,128]{2,1,0:T(8,128)(2,1)} %shard_map.77.refs_2_), calls=%async_computation | async-start | bytes 1048576 | tf_op jit(solution)/shard_map/all_to_all | solution.py:371
  13.1 1.4 %collective-permute-done.refs_0_.refs_4_ = bf16[256,1024]{1,0:T(8,128)(2,1)S(1)} collective-permute-done((bf16[256,1024]{1,0:T(8,128)(2,1)}, bf16[256,1024]{1,0:T(8,128)(2,1)S(1)}, u32[]{:S(2)}, u32[]{:S(2)}) %collective-permute-start) | collective-permute-done | bytes 524320 | tf_op jit(solution)/shard_map/ppermute | solution.py:353
  14.6 0.3 collective-permute-done.1.refs_1_.refs_5_
  14.8 0.8 shard_map.78
  15.7 1.8 %collective-permute-start.3 = (bf16[128,1024]{1,0:T(8,128)(2,1)}, bf16[128,1024]{1,0:T(8,128)(2,1)}, u32[]{:S(2)}, u32[]{:S(2)}) collective-permute-start(bf16[128,1024]{1,0:T(8,128)(2,1)} %get-tuple-element.17), channel_id=1, source_target_pairs={{0,2},{1,3},{2,0},{3,1},{4,6},{5,7},{6,4},{7,5},{8,10},{9,11},{10,... | collective-permute-start | bytes 786440 | tf_op jit(solution)/shard_map/ppermute | solution.py:353
  17.5 2.4 %collective-permute-start.2 = (bf16[128,1024]{1,0:T(8,128)(2,1)}, bf16[128,1024]{1,0:T(8,128)(2,1)}, u32[]{:S(2)}, u32[]{:S(2)}) collective-permute-start(bf16[128,1024]{1,0:T(8,128)(2,1)} %get-tuple-element.16), channel_id=1, source_target_pairs={{0,4},{1,5},{2,6},{3,7},{4,0},{5,1},{6,2},{7,3},{8,12},{9,13},{10,... | collective-permute-start | bytes 786440 | tf_op jit(solution)/shard_map/ppermute | solution.py:353
  20.0 1.2 %constant_dynamic-slice_fusion = bf16[3,1,128,1024]{3,2,1,0:T(8,128)(2,1)S(1)} fusion(bf16[3,8,128,1024]{3,2,1,0:T(8,128)(2,1)} %bitcast.30, s32[]{:T(128)S(6)} %select_n.25), kind=kLoop, calls=%fused_computation.3 | loop fusion | bytes 1572868 | tf_op jit(solution)/shard_map/jit(dynamic_index_in_dim)/dynamic_slice | solution.py:433
  21.2 0.6 collective-permute-start.7
  21.9 4.2 %collective-permute-done.3.refs_1_.refs_7_ = bf16[128,1024]{1,0:T(8,128)(2,1)} collective-permute-done((bf16[128,1024]{1,0:T(8,128)(2,1)}, bf16[128,1024]{1,0:T(8,128)(2,1)}, u32[]{:S(2)}, u32[]{:S(2)}) %collective-permute-start.3) | collective-permute-done | bytes 262176 | tf_op jit(solution)/shard_map/ppermute | solution.py:353
  26.1 1.1 %collective-permute-done.2.refs_0_.refs_6_ = bf16[128,1024]{1,0:T(8,128)(2,1)} collective-permute-done((bf16[128,1024]{1,0:T(8,128)(2,1)}, bf16[128,1024]{1,0:T(8,128)(2,1)}, u32[]{:S(2)}, u32[]{:S(2)}) %collective-permute-start.2) | collective-permute-done | bytes 262176 | tf_op jit(solution)/shard_map/ppermute | solution.py:353
  27.2 1.0 shard_map.79.refs_14_.refs_3_
  28.2 1.0 %collective-permute-start.4 = (bf16[256,1024]{1,0:T(8,128)(2,1)}, bf16[256,1024]{1,0:T(8,128)(2,1)}, u32[]{:S(2)}, u32[]{:S(2)}) collective-permute-start(bf16[256,1024]{1,0:T(8,128)(2,1)} %shard_map.79.refs_14_.refs_3_), channel_id=1, source_target_pairs={{0,2},{1,3},{2,0},{3,1},{4,6},{5,7},{6,4},{7,5},{8,10},{9,11},{10,... | collective-permute-start | bytes 1572872 | tf_op jit(solution)/shard_map/ppermute | solution.py:353
  29.2 1.5 %collective-permute-start.5 = (bf16[256,1024]{1,0:T(8,128)(2,1)}, bf16[256,1024]{1,0:T(8,128)(2,1)}, u32[]{:S(2)}, u32[]{:S(2)}) collective-permute-start(bf16[256,1024]{1,0:T(8,128)(2,1)} %shard_map.79.refs_14_.refs_3_), channel_id=1, source_target_pairs={{0,4},{1,5},{2,6},{3,7},{4,0},{5,1},{6,2},{7,3},{8,12},{9,13},{10,... | collective-permute-start | bytes 1572872 | tf_op jit(solution)/shard_map/ppermute | solution.py:353
  30.7 11.9 %shard_map.80.refs_2_.refs_13_ = bf16[8,256,384]{2,1,0:T(8,128)(2,1)} custom-call(s32[16]{0:T(128)S(1)} %copy-done.5, s32[4]{0:T(128)S(1)} %pad_add_fusion.refs_1_.info_ref, bf16[384,1024]{1,0:T(8,128)(2,1)S(1)} %bitcast.16, bf16[256,1024]{1,0:T(8,128)(2,1)S(1)} %bitcast.25, bf16[256,1024]{1,0:T(8,128)(2,1)S(1)} %collective-permute-done.refs_0_.refs_4_, ...), custom_call_target="tpu_custom_call" | custom-call | flops 13799999488 | bytes 7340032 | tf_op jit(solution)/shard_map/pallas_call | solution.py:42
  42.7 0.2 collective-permute-done.4.refs_0_.refs_4_
  42.8 0.3 collective-permute-done.5.refs_1_.refs_5_
  43.1 1.0 %shard_map.81 = (bf16[128,1024]{1,0:T(8,128)(2,1)S(1)}, bf16[128,1024]{1,0:T(8,128)(2,1)S(1)}) custom-call(bf16[256,1024]{1,0:T(8,128)(2,1)} %collective-permute-done.4.refs_0_.refs_4_, bf16[256,1024]{1,0:T(8,128)(2,1)} %collective-permute-done.5.refs_1_.refs_5_, bf16[8,256,384]{2,1,0:T(8,128)(2,1)} %shard_map.80.refs_2_.refs_13_), custom_call_target="tpu_custom_call" | custom-call | flops 1150000000 | tf_op jit(solution)/shard_map/pallas_call | solution.py:212
  44.2 1.6 %collective-permute-start.11 = (bf16[128,1024]{1,0:T(8,128)(2,1)S(1)}, bf16[128,1024]{1,0:T(8,128)(2,1)S(1)}, u32[]{:S(2)}, u32[]{:S(2)}) collective-permute-start(bf16[128,1024]{1,0:T(8,128)(2,1)S(1)} %get-tuple-element.18), channel_id=1, source_target_pairs={{0,4},{1,5},{2,6},{3,7},{4,0},{5,1},{6,2},{7,3},{8,12},{9,13},{10,... | collective-permute-start | bytes 786440 | tf_op jit(solution)/shard_map/ppermute | solution.py:353
  45.7 0.8 collective-permute-start.12
  46.5 0.5 collective-permute-start.15
  47.0 5.4 %all-to-all-start.1 = ((bf16[8,256,384]{2,1,0:T(8,128)(2,1)}), bf16[8,256,384]{2,1,0:T(8,128)(2,1)}, u32[]{:S(2)}, u32[]{:S(2)}) async-start(bf16[8,256,384]{2,1,0:T(8,128)(2,1)} %shard_map.80.refs_2_.refs_13_), calls=%async_computation.1 | async-start | bytes 3145728 | tf_op jit(solution)/shard_map/all_to_all | solution.py:371
  52.5 0.1 collective-permute-start.16
  52.6 0.1 collective-permute-done.12.refs_7_
  52.7 0.3 collective-permute-start.17
  53.0 1.0 %collective-permute-done.16.refs_11_ = bf16[128,1024]{1,0:T(8,128)(2,1)S(1)} collective-permute-done((bf16[128,1024]{1,0:T(8,128)(2,1)S(1)}, bf16[128,1024]{1,0:T(8,128)(2,1)S(1)}, u32[]{:S(2)}, u32[]{:S(2)}) %collective-permute-start.16) | collective-permute-done | bytes 262176 | tf_op jit(solution)/shard_map/ppermute | solution.py:353
  54.0 0.4 collective-permute-done.17.refs_12_
  54.4 8.0 %shard_map.82 = (bf16[256,128]{1,0:T(8,128)(2,1)S(1)}, bf16[256,128]{1,0:T(8,128)(2,1)S(1)}, bf16[256,128]{1,0:T(8,128)(2,1)S(1)}, bf16[256,128]{1,0:T(8,128)(2,...) custom-call(s32[16]{0:T(128)S(1)} %copy-done.5, ...), custom_call_target="tpu_custom_call" | custom-call | flops 9200000000 | bytes 5242880 | tf_op jit(solution)/shard_map/pallas_call | solution.py:42
  62.4 0.3 collective-permute-start.18
  62.7 0.8 collective-permute-start.19
  63.5 0.9 collective-permute-start.20
  64.3 1.4 %collective-permute-start.21 = (bf16[256,128]{1,0:T(8,128)(2,1)S(1)}, bf16[256,128]{1,0:T(8,128)(2,1)S(1)}, u32[]{:S(2)}, u32[]{:S(2)}) collective-permute-start(bf16[256,128]{1,0:T(8,128)(2,1)S(1)} %get-tuple-element.24), channel_id=1, source_target_pairs={{0,4},{1,5},{2,6},{3,7},{4,0},{5,1},{6,2},{7,3},{8,12},{9,13},{10,... | collective-permute-start | bytes 196616 | tf_op jit(solution)/shard_map/ppermute | solution.py:353
  65.8 0.4 collective-permute-start.22
  66.2 1.5 %collective-permute-start.23 = (bf16[256,128]{1,0:T(8,128)(2,1)S(1)}, bf16[256,128]{1,0:T(8,128)(2,1)S(1)}, u32[]{:S(2)}, u32[]{:S(2)}) collective-permute-start(bf16[256,128]{1,0:T(8,128)(2,1)S(1)} %get-tuple-element.26), channel_id=1, source_target_pairs={{0,6},{1,7},{2,4},{3,5},{4,2},{5,3},{6,0},{7,1},{8,14},{9,15},{10,... | collective-permute-start | bytes 196616 | tf_op jit(solution)/shard_map/ppermute | solution.py:353
  67.7 4.9 %collective-permute-done.19.refs_2_ = bf16[256,128]{1,0:T(8,128)(2,1)S(1)} collective-permute-done((bf16[256,128]{1,0:T(8,128)(2,1)S(1)}, bf16[256,128]{1,0:T(8,128)(2,1)S(1)}, u32[]{:S(2)}, u32[]{:S(2)}) %collective-permute-start.19) | collective-permute-done | bytes 65568 | tf_op jit(solution)/shard_map/ppermute | solution.py:353
  72.7 1.5 %collective-permute-start.24 = (bf16[256,128]{1,0:T(8,128)(2,1)S(1)}, bf16[256,128]{1,0:T(8,128)(2,1)S(1)}, u32[]{:S(2)}, u32[]{:S(2)}) collective-permute-start(bf16[256,128]{1,0:T(8,128)(2,1)S(1)} %get-tuple-element.27), channel_id=1, source_target_pairs={{0,7},{1,6},{2,5},{3,4},{4,3},{5,2},{6,1},{7,0},{8,15},{9,14},{10,... | collective-permute-start | bytes 196616 | tf_op jit(solution)/shard_map/ppermute | solution.py:353
  74.2 5.3 %shard_map.83.refs_10_ = bf16[256,1024]{1,0:T(8,128)(2,1)} custom-call(bf16[8,256,384]{2,1,0:T(8,128)(2,1)} %all-to-all-done.1.grad_ref, bf16[256,1024]{1,0:T(8,128)(2,1)} %bitcast.23, bf16[256,1024]{1,0:T(8,128)(2,1)} %bitcast.26, bf16[3072,1024]{1,0:T(8,128)(2,1)} %bitcast.31), custom_call_target="tpu_custom_call" | custom-call | flops 5750000128 | bytes 6291456 | tf_op jit(solution)/shard_map/pallas_call | solution.py:42
  79.6 1.0 %copy-done.6 = bf16[256,1024]{1,0:T(8,128)(2,1)S(1)} copy-done((bf16[256,1024]{1,0:T(8,128)(2,1)S(1)}, bf16[256,1024]{1,0:T(8,128)(2,1)}, u32[]{:S(2)}) %copy-start.6) | copy-done | bytes 524312
  80.6 1.4 %shard_map.84 = (bf16[256,1024]{1,0:T(8,128)(2,1)S(1)}, bf16[256,1024]{1,0:T(8,128)(2,1)S(1)}) custom-call(s32[4]{0:T(128)S(1)} %pad_add_fusion.refs_1_.info_ref, bf16[256,128]{1,0:T(8,128)(2,1)S(1)} %get-tuple-element.20.refs_0_, bf16[256,128]{1,0:T(8,128)(2,1)S(1)} %collective-permute-done.18.refs_1_, ...), custom_call_target="tpu_custom_call" | custom-call | flops 1150000000 | bytes 2097152 | tf_op jit(solution)/shard_map/pallas_call | solution.py:42
  82.0 1.6 %collective-permute-start.25 = (bf16[256,1024]{1,0:T(8,128)(2,1)S(1)}, bf16[256,1024]{1,0:T(8,128)(2,1)S(1)}, u32[]{:S(2)}, u32[]{:S(2)}) collective-permute-start(bf16[256,1024]{1,0:T(8,128)(2,1)S(1)} %get-tuple-element.28), channel_id=1, source_target_pairs={{0,8},{8,0},{16,24},{24,16},{1,9},{9,1},{17,25},{25,17},{2,10},{10... | collective-permute-start | bytes 1572872 | tf_op jit(solution)/shard_map/ppermute | solution.py:403
  83.6 1.9 %collective-permute-start.26 = (bf16[256,1024]{1,0:T(8,128)(2,1)S(1)}, bf16[256,1024]{1,0:T(8,128)(2,1)S(1)}, u32[]{:S(2)}, u32[]{:S(2)}) collective-permute-start(bf16[256,1024]{1,0:T(8,128)(2,1)S(1)} %get-tuple-element.29), channel_id=1, source_target_pairs={{8,16},{16,8},{9,17},{17,9},{10,18},{18,10},{11,19},{19,11},{12,20... | collective-permute-start | bytes 1572872 | tf_op jit(solution)/shard_map/ppermute | solution.py:403
  85.6 11.0 %collective-permute-done.25 = bf16[256,1024]{1,0:T(8,128)(2,1)S(1)} collective-permute-done((bf16[256,1024]{1,0:T(8,128)(2,1)S(1)}, bf16[256,1024]{1,0:T(8,128)(2,1)S(1)}, u32[]{:S(2)}, u32[]{:S(2)}) %collective-permute-start.25) | collective-permute-done | bytes 524320 | tf_op jit(solution)/shard_map/ppermute | solution.py:403
  96.6 3.6 %collective-permute-done.26 = bf16[256,1024]{1,0:T(8,128)(2,1)S(1)} collective-permute-done((bf16[256,1024]{1,0:T(8,128)(2,1)S(1)}, bf16[256,1024]{1,0:T(8,128)(2,1)S(1)}, u32[]{:S(2)}, u32[]{:S(2)}) %collective-permute-start.26) | collective-permute-done | bytes 524320 | tf_op jit(solution)/shard_map/ppermute | solution.py:403
  100.2 1.0 %select_bitcast_fusion = (bf16[1,256,1024]{2,1,0:T(8,128)(2,1)}, bf16[1,256,1024]{2,1,0:T(8,128)(2,1)}) fusion(bf16[256,1024]{1,0:T(8,128)(2,1)S(1)} %collective-permute-done.26, bf16[256,1024]{1,0:T(8,128)(2,1)S(1)} %collective-permute-done.25, pred[]{:T(512)S(6)} %eq.6), kind=kLoop, calls=%fused_computation | loop fusion | flops 524288 | bytes 2097153 | tf_op jit(solution)/shard_map/broadcast_in_dim | solution.py:454
  (35 shorter events, 0.3 us)
Async XLA Ops:
  0.6 13.9 %collective-permute-start = (bf16[256,1024]{1,0:T(8,128)(2,1)}, bf16[256,1024]{1,0:T(8,128)(2,1)S(1)}, u32[]{:S(2)}, u32[]{:S(2)}) collective-permute-start(bf16[256,1024]{1,0:T(8,128)(2,1)} %bitcast.21), channel_id=1, source_target_pairs={{0,2},{1,3},{2,0},{3,1},{4,6},{5,7},{6,4},{7,5},{8,10},{9,11},{10,... | collective-permute-start | bytes 1572872 | tf_op jit(solution)/shard_map/ppermute | solution.py:353
  1.2 13.6 %collective-permute-start.1 = (bf16[256,1024]{1,0:T(8,128)(2,1)}, bf16[256,1024]{1,0:T(8,128)(2,1)S(1)}, u32[]{:S(2)}, u32[]{:S(2)}) collective-permute-start(bf16[256,1024]{1,0:T(8,128)(2,1)} %bitcast.22), channel_id=1, source_target_pairs={{0,4},{1,5},{2,6},{3,7},{4,0},{5,1},{6,2},{7,3},{8,12},{9,13},{10,... | collective-permute-start | bytes 1572872 | tf_op jit(solution)/shard_map/ppermute | solution.py:353
  2.7 1.6 %copy-start = (bf16[1,1024,1024]{2,1,0:T(8,128)(2,1)S(1)}, bf16[1,1024,1024]{2,1,0:T(8,128)(2,1)}, u32[]{:S(2)}) copy-start(bf16[1,1024,1024]{2,1,0:T(8,128)(2,1)} %param.10) | copy-start | bytes 6291460
  4.3 1.0 %copy-start.3 = (bf16[1,256,1024]{2,1,0:T(8,128)(2,1)S(1)}, bf16[1,256,1024]{2,1,0:T(8,128)(2,1)}, u32[]{:S(2)}) copy-start(bf16[1,256,1024]{2,1,0:T(8,128)(2,1)} %param.8) | copy-start | bytes 1572868
  8.2 18.9 %all-to-all-start = ((bf16[8,256,128]{2,1,0:T(8,128)(2,1)}), bf16[8,256,128]{2,1,0:T(8,128)(2,1)S(1)}, u32[]{:S(2)}, u32[]{:S(2)}) async-start(bf16[8,256,128]{2,1,0:T(8,128)(2,1)} %shard_map.77.refs_2_), calls=%async_computation | async-start | bytes 1048576 | tf_op jit(solution)/shard_map/all_to_all | solution.py:371
  13.1 6.8 %copy-start.2 = (bf16[1,256,1024]{2,1,0:T(8,128)(2,1)S(1)}, bf16[1,256,1024]{2,1,0:T(8,128)(2,1)}, u32[]{:S(2)}) copy-start(bf16[1,256,1024]{2,1,0:T(8,128)(2,1)} %param.7) | copy-start | bytes 1572868
  13.1 14.0 %copy-start.4 = (bf16[1,256,1024]{2,1,0:T(8,128)(2,1)S(1)}, bf16[1,256,1024]{2,1,0:T(8,128)(2,1)}, u32[]{:S(2)}) copy-start(bf16[1,256,1024]{2,1,0:T(8,128)(2,1)} %param.6) | copy-start | bytes 1572868
  15.7 10.4 %collective-permute-start.3 = (bf16[128,1024]{1,0:T(8,128)(2,1)}, bf16[128,1024]{1,0:T(8,128)(2,1)}, u32[]{:S(2)}, u32[]{:S(2)}) collective-permute-start(bf16[128,1024]{1,0:T(8,128)(2,1)} %get-tuple-element.17), channel_id=1, source_target_pairs={{0,2},{1,3},{2,0},{3,1},{4,6},{5,7},{6,4},{7,5},{8,10},{9,11},{10,... | collective-permute-start | bytes 786440 | tf_op jit(solution)/shard_map/ppermute | solution.py:353
  17.5 9.7 %collective-permute-start.2 = (bf16[128,1024]{1,0:T(8,128)(2,1)}, bf16[128,1024]{1,0:T(8,128)(2,1)}, u32[]{:S(2)}, u32[]{:S(2)}) collective-permute-start(bf16[128,1024]{1,0:T(8,128)(2,1)} %get-tuple-element.16), channel_id=1, source_target_pairs={{0,4},{1,5},{2,6},{3,7},{4,0},{5,1},{6,2},{7,3},{8,12},{9,13},{10,... | collective-permute-start | bytes 786440 | tf_op jit(solution)/shard_map/ppermute | solution.py:353
  19.9 8.2 %collective-permute-start.6 = (bf16[256,1024]{1,0:T(8,128)(2,1)S(1)}, bf16[256,1024]{1,0:T(8,128)(2,1)}, u32[]{:S(2)}, u32[]{:S(2)}) collective-permute-start(bf16[256,1024]{1,0:T(8,128)(2,1)S(1)} %bitcast.24), channel_id=1, source_target_pairs={{0,1},{1,0},{2,3},{3,2},{4,5},{5,4},{6,7},{7,6},{8,9},{9,8},{10,11... | collective-permute-start | bytes 1572872 | tf_op jit(solution)/shard_map/ppermute | solution.py:353
  21.2 9.5 %collective-permute-start.7 = (bf16[256,1024]{1,0:T(8,128)(2,1)S(1)}, bf16[256,1024]{1,0:T(8,128)(2,1)}, u32[]{:S(2)}, u32[]{:S(2)}) collective-permute-start(bf16[256,1024]{1,0:T(8,128)(2,1)S(1)} %collective-permute-done.refs_0_.refs_4_), channel_id=1, source_target_pairs={{0,1},{1,0},{2,3},{3,2},{4,5},{5,4},{6,7},{7,6},{8,9},{9,8},{10,11... | collective-permute-start | bytes 1572872 | tf_op jit(solution)/shard_map/ppermute | solution.py:353
  21.8 8.9 %collective-permute-start.8 = (bf16[256,1024]{1,0:T(8,128)(2,1)S(1)}, bf16[256,1024]{1,0:T(8,128)(2,1)}, u32[]{:S(2)}, u32[]{:S(2)}) collective-permute-start(bf16[256,1024]{1,0:T(8,128)(2,1)S(1)} %collective-permute-done.1.refs_1_.refs_5_), channel_id=1, source_target_pairs={{0,1},{1,0},{2,3},{3,2},{4,5},{5,4},{6,7},{7,6},{8,9},{9,8},{10,11... | collective-permute-start | bytes 1572872 | tf_op jit(solution)/shard_map/ppermute | solution.py:353
  26.1 3.1 %collective-permute-start.10 = (bf16[128,1024]{1,0:T(8,128)(2,1)}, bf16[128,1024]{1,0:T(8,128)(2,1)}, u32[]{:S(2)}, u32[]{:S(2)}) collective-permute-start(bf16[128,1024]{1,0:T(8,128)(2,1)} %collective-permute-done.3.refs_1_.refs_7_), channel_id=1, source_target_pairs={{0,1},{1,0},{2,3},{3,2},{4,5},{5,4},{6,7},{7,6},{8,9},{9,8},{10,11... | collective-permute-start | bytes 786440 | tf_op jit(solution)/shard_map/ppermute | solution.py:353
  27.2 3.6 %collective-permute-start.9 = (bf16[128,1024]{1,0:T(8,128)(2,1)}, bf16[128,1024]{1,0:T(8,128)(2,1)}, u32[]{:S(2)}, u32[]{:S(2)}) collective-permute-start(bf16[128,1024]{1,0:T(8,128)(2,1)} %collective-permute-done.2.refs_0_.refs_6_), channel_id=1, source_target_pairs={{0,1},{1,0},{2,3},{3,2},{4,5},{5,4},{6,7},{7,6},{8,9},{9,8},{10,11... | collective-permute-start | bytes 786440 | tf_op jit(solution)/shard_map/ppermute | solution.py:353
  27.2 3.6 %copy-start.5 = (s32[16]{0:T(128)S(1)}, s32[16]{0:T(128)}, u32[]{:S(2)}) copy-start(s32[16]{0:T(128)} %refs_0_.3) | copy-start | bytes 196
  28.2 14.6 %collective-permute-start.4 = (bf16[256,1024]{1,0:T(8,128)(2,1)}, bf16[256,1024]{1,0:T(8,128)(2,1)}, u32[]{:S(2)}, u32[]{:S(2)}) collective-permute-start(bf16[256,1024]{1,0:T(8,128)(2,1)} %shard_map.79.refs_14_.refs_3_), channel_id=1, source_target_pairs={{0,2},{1,3},{2,0},{3,1},{4,6},{5,7},{6,4},{7,5},{8,10},{9,11},{10,... | collective-permute-start | bytes 1572872 | tf_op jit(solution)/shard_map/ppermute | solution.py:353
  29.2 13.9 %collective-permute-start.5 = (bf16[256,1024]{1,0:T(8,128)(2,1)}, bf16[256,1024]{1,0:T(8,128)(2,1)}, u32[]{:S(2)}, u32[]{:S(2)}) collective-permute-start(bf16[256,1024]{1,0:T(8,128)(2,1)} %shard_map.79.refs_14_.refs_3_), channel_id=1, source_target_pairs={{0,4},{1,5},{2,6},{3,7},{4,0},{5,1},{6,2},{7,3},{8,12},{9,13},{10,... | collective-permute-start | bytes 1572872 | tf_op jit(solution)/shard_map/ppermute | solution.py:353
  30.7 22.3 %collective-permute-start.13 = (bf16[256,1024]{1,0:T(8,128)(2,1)}, bf16[256,1024]{1,0:T(8,128)(2,1)}, u32[]{:S(2)}, u32[]{:S(2)}) collective-permute-start(bf16[256,1024]{1,0:T(8,128)(2,1)} %shard_map.79.refs_14_.refs_3_), channel_id=1, source_target_pairs={{0,1},{1,0},{2,3},{3,2},{4,5},{5,4},{6,7},{7,6},{8,9},{9,8},{10,11... | collective-permute-start | bytes 1572872 | tf_op jit(solution)/shard_map/ppermute | solution.py:353
  44.2 8.3 %collective-permute-start.11 = (bf16[128,1024]{1,0:T(8,128)(2,1)S(1)}, bf16[128,1024]{1,0:T(8,128)(2,1)S(1)}, u32[]{:S(2)}, u32[]{:S(2)}) collective-permute-start(bf16[128,1024]{1,0:T(8,128)(2,1)S(1)} %get-tuple-element.18), channel_id=1, source_target_pairs={{0,4},{1,5},{2,6},{3,7},{4,0},{5,1},{6,2},{7,3},{8,12},{9,13},{10,... | collective-permute-start | bytes 786440 | tf_op jit(solution)/shard_map/ppermute | solution.py:353
  45.7 7.0 %collective-permute-start.12 = (bf16[128,1024]{1,0:T(8,128)(2,1)S(1)}, bf16[128,1024]{1,0:T(8,128)(2,1)S(1)}, u32[]{:S(2)}, u32[]{:S(2)}) collective-permute-start(bf16[128,1024]{1,0:T(8,128)(2,1)S(1)} %get-tuple-element.19), channel_id=1, source_target_pairs={{0,2},{1,3},{2,0},{3,1},{4,6},{5,7},{6,4},{7,5},{8,10},{9,11},{10,... | collective-permute-start | bytes 786440 | tf_op jit(solution)/shard_map/ppermute | solution.py:353
  46.5 7.9 %collective-permute-start.14 = (bf16[256,1024]{1,0:T(8,128)(2,1)}, bf16[256,1024]{1,0:T(8,128)(2,1)S(1)}, u32[]{:S(2)}, u32[]{:S(2)}) collective-permute-start(bf16[256,1024]{1,0:T(8,128)(2,1)} %collective-permute-done.4.refs_0_.refs_4_), channel_id=1, source_target_pairs={{0,1},{1,0},{2,3},{3,2},{4,5},{5,4},{6,7},{7,6},{8,9},{9,8},{10,11... | collective-permute-start | bytes 1572872 | tf_op jit(solution)/shard_map/ppermute | solution.py:353
  46.5 7.9 %collective-permute-start.15 = (bf16[256,1024]{1,0:T(8,128)(2,1)}, bf16[256,1024]{1,0:T(8,128)(2,1)S(1)}, u32[]{:S(2)}, u32[]{:S(2)}) collective-permute-start(bf16[256,1024]{1,0:T(8,128)(2,1)} %collective-permute-done.5.refs_1_.refs_5_), channel_id=1, source_target_pairs={{0,1},{1,0},{2,3},{3,2},{4,5},{5,4},{6,7},{7,6},{8,9},{9,8},{10,11... | collective-permute-start | bytes 1572872 | tf_op jit(solution)/shard_map/ppermute | solution.py:353
  47.0 27.2 %all-to-all-start.1 = ((bf16[8,256,384]{2,1,0:T(8,128)(2,1)}), bf16[8,256,384]{2,1,0:T(8,128)(2,1)}, u32[]{:S(2)}, u32[]{:S(2)}) async-start(bf16[8,256,384]{2,1,0:T(8,128)(2,1)} %shard_map.80.refs_2_.refs_13_), calls=%async_computation.1 | async-start | bytes 3145728 | tf_op jit(solution)/shard_map/all_to_all | solution.py:371
  52.5 1.5 %collective-permute-start.16 = (bf16[128,1024]{1,0:T(8,128)(2,1)S(1)}, bf16[128,1024]{1,0:T(8,128)(2,1)S(1)}, u32[]{:S(2)}, u32[]{:S(2)}) collective-permute-start(bf16[128,1024]{1,0:T(8,128)(2,1)S(1)} %collective-permute-done.11.refs_6_), channel_id=1, source_target_pairs={{0,1},{1,0},{2,3},{3,2},{4,5},{5,4},{6,7},{7,6},{8,9},{9,8},{10,11... | collective-permute-start | bytes 786440 | tf_op jit(solution)/shard_map/ppermute | solution.py:353
  52.7 1.7 %collective-permute-start.17 = (bf16[128,1024]{1,0:T(8,128)(2,1)S(1)}, bf16[128,1024]{1,0:T(8,128)(2,1)S(1)}, u32[]{:S(2)}, u32[]{:S(2)}) collective-permute-start(bf16[128,1024]{1,0:T(8,128)(2,1)S(1)} %collective-permute-done.12.refs_7_), channel_id=1, source_target_pairs={{0,1},{1,0},{2,3},{3,2},{4,5},{5,4},{6,7},{7,6},{8,9},{9,8},{10,11... | collective-permute-start | bytes 786440 | tf_op jit(solution)/shard_map/ppermute | solution.py:353
  62.4 3.8 %collective-permute-start.18 = (bf16[256,128]{1,0:T(8,128)(2,1)S(1)}, bf16[256,128]{1,0:T(8,128)(2,1)S(1)}, u32[]{:S(2)}, u32[]{:S(2)}) collective-permute-start(bf16[256,128]{1,0:T(8,128)(2,1)S(1)} %get-tuple-element.21), channel_id=1, source_target_pairs={{0,1},{1,0},{2,3},{3,2},{4,5},{5,4},{6,7},{7,6},{8,9},{9,8},{10,11... | collective-permute-start | bytes 196616 | tf_op jit(solution)/shard_map/ppermute | solution.py:353
  62.7 10.0 %collective-permute-start.19 = (bf16[256,128]{1,0:T(8,128)(2,1)S(1)}, bf16[256,128]{1,0:T(8,128)(2,1)S(1)}, u32[]{:S(2)}, u32[]{:S(2)}) collective-permute-start(bf16[256,128]{1,0:T(8,128)(2,1)S(1)} %get-tuple-element.22), channel_id=1, source_target_pairs={{0,2},{1,3},{2,0},{3,1},{4,6},{5,7},{6,4},{7,5},{8,10},{9,11},{10,... | collective-permute-start | bytes 196616 | tf_op jit(solution)/shard_map/ppermute | solution.py:353
  63.5 16.0 %collective-permute-start.20 = (bf16[256,128]{1,0:T(8,128)(2,1)S(1)}, bf16[256,128]{1,0:T(8,128)(2,1)S(1)}, u32[]{:S(2)}, u32[]{:S(2)}) collective-permute-start(bf16[256,128]{1,0:T(8,128)(2,1)S(1)} %get-tuple-element.23), channel_id=1, source_target_pairs={{0,3},{1,2},{2,1},{3,0},{4,7},{5,6},{6,5},{7,4},{8,11},{9,10},{10,... | collective-permute-start | bytes 196616 | tf_op jit(solution)/shard_map/ppermute | solution.py:353
  64.3 15.1 %collective-permute-start.21 = (bf16[256,128]{1,0:T(8,128)(2,1)S(1)}, bf16[256,128]{1,0:T(8,128)(2,1)S(1)}, u32[]{:S(2)}, u32[]{:S(2)}) collective-permute-start(bf16[256,128]{1,0:T(8,128)(2,1)S(1)} %get-tuple-element.24), channel_id=1, source_target_pairs={{0,4},{1,5},{2,6},{3,7},{4,0},{5,1},{6,2},{7,3},{8,12},{9,13},{10,... | collective-permute-start | bytes 196616 | tf_op jit(solution)/shard_map/ppermute | solution.py:353
  65.8 13.7 %collective-permute-start.22 = (bf16[256,128]{1,0:T(8,128)(2,1)S(1)}, bf16[256,128]{1,0:T(8,128)(2,1)S(1)}, u32[]{:S(2)}, u32[]{:S(2)}) collective-permute-start(bf16[256,128]{1,0:T(8,128)(2,1)S(1)} %get-tuple-element.25), channel_id=1, source_target_pairs={{0,5},{1,4},{2,7},{3,6},{4,1},{5,0},{6,3},{7,2},{8,13},{9,12},{10,... | collective-permute-start | bytes 196616 | tf_op jit(solution)/shard_map/ppermute | solution.py:353
  66.2 13.3 %collective-permute-start.23 = (bf16[256,128]{1,0:T(8,128)(2,1)S(1)}, bf16[256,128]{1,0:T(8,128)(2,1)S(1)}, u32[]{:S(2)}, u32[]{:S(2)}) collective-permute-start(bf16[256,128]{1,0:T(8,128)(2,1)S(1)} %get-tuple-element.26), channel_id=1, source_target_pairs={{0,6},{1,7},{2,4},{3,5},{4,2},{5,3},{6,0},{7,1},{8,14},{9,15},{10,... | collective-permute-start | bytes 196616 | tf_op jit(solution)/shard_map/ppermute | solution.py:353
  72.7 6.9 %collective-permute-start.24 = (bf16[256,128]{1,0:T(8,128)(2,1)S(1)}, bf16[256,128]{1,0:T(8,128)(2,1)S(1)}, u32[]{:S(2)}, u32[]{:S(2)}) collective-permute-start(bf16[256,128]{1,0:T(8,128)(2,1)S(1)} %get-tuple-element.27), channel_id=1, source_target_pairs={{0,7},{1,6},{2,5},{3,4},{4,3},{5,2},{6,1},{7,0},{8,15},{9,14},{10,... | collective-permute-start | bytes 196616 | tf_op jit(solution)/shard_map/ppermute | solution.py:353
  74.2 5.4 %copy-start.1 = (bf16[1,1024,1024]{2,1,0:T(8,128)(2,1)S(1)}, bf16[1,1024,1024]{2,1,0:T(8,128)(2,1)}, u32[]{:S(2)}) copy-start(bf16[1,1024,1024]{2,1,0:T(8,128)(2,1)} %param.10) | copy-start | bytes 6291460
  79.5 1.0 %copy-start.6 = (bf16[256,1024]{1,0:T(8,128)(2,1)S(1)}, bf16[256,1024]{1,0:T(8,128)(2,1)}, u32[]{:S(2)}) copy-start(bf16[256,1024]{1,0:T(8,128)(2,1)} %shard_map.83.refs_10_) | copy-start | bytes 1572868
  82.0 14.6 %collective-permute-start.25 = (bf16[256,1024]{1,0:T(8,128)(2,1)S(1)}, bf16[256,1024]{1,0:T(8,128)(2,1)S(1)}, u32[]{:S(2)}, u32[]{:S(2)}) collective-permute-start(bf16[256,1024]{1,0:T(8,128)(2,1)S(1)} %get-tuple-element.28), channel_id=1, source_target_pairs={{0,8},{8,0},{16,24},{24,16},{1,9},{9,1},{17,25},{25,17},{2,10},{10... | collective-permute-start | bytes 1572872 | tf_op jit(solution)/shard_map/ppermute | solution.py:403
  83.6 16.6 %collective-permute-start.26 = (bf16[256,1024]{1,0:T(8,128)(2,1)S(1)}, bf16[256,1024]{1,0:T(8,128)(2,1)S(1)}, u32[]{:S(2)}, u32[]{:S(2)}) collective-permute-start(bf16[256,1024]{1,0:T(8,128)(2,1)S(1)} %get-tuple-element.29), channel_id=1, source_target_pairs={{8,16},{16,8},{9,17},{17,9},{10,18},{18,10},{11,19},{19,11},{12,20... | collective-permute-start | bytes 1572872 | tf_op jit(solution)/shard_map/ppermute | solution.py:403

commit v13 on v12

--- a/solution.py
+++ b/solution.py
@@ -147,20 +147,25 @@
                         scale[j * TILE : (j + 1) * TILE], (TILE, HD)
                     )
 
-    def visit(c, carry):
+    def visit(pair, carry):
+        swap = (count[2 * pair] < count[2 * pair + 1]).astype(jnp.int32)
+        large, small = 2 * pair + swap, 2 * pair + 1 - swap
         for n in range(1, CAPACITY + 1):
-
-            @pl.when(count[c] == n)
-            def _():
-                held = [member[c * CAPACITY + i] for i in range(n)]
-                if back:
-                    backward_cluster(held, kept, out, scales, grads)
-                else:
-                    forward_cluster(held, kept, out)
+            for m in range(0, n + 1):
+
+                @pl.when((count[large] == n) & (count[small] == m))
+                def _():
+                    for c, size in ((large, n), (small, m)):
+                        if size > 0:
+                            held = [member[c * CAPACITY + i] for i in range(size)]
+                            if back:
+                                backward_cluster(held, kept, out, scales, grads)
+                            else:
+                                forward_cluster(held, kept, out)
 
         return carry
 
-    lax.fori_loop(0, clusters, visit, 0)
+    lax.fori_loop(0, clusters // 2, visit, 0)
     if not back:
         for k in range(HEADS):
             out_refs[k][...] = out[pl.ds(2 * (flip ^ k), 2)].reshape(out_refs[k].shape)
@@ -267,13 +272,11 @@
 
 def finish_kernel(info_ref, *refs):
     att_refs, refs = refs[:HEADS], refs[HEADS:]
-    x_ref, w_ref, grad_ref, first_ref, second_ref, x, sem = refs
+    x, w_ref, grad_ref, first_ref, second_ref = refs
     flip, odd = info_ref[0], info_ref[3]
-    x_copy = fetch(x_ref, x, sem)
     att = jnp.concatenate([ref[...] for ref in att_refs], axis=1)
-    x_copy.wait()
     block = 256
-    for start in range(0, x_ref.shape[1], block):
+    for start in range(0, x.shape[1], block):
         columns = slice(start, start + block)
         w = jnp.concatenate([w_ref[flip ^ k, :, columns] for k in range(HEADS)], axis=0)
         result = low(high(x[:, columns]) + dot(att, w, NN))
@@ -287,15 +290,15 @@
     return call(
         finish_kernel,
         [info, *attention, current, w_fin.reshape(HEADS, HD, width), grad_self],
-        [SMEM] + [VMEM] * HEADS + [HBM] + [VMEM] * 2,
+        [SMEM] + [VMEM] * (HEADS + 3),
         [jax.ShapeDtypeStruct((tokens, width), jnp.bfloat16)] * 2,
-        [pltpu.VMEM((tokens, width), jnp.bfloat16), pltpu.SemaphoreType.DMA],
+        [],
         MICROSECOND,
         2 * width * HEADS * HD,
     )
 
 
-def finish_back_kernel(grad_ref, x_ref, up_ref, w_ref, out_ref, grads, x, up, rows, total, sems):
+def finish_back_kernel(grad_ref, x_ref, up_ref, w_ref, near_ref, out_ref, near, grads, x, up, rows, total, sems):
     chunks = rows.shape[0]
     depth = rows.shape[1]
     held = depth // HD
@@ -305,6 +308,7 @@
     ]
     copies.append(fetch(x_ref, x, sems.at[1 + chunks]))
     copies.append(fetch(up_ref, up, sems.at[2 + chunks]))
+    near_copy = fetch(near_ref, near, sems.at[3 + chunks])
     copies[0].wait()
     for i in range(chunks):
         c, first = i * held // HEADS, i * held % HEADS
@@ -324,27 +328,28 @@
     g = total[...]
     pulled = scale * (g - unit * jnp.mean(unit * g, axis=1, keepdims=True))
     out_ref[...] = low(high(up[...]) + pulled)
-
-
-def finish_back(grads, stored, upstream, w_qkv):
+    near_copy.wait()
+
+
+def finish_back(grads, stored, upstream, w_qkv, near):
     tokens, width = stored.shape
     chunks = 6
     return call(
         finish_back_kernel,
-        [grads, stored, upstream, w_qkv],
-        [HBM] * 4,
-        jax.ShapeDtypeStruct((tokens, width), jnp.bfloat16),
+        [grads, stored, upstream, w_qkv, near],
+        [HBM] * 5,
+        [jax.ShapeDtypeStruct((tokens, width), jnp.bfloat16)] * 2,
         [
             pltpu.VMEM(grads.shape, jnp.bfloat16),
             pltpu.VMEM((tokens, width), jnp.bfloat16),
             pltpu.VMEM((tokens, width), jnp.bfloat16),
             pltpu.VMEM((chunks, w_qkv.shape[0] // chunks, width), jnp.bfloat16),
             pltpu.VMEM((tokens, width), jnp.float32),
-            pltpu.SemaphoreType.DMA((chunks + 3,)),
+            pltpu.SemaphoreType.DMA((chunks + 4,)),
         ],
         MICROSECOND * 5,
         6 * width * HEADS * HD,
-        grant=58 * MIB,
+        grant=52 * MIB,
     )
 
 
@@ -446,8 +451,8 @@
         info, tile_cluster, current_pieces, own_head, spacing, earlier=[grads]
     )
     returned = collect_each(outputs)
-    grad_self = finish_back(returned_grads, stored, upstream, w_rows)
-    first, second = finish(info, returned, current, w_fin, grad_self)
+    grad_self, near = finish_back(returned_grads, stored, upstream, w_rows, current)
+    first, second = finish(info, returned, near, w_fin, grad_self)
     first, second = swapped(first, 0), swapped(second, 1)
     next_input = jnp.where(odd == 1, first, second)
     grad_input = jnp.where(odd == 1, second, first)

time: 102 us -> 101 us (level)
  Pallas kernels: 32.3 us -> 30.6 us
    pallas_call x6, Pallas kernels: 30.4 us -> 27.9 us  [call(): pl.pallas_call(kernel, in_specs=in_specs, out_specs=[VMEM] * len(out_shap...]
    unnamed x14 -> x16, local copies, waits for them, and re-layouts: 3.69 us -> 3.28 us
  transfers between devices with their start and end apart: 29 -> 29, of which waited for: 13 -> 12; matrix products, arithmetic and copies ran while one was open for 1% -> 1% of each run, Pallas kernels for 31% -> 29%
where the time goes in v13:
time: 101 us; the launch traced here: 100 us
  starting transfers between devices  33.7 us (33%)
  Pallas kernels  30.6 us (30%)
  waiting for transfers between devices  29.4 us (29%)
  local copies, waits for them, and re-layouts  4.47 us (4%)
  other arithmetic  1.11 us (1%)
    pallas_call x6, Pallas kernels, call(): pl.pallas_call(kernel, in_specs=in_specs, out_specs=[VMEM] * len(out_shap...  27.9 us
    ppermute x25, starting transfers between devices, partner(): return lax.ppermute(block, 'seq', route)  19.8 us
    ppermute x25, waiting for transfers between devices, partner(): return lax.ppermute(block, 'seq', route)  14.8 us
    ppermute x2, waiting for transfers between devices, swapped(): return lax.ppermute(block, 'pipe', route)  14.7 us
    all_to_all x2, starting transfers between devices, all_swap(): lax.all_to_all(blocks, 'seq', split_axis=0, concat_axis=0, tiled=True)  10.4 us
    ppermute x2, starting transfers between devices, swapped(): return lax.ppermute(block, 'pipe', route)  3.54 us
    unnamed x16, local copies, waits for them, and re-layouts  3.28 us
    pallas_call x2, Pallas kernels, rows_after(): pl.pallas_call(functools.partial(copy_kernel, starts), in_specs=[HBM] * (...  2.66 us
  transfers between devices with their start and end apart: 29, of which 12 were waited for; matrix products, arithmetic and copies ran while one was open for 1% of the time, Pallas kernels for 29%

profile of v13, /device:TPU:18, one launch (start us, length us, event | category | flops | bytes accessed | tf_op | source)
XLA Modules:
  0.0 100.1 jit_solution(17654033685842732552)
XLA Ops:
  0.6 0.6 collective-permute-start
  1.2 1.5 %collective-permute-start.1 = (bf16[256,1024]{1,0:T(8,128)(2,1)}, bf16[256,1024]{1,0:T(8,128)(2,1)S(1)}, u32[]{:S(2)}, u32[]{:S(2)}) collective-permute-start(bf16[256,1024]{1,0:T(8,128)(2,1)} %bitcast.24), channel_id=1, source_target_pairs={{0,4},{1,5},{2,6},{3,7},{4,0},{5,1},{6,2},{7,3},{8,12},{9,13},{10,... | collective-permute-start | bytes 1572872 | tf_op jit(solution)/shard_map/ppermute | solution.py:358
  2.8 1.6 %copy-done = bf16[1,1024,1024]{2,1,0:T(8,128)(2,1)S(1)} copy-done((bf16[1,1024,1024]{2,1,0:T(8,128)(2,1)S(1)}, bf16[1,1024,1024]{2,1,0:T(8,128)(2,1)}, u32[]{:S(2)}) %copy-start) | copy-done | bytes 2097176
  4.3 1.0 %copy-done.4 = bf16[1,256,1024]{2,1,0:T(8,128)(2,1)S(1)} copy-done((bf16[1,256,1024]{2,1,0:T(8,128)(2,1)S(1)}, bf16[1,256,1024]{2,1,0:T(8,128)(2,1)}, u32[]{:S(2)}) %copy-start.4) | copy-done | bytes 524312
  5.4 2.8 %shard_map.77.refs_2_ = bf16[8,256,128]{2,1,0:T(8,128)(2,1)} custom-call(bf16[256,1024]{1,0:T(8,128)(2,1)S(1)} %bitcast.29, bf16[8,128,1024]{2,1,0:T(8,128)(2,1)S(1)} %bitcast.19), custom_call_target="tpu_custom_call" | custom-call | flops 3449999872 | bytes 2097152 | tf_op jit(solution)/shard_map/pallas_call | solution.py:42
  8.2 4.9 %all-to-all-start = ((bf16[8,256,128]{2,1,0:T(8,128)(2,1)}), bf16[8,256,128]{2,1,0:T(8,128)(2,1)S(1)}, u32[]{:S(2)}, u32[]{:S(2)}) async-start(bf16[8,256,128]{2,1,0:T(8,128)(2,1)} %shard_map.77.refs_2_), calls=%async_computation | async-start | bytes 1048576 | tf_op jit(solution)/shard_map/all_to_all | solution.py:376
  13.1 1.4 %collective-permute-done.refs_0_.refs_4_ = bf16[256,1024]{1,0:T(8,128)(2,1)S(1)} collective-permute-done((bf16[256,1024]{1,0:T(8,128)(2,1)}, bf16[256,1024]{1,0:T(8,128)(2,1)S(1)}, u32[]{:S(2)}, u32[]{:S(2)}) %collective-permute-start) | collective-permute-done | bytes 524320 | tf_op jit(solution)/shard_map/ppermute | solution.py:358
  14.6 0.3 collective-permute-done.1.refs_1_.refs_5_
  14.8 0.9 shard_map.78
  15.7 1.8 %collective-permute-start.3 = (bf16[128,1024]{1,0:T(8,128)(2,1)}, bf16[128,1024]{1,0:T(8,128)(2,1)}, u32[]{:S(2)}, u32[]{:S(2)}) collective-permute-start(bf16[128,1024]{1,0:T(8,128)(2,1)} %get-tuple-element.19), channel_id=1, source_target_pairs={{0,2},{1,3},{2,0},{3,1},{4,6},{5,7},{6,4},{7,5},{8,10},{9,11},{10,... | collective-permute-start | bytes 786440 | tf_op jit(solution)/shard_map/ppermute | solution.py:358
  17.5 2.4 %collective-permute-start.2 = (bf16[128,1024]{1,0:T(8,128)(2,1)}, bf16[128,1024]{1,0:T(8,128)(2,1)}, u32[]{:S(2)}, u32[]{:S(2)}) collective-permute-start(bf16[128,1024]{1,0:T(8,128)(2,1)} %get-tuple-element.18), channel_id=1, source_target_pairs={{0,4},{1,5},{2,6},{3,7},{4,0},{5,1},{6,2},{7,3},{8,12},{9,13},{10,... | collective-permute-start | bytes 786440 | tf_op jit(solution)/shard_map/ppermute | solution.py:358
  20.0 1.2 %constant_dynamic-slice_fusion = bf16[3,1,128,1024]{3,2,1,0:T(8,128)(2,1)S(1)} fusion(bf16[3,8,128,1024]{3,2,1,0:T(8,128)(2,1)} %bitcast.30, s32[]{:T(128)S(6)} %select_n.25), kind=kLoop, calls=%fused_computation.3 | loop fusion | bytes 1572868 | tf_op jit(solution)/shard_map/jit(dynamic_index_in_dim)/dynamic_slice | solution.py:438
  21.2 0.6 collective-permute-start.7
  21.9 4.2 %collective-permute-done.3.refs_1_.refs_7_ = bf16[128,1024]{1,0:T(8,128)(2,1)} collective-permute-done((bf16[128,1024]{1,0:T(8,128)(2,1)}, bf16[128,1024]{1,0:T(8,128)(2,1)}, u32[]{:S(2)}, u32[]{:S(2)}) %collective-permute-start.3) | collective-permute-done | bytes 262176 | tf_op jit(solution)/shard_map/ppermute | solution.py:358
  26.1 1.1 %collective-permute-done.2.refs_0_.refs_6_ = bf16[128,1024]{1,0:T(8,128)(2,1)} collective-permute-done((bf16[128,1024]{1,0:T(8,128)(2,1)}, bf16[128,1024]{1,0:T(8,128)(2,1)}, u32[]{:S(2)}, u32[]{:S(2)}) %collective-permute-start.2) | collective-permute-done | bytes 262176 | tf_op jit(solution)/shard_map/ppermute | solution.py:358
  27.2 1.0 shard_map.79.refs_14_.refs_3_
  28.2 1.0 %collective-permute-start.4 = (bf16[256,1024]{1,0:T(8,128)(2,1)}, bf16[256,1024]{1,0:T(8,128)(2,1)S(1)}, u32[]{:S(2)}, u32[]{:S(2)}) collective-permute-start(bf16[256,1024]{1,0:T(8,128)(2,1)} %shard_map.79.refs_14_.refs_3_), channel_id=1, source_target_pairs={{0,2},{1,3},{2,0},{3,1},{4,6},{5,7},{6,4},{7,5},{8,10},{9,11},{10,... | collective-permute-start | bytes 1572872 | tf_op jit(solution)/shard_map/ppermute | solution.py:358
  29.2 1.5 %collective-permute-start.5 = (bf16[256,1024]{1,0:T(8,128)(2,1)}, bf16[256,1024]{1,0:T(8,128)(2,1)}, u32[]{:S(2)}, u32[]{:S(2)}) collective-permute-start(bf16[256,1024]{1,0:T(8,128)(2,1)} %shard_map.79.refs_14_.refs_3_), channel_id=1, source_target_pairs={{0,4},{1,5},{2,6},{3,7},{4,0},{5,1},{6,2},{7,3},{8,12},{9,13},{10,... | collective-permute-start | bytes 1572872 | tf_op jit(solution)/shard_map/ppermute | solution.py:358
  30.7 11.0 %shard_map.80.refs_2_.refs_13_ = bf16[8,256,384]{2,1,0:T(8,128)(2,1)} custom-call(s32[16]{0:T(128)S(1)} %copy-done.5, s32[4]{0:T(128)S(1)} %pad_add_fusion.refs_1_.info_ref, bf16[384,1024]{1,0:T(8,128)(2,1)S(1)} %bitcast.16, bf16[256,1024]{1,0:T(8,128)(2,1)S(1)} %bitcast.26, bf16[256,1024]{1,0:T(8,128)(2,1)S(1)} %collective-permute-done.refs_0_.refs_4_, ...), custom_call_target="tpu_custom_call" | custom-call | flops 13799999488 | bytes 7340032 | tf_op jit(solution)/shard_map/pallas_call | solution.py:42
  41.7 1.0 collective-permute-done.4.refs_0_.refs_4_
  42.7 0.4 collective-permute-done.5.refs_1_.refs_5_
  43.1 1.8 %shard_map.81 = (bf16[128,1024]{1,0:T(8,128)(2,1)}, bf16[128,1024]{1,0:T(8,128)(2,1)}) custom-call(bf16[256,1024]{1,0:T(8,128)(2,1)S(1)} %collective-permute-done.4.refs_0_.refs_4_, bf16[256,1024]{1,0:T(8,128)(2,1)} %collective-permute-done.5.refs_1_.refs_5_, bf16[8,256,384]{2,1,0:T(8,128)(2,1)} %shard_map.80.refs_2_.refs_13_), custom_call_target="tpu_custom_call" | custom-call | flops 1150000000 | tf_op jit(solution)/shard_map/pallas_call | solution.py:217
  44.9 1.6 %collective-permute-start.11 = (bf16[128,1024]{1,0:T(8,128)(2,1)}, bf16[128,1024]{1,0:T(8,128)(2,1)S(1)}, u32[]{:S(2)}, u32[]{:S(2)}) collective-permute-start(bf16[128,1024]{1,0:T(8,128)(2,1)} %get-tuple-element.20), channel_id=1, source_target_pairs={{0,4},{1,5},{2,6},{3,7},{4,0},{5,1},{6,2},{7,3},{8,12},{9,13},{10,... | collective-permute-start | bytes 786440 | tf_op jit(solution)/shard_map/ppermute | solution.py:358
  46.5 0.8 collective-permute-start.12
  47.2 0.5 collective-permute-start.15
  47.7 5.4 %all-to-all-start.1 = ((bf16[8,256,384]{2,1,0:T(8,128)(2,1)}), bf16[8,256,384]{2,1,0:T(8,128)(2,1)}, u32[]{:S(2)}, u32[]{:S(2)}) async-start(bf16[8,256,384]{2,1,0:T(8,128)(2,1)} %shard_map.80.refs_2_.refs_13_), calls=%async_computation.1 | async-start | bytes 3145728 | tf_op jit(solution)/shard_map/all_to_all | solution.py:376
  53.2 0.1 collective-permute-start.16
  53.3 0.1 collective-permute-done.12.refs_7_
  53.5 0.2 collective-permute-start.17
  53.7 1.0 %collective-permute-done.16.refs_11_ = bf16[128,1024]{1,0:T(8,128)(2,1)S(1)} collective-permute-done((bf16[128,1024]{1,0:T(8,128)(2,1)S(1)}, bf16[128,1024]{1,0:T(8,128)(2,1)S(1)}, u32[]{:S(2)}, u32[]{:S(2)}) %collective-permute-start.16) | collective-permute-done | bytes 262176 | tf_op jit(solution)/shard_map/ppermute | solution.py:358
  54.7 0.4 collective-permute-done.17.refs_12_
  55.1 7.3 %shard_map.82 = (bf16[256,128]{1,0:T(8,128)(2,1)S(1)}, bf16[256,128]{1,0:T(8,128)(2,1)S(1)}, bf16[256,128]{1,0:T(8,128)(2,1)S(1)}, bf16[256,128]{1,0:T(8,128)(2,...) custom-call(s32[16]{0:T(128)S(1)} %copy-done.5, ...), custom_call_target="tpu_custom_call" | custom-call | flops 9200000000 | bytes 5242880 | tf_op jit(solution)/shard_map/pallas_call | solution.py:42
  62.4 0.6 copy-done.6
  63.0 0.3 collective-permute-start.18
  63.3 0.9 collective-permute-start.19
  64.2 0.6 collective-permute-start.20
  64.9 1.5 %collective-permute-start.21 = (bf16[256,128]{1,0:T(8,128)(2,1)}, bf16[256,128]{1,0:T(8,128)(2,1)S(1)}, u32[]{:S(2)}, u32[]{:S(2)}) collective-permute-start(bf16[256,128]{1,0:T(8,128)(2,1)} %get-tuple-element.26), channel_id=1, source_target_pairs={{0,4},{1,5},{2,6},{3,7},{4,0},{5,1},{6,2},{7,3},{8,12},{9,13},{10,... | collective-permute-start | bytes 196616 | tf_op jit(solution)/shard_map/ppermute | solution.py:358
  66.4 0.4 collective-permute-start.22
  66.8 1.8 %collective-permute-start.23 = (bf16[256,128]{1,0:T(8,128)(2,1)S(1)}, bf16[256,128]{1,0:T(8,128)(2,1)S(1)}, u32[]{:S(2)}, u32[]{:S(2)}) collective-permute-start(bf16[256,128]{1,0:T(8,128)(2,1)S(1)} %get-tuple-element.28), channel_id=1, source_target_pairs={{0,6},{1,7},{2,4},{3,5},{4,2},{5,3},{6,0},{7,1},{8,14},{9,15},{10,... | collective-permute-start | bytes 196616 | tf_op jit(solution)/shard_map/ppermute | solution.py:358
  68.5 4.9 %collective-permute-done.19.refs_2_ = bf16[256,128]{1,0:T(8,128)(2,1)S(1)} collective-permute-done((bf16[256,128]{1,0:T(8,128)(2,1)S(1)}, bf16[256,128]{1,0:T(8,128)(2,1)S(1)}, u32[]{:S(2)}, u32[]{:S(2)}) %collective-permute-start.19) | collective-permute-done | bytes 65568 | tf_op jit(solution)/shard_map/ppermute | solution.py:358
  73.4 1.5 %collective-permute-start.24 = (bf16[256,128]{1,0:T(8,128)(2,1)S(1)}, bf16[256,128]{1,0:T(8,128)(2,1)S(1)}, u32[]{:S(2)}, u32[]{:S(2)}) collective-permute-start(bf16[256,128]{1,0:T(8,128)(2,1)S(1)} %get-tuple-element.29), channel_id=1, source_target_pairs={{0,7},{1,6},{2,5},{3,4},{4,3},{5,2},{6,1},{7,0},{8,15},{9,14},{10,... | collective-permute-start | bytes 196616 | tf_op jit(solution)/shard_map/ppermute | solution.py:358
  74.9 4.5 %shard_map.83 = (bf16[256,1024]{1,0:T(8,128)(2,1)S(1)}, bf16[256,1024]{1,0:T(8,128)(2,1)S(1)}) custom-call(bf16[8,256,384]{2,1,0:T(8,128)(2,1)} %all-to-all-done.1.grad_ref, bf16[256,1024]{1,0:T(8,128)(2,1)S(1)} %bitcast.27, bf16[256,1024]{1,0:T(8,128)(2,1)} %bitcast.28, bf16[3072,1024]{1,0:T(8,128)(2,1)} %bitcast.31, bf16[256,1024]{1,0:T(8,128)(2,1)} %bitcast.21), custom_call_target="tpu_custom_call" | custom-call | flops 5750000128 | bytes 6291456 | tf_op jit(solution)/shard_map/pallas_call | solution.py:42
  79.5 1.3 %shard_map.84 = (bf16[256,1024]{1,0:T(8,128)(2,1)S(1)}, bf16[256,1024]{1,0:T(8,128)(2,1)S(1)}) custom-call(s32[4]{0:T(128)S(1)} %pad_add_fusion.refs_1_.info_ref, bf16[256,128]{1,0:T(8,128)(2,1)S(1)} %copy-done.7, bf16[256,128]{1,0:T(8,128)(2,1)S(1)} %collective-permute-done.18.refs_1_, bf16[256,128]{1,0:T(8,128)(2,1)S(1)} %collective-permute-done.19.refs_2_, ...), custom_call_target="tpu_custom_call" | custom-call | flops 1150000000 | bytes 2097152 | tf_op jit(solution)/shard_map/pallas_call | solution.py:42
  80.9 1.6 %collective-permute-start.25 = (bf16[256,1024]{1,0:T(8,128)(2,1)S(1)}, bf16[256,1024]{1,0:T(8,128)(2,1)S(1)}, u32[]{:S(2)}, u32[]{:S(2)}) collective-permute-start(bf16[256,1024]{1,0:T(8,128)(2,1)S(1)} %get-tuple-element.32), channel_id=1, source_target_pairs={{0,8},{8,0},{16,24},{24,16},{1,9},{9,1},{17,25},{25,17},{2,10},{10... | collective-permute-start | bytes 1572872 | tf_op jit(solution)/shard_map/ppermute | solution.py:408
  82.5 1.9 %collective-permute-start.26 = (bf16[256,1024]{1,0:T(8,128)(2,1)S(1)}, bf16[256,1024]{1,0:T(8,128)(2,1)S(1)}, u32[]{:S(2)}, u32[]{:S(2)}) collective-permute-start(bf16[256,1024]{1,0:T(8,128)(2,1)S(1)} %get-tuple-element.33), channel_id=1, source_target_pairs={{8,16},{16,8},{9,17},{17,9},{10,18},{18,10},{11,19},{19,11},{12,20... | collective-permute-start | bytes 1572872 | tf_op jit(solution)/shard_map/ppermute | solution.py:408
  84.4 11.0 %collective-permute-done.25 = bf16[256,1024]{1,0:T(8,128)(2,1)S(1)} collective-permute-done((bf16[256,1024]{1,0:T(8,128)(2,1)S(1)}, bf16[256,1024]{1,0:T(8,128)(2,1)S(1)}, u32[]{:S(2)}, u32[]{:S(2)}) %collective-permute-start.25) | collective-permute-done | bytes 524320 | tf_op jit(solution)/shard_map/ppermute | solution.py:408
  95.4 3.6 %collective-permute-done.26 = bf16[256,1024]{1,0:T(8,128)(2,1)S(1)} collective-permute-done((bf16[256,1024]{1,0:T(8,128)(2,1)S(1)}, bf16[256,1024]{1,0:T(8,128)(2,1)S(1)}, u32[]{:S(2)}, u32[]{:S(2)}) %collective-permute-start.26) | collective-permute-done | bytes 524320 | tf_op jit(solution)/shard_map/ppermute | solution.py:408
  99.1 1.0 %select_bitcast_fusion = (bf16[1,256,1024]{2,1,0:T(8,128)(2,1)}, bf16[1,256,1024]{2,1,0:T(8,128)(2,1)}) fusion(bf16[256,1024]{1,0:T(8,128)(2,1)S(1)} %collective-permute-done.26, bf16[256,1024]{1,0:T(8,128)(2,1)S(1)} %collective-permute-done.25, pred[]{:T(512)S(6)} %eq.6), kind=kLoop, calls=%fused_computation | loop fusion | flops 524288 | bytes 2097153 | tf_op jit(solution)/shard_map/broadcast_in_dim | solution.py:459
  (37 shorter events, 0.2 us)
Async XLA Ops:
  0.6 13.9 %collective-permute-start = (bf16[256,1024]{1,0:T(8,128)(2,1)}, bf16[256,1024]{1,0:T(8,128)(2,1)S(1)}, u32[]{:S(2)}, u32[]{:S(2)}) collective-permute-start(bf16[256,1024]{1,0:T(8,128)(2,1)} %bitcast.23), channel_id=1, source_target_pairs={{0,2},{1,3},{2,0},{3,1},{4,6},{5,7},{6,4},{7,5},{8,10},{9,11},{10,... | collective-permute-start | bytes 1572872 | tf_op jit(solution)/shard_map/ppermute | solution.py:358
  1.2 13.6 %collective-permute-start.1 = (bf16[256,1024]{1,0:T(8,128)(2,1)}, bf16[256,1024]{1,0:T(8,128)(2,1)S(1)}, u32[]{:S(2)}, u32[]{:S(2)}) collective-permute-start(bf16[256,1024]{1,0:T(8,128)(2,1)} %bitcast.24), channel_id=1, source_target_pairs={{0,4},{1,5},{2,6},{3,7},{4,0},{5,1},{6,2},{7,3},{8,12},{9,13},{10,... | collective-permute-start | bytes 1572872 | tf_op jit(solution)/shard_map/ppermute | solution.py:358
  2.7 1.6 %copy-start = (bf16[1,1024,1024]{2,1,0:T(8,128)(2,1)S(1)}, bf16[1,1024,1024]{2,1,0:T(8,128)(2,1)}, u32[]{:S(2)}) copy-start(bf16[1,1024,1024]{2,1,0:T(8,128)(2,1)} %param.10) | copy-start | bytes 6291460
  4.3 1.0 %copy-start.4 = (bf16[1,256,1024]{2,1,0:T(8,128)(2,1)S(1)}, bf16[1,256,1024]{2,1,0:T(8,128)(2,1)}, u32[]{:S(2)}) copy-start(bf16[1,256,1024]{2,1,0:T(8,128)(2,1)} %param.8) | copy-start | bytes 1572868
  8.2 18.9 %all-to-all-start = ((bf16[8,256,128]{2,1,0:T(8,128)(2,1)}), bf16[8,256,128]{2,1,0:T(8,128)(2,1)S(1)}, u32[]{:S(2)}, u32[]{:S(2)}) async-start(bf16[8,256,128]{2,1,0:T(8,128)(2,1)} %shard_map.77.refs_2_), calls=%async_computation | async-start | bytes 1048576 | tf_op jit(solution)/shard_map/all_to_all | solution.py:376
  13.1 6.8 %copy-start.3 = (bf16[1,256,1024]{2,1,0:T(8,128)(2,1)S(1)}, bf16[1,256,1024]{2,1,0:T(8,128)(2,1)}, u32[]{:S(2)}) copy-start(bf16[1,256,1024]{2,1,0:T(8,128)(2,1)} %param.7) | copy-start | bytes 1572868
  13.1 14.0 %copy-start.2 = (bf16[1,256,1024]{2,1,0:T(8,128)(2,1)S(1)}, bf16[1,256,1024]{2,1,0:T(8,128)(2,1)}, u32[]{:S(2)}) copy-start(bf16[1,256,1024]{2,1,0:T(8,128)(2,1)} %param.6) | copy-start | bytes 1572868
  15.7 10.4 %collective-permute-start.3 = (bf16[128,1024]{1,0:T(8,128)(2,1)}, bf16[128,1024]{1,0:T(8,128)(2,1)}, u32[]{:S(2)}, u32[]{:S(2)}) collective-permute-start(bf16[128,1024]{1,0:T(8,128)(2,1)} %get-tuple-element.19), channel_id=1, source_target_pairs={{0,2},{1,3},{2,0},{3,1},{4,6},{5,7},{6,4},{7,5},{8,10},{9,11},{10,... | collective-permute-start | bytes 786440 | tf_op jit(solution)/shard_map/ppermute | solution.py:358
  17.5 9.6 %collective-permute-start.2 = (bf16[128,1024]{1,0:T(8,128)(2,1)}, bf16[128,1024]{1,0:T(8,128)(2,1)}, u32[]{:S(2)}, u32[]{:S(2)}) collective-permute-start(bf16[128,1024]{1,0:T(8,128)(2,1)} %get-tuple-element.18), channel_id=1, source_target_pairs={{0,4},{1,5},{2,6},{3,7},{4,0},{5,1},{6,2},{7,3},{8,12},{9,13},{10,... | collective-permute-start | bytes 786440 | tf_op jit(solution)/shard_map/ppermute | solution.py:358
  20.0 8.2 %collective-permute-start.6 = (bf16[256,1024]{1,0:T(8,128)(2,1)S(1)}, bf16[256,1024]{1,0:T(8,128)(2,1)}, u32[]{:S(2)}, u32[]{:S(2)}) collective-permute-start(bf16[256,1024]{1,0:T(8,128)(2,1)S(1)} %bitcast.25), channel_id=1, source_target_pairs={{0,1},{1,0},{2,3},{3,2},{4,5},{5,4},{6,7},{7,6},{8,9},{9,8},{10,11... | collective-permute-start | bytes 1572872 | tf_op jit(solution)/shard_map/ppermute | solution.py:358
  21.2 9.5 %collective-permute-start.7 = (bf16[256,1024]{1,0:T(8,128)(2,1)S(1)}, bf16[256,1024]{1,0:T(8,128)(2,1)}, u32[]{:S(2)}, u32[]{:S(2)}) collective-permute-start(bf16[256,1024]{1,0:T(8,128)(2,1)S(1)} %collective-permute-done.refs_0_.refs_4_), channel_id=1, source_target_pairs={{0,1},{1,0},{2,3},{3,2},{4,5},{5,4},{6,7},{7,6},{8,9},{9,8},{10,11... | collective-permute-start | bytes 1572872 | tf_op jit(solution)/shard_map/ppermute | solution.py:358
  21.8 8.9 %collective-permute-start.8 = (bf16[256,1024]{1,0:T(8,128)(2,1)S(1)}, bf16[256,1024]{1,0:T(8,128)(2,1)}, u32[]{:S(2)}, u32[]{:S(2)}) collective-permute-start(bf16[256,1024]{1,0:T(8,128)(2,1)S(1)} %collective-permute-done.1.refs_1_.refs_5_), channel_id=1, source_target_pairs={{0,1},{1,0},{2,3},{3,2},{4,5},{5,4},{6,7},{7,6},{8,9},{9,8},{10,11... | collective-permute-start | bytes 1572872 | tf_op jit(solution)/shard_map/ppermute | solution.py:358
  26.1 3.1 %collective-permute-start.10 = (bf16[128,1024]{1,0:T(8,128)(2,1)}, bf16[128,1024]{1,0:T(8,128)(2,1)}, u32[]{:S(2)}, u32[]{:S(2)}) collective-permute-start(bf16[128,1024]{1,0:T(8,128)(2,1)} %collective-permute-done.3.refs_1_.refs_7_), channel_id=1, source_target_pairs={{0,1},{1,0},{2,3},{3,2},{4,5},{5,4},{6,7},{7,6},{8,9},{9,8},{10,11... | collective-permute-start | bytes 786440 | tf_op jit(solution)/shard_map/ppermute | solution.py:358
  27.2 3.6 %collective-permute-start.9 = (bf16[128,1024]{1,0:T(8,128)(2,1)}, bf16[128,1024]{1,0:T(8,128)(2,1)}, u32[]{:S(2)}, u32[]{:S(2)}) collective-permute-start(bf16[128,1024]{1,0:T(8,128)(2,1)} %collective-permute-done.2.refs_0_.refs_6_), channel_id=1, source_target_pairs={{0,1},{1,0},{2,3},{3,2},{4,5},{5,4},{6,7},{7,6},{8,9},{9,8},{10,11... | collective-permute-start | bytes 786440 | tf_op jit(solution)/shard_map/ppermute | solution.py:358
  27.2 3.6 %copy-start.5 = (s32[16]{0:T(128)S(1)}, s32[16]{0:T(128)}, u32[]{:S(2)}) copy-start(s32[16]{0:T(128)} %refs_0_.3) | copy-start | bytes 196
  28.2 14.5 %collective-permute-start.4 = (bf16[256,1024]{1,0:T(8,128)(2,1)}, bf16[256,1024]{1,0:T(8,128)(2,1)S(1)}, u32[]{:S(2)}, u32[]{:S(2)}) collective-permute-start(bf16[256,1024]{1,0:T(8,128)(2,1)} %shard_map.79.refs_14_.refs_3_), channel_id=1, source_target_pairs={{0,2},{1,3},{2,0},{3,1},{4,6},{5,7},{6,4},{7,5},{8,10},{9,11},{10,... | collective-permute-start | bytes 1572872 | tf_op jit(solution)/shard_map/ppermute | solution.py:358
  29.2 13.9 %collective-permute-start.5 = (bf16[256,1024]{1,0:T(8,128)(2,1)}, bf16[256,1024]{1,0:T(8,128)(2,1)}, u32[]{:S(2)}, u32[]{:S(2)}) collective-permute-start(bf16[256,1024]{1,0:T(8,128)(2,1)} %shard_map.79.refs_14_.refs_3_), channel_id=1, source_target_pairs={{0,4},{1,5},{2,6},{3,7},{4,0},{5,1},{6,2},{7,3},{8,12},{9,13},{10,... | collective-permute-start | bytes 1572872 | tf_op jit(solution)/shard_map/ppermute | solution.py:358
  30.7 23.0 %collective-permute-start.13 = (bf16[256,1024]{1,0:T(8,128)(2,1)}, bf16[256,1024]{1,0:T(8,128)(2,1)}, u32[]{:S(2)}, u32[]{:S(2)}) collective-permute-start(bf16[256,1024]{1,0:T(8,128)(2,1)} %shard_map.79.refs_14_.refs_3_), channel_id=1, source_target_pairs={{0,1},{1,0},{2,3},{3,2},{4,5},{5,4},{6,7},{7,6},{8,9},{9,8},{10,11... | collective-permute-start | bytes 1572872 | tf_op jit(solution)/shard_map/ppermute | solution.py:358
  44.9 8.3 %collective-permute-start.11 = (bf16[128,1024]{1,0:T(8,128)(2,1)}, bf16[128,1024]{1,0:T(8,128)(2,1)S(1)}, u32[]{:S(2)}, u32[]{:S(2)}) collective-permute-start(bf16[128,1024]{1,0:T(8,128)(2,1)} %get-tuple-element.20), channel_id=1, source_target_pairs={{0,4},{1,5},{2,6},{3,7},{4,0},{5,1},{6,2},{7,3},{8,12},{9,13},{10,... | collective-permute-start | bytes 786440 | tf_op jit(solution)/shard_map/ppermute | solution.py:358
  46.5 7.0 %collective-permute-start.12 = (bf16[128,1024]{1,0:T(8,128)(2,1)}, bf16[128,1024]{1,0:T(8,128)(2,1)S(1)}, u32[]{:S(2)}, u32[]{:S(2)}) collective-permute-start(bf16[128,1024]{1,0:T(8,128)(2,1)} %get-tuple-element.21), channel_id=1, source_target_pairs={{0,2},{1,3},{2,0},{3,1},{4,6},{5,7},{6,4},{7,5},{8,10},{9,11},{10,... | collective-permute-start | bytes 786440 | tf_op jit(solution)/shard_map/ppermute | solution.py:358
  47.2 7.9 %collective-permute-start.14 = (bf16[256,1024]{1,0:T(8,128)(2,1)S(1)}, bf16[256,1024]{1,0:T(8,128)(2,1)S(1)}, u32[]{:S(2)}, u32[]{:S(2)}) collective-permute-start(bf16[256,1024]{1,0:T(8,128)(2,1)S(1)} %collective-permute-done.4.refs_0_.refs_4_), channel_id=1, source_target_pairs={{0,1},{1,0},{2,3},{3,2},{4,5},{5,4},{6,7},{7,6},{8,9},{9,8},{10,11... | collective-permute-start | bytes 1572872 | tf_op jit(solution)/shard_map/ppermute | solution.py:358
  47.2 7.9 %collective-permute-start.15 = (bf16[256,1024]{1,0:T(8,128)(2,1)}, bf16[256,1024]{1,0:T(8,128)(2,1)S(1)}, u32[]{:S(2)}, u32[]{:S(2)}) collective-permute-start(bf16[256,1024]{1,0:T(8,128)(2,1)} %collective-permute-done.5.refs_1_.refs_5_), channel_id=1, source_target_pairs={{0,1},{1,0},{2,3},{3,2},{4,5},{5,4},{6,7},{7,6},{8,9},{9,8},{10,11... | collective-permute-start | bytes 1572872 | tf_op jit(solution)/shard_map/ppermute | solution.py:358
  47.7 27.2 %all-to-all-start.1 = ((bf16[8,256,384]{2,1,0:T(8,128)(2,1)}), bf16[8,256,384]{2,1,0:T(8,128)(2,1)}, u32[]{:S(2)}, u32[]{:S(2)}) async-start(bf16[8,256,384]{2,1,0:T(8,128)(2,1)} %shard_map.80.refs_2_.refs_13_), calls=%async_computation.1 | async-start | bytes 3145728 | tf_op jit(solution)/shard_map/all_to_all | solution.py:376
  53.2 1.5 %collective-permute-start.16 = (bf16[128,1024]{1,0:T(8,128)(2,1)S(1)}, bf16[128,1024]{1,0:T(8,128)(2,1)S(1)}, u32[]{:S(2)}, u32[]{:S(2)}) collective-permute-start(bf16[128,1024]{1,0:T(8,128)(2,1)S(1)} %collective-permute-done.11.refs_6_), channel_id=1, source_target_pairs={{0,1},{1,0},{2,3},{3,2},{4,5},{5,4},{6,7},{7,6},{8,9},{9,8},{10,11... | collective-permute-start | bytes 786440 | tf_op jit(solution)/shard_map/ppermute | solution.py:358
  53.5 1.6 %collective-permute-start.17 = (bf16[128,1024]{1,0:T(8,128)(2,1)S(1)}, bf16[128,1024]{1,0:T(8,128)(2,1)S(1)}, u32[]{:S(2)}, u32[]{:S(2)}) collective-permute-start(bf16[128,1024]{1,0:T(8,128)(2,1)S(1)} %collective-permute-done.12.refs_7_), channel_id=1, source_target_pairs={{0,1},{1,0},{2,3},{3,2},{4,5},{5,4},{6,7},{7,6},{8,9},{9,8},{10,11... | collective-permute-start | bytes 786440 | tf_op jit(solution)/shard_map/ppermute | solution.py:358
  62.4 0.6 copy-start.6
  63.0 3.8 %collective-permute-start.18 = (bf16[256,128]{1,0:T(8,128)(2,1)S(1)}, bf16[256,128]{1,0:T(8,128)(2,1)S(1)}, u32[]{:S(2)}, u32[]{:S(2)}) collective-permute-start(bf16[256,128]{1,0:T(8,128)(2,1)S(1)} %get-tuple-element.23), channel_id=1, source_target_pairs={{0,1},{1,0},{2,3},{3,2},{4,5},{5,4},{6,7},{7,6},{8,9},{9,8},{10,11... | collective-permute-start | bytes 196616 | tf_op jit(solution)/shard_map/ppermute | solution.py:358
  63.3 10.1 %collective-permute-start.19 = (bf16[256,128]{1,0:T(8,128)(2,1)S(1)}, bf16[256,128]{1,0:T(8,128)(2,1)S(1)}, u32[]{:S(2)}, u32[]{:S(2)}) collective-permute-start(bf16[256,128]{1,0:T(8,128)(2,1)S(1)} %get-tuple-element.24), channel_id=1, source_target_pairs={{0,2},{1,3},{2,0},{3,1},{4,6},{5,7},{6,4},{7,5},{8,10},{9,11},{10,... | collective-permute-start | bytes 196616 | tf_op jit(solution)/shard_map/ppermute | solution.py:358
  64.2 15.2 %collective-permute-start.20 = (bf16[256,128]{1,0:T(8,128)(2,1)}, bf16[256,128]{1,0:T(8,128)(2,1)S(1)}, u32[]{:S(2)}, u32[]{:S(2)}) collective-permute-start(bf16[256,128]{1,0:T(8,128)(2,1)} %get-tuple-element.25), channel_id=1, source_target_pairs={{0,3},{1,2},{2,1},{3,0},{4,7},{5,6},{6,5},{7,4},{8,11},{9,10},{10,... | collective-permute-start | bytes 196616 | tf_op jit(solution)/shard_map/ppermute | solution.py:358
  64.9 14.6 %collective-permute-start.21 = (bf16[256,128]{1,0:T(8,128)(2,1)}, bf16[256,128]{1,0:T(8,128)(2,1)S(1)}, u32[]{:S(2)}, u32[]{:S(2)}) collective-permute-start(bf16[256,128]{1,0:T(8,128)(2,1)} %get-tuple-element.26), channel_id=1, source_target_pairs={{0,4},{1,5},{2,6},{3,7},{4,0},{5,1},{6,2},{7,3},{8,12},{9,13},{10,... | collective-permute-start | bytes 196616 | tf_op jit(solution)/shard_map/ppermute | solution.py:358
  66.4 13.1 %collective-permute-start.22 = (bf16[256,128]{1,0:T(8,128)(2,1)}, bf16[256,128]{1,0:T(8,128)(2,1)S(1)}, u32[]{:S(2)}, u32[]{:S(2)}) collective-permute-start(bf16[256,128]{1,0:T(8,128)(2,1)} %get-tuple-element.27), channel_id=1, source_target_pairs={{0,5},{1,4},{2,7},{3,6},{4,1},{5,0},{6,3},{7,2},{8,13},{9,12},{10,... | collective-permute-start | bytes 196616 | tf_op jit(solution)/shard_map/ppermute | solution.py:358
  66.8 12.7 %collective-permute-start.23 = (bf16[256,128]{1,0:T(8,128)(2,1)S(1)}, bf16[256,128]{1,0:T(8,128)(2,1)S(1)}, u32[]{:S(2)}, u32[]{:S(2)}) collective-permute-start(bf16[256,128]{1,0:T(8,128)(2,1)S(1)} %get-tuple-element.28), channel_id=1, source_target_pairs={{0,6},{1,7},{2,4},{3,5},{4,2},{5,3},{6,0},{7,1},{8,14},{9,15},{10,... | collective-permute-start | bytes 196616 | tf_op jit(solution)/shard_map/ppermute | solution.py:358
  73.4 6.1 %collective-permute-start.24 = (bf16[256,128]{1,0:T(8,128)(2,1)S(1)}, bf16[256,128]{1,0:T(8,128)(2,1)S(1)}, u32[]{:S(2)}, u32[]{:S(2)}) collective-permute-start(bf16[256,128]{1,0:T(8,128)(2,1)S(1)} %get-tuple-element.29), channel_id=1, source_target_pairs={{0,7},{1,6},{2,5},{3,4},{4,3},{5,2},{6,1},{7,0},{8,15},{9,14},{10,... | collective-permute-start | bytes 196616 | tf_op jit(solution)/shard_map/ppermute | solution.py:358
  74.9 4.6 %copy-start.1 = (bf16[1,1024,1024]{2,1,0:T(8,128)(2,1)S(1)}, bf16[1,1024,1024]{2,1,0:T(8,128)(2,1)}, u32[]{:S(2)}) copy-start(bf16[1,1024,1024]{2,1,0:T(8,128)(2,1)} %param.10) | copy-start | bytes 6291460
  74.9 4.6 %copy-start.7 = (bf16[256,128]{1,0:T(8,128)(2,1)S(1)}, bf16[256,128]{1,0:T(8,128)(2,1)}, u32[]{:S(2)}) copy-start(bf16[256,128]{1,0:T(8,128)(2,1)} %copy-done.6) | copy-start | bytes 196612
  80.9 14.6 %collective-permute-start.25 = (bf16[256,1024]{1,0:T(8,128)(2,1)S(1)}, bf16[256,1024]{1,0:T(8,128)(2,1)S(1)}, u32[]{:S(2)}, u32[]{:S(2)}) collective-permute-start(bf16[256,1024]{1,0:T(8,128)(2,1)S(1)} %get-tuple-element.32), channel_id=1, source_target_pairs={{0,8},{8,0},{16,24},{24,16},{1,9},{9,1},{17,25},{25,17},{2,10},{10... | collective-permute-start | bytes 1572872 | tf_op jit(solution)/shard_map/ppermute | solution.py:408
  82.5 16.6 %collective-permute-start.26 = (bf16[256,1024]{1,0:T(8,128)(2,1)S(1)}, bf16[256,1024]{1,0:T(8,128)(2,1)S(1)}, u32[]{:S(2)}, u32[]{:S(2)}) collective-permute-start(bf16[256,1024]{1,0:T(8,128)(2,1)S(1)} %get-tuple-element.33), channel_id=1, source_target_pairs={{8,16},{16,8},{9,17},{17,9},{10,18},{18,10},{11,19},{19,11},{12,20... | collective-permute-start | bytes 1572872 | tf_op jit(solution)/shard_map/ppermute | solution.py:408

commit v14 on v13

--- a/solution.py
+++ b/solution.py
@@ -198,7 +198,7 @@
         [SMEM, SMEM] + [VMEM] * (len(operands) - 2) + [HBM] * len(earlier),
         shape,
         scratch,
-        MICROSECOND * (12 if back else 8),
+        MICROSECOND * (15 if back else 9),
         2 * tokens * (width + 2 * wide),
     )
 
@@ -221,7 +221,7 @@
         out_shape=[jax.ShapeDtypeStruct((rows, *a.shape[1:]), a.dtype) for a in arrays],
         scratch_shapes=[pltpu.SemaphoreType.DMA((len(arrays),))],
         compiler_params=pltpu.CompilerParams(vmem_limit_bytes=24 * MIB),
-        cost_estimate=pl.CostEstimate(flops=MICROSECOND, bytes_accessed=0, transcendentals=0),
+        cost_estimate=pl.CostEstimate(flops=0, bytes_accessed=0, transcendentals=0),
     )(*arrays, *earlier)
 
 
@@ -368,7 +368,7 @@
 
 
 def swap(blocks):
-    moved = {k: partner(blocks[k], k) for k in (2, 4, 6, 3, 5, 7, 1)}
+    moved = {k: partner(blocks[k], k) for k in (7, 5, 3, 6, 4, 2, 1)}
     return [blocks[0]] + [moved[k] for k in range(1, HEADS)]
 
 
@@ -453,7 +453,8 @@
     returned = collect_each(outputs)
     grad_self, near = finish_back(returned_grads, stored, upstream, w_rows, current)
     first, second = finish(info, returned, near, w_fin, grad_self)
-    first, second = swapped(first, 0), swapped(second, 1)
+    second = swapped(second, 1)
+    first = swapped(first, 0)
     next_input = jnp.where(odd == 1, first, second)
     grad_input = jnp.where(odd == 1, second, first)
     return (next_input[None], grad_input[None])

time: 101 us -> 100 us (0.990)
    unnamed x16 -> x20, local copies, waits for them, and re-layouts: 3.28 us -> 3.29 us
where the time goes in v14:
time: 100 us; the launch traced here: 99.3 us
  starting transfers between devices  33.6 us (34%)
  Pallas kernels  29.7 us (30%)
  waiting for transfers between devices  29.6 us (30%)
  local copies, waits for them, and re-layouts  4.48 us (4%)
  other arithmetic  1.11 us (1%)
    pallas_call x6, Pallas kernels, call(): pl.pallas_call(kernel, in_specs=in_specs, out_specs=[VMEM] * len(out_shap...  27.9 us
    ppermute x25, starting transfers between devices, partner(): return lax.ppermute(block, 'seq', route)  19.5 us
    ppermute x25, waiting for transfers between devices, partner(): return lax.ppermute(block, 'seq', route)  14.9 us
    ppermute x2, waiting for transfers between devices, swapped(): return lax.ppermute(block, 'pipe', route)  14.7 us
    all_to_all x2, starting transfers between devices, all_swap(): lax.all_to_all(blocks, 'seq', split_axis=0, concat_axis=0, tiled=True)  10.5 us
    ppermute x2, starting transfers between devices, swapped(): return lax.ppermute(block, 'pipe', route)  3.55 us
    unnamed x20, local copies, waits for them, and re-layouts  3.29 us
  transfers between devices with their start and end apart: 29, of which 12 were waited for; matrix products, arithmetic and copies ran while one was open for 1% of the time, Pallas kernels for 29%

profile of v14, /device:TPU:18, one launch (start us, length us, event | category | flops | bytes accessed | tf_op | source)
XLA Modules:
  0.0 99.3 jit_solution(63404727884059155)
XLA Ops:
  0.6 0.6 collective-permute-start
  1.2 1.5 %collective-permute-start.1 = (bf16[256,1024]{1,0:T(8,128)(2,1)}, bf16[256,1024]{1,0:T(8,128)(2,1)S(1)}, u32[]{:S(2)}, u32[]{:S(2)}) collective-permute-start(bf16[256,1024]{1,0:T(8,128)(2,1)} %bitcast.24), channel_id=1, source_target_pairs={{0,4},{1,5},{2,6},{3,7},{4,0},{5,1},{6,2},{7,3},{8,12},{9,13},{10,... | collective-permute-start | bytes 1572872 | tf_op jit(solution)/shard_map/ppermute | solution.py:358
  2.8 1.6 %copy-done = bf16[1,1024,1024]{2,1,0:T(8,128)(2,1)S(1)} copy-done((bf16[1,1024,1024]{2,1,0:T(8,128)(2,1)S(1)}, bf16[1,1024,1024]{2,1,0:T(8,128)(2,1)}, u32[]{:S(2)}) %copy-start) | copy-done | bytes 2097176
  4.3 1.0 %copy-done.6 = bf16[1,256,1024]{2,1,0:T(8,128)(2,1)S(1)} copy-done((bf16[1,256,1024]{2,1,0:T(8,128)(2,1)S(1)}, bf16[1,256,1024]{2,1,0:T(8,128)(2,1)}, u32[]{:S(2)}) %copy-start.6) | copy-done | bytes 524312
  5.4 2.8 %shard_map.77.refs_2_ = bf16[8,256,128]{2,1,0:T(8,128)(2,1)} custom-call(bf16[256,1024]{1,0:T(8,128)(2,1)S(1)} %bitcast.29, bf16[8,128,1024]{2,1,0:T(8,128)(2,1)S(1)} %bitcast.19), custom_call_target="tpu_custom_call" | custom-call | flops 3449999872 | bytes 2097152 | tf_op jit(solution)/shard_map/pallas_call | solution.py:42
  8.2 5.0 %all-to-all-start = ((bf16[8,256,128]{2,1,0:T(8,128)(2,1)}), bf16[8,256,128]{2,1,0:T(8,128)(2,1)S(1)}, u32[]{:S(2)}, u32[]{:S(2)}) async-start(bf16[8,256,128]{2,1,0:T(8,128)(2,1)} %shard_map.77.refs_2_), calls=%async_computation | async-start | bytes 1048576 | tf_op jit(solution)/shard_map/all_to_all | solution.py:376
  13.3 1.3 %collective-permute-done.refs_0_.refs_4_ = bf16[256,1024]{1,0:T(8,128)(2,1)S(1)} collective-permute-done((bf16[256,1024]{1,0:T(8,128)(2,1)}, bf16[256,1024]{1,0:T(8,128)(2,1)S(1)}, u32[]{:S(2)}, u32[]{:S(2)}) %collective-permute-start) | collective-permute-done | bytes 524320 | tf_op jit(solution)/shard_map/ppermute | solution.py:358
  14.6 0.3 collective-permute-done.1.refs_1_.refs_5_
  14.8 0.9 shard_map.78
  15.7 1.6 %collective-permute-start.3 = (bf16[128,1024]{1,0:T(8,128)(2,1)}, bf16[128,1024]{1,0:T(8,128)(2,1)}, u32[]{:S(2)}, u32[]{:S(2)}) collective-permute-start(bf16[128,1024]{1,0:T(8,128)(2,1)} %get-tuple-element.19), channel_id=1, source_target_pairs={{0,2},{1,3},{2,0},{3,1},{4,6},{5,7},{6,4},{7,5},{8,10},{9,11},{10,... | collective-permute-start | bytes 786440 | tf_op jit(solution)/shard_map/ppermute | solution.py:358
  17.3 2.4 %collective-permute-start.2 = (bf16[128,1024]{1,0:T(8,128)(2,1)}, bf16[128,1024]{1,0:T(8,128)(2,1)}, u32[]{:S(2)}, u32[]{:S(2)}) collective-permute-start(bf16[128,1024]{1,0:T(8,128)(2,1)} %get-tuple-element.18), channel_id=1, source_target_pairs={{0,4},{1,5},{2,6},{3,7},{4,0},{5,1},{6,2},{7,3},{8,12},{9,13},{10,... | collective-permute-start | bytes 786440 | tf_op jit(solution)/shard_map/ppermute | solution.py:358
  19.8 1.2 %constant_dynamic-slice_fusion = bf16[3,1,128,1024]{3,2,1,0:T(8,128)(2,1)S(1)} fusion(bf16[3,8,128,1024]{3,2,1,0:T(8,128)(2,1)} %bitcast.30, s32[]{:T(128)S(6)} %select_n.25), kind=kLoop, calls=%fused_computation.3 | loop fusion | bytes 1572868 | tf_op jit(solution)/shard_map/jit(dynamic_index_in_dim)/dynamic_slice | solution.py:438
  21.0 0.6 collective-permute-start.7
  21.6 4.6 %collective-permute-done.3.refs_1_.refs_7_ = bf16[128,1024]{1,0:T(8,128)(2,1)} collective-permute-done((bf16[128,1024]{1,0:T(8,128)(2,1)}, bf16[128,1024]{1,0:T(8,128)(2,1)}, u32[]{:S(2)}, u32[]{:S(2)}) %collective-permute-start.3) | collective-permute-done | bytes 262176 | tf_op jit(solution)/shard_map/ppermute | solution.py:358
  26.2 1.1 %collective-permute-done.2.refs_0_.refs_6_ = bf16[128,1024]{1,0:T(8,128)(2,1)} collective-permute-done((bf16[128,1024]{1,0:T(8,128)(2,1)}, bf16[128,1024]{1,0:T(8,128)(2,1)}, u32[]{:S(2)}, u32[]{:S(2)}) %collective-permute-start.2) | collective-permute-done | bytes 262176 | tf_op jit(solution)/shard_map/ppermute | solution.py:358
  27.4 1.0 shard_map.79.refs_14_.refs_3_
  28.4 1.0 %collective-permute-start.4 = (bf16[256,1024]{1,0:T(8,128)(2,1)}, bf16[256,1024]{1,0:T(8,128)(2,1)S(1)}, u32[]{:S(2)}, u32[]{:S(2)}) collective-permute-start(bf16[256,1024]{1,0:T(8,128)(2,1)} %shard_map.79.refs_14_.refs_3_), channel_id=1, source_target_pairs={{0,2},{1,3},{2,0},{3,1},{4,6},{5,7},{6,4},{7,5},{8,10},{9,11},{10,... | collective-permute-start | bytes 1572872 | tf_op jit(solution)/shard_map/ppermute | solution.py:358
  29.4 1.5 %collective-permute-start.5 = (bf16[256,1024]{1,0:T(8,128)(2,1)}, bf16[256,1024]{1,0:T(8,128)(2,1)S(1)}, u32[]{:S(2)}, u32[]{:S(2)}) collective-permute-start(bf16[256,1024]{1,0:T(8,128)(2,1)} %shard_map.79.refs_14_.refs_3_), channel_id=1, source_target_pairs={{0,4},{1,5},{2,6},{3,7},{4,0},{5,1},{6,2},{7,3},{8,12},{9,13},{10,... | collective-permute-start | bytes 1572872 | tf_op jit(solution)/shard_map/ppermute | solution.py:358
  30.9 11.0 %shard_map.80.refs_2_.refs_13_ = bf16[8,256,384]{2,1,0:T(8,128)(2,1)} custom-call(s32[16]{0:T(128)S(1)} %copy-done.7, s32[4]{0:T(128)S(1)} %pad_add_fusion.refs_1_.info_ref, bf16[384,1024]{1,0:T(8,128)(2,1)S(1)} %bitcast.16, bf16[256,1024]{1,0:T(8,128)(2,1)S(1)} %bitcast.26, bf16[256,1024]{1,0:T(8,128)(2,1)S(1)} %collective-permute-done.refs_0_.refs_4_, ...), custom_call_target="tpu_custom_call" | custom-call | flops 17250000896 | bytes 7340032 | tf_op jit(solution)/shard_map/pallas_call | solution.py:42
  41.9 1.0 collective-permute-done.4.refs_0_.refs_4_
  42.9 0.3 collective-permute-done.5.refs_1_.refs_5_
  43.2 0.9 shard_map.81
  44.0 1.6 %collective-permute-start.11 = (bf16[128,1024]{1,0:T(8,128)(2,1)}, bf16[128,1024]{1,0:T(8,128)(2,1)}, u32[]{:S(2)}, u32[]{:S(2)}) collective-permute-start(bf16[128,1024]{1,0:T(8,128)(2,1)} %get-tuple-element.20), channel_id=1, source_target_pairs={{0,4},{1,5},{2,6},{3,7},{4,0},{5,1},{6,2},{7,3},{8,12},{9,13},{10,... | collective-permute-start | bytes 786440 | tf_op jit(solution)/shard_map/ppermute | solution.py:358
  45.6 0.7 collective-permute-start.12
  46.3 0.5 collective-permute-start.15
  46.9 5.5 %all-to-all-start.1 = ((bf16[8,256,384]{2,1,0:T(8,128)(2,1)}), bf16[8,256,384]{2,1,0:T(8,128)(2,1)}, u32[]{:S(2)}, u32[]{:S(2)}) async-start(bf16[8,256,384]{2,1,0:T(8,128)(2,1)} %shard_map.80.refs_2_.refs_13_), calls=%async_computation.1 | async-start | bytes 3145728 | tf_op jit(solution)/shard_map/all_to_all | solution.py:376
  52.3 0.2 collective-permute-start.16
  52.5 0.2 collective-permute-done.12.refs_7_
  52.7 0.2 collective-permute-start.17
  52.9 1.2 %collective-permute-done.16.refs_11_ = bf16[128,1024]{1,0:T(8,128)(2,1)S(1)} collective-permute-done((bf16[128,1024]{1,0:T(8,128)(2,1)}, bf16[128,1024]{1,0:T(8,128)(2,1)S(1)}, u32[]{:S(2)}, u32[]{:S(2)}) %collective-permute-start.16) | collective-permute-done | bytes 262176 | tf_op jit(solution)/shard_map/ppermute | solution.py:358
  54.1 0.4 collective-permute-done.17.refs_12_
  54.5 7.3 %shard_map.82 = (bf16[256,128]{1,0:T(8,128)(2,1)S(1)}, bf16[256,128]{1,0:T(8,128)(2,1)S(1)}, bf16[256,128]{1,0:T(8,128)(2,1)S(1)}, bf16[256,128]{1,0:T(8,128)(2,...) custom-call(s32[16]{0:T(128)S(1)} %copy-done.7, ...), custom_call_target="tpu_custom_call" | custom-call | flops 10350000128 | bytes 5242880 | tf_op jit(solution)/shard_map/pallas_call | solution.py:42
  61.8 0.6 copy-done.8
  62.4 0.2 collective-permute-start.18
  62.6 1.0 collective-permute-start.19
  63.6 0.7 collective-permute-start.20
  64.3 1.5 %collective-permute-start.21 = (bf16[256,128]{1,0:T(8,128)(2,1)}, bf16[256,128]{1,0:T(8,128)(2,1)S(1)}, u32[]{:S(2)}, u32[]{:S(2)}) collective-permute-start(bf16[256,128]{1,0:T(8,128)(2,1)} %get-tuple-element.26), channel_id=1, source_target_pairs={{0,4},{1,5},{2,6},{3,7},{4,0},{5,1},{6,2},{7,3},{8,12},{9,13},{10,... | collective-permute-start | bytes 196616 | tf_op jit(solution)/shard_map/ppermute | solution.py:358
  65.8 0.3 collective-permute-start.22
  66.1 1.8 %collective-permute-start.23 = (bf16[256,128]{1,0:T(8,128)(2,1)S(1)}, bf16[256,128]{1,0:T(8,128)(2,1)S(1)}, u32[]{:S(2)}, u32[]{:S(2)}) collective-permute-start(bf16[256,128]{1,0:T(8,128)(2,1)S(1)} %get-tuple-element.28), channel_id=1, source_target_pairs={{0,6},{1,7},{2,4},{3,5},{4,2},{5,3},{6,0},{7,1},{8,14},{9,15},{10,... | collective-permute-start | bytes 196616 | tf_op jit(solution)/shard_map/ppermute | solution.py:358
  67.9 4.6 %collective-permute-done.19.refs_2_ = bf16[256,128]{1,0:T(8,128)(2,1)S(1)} collective-permute-done((bf16[256,128]{1,0:T(8,128)(2,1)S(1)}, bf16[256,128]{1,0:T(8,128)(2,1)S(1)}, u32[]{:S(2)}, u32[]{:S(2)}) %collective-permute-start.19) | collective-permute-done | bytes 65568 | tf_op jit(solution)/shard_map/ppermute | solution.py:358
  72.5 1.5 %collective-permute-start.24 = (bf16[256,128]{1,0:T(8,128)(2,1)S(1)}, bf16[256,128]{1,0:T(8,128)(2,1)S(1)}, u32[]{:S(2)}, u32[]{:S(2)}) collective-permute-start(bf16[256,128]{1,0:T(8,128)(2,1)S(1)} %get-tuple-element.29), channel_id=1, source_target_pairs={{0,7},{1,6},{2,5},{3,4},{4,3},{5,2},{6,1},{7,0},{8,15},{9,14},{10,... | collective-permute-start | bytes 196616 | tf_op jit(solution)/shard_map/ppermute | solution.py:358
  74.1 4.5 %shard_map.83 = (bf16[256,1024]{1,0:T(8,128)(2,1)S(1)}, bf16[256,1024]{1,0:T(8,128)(2,1)S(1)}) custom-call(bf16[8,256,384]{2,1,0:T(8,128)(2,1)} %all-to-all-done.1.grad_ref, bf16[256,1024]{1,0:T(8,128)(2,1)S(1)} %bitcast.27, bf16[256,1024]{1,0:T(8,128)(2,1)} %bitcast.28, bf16[3072,1024]{1,0:T(8,128)(2,1)} %bitcast.31, bf16[256,1024]{1,0:T(8,128)(2,1)} %bitcast.21), custom_call_target="tpu_custom_call" | custom-call | flops 5750000128 | bytes 6291456 | tf_op jit(solution)/shard_map/pallas_call | solution.py:42
  78.7 1.3 %shard_map.84 = (bf16[256,1024]{1,0:T(8,128)(2,1)S(1)}, bf16[256,1024]{1,0:T(8,128)(2,1)S(1)}) custom-call(s32[4]{0:T(128)S(1)} %pad_add_fusion.refs_1_.info_ref, bf16[256,128]{1,0:T(8,128)(2,1)S(1)} %copy-done.9, bf16[256,128]{1,0:T(8,128)(2,1)S(1)} %collective-permute-done.18.refs_1_, bf16[256,128]{1,0:T(8,128)(2,1)S(1)} %collective-permute-done.19.refs_2_, ...), custom_call_target="tpu_custom_call" | custom-call | flops 1150000000 | bytes 2097152 | tf_op jit(solution)/shard_map/pallas_call | solution.py:42
  80.0 1.6 %collective-permute-start.25 = (bf16[256,1024]{1,0:T(8,128)(2,1)S(1)}, bf16[256,1024]{1,0:T(8,128)(2,1)S(1)}, u32[]{:S(2)}, u32[]{:S(2)}) collective-permute-start(bf16[256,1024]{1,0:T(8,128)(2,1)S(1)} %get-tuple-element.32), channel_id=1, source_target_pairs={{0,8},{8,0},{16,24},{24,16},{1,9},{9,1},{17,25},{25,17},{2,10},{10... | collective-permute-start | bytes 1572872 | tf_op jit(solution)/shard_map/ppermute | solution.py:408
  81.6 1.9 %collective-permute-start.26 = (bf16[256,1024]{1,0:T(8,128)(2,1)S(1)}, bf16[256,1024]{1,0:T(8,128)(2,1)S(1)}, u32[]{:S(2)}, u32[]{:S(2)}) collective-permute-start(bf16[256,1024]{1,0:T(8,128)(2,1)S(1)} %get-tuple-element.33), channel_id=1, source_target_pairs={{8,16},{16,8},{9,17},{17,9},{10,18},{18,10},{11,19},{19,11},{12,20... | collective-permute-start | bytes 1572872 | tf_op jit(solution)/shard_map/ppermute | solution.py:408
  83.6 11.0 %collective-permute-done.25 = bf16[256,1024]{1,0:T(8,128)(2,1)S(1)} collective-permute-done((bf16[256,1024]{1,0:T(8,128)(2,1)S(1)}, bf16[256,1024]{1,0:T(8,128)(2,1)S(1)}, u32[]{:S(2)}, u32[]{:S(2)}) %collective-permute-start.25) | collective-permute-done | bytes 524320 | tf_op jit(solution)/shard_map/ppermute | solution.py:408
  94.6 3.7 %collective-permute-done.26 = bf16[256,1024]{1,0:T(8,128)(2,1)S(1)} collective-permute-done((bf16[256,1024]{1,0:T(8,128)(2,1)S(1)}, bf16[256,1024]{1,0:T(8,128)(2,1)S(1)}, u32[]{:S(2)}, u32[]{:S(2)}) %collective-permute-start.26) | collective-permute-done | bytes 524320 | tf_op jit(solution)/shard_map/ppermute | solution.py:408
  98.2 1.0 %select_bitcast_fusion = (bf16[1,256,1024]{2,1,0:T(8,128)(2,1)}, bf16[1,256,1024]{2,1,0:T(8,128)(2,1)}) fusion(bf16[256,1024]{1,0:T(8,128)(2,1)S(1)} %collective-permute-done.26, bf16[256,1024]{1,0:T(8,128)(2,1)S(1)} %collective-permute-done.25, pred[]{:T(512)S(6)} %eq.6), kind=kLoop, calls=%fused_computation | loop fusion | flops 524288 | bytes 2097153 | tf_op jit(solution)/shard_map/broadcast_in_dim | solution.py:460
  (41 shorter events, 0.3 us)
Async XLA Ops:
  0.6 13.9 %collective-permute-start = (bf16[256,1024]{1,0:T(8,128)(2,1)}, bf16[256,1024]{1,0:T(8,128)(2,1)S(1)}, u32[]{:S(2)}, u32[]{:S(2)}) collective-permute-start(bf16[256,1024]{1,0:T(8,128)(2,1)} %bitcast.23), channel_id=1, source_target_pairs={{0,2},{1,3},{2,0},{3,1},{4,6},{5,7},{6,4},{7,5},{8,10},{9,11},{10,... | collective-permute-start | bytes 1572872 | tf_op jit(solution)/shard_map/ppermute | solution.py:358
  1.2 13.6 %collective-permute-start.1 = (bf16[256,1024]{1,0:T(8,128)(2,1)}, bf16[256,1024]{1,0:T(8,128)(2,1)S(1)}, u32[]{:S(2)}, u32[]{:S(2)}) collective-permute-start(bf16[256,1024]{1,0:T(8,128)(2,1)} %bitcast.24), channel_id=1, source_target_pairs={{0,4},{1,5},{2,6},{3,7},{4,0},{5,1},{6,2},{7,3},{8,12},{9,13},{10,... | collective-permute-start | bytes 1572872 | tf_op jit(solution)/shard_map/ppermute | solution.py:358
  2.7 1.6 %copy-start = (bf16[1,1024,1024]{2,1,0:T(8,128)(2,1)S(1)}, bf16[1,1024,1024]{2,1,0:T(8,128)(2,1)}, u32[]{:S(2)}) copy-start(bf16[1,1024,1024]{2,1,0:T(8,128)(2,1)} %param.10) | copy-start | bytes 6291460
  4.3 1.0 %copy-start.6 = (bf16[1,256,1024]{2,1,0:T(8,128)(2,1)S(1)}, bf16[1,256,1024]{2,1,0:T(8,128)(2,1)}, u32[]{:S(2)}) copy-start(bf16[1,256,1024]{2,1,0:T(8,128)(2,1)} %param.8) | copy-start | bytes 1572868
  8.2 11.5 %copy-start.3 = (bf16[1,256,1024]{2,1,0:T(8,128)(2,1)S(1)}, bf16[1,256,1024]{2,1,0:T(8,128)(2,1)}, u32[]{:S(2)}) copy-start(bf16[1,256,1024]{2,1,0:T(8,128)(2,1)} %param.7) | copy-start | bytes 1572868
  8.2 19.1 %copy-start.2 = (bf16[1,256,1024]{2,1,0:T(8,128)(2,1)S(1)}, bf16[1,256,1024]{2,1,0:T(8,128)(2,1)}, u32[]{:S(2)}) copy-start(bf16[1,256,1024]{2,1,0:T(8,128)(2,1)} %param.6) | copy-start | bytes 1572868
  8.2 19.1 %all-to-all-start = ((bf16[8,256,128]{2,1,0:T(8,128)(2,1)}), bf16[8,256,128]{2,1,0:T(8,128)(2,1)S(1)}, u32[]{:S(2)}, u32[]{:S(2)}) async-start(bf16[8,256,128]{2,1,0:T(8,128)(2,1)} %shard_map.77.refs_2_), calls=%async_computation | async-start | bytes 1048576 | tf_op jit(solution)/shard_map/all_to_all | solution.py:376
  15.7 10.5 %collective-permute-start.3 = (bf16[128,1024]{1,0:T(8,128)(2,1)}, bf16[128,1024]{1,0:T(8,128)(2,1)}, u32[]{:S(2)}, u32[]{:S(2)}) collective-permute-start(bf16[128,1024]{1,0:T(8,128)(2,1)} %get-tuple-element.19), channel_id=1, source_target_pairs={{0,2},{1,3},{2,0},{3,1},{4,6},{5,7},{6,4},{7,5},{8,10},{9,11},{10,... | collective-permute-start | bytes 786440 | tf_op jit(solution)/shard_map/ppermute | solution.py:358
  17.3 10.0 %collective-permute-start.2 = (bf16[128,1024]{1,0:T(8,128)(2,1)}, bf16[128,1024]{1,0:T(8,128)(2,1)}, u32[]{:S(2)}, u32[]{:S(2)}) collective-permute-start(bf16[128,1024]{1,0:T(8,128)(2,1)} %get-tuple-element.18), channel_id=1, source_target_pairs={{0,4},{1,5},{2,6},{3,7},{4,0},{5,1},{6,2},{7,3},{8,12},{9,13},{10,... | collective-permute-start | bytes 786440 | tf_op jit(solution)/shard_map/ppermute | solution.py:358
  19.7 8.7 %collective-permute-start.6 = (bf16[256,1024]{1,0:T(8,128)(2,1)S(1)}, bf16[256,1024]{1,0:T(8,128)(2,1)}, u32[]{:S(2)}, u32[]{:S(2)}) collective-permute-start(bf16[256,1024]{1,0:T(8,128)(2,1)S(1)} %bitcast.25), channel_id=1, source_target_pairs={{0,1},{1,0},{2,3},{3,2},{4,5},{5,4},{6,7},{7,6},{8,9},{9,8},{10,11... | collective-permute-start | bytes 1572872 | tf_op jit(solution)/shard_map/ppermute | solution.py:358
  21.0 9.9 %collective-permute-start.7 = (bf16[256,1024]{1,0:T(8,128)(2,1)S(1)}, bf16[256,1024]{1,0:T(8,128)(2,1)}, u32[]{:S(2)}, u32[]{:S(2)}) collective-permute-start(bf16[256,1024]{1,0:T(8,128)(2,1)S(1)} %collective-permute-done.refs_0_.refs_4_), channel_id=1, source_target_pairs={{0,1},{1,0},{2,3},{3,2},{4,5},{5,4},{6,7},{7,6},{8,9},{9,8},{10,11... | collective-permute-start | bytes 1572872 | tf_op jit(solution)/shard_map/ppermute | solution.py:358
  21.5 9.4 %collective-permute-start.8 = (bf16[256,1024]{1,0:T(8,128)(2,1)S(1)}, bf16[256,1024]{1,0:T(8,128)(2,1)}, u32[]{:S(2)}, u32[]{:S(2)}) collective-permute-start(bf16[256,1024]{1,0:T(8,128)(2,1)S(1)} %collective-permute-done.1.refs_1_.refs_5_), channel_id=1, source_target_pairs={{0,1},{1,0},{2,3},{3,2},{4,5},{5,4},{6,7},{7,6},{8,9},{9,8},{10,11... | collective-permute-start | bytes 1572872 | tf_op jit(solution)/shard_map/ppermute | solution.py:358
  26.2 3.2 %collective-permute-start.10 = (bf16[128,1024]{1,0:T(8,128)(2,1)}, bf16[128,1024]{1,0:T(8,128)(2,1)}, u32[]{:S(2)}, u32[]{:S(2)}) collective-permute-start(bf16[128,1024]{1,0:T(8,128)(2,1)} %collective-permute-done.3.refs_1_.refs_7_), channel_id=1, source_target_pairs={{0,1},{1,0},{2,3},{3,2},{4,5},{5,4},{6,7},{7,6},{8,9},{9,8},{10,11... | collective-permute-start | bytes 786440 | tf_op jit(solution)/shard_map/ppermute | solution.py:358
  27.3 3.6 %collective-permute-start.9 = (bf16[128,1024]{1,0:T(8,128)(2,1)}, bf16[128,1024]{1,0:T(8,128)(2,1)}, u32[]{:S(2)}, u32[]{:S(2)}) collective-permute-start(bf16[128,1024]{1,0:T(8,128)(2,1)} %collective-permute-done.2.refs_0_.refs_6_), channel_id=1, source_target_pairs={{0,1},{1,0},{2,3},{3,2},{4,5},{5,4},{6,7},{7,6},{8,9},{9,8},{10,11... | collective-permute-start | bytes 786440 | tf_op jit(solution)/shard_map/ppermute | solution.py:358
  27.4 3.5 %copy-start.4 = (bf16[1,256,1024]{2,1,0:T(8,128)(2,1)S(1)}, bf16[1,256,1024]{2,1,0:T(8,128)(2,1)}, u32[]{:S(2)}) copy-start(bf16[1,256,1024]{2,1,0:T(8,128)(2,1)} %param.7) | copy-start | bytes 1572868
  27.4 3.5 %copy-start.7 = (s32[16]{0:T(128)S(1)}, s32[16]{0:T(128)}, u32[]{:S(2)}) copy-start(s32[16]{0:T(128)} %refs_0_.3) | copy-start | bytes 196
  28.4 14.5 %collective-permute-start.4 = (bf16[256,1024]{1,0:T(8,128)(2,1)}, bf16[256,1024]{1,0:T(8,128)(2,1)S(1)}, u32[]{:S(2)}, u32[]{:S(2)}) collective-permute-start(bf16[256,1024]{1,0:T(8,128)(2,1)} %shard_map.79.refs_14_.refs_3_), channel_id=1, source_target_pairs={{0,2},{1,3},{2,0},{3,1},{4,6},{5,7},{6,4},{7,5},{8,10},{9,11},{10,... | collective-permute-start | bytes 1572872 | tf_op jit(solution)/shard_map/ppermute | solution.py:358
  29.4 13.8 %collective-permute-start.5 = (bf16[256,1024]{1,0:T(8,128)(2,1)}, bf16[256,1024]{1,0:T(8,128)(2,1)S(1)}, u32[]{:S(2)}, u32[]{:S(2)}) collective-permute-start(bf16[256,1024]{1,0:T(8,128)(2,1)} %shard_map.79.refs_14_.refs_3_), channel_id=1, source_target_pairs={{0,4},{1,5},{2,6},{3,7},{4,0},{5,1},{6,2},{7,3},{8,12},{9,13},{10,... | collective-permute-start | bytes 1572872 | tf_op jit(solution)/shard_map/ppermute | solution.py:358
  30.9 22.0 %collective-permute-start.13 = (bf16[256,1024]{1,0:T(8,128)(2,1)}, bf16[256,1024]{1,0:T(8,128)(2,1)}, u32[]{:S(2)}, u32[]{:S(2)}) collective-permute-start(bf16[256,1024]{1,0:T(8,128)(2,1)} %shard_map.79.refs_14_.refs_3_), channel_id=1, source_target_pairs={{0,1},{1,0},{2,3},{3,2},{4,5},{5,4},{6,7},{7,6},{8,9},{9,8},{10,11... | collective-permute-start | bytes 1572872 | tf_op jit(solution)/shard_map/ppermute | solution.py:358
  44.0 8.3 %collective-permute-start.11 = (bf16[128,1024]{1,0:T(8,128)(2,1)}, bf16[128,1024]{1,0:T(8,128)(2,1)}, u32[]{:S(2)}, u32[]{:S(2)}) collective-permute-start(bf16[128,1024]{1,0:T(8,128)(2,1)} %get-tuple-element.20), channel_id=1, source_target_pairs={{0,4},{1,5},{2,6},{3,7},{4,0},{5,1},{6,2},{7,3},{8,12},{9,13},{10,... | collective-permute-start | bytes 786440 | tf_op jit(solution)/shard_map/ppermute | solution.py:358
  45.6 7.1 %collective-permute-start.12 = (bf16[128,1024]{1,0:T(8,128)(2,1)}, bf16[128,1024]{1,0:T(8,128)(2,1)}, u32[]{:S(2)}, u32[]{:S(2)}) collective-permute-start(bf16[128,1024]{1,0:T(8,128)(2,1)} %get-tuple-element.21), channel_id=1, source_target_pairs={{0,2},{1,3},{2,0},{3,1},{4,6},{5,7},{6,4},{7,5},{8,10},{9,11},{10,... | collective-permute-start | bytes 786440 | tf_op jit(solution)/shard_map/ppermute | solution.py:358
  46.3 8.2 %collective-permute-start.14 = (bf16[256,1024]{1,0:T(8,128)(2,1)S(1)}, bf16[256,1024]{1,0:T(8,128)(2,1)S(1)}, u32[]{:S(2)}, u32[]{:S(2)}) collective-permute-start(bf16[256,1024]{1,0:T(8,128)(2,1)S(1)} %collective-permute-done.4.refs_0_.refs_4_), channel_id=1, source_target_pairs={{0,1},{1,0},{2,3},{3,2},{4,5},{5,4},{6,7},{7,6},{8,9},{9,8},{10,11... | collective-permute-start | bytes 1572872 | tf_op jit(solution)/shard_map/ppermute | solution.py:358
  46.3 8.2 %collective-permute-start.15 = (bf16[256,1024]{1,0:T(8,128)(2,1)S(1)}, bf16[256,1024]{1,0:T(8,128)(2,1)S(1)}, u32[]{:S(2)}, u32[]{:S(2)}) collective-permute-start(bf16[256,1024]{1,0:T(8,128)(2,1)S(1)} %collective-permute-done.5.refs_1_.refs_5_), channel_id=1, source_target_pairs={{0,1},{1,0},{2,3},{3,2},{4,5},{5,4},{6,7},{7,6},{8,9},{9,8},{10,11... | collective-permute-start | bytes 1572872 | tf_op jit(solution)/shard_map/ppermute | solution.py:358
  46.9 27.2 %all-to-all-start.1 = ((bf16[8,256,384]{2,1,0:T(8,128)(2,1)}), bf16[8,256,384]{2,1,0:T(8,128)(2,1)}, u32[]{:S(2)}, u32[]{:S(2)}) async-start(bf16[8,256,384]{2,1,0:T(8,128)(2,1)} %shard_map.80.refs_2_.refs_13_), calls=%async_computation.1 | async-start | bytes 3145728 | tf_op jit(solution)/shard_map/all_to_all | solution.py:376
  52.3 21.8 %copy-start.5 = (bf16[1,256,1024]{2,1,0:T(8,128)(2,1)S(1)}, bf16[1,256,1024]{2,1,0:T(8,128)(2,1)}, u32[]{:S(2)}) copy-start(bf16[1,256,1024]{2,1,0:T(8,128)(2,1)} %param.7) | copy-start | bytes 1572868
  52.3 1.8 %collective-permute-start.16 = (bf16[128,1024]{1,0:T(8,128)(2,1)}, bf16[128,1024]{1,0:T(8,128)(2,1)S(1)}, u32[]{:S(2)}, u32[]{:S(2)}) collective-permute-start(bf16[128,1024]{1,0:T(8,128)(2,1)} %collective-permute-done.11.refs_6_), channel_id=1, source_target_pairs={{0,1},{1,0},{2,3},{3,2},{4,5},{5,4},{6,7},{7,6},{8,9},{9,8},{10,11... | collective-permute-start | bytes 786440 | tf_op jit(solution)/shard_map/ppermute | solution.py:358
  52.7 1.8 %collective-permute-start.17 = (bf16[128,1024]{1,0:T(8,128)(2,1)}, bf16[128,1024]{1,0:T(8,128)(2,1)S(1)}, u32[]{:S(2)}, u32[]{:S(2)}) collective-permute-start(bf16[128,1024]{1,0:T(8,128)(2,1)} %collective-permute-done.12.refs_7_), channel_id=1, source_target_pairs={{0,1},{1,0},{2,3},{3,2},{4,5},{5,4},{6,7},{7,6},{8,9},{9,8},{10,11... | collective-permute-start | bytes 786440 | tf_op jit(solution)/shard_map/ppermute | solution.py:358
  61.8 0.6 copy-start.8
  62.4 3.7 %collective-permute-start.18 = (bf16[256,128]{1,0:T(8,128)(2,1)S(1)}, bf16[256,128]{1,0:T(8,128)(2,1)S(1)}, u32[]{:S(2)}, u32[]{:S(2)}) collective-permute-start(bf16[256,128]{1,0:T(8,128)(2,1)S(1)} %get-tuple-element.23), channel_id=1, source_target_pairs={{0,1},{1,0},{2,3},{3,2},{4,5},{5,4},{6,7},{7,6},{8,9},{9,8},{10,11... | collective-permute-start | bytes 196616 | tf_op jit(solution)/shard_map/ppermute | solution.py:358
  62.6 9.9 %collective-permute-start.19 = (bf16[256,128]{1,0:T(8,128)(2,1)S(1)}, bf16[256,128]{1,0:T(8,128)(2,1)S(1)}, u32[]{:S(2)}, u32[]{:S(2)}) collective-permute-start(bf16[256,128]{1,0:T(8,128)(2,1)S(1)} %get-tuple-element.24), channel_id=1, source_target_pairs={{0,2},{1,3},{2,0},{3,1},{4,6},{5,7},{6,4},{7,5},{8,10},{9,11},{10,... | collective-permute-start | bytes 196616 | tf_op jit(solution)/shard_map/ppermute | solution.py:358
  63.6 15.0 %collective-permute-start.20 = (bf16[256,128]{1,0:T(8,128)(2,1)}, bf16[256,128]{1,0:T(8,128)(2,1)S(1)}, u32[]{:S(2)}, u32[]{:S(2)}) collective-permute-start(bf16[256,128]{1,0:T(8,128)(2,1)} %get-tuple-element.25), channel_id=1, source_target_pairs={{0,3},{1,2},{2,1},{3,0},{4,7},{5,6},{6,5},{7,4},{8,11},{9,10},{10,... | collective-permute-start | bytes 196616 | tf_op jit(solution)/shard_map/ppermute | solution.py:358
  64.3 14.3 %collective-permute-start.21 = (bf16[256,128]{1,0:T(8,128)(2,1)}, bf16[256,128]{1,0:T(8,128)(2,1)S(1)}, u32[]{:S(2)}, u32[]{:S(2)}) collective-permute-start(bf16[256,128]{1,0:T(8,128)(2,1)} %get-tuple-element.26), channel_id=1, source_target_pairs={{0,4},{1,5},{2,6},{3,7},{4,0},{5,1},{6,2},{7,3},{8,12},{9,13},{10,... | collective-permute-start | bytes 196616 | tf_op jit(solution)/shard_map/ppermute | solution.py:358
  65.8 12.8 %collective-permute-start.22 = (bf16[256,128]{1,0:T(8,128)(2,1)}, bf16[256,128]{1,0:T(8,128)(2,1)S(1)}, u32[]{:S(2)}, u32[]{:S(2)}) collective-permute-start(bf16[256,128]{1,0:T(8,128)(2,1)} %get-tuple-element.27), channel_id=1, source_target_pairs={{0,5},{1,4},{2,7},{3,6},{4,1},{5,0},{6,3},{7,2},{8,13},{9,12},{10,... | collective-permute-start | bytes 196616 | tf_op jit(solution)/shard_map/ppermute | solution.py:358
  66.1 12.5 %collective-permute-start.23 = (bf16[256,128]{1,0:T(8,128)(2,1)S(1)}, bf16[256,128]{1,0:T(8,128)(2,1)S(1)}, u32[]{:S(2)}, u32[]{:S(2)}) collective-permute-start(bf16[256,128]{1,0:T(8,128)(2,1)S(1)} %get-tuple-element.28), channel_id=1, source_target_pairs={{0,6},{1,7},{2,4},{3,5},{4,2},{5,3},{6,0},{7,1},{8,14},{9,15},{10,... | collective-permute-start | bytes 196616 | tf_op jit(solution)/shard_map/ppermute | solution.py:358
  72.5 6.1 %collective-permute-start.24 = (bf16[256,128]{1,0:T(8,128)(2,1)S(1)}, bf16[256,128]{1,0:T(8,128)(2,1)S(1)}, u32[]{:S(2)}, u32[]{:S(2)}) collective-permute-start(bf16[256,128]{1,0:T(8,128)(2,1)S(1)} %get-tuple-element.29), channel_id=1, source_target_pairs={{0,7},{1,6},{2,5},{3,4},{4,3},{5,2},{6,1},{7,0},{8,15},{9,14},{10,... | collective-permute-start | bytes 196616 | tf_op jit(solution)/shard_map/ppermute | solution.py:358
  74.1 4.6 %copy-start.1 = (bf16[1,1024,1024]{2,1,0:T(8,128)(2,1)S(1)}, bf16[1,1024,1024]{2,1,0:T(8,128)(2,1)}, u32[]{:S(2)}) copy-start(bf16[1,1024,1024]{2,1,0:T(8,128)(2,1)} %param.10) | copy-start | bytes 6291460
  74.1 4.6 %copy-start.9 = (bf16[256,128]{1,0:T(8,128)(2,1)S(1)}, bf16[256,128]{1,0:T(8,128)(2,1)}, u32[]{:S(2)}) copy-start(bf16[256,128]{1,0:T(8,128)(2,1)} %copy-done.8) | copy-start | bytes 196612
  80.0 14.6 %collective-permute-start.25 = (bf16[256,1024]{1,0:T(8,128)(2,1)S(1)}, bf16[256,1024]{1,0:T(8,128)(2,1)S(1)}, u32[]{:S(2)}, u32[]{:S(2)}) collective-permute-start(bf16[256,1024]{1,0:T(8,128)(2,1)S(1)} %get-tuple-element.32), channel_id=1, source_target_pairs={{0,8},{8,0},{16,24},{24,16},{1,9},{9,1},{17,25},{25,17},{2,10},{10... | collective-permute-start | bytes 1572872 | tf_op jit(solution)/shard_map/ppermute | solution.py:408
  81.6 16.6 %collective-permute-start.26 = (bf16[256,1024]{1,0:T(8,128)(2,1)S(1)}, bf16[256,1024]{1,0:T(8,128)(2,1)S(1)}, u32[]{:S(2)}, u32[]{:S(2)}) collective-permute-start(bf16[256,1024]{1,0:T(8,128)(2,1)S(1)} %get-tuple-element.33), channel_id=1, source_target_pairs={{8,16},{16,8},{9,17},{17,9},{10,18},{18,10},{11,19},{19,11},{12,20... | collective-permute-start | bytes 1572872 | tf_op jit(solution)/shard_map/ppermute | solution.py:408
